TPU v7x, 32 devices: a whole 2x2x4 slice. The times are simulated.
32 devices in a mesh: grp: 2 (over y), sec: 4 (over z), mpo: 4 (over x, core).
Axes of the slice: x: 2, y: 2, z: 4, core: 2. Of those that a mesh axis runs over, the one named last changes fastest.
Arguments:
- wave_blocks: bfloat16 [8, 512, 512], P(('grp', 'sec')), parts along dimension 0, may hold values from -6 to 6
- left_env: bfloat16 [8, 12, 512, 512], P(('grp', 'sec'), 'mpo'), parts along dimension 0, may hold values from -0.25 to 0.25
- right_env: bfloat16 [8, 12, 512, 512], P(('grp', 'sec'), 'mpo'), parts along dimension 0, may hold values from -0.25 to 0.25
- term_class: int32 [8, 12], P(('grp', 'sec'), 'mpo'), parts along dimension 0, may hold values from 0 to 4
- term_id: int32 [8, 12], P(('grp', 'sec'), 'mpo'), parts along dimension 0, may hold values from 0 to 49
- block_dims: int32 [8, 2], P('grp'), parts along dimension 0, may hold values from 1 to 8, as said below
- pair_table: int32 [8, 5], P('grp'), parts along dimension 0, may hold values from 0 to 3
- mpo_coef: float32 [50], replicated, may hold values from 0.5 to 1.5
Outputs:
- sigma: bfloat16 [8, 512, 512], P('grp', 'sec', 'mpo'), parts along dimension 0
There are 2 independent parts, one for each index of `grp`. A program takes and returns all parts, laid end to end along the dimension named above; an argument that names none is the same for every part. Nothing has to cross between parts.
Inputs may be any that keep to these rules, and one draw needn't show every extreme that they name: `block_dims`: some block has 8 units of left states and some block has 8 units of right states.
All inputs are finite; a program needn't handle non-finite values.
Results may differ from a plain program's by a relative error of at most 0.013.
Values may be sent and summed in bfloat16 or wider, within the bound.
No kernel may reach another device: no remote copies, remote signals or barrier semaphores. Data moves between devices by JAX's collectives and lax.ppermute only.
A program may use at most 64 MiB of HBM per device.

v0:
```python
import jax
import jax.numpy as jnp
from jax import lax
from jax.sharding import PartitionSpec as P


def on_device(
    wave_blocks, left_env, right_env, term_class, term_id, block_dims, pair_table, mpo_coef
):
    sec_count = lax.axis_size("sec")
    mpo_count = lax.axis_size("mpo")
    local_blocks = wave_blocks.shape[0]
    block_width = wave_blocks.shape[1]
    total_blocks = block_dims.shape[0]
    classes = pair_table.shape[1]
    tile_states = block_width // 8
    positions = jnp.arange(block_width)
    first = lax.axis_index("sec") * local_blocks
    own_dims = lax.dynamic_slice_in_dim(block_dims, first, local_blocks, 0)
    row_ok = positions[None, :] < own_dims[:, 0:1] * tile_states
    col_ok = positions[None, :] < own_dims[:, 1:2] * tile_states
    masked = jnp.where(
        row_ok[:, :, None] & col_ok[:, None, :], wave_blocks, jnp.zeros_like(wave_blocks)
    )
    left_part = jnp.einsum(
        "bjxy,byz->bjxz", left_env, masked, preferred_element_type=jnp.float32
    ).astype(jnp.bfloat16)
    contrib = jnp.einsum(
        "bjxz,bjwz->bjxw", left_part, right_env, preferred_element_type=jnp.float32
    )
    weights = jnp.sum(
        jnp.where(
            term_id[:, :, None] == jnp.arange(mpo_coef.shape[0])[None, None, :],
            mpo_coef[None, None, :],
            0.0,
        ),
        axis=-1,
    )
    picks = (term_class[:, :, None] == jnp.arange(classes)[None, None, :]).astype(
        jnp.float32
    ) * weights[:, :, None]
    grouped = jnp.einsum("bjc,bjxw->bcxw", picks, contrib, precision=lax.Precision.HIGHEST).astype(
        jnp.bfloat16
    )
    targets = pair_table.reshape(-1)
    routing = targets[None, :] == jnp.arange(total_blocks)[:, None]
    strip_rows = block_width // sec_count
    strip_cols = block_width // mpo_count
    outgoing = grouped.reshape(local_blocks * classes, block_width, block_width)
    arrived = lax.all_to_all(
        lax.all_to_all(outgoing, "sec", split_axis=1, concat_axis=0, tiled=True),
        "mpo",
        split_axis=2,
        concat_axis=0,
        tiled=True,
    )
    arrived = arrived.reshape(mpo_count, total_blocks * classes, strip_rows, strip_cols)
    summed = jnp.einsum(
        "tk,mkrw->trw", routing.astype(jnp.bfloat16), arrived, preferred_element_type=jnp.float32
    )
    row_index = lax.axis_index("sec") * strip_rows + jnp.arange(strip_rows)
    col_index = lax.axis_index("mpo") * strip_cols + jnp.arange(strip_cols)
    rows_in = row_index[None, :] < block_dims[:, 0:1] * tile_states
    cols_in = col_index[None, :] < block_dims[:, 1:2] * tile_states
    inside = rows_in[:, :, None] & cols_in[:, None, :]
    return jnp.where(inside, summed, 0.0).astype(jnp.bfloat16)


def solution(mesh):
    placed = (
        P(("grp", "sec"), None, None),
        P(("grp", "sec"), "mpo", None, None),
        P(("grp", "sec"), "mpo", None, None),
        P(("grp", "sec"), "mpo"),
        P(("grp", "sec"), "mpo"),
        P("grp", None),
        P("grp", None),
        P(),
    )
    return jax.shard_map(
        on_device, mesh=mesh, in_specs=placed, out_specs=P("grp", "sec", "mpo"), check_vma=False
    )
```

profile of v0, /device:TPU:0, one launch (start us, length us, event | category | flops | bytes accessed | tf_op | source)
XLA Modules:
  0.0 174.4 jit_solution(12551963304396550498)
XLA Ops:
  0.0 0.0 copy-start
  0.0 0.9 constant_dynamic-slice_fusion
  0.9 0.5 fusion.35
  2.7 0.8 fusion.27
  3.5 0.0 copy-done
  3.5 0.0 copy-start.3
  3.5 5.3 %fusion.5 = f32[3,512,512]{2,1,0:T(8,128)} fusion(bf16[1,3,512,512]{3,2,1,0:T(8,128)(2,1)S(1)} %copy-done, bf16[1,3,512,512]{3,2,1,0:T(8,128)(2,1)} %param.9, bf16[1,512,512]{2,1,0:T(8,128)(2,1)} %param.8, pred[512]{0:T(512)(128)(4,1)S(1)} %get-tuple-element.9, pred[512]{0:T(512)(128)(4,1)S(1)} %get-tuple-element.10), kind=kOutput, calls=%fused_computation.5 | convolution fusion | flops 1611923456 | bytes 6816768 | tf_op jit(solution)/shard_map/bjxz,bjwz->bjxw/dot_general | solution.py:28
  8.9 0.0 copy-done.3
  8.9 13.2 %fusion.2 = bf16[5,512,512]{2,0,1:T(8,128)(2,1)S(1)} fusion(f32[3,512,512]{2,1,0:T(8,128)} %fusion.5, f32[3]{0:T(128)S(1)} %fusion.27, s32[3]{0:T(128)S(1)} %bitcast.44), kind=kOutput, calls=%fused_computation.3 | convolution fusion | flops 48496672 | bytes 5767192 | tf_op jit(solution)/shard_map/bjc,bjxw->bcxw/dot_general | solution.py:42
  22.0 99.3 %all_to_all.27 = bf16[5,512,512]{2,0,1:T(8,128)(2,1)S(1)} all-to-all(bf16[5,512,512]{2,0,1:T(8,128)(2,1)S(1)} %fusion.2), channel_id=1, replica_groups=mesh['grp'=2,'sec'=4,'mpo'=4] {'sec'}, dimensions={1} | all-to-all | bytes 5242880 | tf_op jit(solution)/shard_map/all_to_all | solution.py:51
  121.3 2.6 %copy.23 = bf16[5,4,128,512]{3,2,0,1:T(8,128)(2,1)} copy(bf16[5,4,128,512]{3,0,2,1:T(8,128)(2,1)S(1)} %bitcast.42) | data formatting | bytes 5242880 | tf_op jit(solution)/shard_map/all_to_all | solution.py:51
  123.9 4.7 %copy.24 = bf16[20,128,512]{1,0,2:T(8,128)(2,1)} copy(bf16[20,128,512]{2,1,0:T(8,128)(2,1)} %bitcast.43) | data formatting | bytes 5242880 | tf_op jit(solution)/shard_map/all_to_all | solution.py:51
  128.6 0.0 copy-start.2
  128.6 0.0 copy-start.1
  128.6 4.8 %all-to-all-start.1 = ((bf16[20,128,512]{1,0,2:T(8,128)(2,1)}), bf16[20,128,512]{1,0,2:T(8,128)(2,1)}, u32[]{:S(2)}, u32[]{:S(2)}) async-start(bf16[20,128,512]{1,0,2:T(8,128)(2,1)} %copy.24), calls=%async_computation.1 | async-start | bytes 6291456 | tf_op jit(solution)/shard_map/all_to_all | solution.py:50
  133.4 0.0 copy-done.2
  133.4 0.1 eq.58
  133.5 0.0 copy-done.1
  133.5 0.1 broadcast_compare_fusion.1
  133.6 0.1 broadcast_compare_fusion
  133.7 36.7 %all-to-all-done.1 = bf16[20,128,512]{1,0,2:T(8,128)(2,1)} async-done(((bf16[20,128,512]{1,0,2:T(8,128)(2,1)}), bf16[20,128,512]{1,0,2:T(8,128)(2,1)}, u32[]{:S(2)}, u32[]{:S(2)}) %all-to-all-start.1) | async-done | bytes 2621472 | tf_op jit(solution)/shard_map/all_to_all | solution.py:50
  170.4 2.4 %convert_reduce_fusion = bf16[20,128,128]{1,0,2:T(8,128)(2,1)S(1)} fusion(bf16[20,128,4,128]{1,0,3,2:T(8,128)(2,1)} %bitcast.19), kind=kLoop, calls=%fused_computation | loop fusion | flops 2293760 | bytes 3276800 | tf_op jit(solution)/shard_map/tk,mkrw->trw/reduce_sum | solution.py:58
  172.7 0.7 copy.26
  173.4 0.3 fusion.13
  173.7 0.7 copy.27
  (4 shorter events, 0.0 us)
Async XLA Ops:
  0.0 3.5 %copy-start = (bf16[1,3,512,512]{3,2,1,0:T(8,128)(2,1)S(1)}, bf16[1,3,512,512]{3,2,1,0:T(8,128)(2,1)}, u32[]{:S(2)}) copy-start(bf16[1,3,512,512]{3,2,1,0:T(8,128)(2,1)} %param.10) | copy-start | bytes 4718596
  3.5 5.3 %copy-start.3 = (s32[1,3]{1,0:T(1,128)S(1)}, s32[1,3]{1,0:T(1,128)}, u32[]{:S(2)}) copy-start(s32[1,3]{1,0:T(1,128)} %param.11) | copy-start | bytes 40
  128.6 4.8 %copy-start.2 = (s32[4,5]{1,0:T(4,128)S(1)}, s32[4,5]{1,0:T(4,128)}, u32[]{:S(2)}) copy-start(s32[4,5]{1,0:T(4,128)} %param.14) | copy-start | bytes 244
  128.6 4.9 %copy-start.1 = (s32[4,2]{0,1:T(2,128)S(1)}, s32[4,2]{0,1:T(2,128)}, u32[]{:S(2)}) copy-start(s32[4,2]{0,1:T(2,128)} %param.13) | copy-start | bytes 100
  128.6 41.8 %all-to-all-start.1 = ((bf16[20,128,512]{1,0,2:T(8,128)(2,1)}), bf16[20,128,512]{1,0,2:T(8,128)(2,1)}, u32[]{:S(2)}, u32[]{:S(2)}) async-start(bf16[20,128,512]{1,0,2:T(8,128)(2,1)} %copy.24), calls=%async_computation.1 | async-start | bytes 6291456 | tf_op jit(solution)/shard_map/all_to_all | solution.py:50
where the time goes:
time: 175 us; the launch traced here: 174 us
  blocking collectives  99.3 us (57%)
  waiting for transfers between devices  36.7 us (21%)
  matrix products  18.8 us (11%)
  local copies, waits for them, and re-layouts  10.1 us (6%)
  starting transfers between devices  4.77 us (3%)
  other arithmetic  3.4 us (2%)
    all_to_all x1, blocking collectives, on_device(): lax.all_to_all(outgoing, 'sec', split_axis=1, concat_axis=0, tiled=True)  99.3 us
    all_to_all x1, waiting for transfers between devices, on_device(): lax.all_to_all(lax.all_to_all(outgoing, 'sec', split_axis=1, concat_axis=...  36.7 us
    dot_general x1, matrix products, on_device(): jnp.einsum('bjc,bjxw->bcxw', picks, contrib, precision=lax.Precision.HIGH...  13.2 us
    all_to_all x2, local copies, waits for them, and re-layouts, on_device(): lax.all_to_all(outgoing, 'sec', split_axis=1, concat_axis=0, tiled=True)  7.28 us
    dot_general x1, matrix products, on_device(): jnp.einsum('bjxz,bjwz->bjxw', left_part, right_env, preferred_element_typ...  5.33 us
    all_to_all x1, starting transfers between devices, on_device(): lax.all_to_all(lax.all_to_all(outgoing, 'sec', split_axis=1, concat_axis=...  4.77 us
  transfers between devices with their start and end apart: 1, of which 1 were waited for; matrix products, arithmetic and copies ran while one was open for 0% of the time, Pallas kernels for 0%

commit v1 on v0

--- a/solution.py
+++ b/solution.py
@@ -1,10 +1,184 @@
+import functools
+
 import jax
 import jax.numpy as jnp
 from jax import lax
+from jax.experimental import pallas as pl
+from jax.experimental.pallas import tpu as pltpu
 from jax.sharding import PartitionSpec as P
 
-
-def on_device(
+CHUNKS = 2
+COLUMN_ORDER = (3, 1, 2, 0)
+
+
+def term_kernel(
+    cls_ref,
+    tid_ref,
+    pair_ref,
+    dims_ref,
+    coef_ref,
+    wave_hbm,
+    left_hbm,
+    right_hbm,
+    *rest,
+    chunks,
+    terms,
+    targets,
+):
+    outs, (wave, left, right, wave_sem, left_sem, right_sem) = rest[:-6], rest[-6:]
+    width = wave.shape[0]
+    strip = width // 4
+    rows = strip // chunks
+    sec = lax.axis_index("sec")
+    mpo = lax.axis_index("mpo")
+
+    wave_copy = pltpu.make_async_copy(wave_hbm.at[0], wave, wave_sem)
+    wave_copy.start()
+    left_copies, right_copies = [], []
+    for j in range(terms):
+        for q in range(4):
+            src = pl.multiple_of((sec ^ q) * strip, strip)
+            copy = pltpu.make_async_copy(
+                left_hbm.at[0, j, pl.ds(src, strip)],
+                left.at[j, pl.ds(q * strip, strip)],
+                left_sem.at[j, q],
+            )
+            copy.start()
+            left_copies.append(copy)
+    for j in range(terms):
+        for p, r in enumerate(COLUMN_ORDER):
+            src = pl.multiple_of((mpo ^ r) * strip, strip)
+            copy = pltpu.make_async_copy(
+                right_hbm.at[0, j, pl.ds(src, strip)],
+                right.at[j, pl.ds(p * strip, strip)],
+                right_sem.at[j, p],
+            )
+            copy.start()
+            right_copies.append(copy)
+
+    unit = width // 8
+    weights, target = [], []
+    for j in range(terms):
+        weights.append(coef_ref[tid_ref[0, j]])
+        target.append(pair_ref[sec, cls_ref[0, j]])
+    scale = [
+        [jnp.where(target[j] == t, weights[j], 0.0) for j in range(terms)] for t in range(targets)
+    ]
+
+    wave_copy.wait()
+    row_pos = lax.broadcasted_iota(jnp.int32, (width, width), 0)
+    col_pos = lax.broadcasted_iota(jnp.int32, (width, width), 1)
+    inside = (row_pos < dims_ref[sec, 0] * unit) & (col_pos < dims_ref[sec, 1] * unit)
+    wave[...] = jnp.where(inside, wave[...].astype(jnp.float32), 0.0).astype(jnp.bfloat16)
+    for copy in left_copies:
+        copy.wait()
+    for h in range(chunks):
+        parts = []
+        for j in range(terms):
+            own = jnp.concatenate(
+                [left[j, q * strip + h * rows : q * strip + (h + 1) * rows, :] for q in range(4)],
+                axis=0,
+            )
+            half = jnp.dot(own, wave[...], preferred_element_type=jnp.float32).astype(jnp.bfloat16)
+            if h == 0:
+                for copy in right_copies[4 * j : 4 * j + 4]:
+                    copy.wait()
+            parts.append(
+                lax.dot_general(
+                    half, right[j], (((1,), (1,)), ((), ())), preferred_element_type=jnp.float32
+                )
+            )
+        for p in range(4):
+            for t in range(targets):
+                total = scale[t][0] * parts[0][:, p * strip : (p + 1) * strip]
+                for j in range(1, terms):
+                    total += scale[t][j] * parts[j][:, p * strip : (p + 1) * strip]
+                outs[4 * h + p][:, t] = total.astype(jnp.bfloat16).reshape(4, rows, strip)
+
+
+def final_kernel(dims_ref, *rest, chunks):
+    pieces, out_ref = rest[:-1], rest[-1]
+    targets, strip, _ = out_ref.shape
+    rows = strip // chunks
+    per = len(pieces) // chunks
+    unit = dims_ref.shape[0] * strip // 8
+    sec = lax.axis_index("sec")
+    mpo = lax.axis_index("mpo")
+    col_pos = mpo * strip + lax.broadcasted_iota(jnp.int32, (rows, strip), 1)
+    for h in range(chunks):
+        row_pos = sec * strip + h * rows + lax.broadcasted_iota(jnp.int32, (rows, strip), 0)
+        for t in range(targets):
+            total = pieces[per * h][t].astype(jnp.float32)
+            for piece in pieces[per * h + 1 : per * (h + 1)]:
+                total += piece[t].astype(jnp.float32)
+            inside = (row_pos < dims_ref[t, 0] * unit) & (col_pos < dims_ref[t, 1] * unit)
+            out_ref[t, h * rows : (h + 1) * rows, :] = jnp.where(inside, total, 0.0).astype(
+                jnp.bfloat16
+            )
+
+
+def add(*arrays):
+    total = arrays[0].astype(jnp.float32)
+    for array in arrays[1:]:
+        total = total + array.astype(jnp.float32)
+    return total.astype(jnp.bfloat16)
+
+
+def swap(array, axis, mask):
+    return lax.ppermute(array, axis, [(i, i ^ mask) for i in range(lax.axis_size(axis))])
+
+
+def by_targets(
+    wave_blocks, left_env, right_env, term_class, term_id, block_dims, pair_table, mpo_coef
+):
+    width = wave_blocks.shape[1]
+    terms = left_env.shape[1]
+    targets = block_dims.shape[0]
+    strip = width // 4
+    rows = strip // CHUNKS
+    smem = pl.BlockSpec(memory_space=pltpu.SMEM)
+    vmem = pl.BlockSpec(memory_space=pltpu.VMEM)
+    hbm = pl.BlockSpec(memory_space=pl.ANY)
+    shape = jax.ShapeDtypeStruct((4, targets, rows, strip), jnp.bfloat16)
+    outs = pl.pallas_call(
+        functools.partial(term_kernel, chunks=CHUNKS, terms=terms, targets=targets),
+        out_shape=[shape] * (4 * CHUNKS),
+        in_specs=[smem] * 5 + [hbm] * 3,
+        out_specs=[vmem] * (4 * CHUNKS),
+        scratch_shapes=[
+            pltpu.VMEM((width, width), jnp.bfloat16),
+            pltpu.VMEM((terms, width, width), jnp.bfloat16),
+            pltpu.VMEM((terms, width, width), jnp.bfloat16),
+            pltpu.SemaphoreType.DMA,
+            pltpu.SemaphoreType.DMA((terms, 4)),
+            pltpu.SemaphoreType.DMA((terms, 4)),
+        ],
+        compiler_params=pltpu.CompilerParams(vmem_limit_bytes=40 * 1024 * 1024),
+        cost_estimate=pl.CostEstimate(
+            flops=4 * terms * width**3, bytes_accessed=6 * 1024 * 1024, transcendentals=0
+        ),
+        name="terms",
+    )(term_class, term_id, pair_table, block_dims, mpo_coef, wave_blocks, left_env, right_env)
+    pieces = []
+    for h in range(CHUNKS):
+        far_send, near_send, far_keep, near_keep = outs[4 * h : 4 * h + 4]
+        far = add(far_keep, swap(far_send, "mpo", 1))
+        near = swap(near_send, "mpo", 1)
+        crossed = swap(far, "mpo", 2)
+        own = [add(near_keep[q], near[q], crossed[q]) for q in range(4)]
+        pieces.append(own[0])
+        for q in (2, 3, 1):
+            pieces.append(swap(own[q], "sec", q))
+    return pl.pallas_call(
+        functools.partial(final_kernel, chunks=CHUNKS),
+        out_shape=jax.ShapeDtypeStruct((targets, strip, strip), jnp.bfloat16),
+        in_specs=[smem] + [vmem] * len(pieces),
+        out_specs=vmem,
+        name="final",
+    )(block_dims, *pieces)
+
+
+def by_classes(
     wave_blocks, left_env, right_env, term_class, term_id, block_dims, pair_table, mpo_coef
 ):
     sec_count = lax.axis_size("sec")
@@ -77,6 +251,14 @@
         P("grp", None),
         P(),
     )
+
+    def on_device(*arrays):
+        wave_blocks, block_dims = arrays[0], arrays[5]
+        small = wave_blocks.shape[0] == 1 and block_dims.shape[0] == 4
+        if small and mesh.shape["sec"] == 4 and mesh.shape["mpo"] == 4:
+            return by_targets(*arrays)
+        return by_classes(*arrays)
+
     return jax.shard_map(
         on_device, mesh=mesh, in_specs=placed, out_specs=P("grp", "sec", "mpo"), check_vma=False
     )

time: 175 us -> 46.9 us (0.27)
  blocking collectives: 99.3 us -> 0 us
  waiting for transfers between devices: 36.7 us -> 13.6 us
  matrix products: 18.8 us -> 0 us
  Pallas kernels: 0 us -> 10 us
  starting transfers between devices: 4.77 us -> 13.3 us
  local copies, waits for them, and re-layouts: 10.1 us -> 7.89 us
  other arithmetic: 3.4 us -> 1.63 us
    all_to_all x1 -> x0, blocking collectives: 99.3 us -> none  [on_device(): lax.all_to_all(outgoing, 'sec', split_axis=1, concat_axis=0, tiled=True)]
    all_to_all x1 -> x0, waiting for transfers between devices: 36.7 us -> none  [on_device(): lax.all_to_all(lax.all_to_all(outgoing, 'sec', split_axis=1, concat_axis=...]
    dot_general x3 -> x0, matrix products: 18.8 us -> none  [the longest x1 13.2 us: on_device(): jnp.einsum('bjc,bjxw->bcxw', picks, contrib, precision=lax.Precision.HIGH...]
    ppermute x0 -> x12, waiting for transfers between devices: none -> 13.6 us  [swap(): lax.ppermute(array, axis, [(i, i ^ mask) for i in range(lax.axis_size(axi...]
    ppermute x0 -> x12, starting transfers between devices: none -> 13.3 us  [swap(): lax.ppermute(array, axis, [(i, i ^ mask) for i in range(lax.axis_size(axi...]
    pallas_call x0 -> x2, Pallas kernels: none -> 10 us  [the longest x1 8.22 us: by_targets(): pl.pallas_call(functools.partial(term_kernel, chunks=CHUNKS, terms=terms,...]
    unnamed x8 -> x29, local copies, waits for them, and re-layouts: 0.02 us -> 7.89 us
    all_to_all x2 -> x0, local copies, waits for them, and re-layouts: 7.28 us -> none  [on_device(): lax.all_to_all(outgoing, 'sec', split_axis=1, concat_axis=0, tiled=True)]
  transfers between devices with their start and end apart: 1 -> 12, of which waited for: 1 -> 5; matrix products, arithmetic and copies ran while one was open for 0% -> 3% of each run, Pallas kernels for 0% -> 0%
where the time goes in v1:
time: 46.9 us; the launch traced here: 46.6 us
  waiting for transfers between devices  13.6 us (29%)
  starting transfers between devices  13.3 us (28%)
  Pallas kernels  10 us (21%)
  local copies, waits for them, and re-layouts  7.89 us (17%)
  other arithmetic  1.63 us (3%)
    ppermute x12, waiting for transfers between devices, swap(): lax.ppermute(array, axis, [(i, i ^ mask) for i in range(lax.axis_size(axi...  13.6 us
    ppermute x12, starting transfers between devices, swap(): lax.ppermute(array, axis, [(i, i ^ mask) for i in range(lax.axis_size(axi...  13.3 us
    pallas_call x1, Pallas kernels, by_targets(): pl.pallas_call(functools.partial(term_kernel, chunks=CHUNKS, terms=terms,...  8.22 us
    unnamed x29, local copies, waits for them, and re-layouts  7.89 us
    pallas_call x1, Pallas kernels, by_targets(): pl.pallas_call(functools.partial(final_kernel, chunks=CHUNKS), out_shape=...  1.82 us
    convert_element_type x4, other arithmetic, add(): return total.astype(jnp.bfloat16)  1.63 us
  transfers between devices with their start and end apart: 12, of which 5 were waited for; matrix products, arithmetic and copies ran while one was open for 3% of the time, Pallas kernels for 0%

profile of v1, /device:TPU:0, one launch (start us, length us, event | category | flops | bytes accessed | tf_op | source)
XLA Modules:
  0.0 46.6 jit_solution(11805180955514142278)
XLA Ops:
  0.0 0.8 %copy.10.dims_ref = s32[4,2]{1,0:T(4,128)S(1)} copy(s32[4,2]{0,1:T(2,128)} %param.13) | data formatting | bytes 64 | tf_op args[5]
  0.8 0.0 copy-start.1
  0.8 1.4 %copy-done.1 = bf16[1,3,512,512]{3,2,1,0:T(8,128)(2,1)S(1)} copy-done((bf16[1,3,512,512]{3,2,1,0:T(8,128)(2,1)S(1)}, bf16[1,3,512,512]{3,2,1,0:T(8,128)(2,1)}, u32[]{:S(2)}) %copy-start.1) | copy-done | bytes 1572888
  2.2 0.0 copy-start.2
  2.2 1.4 %copy-done.2 = bf16[1,3,512,512]{3,2,1,0:T(8,128)(2,1)S(1)} copy-done((bf16[1,3,512,512]{3,2,1,0:T(8,128)(2,1)S(1)}, bf16[1,3,512,512]{3,2,1,0:T(8,128)(2,1)}, u32[]{:S(2)}) %copy-start.2) | copy-done | bytes 1572888
  3.6 0.0 copy-start.3
  3.6 1.0 %copy-done.3 = bf16[1,512,512]{2,1,0:T(8,128)(2,1)S(1)} copy-done((bf16[1,512,512]{2,1,0:T(8,128)(2,1)S(1)}, bf16[1,512,512]{2,1,0:T(8,128)(2,1)}, u32[]{:S(2)}) %copy-start.3) | copy-done | bytes 524312
  4.6 0.0 copy-start.4
  4.6 0.7 %copy-done.4 = s32[4,5]{1,0:T(4,128)S(1)} copy-done((s32[4,5]{1,0:T(4,128)S(1)}, s32[4,5]{1,0:T(4,128)}, u32[]{:S(2)}) %copy-start.4) | copy-done | bytes 104
  5.3 0.0 copy-start.5
  5.3 0.7 %copy-done.5 = s32[1,3]{1,0:T(1,128)S(1)} copy-done((s32[1,3]{1,0:T(1,128)S(1)}, s32[1,3]{1,0:T(1,128)}, u32[]{:S(2)}) %copy-start.5) | copy-done | bytes 36
  6.0 0.0 copy-start.6
  6.0 0.7 %copy-done.6 = s32[1,3]{1,0:T(1,128)S(1)} copy-done((s32[1,3]{1,0:T(1,128)S(1)}, s32[1,3]{1,0:T(1,128)}, u32[]{:S(2)}) %copy-start.6) | copy-done | bytes 36
  6.6 0.0 copy-start.7
  6.6 0.7 %copy-done.7 = f32[50]{0:T(128)S(1)} copy-done((f32[50]{0:T(128)S(1)}, f32[50]{0:T(128)}, u32[]{:S(2)}) %copy-start.7) | copy-done | bytes 224
  7.3 0.0 copy-start
  7.3 8.2 %terms.1 = (bf16[4,4,64,128]{3,2,1,0:T(8,128)(2,1)S(1)}, bf16[4,4,64,128]{3,2,1,0:T(8,128)(2,1)S(1)}, bf16[4,4,64,128]{3,2,1,0:T(8,128)(2,1)S(1)}, bf16[4,4,64,1...) custom-call(s32[1,3]{1,0:T(1,128)S(1)} %copy-done.5, ...), custom_call_target="tpu_custom_call" | custom-call | flops 1610612736 | bytes 6291456 | tf_op jit(solution)/shard_map/terms/pallas_call | solution.py:143
  15.5 0.0 copy-done
  15.5 0.5 %collective-permute-start.1 = (bf16[4,4,64,128]{3,2,1,0:T(8,128)(2,1)S(1)}, bf16[4,4,64,128]{3,2,1,0:T(8,128)(2,1)S(1)}, u32[]{:S(2)}, u32[]{:S(2)}) collective-permute-start(bf16[4,4,64,128]{3,2,1,0:T(8,128)(2,1)S(1)} %get-tuple-element.16), channel_id=1, source_target_pairs={{0,1},{1,0},{2,3},{3,2},{4,5},{5,4},{6,7},{7,6},{8,9},{9,8},{10,11... | collective-permute-start | bytes 786440 | tf_op jit(solution)/shard_map/ppermute | solution.py:128
  16.0 0.1 collective-permute-start.7
  16.1 0.4 collective-permute-start
  16.5 0.1 collective-permute-start.6
  16.6 0.6 %collective-permute-done.1 = bf16[4,4,64,128]{3,2,1,0:T(8,128)(2,1)S(1)} collective-permute-done((bf16[4,4,64,128]{3,2,1,0:T(8,128)(2,1)S(1)}, bf16[4,4,64,128]{3,2,1,0:T(8,128)(2,1)S(1)}, u32[]{:S(2)}, u32[]{:S(2)}) %collective-permute-start.1) | collective-permute-done | bytes 262176 | tf_op jit(solution)/shard_map/ppermute | solution.py:128
  17.2 0.1 add_convert_fusion.1
  17.3 2.9 %collective-permute-start.2 = (bf16[4,4,64,128]{3,2,1,0:T(8,128)(2,1)S(1)}, bf16[4,4,64,128]{3,2,1,0:T(8,128)(2,1)S(1)}, u32[]{:S(2)}, u32[]{:S(2)}) collective-permute-start(bf16[4,4,64,128]{3,2,1,0:T(8,128)(2,1)S(1)} %add_convert_fusion.1), channel_id=1, source_target_pairs={{0,2},{1,3},{2,0},{3,1},{4,6},{5,7},{6,4},{7,5},{8,10},{9,11},{10,... | collective-permute-start | bytes 786440 | tf_op jit(solution)/shard_map/ppermute | solution.py:128
  20.2 0.0 collective-permute-done.7
  20.2 0.1 add_convert_fusion
  20.3 0.3 collective-permute-start.8
  20.6 0.0 collective-permute-done
  20.6 6.7 %collective-permute-done.2 = bf16[4,4,64,128]{3,2,1,0:T(8,128)(2,1)S(1)} collective-permute-done((bf16[4,4,64,128]{3,2,1,0:T(8,128)(2,1)S(1)}, bf16[4,4,64,128]{3,2,1,0:T(8,128)(2,1)S(1)}, u32[]{:S(2)}, u32[]{:S(2)}) %collective-permute-start.2) | collective-permute-done | bytes 262176 | tf_op jit(solution)/shard_map/ppermute | solution.py:128
  27.3 0.7 %fusion.3 = (bf16[4,64,128]{2,1,0:T(8,128)(2,1)S(1)}, bf16[4,64,128]{2,1,0:T(8,128)(2,1)S(1)}, bf16[4,64,128]{2,1,0:T(8,128)(2,1)S(1)}, bf16[4,64,128]{2,1,0:T(8,128)(2,1)}) fusion(bf16[4,4,64,128]{3,2,1,0:T(8,128)(2,1)S(1)} %collective-permute-done.2, bf16[4,4,64,128]{3,2,1,0:T(8,128)(2,1)S(1)} %collective-permute-done, ...), kind=kLoop, calls=%fused_computation.13 | loop fusion | flops 786432 | bytes 1048576 | tf_op jit(solution)/shard_map/convert_element_type | solution.py:124
  28.0 2.1 %collective-permute-start.5 = (bf16[4,64,128]{2,1,0:T(8,128)(2,1)S(1)}, bf16[4,64,128]{2,1,0:T(8,128)(2,1)S(1)}, u32[]{:S(2)}, u32[]{:S(2)}) collective-permute-start(bf16[4,64,128]{2,1,0:T(8,128)(2,1)S(1)} %get-tuple-element.25), channel_id=1, source_target_pairs={{0,4},{4,0},{8,12},{12,8},{1,5},{5,1},{9,13},{13,9},{2,6},{6,2},{1... | collective-permute-start | bytes 196616 | tf_op jit(solution)/shard_map/ppermute | solution.py:128
  30.2 2.5 %collective-permute-start.4 = (bf16[4,64,128]{2,1,0:T(8,128)(2,1)S(1)}, bf16[4,64,128]{2,1,0:T(8,128)(2,1)S(1)}, u32[]{:S(2)}, u32[]{:S(2)}) collective-permute-start(bf16[4,64,128]{2,1,0:T(8,128)(2,1)S(1)} %get-tuple-element.26), channel_id=1, source_target_pairs={{0,12},{4,8},{8,4},{12,0},{1,13},{5,9},{9,5},{13,1},{2,14},{6,10},... | collective-permute-start | bytes 196616 | tf_op jit(solution)/shard_map/ppermute | solution.py:128
  32.6 0.1 collective-permute-start.3
  32.8 0.0 collective-permute-done.6
  32.8 0.0 collective-permute-done.8
  32.8 0.7 %fusion.7 = (bf16[4,64,128]{2,1,0:T(8,128)(2,1)S(1)}, bf16[4,64,128]{2,1,0:T(8,128)(2,1)S(1)}, bf16[4,64,128]{2,1,0:T(8,128)(2,1)S(1)}, bf16[4,64,128]{2,1,0:T(8,128)(2,1)}) fusion(bf16[4,4,64,128]{3,2,1,0:T(8,128)(2,1)S(1)} %collective-permute-done.8, bf16[4,4,64,128]{3,2,1,0:T(8,128)(2,1)S(1)} %collective-permute-done.6, ...), kind=kLoop, calls=%fused_computation.17 | loop fusion | flops 786432 | bytes 1048576 | tf_op jit(solution)/shard_map/convert_element_type | solution.py:124
  33.5 1.8 %collective-permute-start.11 = (bf16[4,64,128]{2,1,0:T(8,128)(2,1)S(1)}, bf16[4,64,128]{2,1,0:T(8,128)(2,1)S(1)}, u32[]{:S(2)}, u32[]{:S(2)}) collective-permute-start(bf16[4,64,128]{2,1,0:T(8,128)(2,1)S(1)} %get-tuple-element.21), channel_id=1, source_target_pairs={{0,4},{4,0},{8,12},{12,8},{1,5},{5,1},{9,13},{13,9},{2,6},{6,2},{1... | collective-permute-start | bytes 196616 | tf_op jit(solution)/shard_map/ppermute | solution.py:128
  35.3 2.5 %collective-permute-start.10 = (bf16[4,64,128]{2,1,0:T(8,128)(2,1)S(1)}, bf16[4,64,128]{2,1,0:T(8,128)(2,1)S(1)}, u32[]{:S(2)}, u32[]{:S(2)}) collective-permute-start(bf16[4,64,128]{2,1,0:T(8,128)(2,1)S(1)} %get-tuple-element.22), channel_id=1, source_target_pairs={{0,12},{4,8},{8,4},{12,0},{1,13},{5,9},{9,5},{13,1},{2,14},{6,10},... | collective-permute-start | bytes 196616 | tf_op jit(solution)/shard_map/ppermute | solution.py:128
  37.8 0.0 collective-permute-done.5.rest_3_
  37.8 0.0 copy-start.8
  37.8 0.0 collective-permute-start.9
  37.8 0.0 collective-permute-done.4.rest_2_
  37.8 0.0 copy-start.9
  37.8 1.9 %collective-permute-done.3.rest_1_ = bf16[4,64,128]{2,1,0:T(8,128)(2,1)S(1)} collective-permute-done((bf16[4,64,128]{2,1,0:T(8,128)(2,1)S(1)}, bf16[4,64,128]{2,1,0:T(8,128)(2,1)S(1)}, u32[]{:S(2)}, u32[]{:S(2)}) %collective-permute-start.3) | collective-permute-done | bytes 65568 | tf_op jit(solution)/shard_map/ppermute | solution.py:128
  39.7 0.0 copy-start.10
  39.7 0.0 collective-permute-done.11.rest_7_
  39.7 0.0 copy-start.11
  39.7 1.8 %collective-permute-done.10.rest_6_ = bf16[4,64,128]{2,1,0:T(8,128)(2,1)S(1)} collective-permute-done((bf16[4,64,128]{2,1,0:T(8,128)(2,1)S(1)}, bf16[4,64,128]{2,1,0:T(8,128)(2,1)S(1)}, u32[]{:S(2)}, u32[]{:S(2)}) %collective-permute-start.10) | collective-permute-done | bytes 65568 | tf_op jit(solution)/shard_map/ppermute | solution.py:128
  41.5 0.0 copy-start.12
  41.5 2.6 %collective-permute-done.9.rest_5_ = bf16[4,64,128]{2,1,0:T(8,128)(2,1)S(1)} collective-permute-done((bf16[4,64,128]{2,1,0:T(8,128)(2,1)S(1)}, bf16[4,64,128]{2,1,0:T(8,128)(2,1)S(1)}, u32[]{:S(2)}, u32[]{:S(2)}) %collective-permute-start.9) | collective-permute-done | bytes 65568 | tf_op jit(solution)/shard_map/ppermute | solution.py:128
  44.1 0.0 copy-start.13
  44.1 0.0 copy-done.8
  44.1 0.0 copy-done.9
  44.1 0.0 copy-done.10
  44.1 0.0 copy-done.11
  44.1 0.0 copy-done.12
  44.2 0.6 %copy-done.13 = bf16[4,64,128]{2,1,0:T(8,128)(2,1)} copy-done((bf16[4,64,128]{2,1,0:T(8,128)(2,1)}, bf16[4,64,128]{2,1,0:T(8,128)(2,1)S(1)}, u32[]{:S(2)}) %copy-start.13) | copy-done | bytes 65560
  44.8 1.8 %final.1 = bf16[4,128,128]{2,1,0:T(8,128)(2,1)} custom-call(s32[4,2]{1,0:T(4,128)} %copy-done, bf16[4,64,128]{2,1,0:T(8,128)(2,1)} %get-tuple-element.28.rest_0_, bf16[4,64,128]{2,1,0:T(8,128)(2,1)} %copy-done.10, bf16[4,64,128]{2,1,0:T(8,128)(2,1)} %copy-done.9, bf16[4,64,128]{2,1,0:T(8,128)(2,1)} %copy-done.8, ...), custom_call_target="tpu_custom_call" | custom-call | tf_op jit(solution)/shard_map/final/pallas_call | solution.py:172
Async XLA Ops:
  0.8 1.4 %copy-start.1 = (bf16[1,3,512,512]{3,2,1,0:T(8,128)(2,1)S(1)}, bf16[1,3,512,512]{3,2,1,0:T(8,128)(2,1)}, u32[]{:S(2)}) copy-start(bf16[1,3,512,512]{3,2,1,0:T(8,128)(2,1)} %left_hbm.1) | copy-start | bytes 4718596
  2.2 1.4 %copy-start.2 = (bf16[1,3,512,512]{3,2,1,0:T(8,128)(2,1)S(1)}, bf16[1,3,512,512]{3,2,1,0:T(8,128)(2,1)}, u32[]{:S(2)}) copy-start(bf16[1,3,512,512]{3,2,1,0:T(8,128)(2,1)} %right_hbm.1) | copy-start | bytes 4718596
  3.6 1.0 %copy-start.3 = (bf16[1,512,512]{2,1,0:T(8,128)(2,1)S(1)}, bf16[1,512,512]{2,1,0:T(8,128)(2,1)}, u32[]{:S(2)}) copy-start(bf16[1,512,512]{2,1,0:T(8,128)(2,1)} %wave_hbm.1) | copy-start | bytes 1572868
  4.6 0.7 %copy-start.4 = (s32[4,5]{1,0:T(4,128)S(1)}, s32[4,5]{1,0:T(4,128)}, u32[]{:S(2)}) copy-start(s32[4,5]{1,0:T(4,128)} %pair_ref.1) | copy-start | bytes 244
  5.3 0.7 %copy-start.5 = (s32[1,3]{1,0:T(1,128)S(1)}, s32[1,3]{1,0:T(1,128)}, u32[]{:S(2)}) copy-start(s32[1,3]{1,0:T(1,128)} %cls_ref.1) | copy-start | bytes 40
  6.0 0.7 %copy-start.6 = (s32[1,3]{1,0:T(1,128)S(1)}, s32[1,3]{1,0:T(1,128)}, u32[]{:S(2)}) copy-start(s32[1,3]{1,0:T(1,128)} %tid_ref.1) | copy-start | bytes 40
  6.6 0.7 %copy-start.7 = (f32[50]{0:T(128)S(1)}, f32[50]{0:T(128)}, u32[]{:S(2)}) copy-start(f32[50]{0:T(128)} %coef_ref.1) | copy-start | bytes 604
  7.3 8.2 %copy-start = (s32[4,2]{1,0:T(4,128)}, s32[4,2]{1,0:T(4,128)S(1)}, u32[]{:S(2)}) copy-start(s32[4,2]{1,0:T(4,128)S(1)} %copy.10.dims_ref) | copy-start | bytes 100
  15.5 1.7 %collective-permute-start.1 = (bf16[4,4,64,128]{3,2,1,0:T(8,128)(2,1)S(1)}, bf16[4,4,64,128]{3,2,1,0:T(8,128)(2,1)S(1)}, u32[]{:S(2)}, u32[]{:S(2)}) collective-permute-start(bf16[4,4,64,128]{3,2,1,0:T(8,128)(2,1)S(1)} %get-tuple-element.16), channel_id=1, source_target_pairs={{0,1},{1,0},{2,3},{3,2},{4,5},{5,4},{6,7},{7,6},{8,9},{9,8},{10,11... | collective-permute-start | bytes 786440 | tf_op jit(solution)/shard_map/ppermute | solution.py:128
  16.0 4.2 %collective-permute-start.7 = (bf16[4,4,64,128]{3,2,1,0:T(8,128)(2,1)S(1)}, bf16[4,4,64,128]{3,2,1,0:T(8,128)(2,1)S(1)}, u32[]{:S(2)}, u32[]{:S(2)}) collective-permute-start(bf16[4,4,64,128]{3,2,1,0:T(8,128)(2,1)S(1)} %get-tuple-element.20), channel_id=1, source_target_pairs={{0,1},{1,0},{2,3},{3,2},{4,5},{5,4},{6,7},{7,6},{8,9},{9,8},{10,11... | collective-permute-start | bytes 786440 | tf_op jit(solution)/shard_map/ppermute | solution.py:128
  16.1 4.5 %collective-permute-start = (bf16[4,4,64,128]{3,2,1,0:T(8,128)(2,1)S(1)}, bf16[4,4,64,128]{3,2,1,0:T(8,128)(2,1)S(1)}, u32[]{:S(2)}, u32[]{:S(2)}) collective-permute-start(bf16[4,4,64,128]{3,2,1,0:T(8,128)(2,1)S(1)} %get-tuple-element.14), channel_id=1, source_target_pairs={{0,1},{1,0},{2,3},{3,2},{4,5},{5,4},{6,7},{7,6},{8,9},{9,8},{10,11... | collective-permute-start | bytes 786440 | tf_op jit(solution)/shard_map/ppermute | solution.py:128
  16.5 16.2 %collective-permute-start.6 = (bf16[4,4,64,128]{3,2,1,0:T(8,128)(2,1)S(1)}, bf16[4,4,64,128]{3,2,1,0:T(8,128)(2,1)S(1)}, u32[]{:S(2)}, u32[]{:S(2)}) collective-permute-start(bf16[4,4,64,128]{3,2,1,0:T(8,128)(2,1)S(1)} %get-tuple-element.18), channel_id=1, source_target_pairs={{0,1},{1,0},{2,3},{3,2},{4,5},{5,4},{6,7},{7,6},{8,9},{9,8},{10,11... | collective-permute-start | bytes 786440 | tf_op jit(solution)/shard_map/ppermute | solution.py:128
  17.3 10.0 %collective-permute-start.2 = (bf16[4,4,64,128]{3,2,1,0:T(8,128)(2,1)S(1)}, bf16[4,4,64,128]{3,2,1,0:T(8,128)(2,1)S(1)}, u32[]{:S(2)}, u32[]{:S(2)}) collective-permute-start(bf16[4,4,64,128]{3,2,1,0:T(8,128)(2,1)S(1)} %add_convert_fusion.1), channel_id=1, source_target_pairs={{0,2},{1,3},{2,0},{3,1},{4,6},{5,7},{6,4},{7,5},{8,10},{9,11},{10,... | collective-permute-start | bytes 786440 | tf_op jit(solution)/shard_map/ppermute | solution.py:128
  20.3 12.5 %collective-permute-start.8 = (bf16[4,4,64,128]{3,2,1,0:T(8,128)(2,1)S(1)}, bf16[4,4,64,128]{3,2,1,0:T(8,128)(2,1)S(1)}, u32[]{:S(2)}, u32[]{:S(2)}) collective-permute-start(bf16[4,4,64,128]{3,2,1,0:T(8,128)(2,1)S(1)} %add_convert_fusion), channel_id=1, source_target_pairs={{0,2},{1,3},{2,0},{3,1},{4,6},{5,7},{6,4},{7,5},{8,10},{9,11},{10,... | collective-permute-start | bytes 786440 | tf_op jit(solution)/shard_map/ppermute | solution.py:128
  28.0 9.8 %collective-permute-start.5 = (bf16[4,64,128]{2,1,0:T(8,128)(2,1)S(1)}, bf16[4,64,128]{2,1,0:T(8,128)(2,1)S(1)}, u32[]{:S(2)}, u32[]{:S(2)}) collective-permute-start(bf16[4,64,128]{2,1,0:T(8,128)(2,1)S(1)} %get-tuple-element.25), channel_id=1, source_target_pairs={{0,4},{4,0},{8,12},{12,8},{1,5},{5,1},{9,13},{13,9},{2,6},{6,2},{1... | collective-permute-start | bytes 196616 | tf_op jit(solution)/shard_map/ppermute | solution.py:128
  30.2 7.6 %collective-permute-start.4 = (bf16[4,64,128]{2,1,0:T(8,128)(2,1)S(1)}, bf16[4,64,128]{2,1,0:T(8,128)(2,1)S(1)}, u32[]{:S(2)}, u32[]{:S(2)}) collective-permute-start(bf16[4,64,128]{2,1,0:T(8,128)(2,1)S(1)} %get-tuple-element.26), channel_id=1, source_target_pairs={{0,12},{4,8},{8,4},{12,0},{1,13},{5,9},{9,5},{13,1},{2,14},{6,10},... | collective-permute-start | bytes 196616 | tf_op jit(solution)/shard_map/ppermute | solution.py:128
  32.6 7.1 %collective-permute-start.3 = (bf16[4,64,128]{2,1,0:T(8,128)(2,1)S(1)}, bf16[4,64,128]{2,1,0:T(8,128)(2,1)S(1)}, u32[]{:S(2)}, u32[]{:S(2)}) collective-permute-start(bf16[4,64,128]{2,1,0:T(8,128)(2,1)S(1)} %get-tuple-element.27), channel_id=1, source_target_pairs={{0,8},{4,12},{8,0},{12,4},{1,9},{5,13},{9,1},{13,5},{2,10},{6,14},... | collective-permute-start | bytes 196616 | tf_op jit(solution)/shard_map/ppermute | solution.py:128
  33.5 6.2 %collective-permute-start.11 = (bf16[4,64,128]{2,1,0:T(8,128)(2,1)S(1)}, bf16[4,64,128]{2,1,0:T(8,128)(2,1)S(1)}, u32[]{:S(2)}, u32[]{:S(2)}) collective-permute-start(bf16[4,64,128]{2,1,0:T(8,128)(2,1)S(1)} %get-tuple-element.21), channel_id=1, source_target_pairs={{0,4},{4,0},{8,12},{12,8},{1,5},{5,1},{9,13},{13,9},{2,6},{6,2},{1... | collective-permute-start | bytes 196616 | tf_op jit(solution)/shard_map/ppermute | solution.py:128
  35.3 6.2 %collective-permute-start.10 = (bf16[4,64,128]{2,1,0:T(8,128)(2,1)S(1)}, bf16[4,64,128]{2,1,0:T(8,128)(2,1)S(1)}, u32[]{:S(2)}, u32[]{:S(2)}) collective-permute-start(bf16[4,64,128]{2,1,0:T(8,128)(2,1)S(1)} %get-tuple-element.22), channel_id=1, source_target_pairs={{0,12},{4,8},{8,4},{12,0},{1,13},{5,9},{9,5},{13,1},{2,14},{6,10},... | collective-permute-start | bytes 196616 | tf_op jit(solution)/shard_map/ppermute | solution.py:128
  37.8 6.3 %copy-start.8 = (bf16[4,64,128]{2,1,0:T(8,128)(2,1)}, bf16[4,64,128]{2,1,0:T(8,128)(2,1)S(1)}, u32[]{:S(2)}) copy-start(bf16[4,64,128]{2,1,0:T(8,128)(2,1)S(1)} %collective-permute-done.5.rest_3_) | copy-start | bytes 196612
  37.8 6.3 %collective-permute-start.9 = (bf16[4,64,128]{2,1,0:T(8,128)(2,1)S(1)}, bf16[4,64,128]{2,1,0:T(8,128)(2,1)S(1)}, u32[]{:S(2)}, u32[]{:S(2)}) collective-permute-start(bf16[4,64,128]{2,1,0:T(8,128)(2,1)S(1)} %get-tuple-element.23), channel_id=1, source_target_pairs={{0,8},{4,12},{8,0},{12,4},{1,9},{5,13},{9,1},{13,5},{2,10},{6,14},... | collective-permute-start | bytes 196616 | tf_op jit(solution)/shard_map/ppermute | solution.py:128
  37.8 6.3 %copy-start.9 = (bf16[4,64,128]{2,1,0:T(8,128)(2,1)}, bf16[4,64,128]{2,1,0:T(8,128)(2,1)S(1)}, u32[]{:S(2)}) copy-start(bf16[4,64,128]{2,1,0:T(8,128)(2,1)S(1)} %collective-permute-done.4.rest_2_) | copy-start | bytes 196612
  39.7 4.4 %copy-start.10 = (bf16[4,64,128]{2,1,0:T(8,128)(2,1)}, bf16[4,64,128]{2,1,0:T(8,128)(2,1)S(1)}, u32[]{:S(2)}) copy-start(bf16[4,64,128]{2,1,0:T(8,128)(2,1)S(1)} %collective-permute-done.3.rest_1_) | copy-start | bytes 196612
  39.7 4.4 %copy-start.11 = (bf16[4,64,128]{2,1,0:T(8,128)(2,1)}, bf16[4,64,128]{2,1,0:T(8,128)(2,1)S(1)}, u32[]{:S(2)}) copy-start(bf16[4,64,128]{2,1,0:T(8,128)(2,1)S(1)} %collective-permute-done.11.rest_7_) | copy-start | bytes 196612
  41.5 2.7 %copy-start.12 = (bf16[4,64,128]{2,1,0:T(8,128)(2,1)}, bf16[4,64,128]{2,1,0:T(8,128)(2,1)S(1)}, u32[]{:S(2)}) copy-start(bf16[4,64,128]{2,1,0:T(8,128)(2,1)S(1)} %collective-permute-done.10.rest_6_) | copy-start | bytes 196612
  44.1 0.6 %copy-start.13 = (bf16[4,64,128]{2,1,0:T(8,128)(2,1)}, bf16[4,64,128]{2,1,0:T(8,128)(2,1)S(1)}, u32[]{:S(2)}) copy-start(bf16[4,64,128]{2,1,0:T(8,128)(2,1)S(1)} %collective-permute-done.9.rest_5_) | copy-start | bytes 196612

commit v2 on v0

--- a/solution.py
+++ b/solution.py
@@ -1,10 +1,252 @@
+import functools
+
 import jax
 import jax.numpy as jnp
 from jax import lax
+from jax.experimental import pallas as pl
+from jax.experimental.pallas import tpu as pltpu
 from jax.sharding import PartitionSpec as P
 
-
-def on_device(
+CALLS = 2
+SPLIT = 2
+COLUMN_ORDER = (3, 1, 2, 0)
+SMALL = pltpu.CompilerParams(vmem_limit_bytes=4 * 1024 * 1024)
+
+
+def term_kernel(
+    cls_hbm,
+    tid_hbm,
+    pair_hbm,
+    dims_hbm,
+    coef_hbm,
+    wave_hbm,
+    left_hbm,
+    right_hbm,
+    send_ref,
+    keep_ref,
+    cls,
+    tid,
+    pair,
+    dims,
+    coef,
+    wave,
+    left,
+    right,
+    total,
+    scalar_sems,
+    wave_sem,
+    left_sems,
+    right_sems,
+    *,
+    call,
+):
+    width = wave.shape[0]
+    terms = left.shape[0]
+    targets = total.shape[0]
+    strip = width // 4
+    share = left.shape[1] // 4
+    split = send_ref.shape[1]
+    rows = share // split
+    unit = width // 8
+    sec = lax.axis_index("sec")
+    mpo = lax.axis_index("mpo")
+
+    scalars = [
+        pltpu.make_async_copy(src, dst, scalar_sems.at[n])
+        for n, (src, dst) in enumerate(
+            ((cls_hbm, cls), (tid_hbm, tid), (pair_hbm, pair), (dims_hbm, dims), (coef_hbm, coef))
+        )
+    ]
+    for copy in scalars:
+        copy.start()
+    wave_copy = pltpu.make_async_copy(wave_hbm.at[0], wave, wave_sem)
+    wave_copy.start()
+
+    def fetch(j, carry):
+        for q in range(4):
+            src = pl.multiple_of((sec ^ q) * strip + call * share, 16)
+            pltpu.make_async_copy(
+                left_hbm.at[0, j, pl.ds(src, share)],
+                left.at[j, pl.ds(q * share, share)],
+                left_sems.at[j],
+            ).start()
+        for p, r in enumerate(COLUMN_ORDER):
+            src = pl.multiple_of((mpo ^ r) * strip, strip)
+            pltpu.make_async_copy(
+                right_hbm.at[0, j, pl.ds(src, strip)],
+                right.at[j, pl.ds(p * strip, strip)],
+                right_sems.at[j],
+            ).start()
+        return carry
+
+    lax.fori_loop(0, terms, fetch, 0)
+    total[...] = jnp.zeros_like(total)
+    for copy in scalars:
+        copy.wait()
+    wave_copy.wait()
+    row_limit = dims[0, sec] * unit
+    col_limit = dims[1, sec] * unit
+
+    def mask(i, carry):
+        base = pl.multiple_of(i * 64, 64)
+        row_pos = base + lax.broadcasted_iota(jnp.int32, (64, width), 0)
+        col_pos = lax.broadcasted_iota(jnp.int32, (64, width), 1)
+        inside = (row_pos < row_limit) & (col_pos < col_limit)
+        band = wave[pl.ds(base, 64), :].astype(jnp.float32)
+        wave[pl.ds(base, 64), :] = jnp.where(inside, band, 0.0).astype(jnp.bfloat16)
+        return carry
+
+    lax.fori_loop(0, width // 64, mask, 0)
+
+    def term(j, carry):
+        pltpu.make_async_copy(
+            left_hbm.at[0, j, pl.ds(0, 4 * share)], left.at[j], left_sems.at[j]
+        ).wait()
+        half = jnp.dot(left[j], wave[...], preferred_element_type=jnp.float32)
+        half = half.astype(jnp.bfloat16)
+        pltpu.make_async_copy(right_hbm.at[0, j], right.at[j], right_sems.at[j]).wait()
+        contrib = lax.dot_general(
+            half, right[j], (((1,), (1,)), ((), ())), preferred_element_type=jnp.float32
+        )
+        target = pair[sec, cls[0, j]]
+        total[target] += coef[tid[0, j]] * contrib
+        return carry
+
+    lax.fori_loop(0, terms, term, 0)
+
+    lane = lax.broadcasted_iota(jnp.int32, (rows, strip), 1)
+    line = lax.broadcasted_iota(jnp.int32, (rows, strip), 0)
+
+    def store(t, carry):
+        for p, r in enumerate(COLUMN_ORDER):
+            out_ref = send_ref if p < 2 else keep_ref
+            cols_in = (mpo ^ r) * strip + lane < dims[1, t] * unit
+            for q in range(4):
+                for g in range(split):
+                    first = (sec ^ q) * strip + call * share + g * rows
+                    inside = cols_in & (first + line < dims[0, t] * unit)
+                    at = q * share + g * rows
+                    value = total[t, at : at + rows, p * strip : (p + 1) * strip]
+                    out_ref[p % 2, g, q, t] = jnp.where(inside, value, 0.0).astype(jnp.bfloat16)
+        return carry
+
+    lax.fori_loop(0, targets, store, 0)
+
+
+def far_kernel(keep_ref, recv_ref, *rest, piece):
+    far_ref = rest[-1]
+    far_ref[...] = add(keep_ref[0, piece], recv_ref[0, piece])
+
+
+def own_kernel(keep_ref, recv_ref, cross_ref, *own_refs, piece):
+    for q, own_ref in enumerate(own_refs):
+        own_ref[...] = add(keep_ref[1, piece, q], recv_ref[1, piece, q], cross_ref[q])
+
+
+def final_kernel(*refs):
+    pieces, out_ref = refs[:-1], refs[-1]
+    rows = pieces[0].shape[1]
+    for h in range(out_ref.shape[1] // rows):
+        out_ref[:, h * rows : (h + 1) * rows, :] = add(
+            *[piece[...] for piece in pieces[4 * h : 4 * h + 4]]
+        )
+
+
+def add(*arrays):
+    total = arrays[0].astype(jnp.float32)
+    for array in arrays[1:]:
+        total = total + array.astype(jnp.float32)
+    return total.astype(jnp.bfloat16)
+
+
+def swap(array, axis, mask):
+    return lax.ppermute(array, axis, [(i, i ^ mask) for i in range(lax.axis_size(axis))])
+
+
+def by_targets(
+    wave_blocks, left_env, right_env, term_class, term_id, block_dims, pair_table, mpo_coef
+):
+    width = wave_blocks.shape[1]
+    terms = left_env.shape[1]
+    targets = block_dims.shape[0]
+    strip = width // 4
+    share = strip // CALLS
+    rows = share // SPLIT
+    vmem = pl.BlockSpec(memory_space=pltpu.VMEM)
+    hbm = pl.BlockSpec(memory_space=pltpu.HBM)
+    anywhere = pl.BlockSpec(memory_space=pl.ANY)
+    block = jax.ShapeDtypeStruct((4, targets, rows, strip), jnp.bfloat16)
+    part = jax.ShapeDtypeStruct((targets, rows, strip), jnp.bfloat16)
+    pair_out = jax.ShapeDtypeStruct((2, SPLIT) + block.shape, jnp.bfloat16)
+    scalars = (term_class, term_id, pair_table, block_dims.T, mpo_coef)
+    operands = [
+        pltpu.with_memory_space_constraint(x, pltpu.HBM)
+        for x in (*scalars, wave_blocks, left_env, right_env)
+    ]
+    kept, received = [], []
+    for call in range(CALLS):
+        send, keep = pl.pallas_call(
+            functools.partial(term_kernel, call=call),
+            out_shape=[pair_out] * 2,
+            in_specs=[hbm] * 8,
+            out_specs=[vmem] * 2,
+            scratch_shapes=[pltpu.SMEM(scalar.shape, scalar.dtype) for scalar in scalars]
+            + [
+                pltpu.VMEM((width, width), jnp.bfloat16),
+                pltpu.VMEM((terms, 4 * share, width), jnp.bfloat16),
+                pltpu.VMEM((terms, width, width), jnp.bfloat16),
+                pltpu.VMEM((targets, 4 * share, width), jnp.float32),
+                pltpu.SemaphoreType.DMA((len(scalars),)),
+                pltpu.SemaphoreType.DMA,
+                pltpu.SemaphoreType.DMA((terms,)),
+                pltpu.SemaphoreType.DMA((terms,)),
+            ],
+            compiler_params=pltpu.CompilerParams(vmem_limit_bytes=20 * 1024 * 1024),
+            cost_estimate=pl.CostEstimate(
+                flops=4 * terms * width**3 // CALLS,
+                bytes_accessed=4 * 1024 * 1024,
+                transcendentals=0,
+            ),
+            name=f"terms_{call}",
+        )(*operands)
+        kept.append(keep)
+        received.append(swap(send, "mpo", 1))
+    pieces = []
+    after = []
+    for h in range(CALLS * SPLIT):
+        keep, recv = kept[h // SPLIT], received[h // SPLIT]
+        far = pl.pallas_call(
+            functools.partial(far_kernel, piece=h % SPLIT),
+            out_shape=block,
+            in_specs=[vmem, vmem] + [anywhere] * len(after),
+            out_specs=vmem,
+            compiler_params=SMALL,
+            name=f"far_{h}",
+        )(keep, recv, *after)
+        crossed = swap(far, "mpo", 2)
+        after = [crossed]
+        own = pl.pallas_call(
+            functools.partial(own_kernel, piece=h % SPLIT),
+            out_shape=[part] * 4,
+            in_specs=[vmem] * 3,
+            out_specs=[vmem] * 4,
+            compiler_params=SMALL,
+            name=f"own_{h}",
+        )(keep, recv, crossed)
+        pieces.append(own[0])
+        for q in (1, 2, 3):
+            pieces.append(swap(own[q], "sec", q))
+    return pl.pallas_call(
+        final_kernel,
+        out_shape=jax.ShapeDtypeStruct((targets, strip, strip), jnp.bfloat16),
+        in_specs=[vmem] * len(pieces),
+        out_specs=vmem,
+        compiler_params=SMALL,
+        name="final",
+    )(*pieces)
+
+
+def by_classes(
     wave_blocks, left_env, right_env, term_class, term_id, block_dims, pair_table, mpo_coef
 ):
     sec_count = lax.axis_size("sec")
@@ -77,6 +319,14 @@
         P("grp", None),
         P(),
     )
+
+    def on_device(*arrays):
+        wave_blocks, block_dims = arrays[0], arrays[5]
+        small = wave_blocks.shape[0] == 1 and block_dims.shape[0] == 4
+        if small and mesh.shape["sec"] == 4 and mesh.shape["mpo"] == 4:
+            return by_targets(*arrays)
+        return by_classes(*arrays)
+
     return jax.shard_map(
         on_device, mesh=mesh, in_specs=placed, out_specs=P("grp", "sec", "mpo"), check_vma=False
     )

time: 175 us -> 51.3 us (0.29)
  blocking collectives: 99.3 us -> 0 us
  starting transfers between devices: 4.77 us -> 26.8 us
  waiting for transfers between devices: 36.7 us -> 16.2 us
  matrix products: 18.8 us -> 0 us
  local copies, waits for them, and re-layouts: 10.1 us -> 0 us
  Pallas kernels: 0 us -> 8.18 us
  other arithmetic: 3.4 us -> 0 us
    all_to_all x1 -> x0, blocking collectives: 99.3 us -> none  [on_device(): lax.all_to_all(outgoing, 'sec', split_axis=1, concat_axis=0, tiled=True)]
    all_to_all x1 -> x0, waiting for transfers between devices: 36.7 us -> none  [on_device(): lax.all_to_all(lax.all_to_all(outgoing, 'sec', split_axis=1, concat_axis=...]
    ppermute x0 -> x18, starting transfers between devices: none -> 26.8 us  [swap(): lax.ppermute(array, axis, [(i, i ^ mask) for i in range(lax.axis_size(axi...]
    dot_general x3 -> x0, matrix products: 18.8 us -> none  [the longest x1 13.2 us: on_device(): jnp.einsum('bjc,bjxw->bcxw', picks, contrib, precision=lax.Precision.HIGH...]
    ppermute x0 -> x18, waiting for transfers between devices: none -> 16.2 us  [swap(): lax.ppermute(array, axis, [(i, i ^ mask) for i in range(lax.axis_size(axi...]
    pallas_call x0 -> x11, Pallas kernels: none -> 8.18 us  [the longest x2 7.12 us: by_targets(): pl.pallas_call(functools.partial(term_kernel, call=call), out_shape=[pair...]
    all_to_all x2 -> x0, local copies, waits for them, and re-layouts: 7.28 us -> none  [on_device(): lax.all_to_all(outgoing, 'sec', split_axis=1, concat_axis=0, tiled=True)]
    all_to_all x1 -> x0, starting transfers between devices: 4.77 us -> none  [on_device(): lax.all_to_all(lax.all_to_all(outgoing, 'sec', split_axis=1, concat_axis=...]
  transfers between devices with their start and end apart: 1 -> 18, of which waited for: 1 -> 8; matrix products, arithmetic and copies ran while one was open for 0% -> 0% of each run, Pallas kernels for 0% -> 7%
where the time goes in v2:
time: 51.3 us; the launch traced here: 51.2 us
  starting transfers between devices  26.8 us (52%)
  waiting for transfers between devices  16.2 us (32%)
  Pallas kernels  8.18 us (16%)
    ppermute x18, starting transfers between devices, swap(): lax.ppermute(array, axis, [(i, i ^ mask) for i in range(lax.axis_size(axi...  26.8 us
    ppermute x18, waiting for transfers between devices, swap(): lax.ppermute(array, axis, [(i, i ^ mask) for i in range(lax.axis_size(axi...  16.2 us
    pallas_call x2, Pallas kernels, by_targets(): pl.pallas_call(functools.partial(term_kernel, call=call), out_shape=[pair...  7.12 us
  transfers between devices with their start and end apart: 18, of which 8 were waited for; matrix products, arithmetic and copies ran while one was open for 0% of the time, Pallas kernels for 7%

profile of v2, /device:TPU:0, one launch (start us, length us, event | category | flops | bytes accessed | tf_op | source)
XLA Modules:
  0.0 51.2 jit_solution(2282492452091091588)
XLA Ops:
  0.0 3.6 %terms_0.1 = (bf16[2,2,4,4,32,128]{5,4,3,2,1,0:T(8,128)(2,1)S(1)}, bf16[2,2,4,4,32,128]{5,4,3,2,1,0:T(8,128)(2,1)S(1)}) custom-call(s32[1,3]{1,0:T(1,128)} %cls_hbm.3, s32[1,3]{1,0:T(1,128)} %tid_hbm.3, s32[4,5]{1,0:T(4,128)} %pair_hbm.3, s32[2,4]{1,0:T(2,128)} %bitcast.1, f32[50]{0:T(128)} %coef_hbm.3, bf16[1,512,512]{2,1,0:T(8,128)(2,1)} %wave_hbm.3, ...), custom_call_target="tpu_custom_call" | custom-call | flops 805306368 | bytes 4194304 | tf_op jit(solution)/shard_map/terms_0/pallas_call | solution.py:188
  3.6 0.5 %collective-permute-start = (bf16[2,2,4,4,32,128]{5,4,3,2,1,0:T(8,128)(2,1)S(1)}, bf16[2,2,4,4,32,128]{5,4,3,2,1,0:T(8,128)(2,1)S(1)}, u32[]{:S(2)}, u32[]{:S(2)}) collective-permute-start(bf16[2,2,4,4,32,128]{5,4,3,2,1,0:T(8,128)(2,1)S(1)} %get-tuple-element.26), channel_id=1, source_target_pairs={{0,1},{1,0},{2,3},{3,2},{4,5},{5,4},{6,7},{7,6},{8,9},{9,8},{10,11... | collective-permute-start | bytes 1572872 | tf_op jit(solution)/shard_map/ppermute | solution.py:163
  4.1 3.6 %terms_1.1 = (bf16[2,2,4,4,32,128]{5,4,3,2,1,0:T(8,128)(2,1)S(1)}, bf16[2,2,4,4,32,128]{5,4,3,2,1,0:T(8,128)(2,1)S(1)}) custom-call(s32[1,3]{1,0:T(1,128)} %cls_hbm.3, s32[1,3]{1,0:T(1,128)} %tid_hbm.3, s32[4,5]{1,0:T(4,128)} %pair_hbm.3, s32[2,4]{1,0:T(2,128)} %bitcast.2, f32[50]{0:T(128)} %coef_hbm.3, bf16[1,512,512]{2,1,0:T(8,128)(2,1)} %wave_hbm.3, ...), custom_call_target="tpu_custom_call" | custom-call | flops 805306368 | bytes 4194304 | tf_op jit(solution)/shard_map/terms_1/pallas_call | solution.py:188
  7.7 0.1 collective-permute-start.9
  7.8 0.0 collective-permute-done.recv_ref
  7.8 3.0 %collective-permute-start.1 = (bf16[4,4,32,128]{3,2,1,0:T(8,128)(2,1)S(1)}, bf16[4,4,32,128]{3,2,1,0:T(8,128)(2,1)S(1)}, u32[]{:S(2)}, u32[]{:S(2)}) collective-permute-start(bf16[4,4,32,128]{3,2,1,0:T(8,128)(2,1)S(1)} %far_0.1), channel_id=1, source_target_pairs={{0,2},{1,3},{2,0},{3,1},{4,6},{5,7},{6,4},{7,5},{8,10},{9,11},{10,... | collective-permute-start | bytes 393224 | tf_op jit(solution)/shard_map/ppermute | solution.py:163
  10.8 3.7 %collective-permute-done.1.cross_ref.rest_0_ = bf16[4,4,32,128]{3,2,1,0:T(8,128)(2,1)S(1)} collective-permute-done((bf16[4,4,32,128]{3,2,1,0:T(8,128)(2,1)S(1)}, bf16[4,4,32,128]{3,2,1,0:T(8,128)(2,1)S(1)}, u32[]{:S(2)}, u32[]{:S(2)}) %collective-permute-start.1) | collective-permute-done | bytes 131104 | tf_op jit(solution)/shard_map/ppermute | solution.py:163
  14.5 1.8 %collective-permute-start.5 = (bf16[4,4,32,128]{3,2,1,0:T(8,128)(2,1)S(1)}, bf16[4,4,32,128]{3,2,1,0:T(8,128)(2,1)S(1)}, u32[]{:S(2)}, u32[]{:S(2)}) collective-permute-start(bf16[4,4,32,128]{3,2,1,0:T(8,128)(2,1)S(1)} %far_1.1), channel_id=1, source_target_pairs={{0,2},{1,3},{2,0},{3,1},{4,6},{5,7},{6,4},{7,5},{8,10},{9,11},{10,... | collective-permute-start | bytes 393224 | tf_op jit(solution)/shard_map/ppermute | solution.py:163
  16.3 0.0 collective-permute-done.9.recv_ref
  16.3 3.2 %collective-permute-done.5.cross_ref.rest_0_ = bf16[4,4,32,128]{3,2,1,0:T(8,128)(2,1)S(1)} collective-permute-done((bf16[4,4,32,128]{3,2,1,0:T(8,128)(2,1)S(1)}, bf16[4,4,32,128]{3,2,1,0:T(8,128)(2,1)S(1)}, u32[]{:S(2)}, u32[]{:S(2)}) %collective-permute-start.5) | collective-permute-done | bytes 131104 | tf_op jit(solution)/shard_map/ppermute | solution.py:163
  19.6 1.8 %collective-permute-start.10 = (bf16[4,4,32,128]{3,2,1,0:T(8,128)(2,1)S(1)}, bf16[4,4,32,128]{3,2,1,0:T(8,128)(2,1)S(1)}, u32[]{:S(2)}, u32[]{:S(2)}) collective-permute-start(bf16[4,4,32,128]{3,2,1,0:T(8,128)(2,1)S(1)} %far_2.1), channel_id=1, source_target_pairs={{0,2},{1,3},{2,0},{3,1},{4,6},{5,7},{6,4},{7,5},{8,10},{9,11},{10,... | collective-permute-start | bytes 393224 | tf_op jit(solution)/shard_map/ppermute | solution.py:163
  21.4 3.3 %collective-permute-done.10.cross_ref.rest_0_ = bf16[4,4,32,128]{3,2,1,0:T(8,128)(2,1)S(1)} collective-permute-done((bf16[4,4,32,128]{3,2,1,0:T(8,128)(2,1)S(1)}, bf16[4,4,32,128]{3,2,1,0:T(8,128)(2,1)S(1)}, u32[]{:S(2)}, u32[]{:S(2)}) %collective-permute-start.10) | collective-permute-done | bytes 131104 | tf_op jit(solution)/shard_map/ppermute | solution.py:163
  24.7 2.2 %collective-permute-start.14 = (bf16[4,4,32,128]{3,2,1,0:T(8,128)(2,1)S(1)}, bf16[4,4,32,128]{3,2,1,0:T(8,128)(2,1)S(1)}, u32[]{:S(2)}, u32[]{:S(2)}) collective-permute-start(bf16[4,4,32,128]{3,2,1,0:T(8,128)(2,1)S(1)} %far_3.1), channel_id=1, source_target_pairs={{0,2},{1,3},{2,0},{3,1},{4,6},{5,7},{6,4},{7,5},{8,10},{9,11},{10,... | collective-permute-start | bytes 393224 | tf_op jit(solution)/shard_map/ppermute | solution.py:163
  26.9 0.1 own_0.1
  27.0 1.6 %collective-permute-start.2 = (bf16[4,32,128]{2,1,0:T(8,128)(2,1)S(1)}, bf16[4,32,128]{2,1,0:T(8,128)(2,1)S(1)}, u32[]{:S(2)}, u32[]{:S(2)}) collective-permute-start(bf16[4,32,128]{2,1,0:T(8,128)(2,1)S(1)} %get-tuple-element.28), channel_id=1, source_target_pairs={{0,4},{4,0},{8,12},{12,8},{1,5},{5,1},{9,13},{13,9},{2,6},{6,2},{1... | collective-permute-start | bytes 98312 | tf_op jit(solution)/shard_map/ppermute | solution.py:163
  28.6 2.6 %collective-permute-start.3 = (bf16[4,32,128]{2,1,0:T(8,128)(2,1)S(1)}, bf16[4,32,128]{2,1,0:T(8,128)(2,1)S(1)}, u32[]{:S(2)}, u32[]{:S(2)}) collective-permute-start(bf16[4,32,128]{2,1,0:T(8,128)(2,1)S(1)} %get-tuple-element.29), channel_id=1, source_target_pairs={{0,8},{4,12},{8,0},{12,4},{1,9},{5,13},{9,1},{13,5},{2,10},{6,14},... | collective-permute-start | bytes 98312 | tf_op jit(solution)/shard_map/ppermute | solution.py:163
  31.2 0.2 collective-permute-start.4
  31.4 0.1 own_1.1
  31.5 0.7 %collective-permute-start.6 = (bf16[4,32,128]{2,1,0:T(8,128)(2,1)S(1)}, bf16[4,32,128]{2,1,0:T(8,128)(2,1)S(1)}, u32[]{:S(2)}, u32[]{:S(2)}) collective-permute-start(bf16[4,32,128]{2,1,0:T(8,128)(2,1)S(1)} %get-tuple-element.32), channel_id=1, source_target_pairs={{0,4},{4,0},{8,12},{12,8},{1,5},{5,1},{9,13},{13,9},{2,6},{6,2},{1... | collective-permute-start | bytes 98312 | tf_op jit(solution)/shard_map/ppermute | solution.py:163
  32.2 0.1 own_2.1
  32.3 0.0 collective-permute-done.2.refs_1_
  32.3 3.6 %collective-permute-start.7 = (bf16[4,32,128]{2,1,0:T(8,128)(2,1)S(1)}, bf16[4,32,128]{2,1,0:T(8,128)(2,1)S(1)}, u32[]{:S(2)}, u32[]{:S(2)}) collective-permute-start(bf16[4,32,128]{2,1,0:T(8,128)(2,1)S(1)} %get-tuple-element.33), channel_id=1, source_target_pairs={{0,8},{4,12},{8,0},{12,4},{1,9},{5,13},{9,1},{13,5},{2,10},{6,14},... | collective-permute-start | bytes 98312 | tf_op jit(solution)/shard_map/ppermute | solution.py:163
  35.8 0.0 collective-permute-done.3.refs_2_
  35.8 0.5 collective-permute-start.8
  36.3 0.0 collective-permute-done.14.cross_ref
  36.3 0.3 collective-permute-start.11
  36.7 0.1 own_3.1
  36.7 0.2 collective-permute-done.4.refs_3_
  36.9 3.4 %collective-permute-start.12 = (bf16[4,32,128]{2,1,0:T(8,128)(2,1)S(1)}, bf16[4,32,128]{2,1,0:T(8,128)(2,1)S(1)}, u32[]{:S(2)}, u32[]{:S(2)}) collective-permute-start(bf16[4,32,128]{2,1,0:T(8,128)(2,1)S(1)} %get-tuple-element.39), channel_id=1, source_target_pairs={{0,8},{4,12},{8,0},{12,4},{1,9},{5,13},{9,1},{13,5},{2,10},{6,14},... | collective-permute-start | bytes 98312 | tf_op jit(solution)/shard_map/ppermute | solution.py:163
  40.4 0.0 collective-permute-done.6.refs_5_
  40.4 0.5 collective-permute-start.13
  40.9 0.0 collective-permute-done.7.refs_6_
  40.9 0.1 collective-permute-start.15
  41.0 0.5 %collective-permute-done.8.refs_7_ = bf16[4,32,128]{2,1,0:T(8,128)(2,1)S(1)} collective-permute-done((bf16[4,32,128]{2,1,0:T(8,128)(2,1)S(1)}, bf16[4,32,128]{2,1,0:T(8,128)(2,1)S(1)}, u32[]{:S(2)}, u32[]{:S(2)}) %collective-permute-start.8) | collective-permute-done | bytes 32800 | tf_op jit(solution)/shard_map/ppermute | solution.py:163
  41.5 3.2 %collective-permute-start.16 = (bf16[4,32,128]{2,1,0:T(8,128)(2,1)S(1)}, bf16[4,32,128]{2,1,0:T(8,128)(2,1)S(1)}, u32[]{:S(2)}, u32[]{:S(2)}) collective-permute-start(bf16[4,32,128]{2,1,0:T(8,128)(2,1)S(1)} %get-tuple-element.43), channel_id=1, source_target_pairs={{0,8},{4,12},{8,0},{12,4},{1,9},{5,13},{9,1},{13,5},{2,10},{6,14},... | collective-permute-start | bytes 98312 | tf_op jit(solution)/shard_map/ppermute | solution.py:163
  44.8 0.0 collective-permute-done.11.refs_9_
  44.8 0.5 collective-permute-start.17
  45.3 0.0 collective-permute-done.12.refs_10_
  45.3 0.8 %collective-permute-done.13.refs_11_ = bf16[4,32,128]{2,1,0:T(8,128)(2,1)S(1)} collective-permute-done((bf16[4,32,128]{2,1,0:T(8,128)(2,1)S(1)}, bf16[4,32,128]{2,1,0:T(8,128)(2,1)S(1)}, u32[]{:S(2)}, u32[]{:S(2)}) %collective-permute-start.13) | collective-permute-done | bytes 32800 | tf_op jit(solution)/shard_map/ppermute | solution.py:163
  46.1 0.0 collective-permute-done.15.refs_13_
  46.1 0.6 %collective-permute-done.16.refs_14_ = bf16[4,32,128]{2,1,0:T(8,128)(2,1)S(1)} collective-permute-done((bf16[4,32,128]{2,1,0:T(8,128)(2,1)S(1)}, bf16[4,32,128]{2,1,0:T(8,128)(2,1)S(1)}, u32[]{:S(2)}, u32[]{:S(2)}) %collective-permute-start.16) | collective-permute-done | bytes 32800 | tf_op jit(solution)/shard_map/ppermute | solution.py:163
  46.6 3.8 %collective-permute-done.17.refs_15_ = bf16[4,32,128]{2,1,0:T(8,128)(2,1)S(1)} collective-permute-done((bf16[4,32,128]{2,1,0:T(8,128)(2,1)S(1)}, bf16[4,32,128]{2,1,0:T(8,128)(2,1)S(1)}, u32[]{:S(2)}, u32[]{:S(2)}) %collective-permute-start.17) | collective-permute-done | bytes 32800 | tf_op jit(solution)/shard_map/ppermute | solution.py:163
  50.5 0.7 %final.1 = bf16[4,128,128]{2,1,0:T(8,128)(2,1)} custom-call(bf16[4,32,128]{2,1,0:T(8,128)(2,1)S(1)} %get-tuple-element.27.refs_0_, bf16[4,32,128]{2,1,0:T(8,128)(2,1)S(1)} %collective-permute-done.2.refs_1_, bf16[4,32,128]{2,1,0:T(8,128)(2,1)S(1)} %collective-permute-done.3.refs_2_, bf16[4,32,128]{2,1,0:T(8,128)(2,1)S(1)} %collective-permute-done.4.refs_3_, ...), custom_call_target="tpu_custom_call" | custom-call | tf_op jit(solution)/shard_map/final/pallas_call | solution.py:239
  (4 shorter events, 0.1 us)
Async XLA Ops:
  3.6 4.2 %collective-permute-start = (bf16[2,2,4,4,32,128]{5,4,3,2,1,0:T(8,128)(2,1)S(1)}, bf16[2,2,4,4,32,128]{5,4,3,2,1,0:T(8,128)(2,1)S(1)}, u32[]{:S(2)}, u32[]{:S(2)}) collective-permute-start(bf16[2,2,4,4,32,128]{5,4,3,2,1,0:T(8,128)(2,1)S(1)} %get-tuple-element.26), channel_id=1, source_target_pairs={{0,1},{1,0},{2,3},{3,2},{4,5},{5,4},{6,7},{7,6},{8,9},{9,8},{10,11... | collective-permute-start | bytes 1572872 | tf_op jit(solution)/shard_map/ppermute | solution.py:163
  7.7 8.7 %collective-permute-start.9 = (bf16[2,2,4,4,32,128]{5,4,3,2,1,0:T(8,128)(2,1)S(1)}, bf16[2,2,4,4,32,128]{5,4,3,2,1,0:T(8,128)(2,1)S(1)}, u32[]{:S(2)}, u32[]{:S(2)}) collective-permute-start(bf16[2,2,4,4,32,128]{5,4,3,2,1,0:T(8,128)(2,1)S(1)} %get-tuple-element.36), channel_id=1, source_target_pairs={{0,1},{1,0},{2,3},{3,2},{4,5},{5,4},{6,7},{7,6},{8,9},{9,8},{10,11... | collective-permute-start | bytes 1572872 | tf_op jit(solution)/shard_map/ppermute | solution.py:163
  7.8 6.7 %collective-permute-start.1 = (bf16[4,4,32,128]{3,2,1,0:T(8,128)(2,1)S(1)}, bf16[4,4,32,128]{3,2,1,0:T(8,128)(2,1)S(1)}, u32[]{:S(2)}, u32[]{:S(2)}) collective-permute-start(bf16[4,4,32,128]{3,2,1,0:T(8,128)(2,1)S(1)} %far_0.1), channel_id=1, source_target_pairs={{0,2},{1,3},{2,0},{3,1},{4,6},{5,7},{6,4},{7,5},{8,10},{9,11},{10,... | collective-permute-start | bytes 393224 | tf_op jit(solution)/shard_map/ppermute | solution.py:163
  14.5 5.0 %collective-permute-start.5 = (bf16[4,4,32,128]{3,2,1,0:T(8,128)(2,1)S(1)}, bf16[4,4,32,128]{3,2,1,0:T(8,128)(2,1)S(1)}, u32[]{:S(2)}, u32[]{:S(2)}) collective-permute-start(bf16[4,4,32,128]{3,2,1,0:T(8,128)(2,1)S(1)} %far_1.1), channel_id=1, source_target_pairs={{0,2},{1,3},{2,0},{3,1},{4,6},{5,7},{6,4},{7,5},{8,10},{9,11},{10,... | collective-permute-start | bytes 393224 | tf_op jit(solution)/shard_map/ppermute | solution.py:163
  19.6 5.1 %collective-permute-start.10 = (bf16[4,4,32,128]{3,2,1,0:T(8,128)(2,1)S(1)}, bf16[4,4,32,128]{3,2,1,0:T(8,128)(2,1)S(1)}, u32[]{:S(2)}, u32[]{:S(2)}) collective-permute-start(bf16[4,4,32,128]{3,2,1,0:T(8,128)(2,1)S(1)} %far_2.1), channel_id=1, source_target_pairs={{0,2},{1,3},{2,0},{3,1},{4,6},{5,7},{6,4},{7,5},{8,10},{9,11},{10,... | collective-permute-start | bytes 393224 | tf_op jit(solution)/shard_map/ppermute | solution.py:163
  24.7 11.6 %collective-permute-start.14 = (bf16[4,4,32,128]{3,2,1,0:T(8,128)(2,1)S(1)}, bf16[4,4,32,128]{3,2,1,0:T(8,128)(2,1)S(1)}, u32[]{:S(2)}, u32[]{:S(2)}) collective-permute-start(bf16[4,4,32,128]{3,2,1,0:T(8,128)(2,1)S(1)} %far_3.1), channel_id=1, source_target_pairs={{0,2},{1,3},{2,0},{3,1},{4,6},{5,7},{6,4},{7,5},{8,10},{9,11},{10,... | collective-permute-start | bytes 393224 | tf_op jit(solution)/shard_map/ppermute | solution.py:163
  27.0 5.3 %collective-permute-start.2 = (bf16[4,32,128]{2,1,0:T(8,128)(2,1)S(1)}, bf16[4,32,128]{2,1,0:T(8,128)(2,1)S(1)}, u32[]{:S(2)}, u32[]{:S(2)}) collective-permute-start(bf16[4,32,128]{2,1,0:T(8,128)(2,1)S(1)} %get-tuple-element.28), channel_id=1, source_target_pairs={{0,4},{4,0},{8,12},{12,8},{1,5},{5,1},{9,13},{13,9},{2,6},{6,2},{1... | collective-permute-start | bytes 98312 | tf_op jit(solution)/shard_map/ppermute | solution.py:163
  28.6 7.2 %collective-permute-start.3 = (bf16[4,32,128]{2,1,0:T(8,128)(2,1)S(1)}, bf16[4,32,128]{2,1,0:T(8,128)(2,1)S(1)}, u32[]{:S(2)}, u32[]{:S(2)}) collective-permute-start(bf16[4,32,128]{2,1,0:T(8,128)(2,1)S(1)} %get-tuple-element.29), channel_id=1, source_target_pairs={{0,8},{4,12},{8,0},{12,4},{1,9},{5,13},{9,1},{13,5},{2,10},{6,14},... | collective-permute-start | bytes 98312 | tf_op jit(solution)/shard_map/ppermute | solution.py:163
  31.2 5.7 %collective-permute-start.4 = (bf16[4,32,128]{2,1,0:T(8,128)(2,1)S(1)}, bf16[4,32,128]{2,1,0:T(8,128)(2,1)S(1)}, u32[]{:S(2)}, u32[]{:S(2)}) collective-permute-start(bf16[4,32,128]{2,1,0:T(8,128)(2,1)S(1)} %get-tuple-element.30), channel_id=1, source_target_pairs={{0,12},{4,8},{8,4},{12,0},{1,13},{5,9},{9,5},{13,1},{2,14},{6,10},... | collective-permute-start | bytes 98312 | tf_op jit(solution)/shard_map/ppermute | solution.py:163
  31.5 8.9 %collective-permute-start.6 = (bf16[4,32,128]{2,1,0:T(8,128)(2,1)S(1)}, bf16[4,32,128]{2,1,0:T(8,128)(2,1)S(1)}, u32[]{:S(2)}, u32[]{:S(2)}) collective-permute-start(bf16[4,32,128]{2,1,0:T(8,128)(2,1)S(1)} %get-tuple-element.32), channel_id=1, source_target_pairs={{0,4},{4,0},{8,12},{12,8},{1,5},{5,1},{9,13},{13,9},{2,6},{6,2},{1... | collective-permute-start | bytes 98312 | tf_op jit(solution)/shard_map/ppermute | solution.py:163
  32.3 8.6 %collective-permute-start.7 = (bf16[4,32,128]{2,1,0:T(8,128)(2,1)S(1)}, bf16[4,32,128]{2,1,0:T(8,128)(2,1)S(1)}, u32[]{:S(2)}, u32[]{:S(2)}) collective-permute-start(bf16[4,32,128]{2,1,0:T(8,128)(2,1)S(1)} %get-tuple-element.33), channel_id=1, source_target_pairs={{0,8},{4,12},{8,0},{12,4},{1,9},{5,13},{9,1},{13,5},{2,10},{6,14},... | collective-permute-start | bytes 98312 | tf_op jit(solution)/shard_map/ppermute | solution.py:163
  35.8 5.7 %collective-permute-start.8 = (bf16[4,32,128]{2,1,0:T(8,128)(2,1)S(1)}, bf16[4,32,128]{2,1,0:T(8,128)(2,1)S(1)}, u32[]{:S(2)}, u32[]{:S(2)}) collective-permute-start(bf16[4,32,128]{2,1,0:T(8,128)(2,1)S(1)} %get-tuple-element.34), channel_id=1, source_target_pairs={{0,12},{4,8},{8,4},{12,0},{1,13},{5,9},{9,5},{13,1},{2,14},{6,10},... | collective-permute-start | bytes 98312 | tf_op jit(solution)/shard_map/ppermute | solution.py:163
  36.3 8.4 %collective-permute-start.11 = (bf16[4,32,128]{2,1,0:T(8,128)(2,1)S(1)}, bf16[4,32,128]{2,1,0:T(8,128)(2,1)S(1)}, u32[]{:S(2)}, u32[]{:S(2)}) collective-permute-start(bf16[4,32,128]{2,1,0:T(8,128)(2,1)S(1)} %get-tuple-element.38), channel_id=1, source_target_pairs={{0,4},{4,0},{8,12},{12,8},{1,5},{5,1},{9,13},{13,9},{2,6},{6,2},{1... | collective-permute-start | bytes 98312 | tf_op jit(solution)/shard_map/ppermute | solution.py:163
  36.9 8.3 %collective-permute-start.12 = (bf16[4,32,128]{2,1,0:T(8,128)(2,1)S(1)}, bf16[4,32,128]{2,1,0:T(8,128)(2,1)S(1)}, u32[]{:S(2)}, u32[]{:S(2)}) collective-permute-start(bf16[4,32,128]{2,1,0:T(8,128)(2,1)S(1)} %get-tuple-element.39), channel_id=1, source_target_pairs={{0,8},{4,12},{8,0},{12,4},{1,9},{5,13},{9,1},{13,5},{2,10},{6,14},... | collective-permute-start | bytes 98312 | tf_op jit(solution)/shard_map/ppermute | solution.py:163
  40.4 5.7 %collective-permute-start.13 = (bf16[4,32,128]{2,1,0:T(8,128)(2,1)S(1)}, bf16[4,32,128]{2,1,0:T(8,128)(2,1)S(1)}, u32[]{:S(2)}, u32[]{:S(2)}) collective-permute-start(bf16[4,32,128]{2,1,0:T(8,128)(2,1)S(1)} %get-tuple-element.40), channel_id=1, source_target_pairs={{0,12},{4,8},{8,4},{12,0},{1,13},{5,9},{9,5},{13,1},{2,14},{6,10},... | collective-permute-start | bytes 98312 | tf_op jit(solution)/shard_map/ppermute | solution.py:163
  40.9 5.2 %collective-permute-start.15 = (bf16[4,32,128]{2,1,0:T(8,128)(2,1)S(1)}, bf16[4,32,128]{2,1,0:T(8,128)(2,1)S(1)}, u32[]{:S(2)}, u32[]{:S(2)}) collective-permute-start(bf16[4,32,128]{2,1,0:T(8,128)(2,1)S(1)} %get-tuple-element.42), channel_id=1, source_target_pairs={{0,4},{4,0},{8,12},{12,8},{1,5},{5,1},{9,13},{13,9},{2,6},{6,2},{1... | collective-permute-start | bytes 98312 | tf_op jit(solution)/shard_map/ppermute | solution.py:163
  41.5 5.1 %collective-permute-start.16 = (bf16[4,32,128]{2,1,0:T(8,128)(2,1)S(1)}, bf16[4,32,128]{2,1,0:T(8,128)(2,1)S(1)}, u32[]{:S(2)}, u32[]{:S(2)}) collective-permute-start(bf16[4,32,128]{2,1,0:T(8,128)(2,1)S(1)} %get-tuple-element.43), channel_id=1, source_target_pairs={{0,8},{4,12},{8,0},{12,4},{1,9},{5,13},{9,1},{13,5},{2,10},{6,14},... | collective-permute-start | bytes 98312 | tf_op jit(solution)/shard_map/ppermute | solution.py:163
  44.8 5.7 %collective-permute-start.17 = (bf16[4,32,128]{2,1,0:T(8,128)(2,1)S(1)}, bf16[4,32,128]{2,1,0:T(8,128)(2,1)S(1)}, u32[]{:S(2)}, u32[]{:S(2)}) collective-permute-start(bf16[4,32,128]{2,1,0:T(8,128)(2,1)S(1)} %get-tuple-element.44), channel_id=1, source_target_pairs={{0,12},{4,8},{8,4},{12,0},{1,13},{5,9},{9,5},{13,1},{2,14},{6,10},... | collective-permute-start | bytes 98312 | tf_op jit(solution)/shard_map/ppermute | solution.py:163

commit v3 on v2

--- a/solution.py
+++ b/solution.py
@@ -6,11 +6,6 @@
 from jax.experimental import pallas as pl
 from jax.experimental.pallas import tpu as pltpu
 from jax.sharding import PartitionSpec as P
-
-CALLS = 2
-SPLIT = 2
-COLUMN_ORDER = (3, 1, 2, 0)
-SMALL = pltpu.CompilerParams(vmem_limit_bytes=4 * 1024 * 1024)
 
 
 def term_kernel(
@@ -22,8 +17,7 @@
     wave_hbm,
     left_hbm,
     right_hbm,
-    send_ref,
-    keep_ref,
+    out_ref,
     cls,
     tid,
     pair,
@@ -45,7 +39,7 @@
     targets = total.shape[0]
     strip = width // 4
     share = left.shape[1] // 4
-    split = send_ref.shape[1]
+    split = 1
     rows = share // split
     unit = width // 8
     sec = lax.axis_index("sec")
@@ -64,14 +58,14 @@
 
     def fetch(j, carry):
         for q in range(4):
-            src = pl.multiple_of((sec ^ q) * strip + call * share, 16)
+            src = q * strip + call * share
             pltpu.make_async_copy(
                 left_hbm.at[0, j, pl.ds(src, share)],
                 left.at[j, pl.ds(q * share, share)],
                 left_sems.at[j],
             ).start()
-        for p, r in enumerate(COLUMN_ORDER):
-            src = pl.multiple_of((mpo ^ r) * strip, strip)
+        for p in range(4):
+            src = p * strip
             pltpu.make_async_copy(
                 right_hbm.at[0, j, pl.ds(src, strip)],
                 right.at[j, pl.ds(p * strip, strip)],
@@ -118,49 +112,18 @@
     line = lax.broadcasted_iota(jnp.int32, (rows, strip), 0)
 
     def store(t, carry):
-        for p, r in enumerate(COLUMN_ORDER):
-            out_ref = send_ref if p < 2 else keep_ref
-            cols_in = (mpo ^ r) * strip + lane < dims[1, t] * unit
+        for p in range(4):
+            cols_in = p * strip + lane < dims[1, t] * unit
             for q in range(4):
                 for g in range(split):
-                    first = (sec ^ q) * strip + call * share + g * rows
+                    first = q * strip + call * share + g * rows
                     inside = cols_in & (first + line < dims[0, t] * unit)
                     at = q * share + g * rows
                     value = total[t, at : at + rows, p * strip : (p + 1) * strip]
-                    out_ref[p % 2, g, q, t] = jnp.where(inside, value, 0.0).astype(jnp.bfloat16)
+                    out_ref[p, q, t] = jnp.where(inside, value, 0.0).astype(jnp.bfloat16)
         return carry
 
     lax.fori_loop(0, targets, store, 0)
-
-
-def far_kernel(keep_ref, recv_ref, *rest, piece):
-    far_ref = rest[-1]
-    far_ref[...] = add(keep_ref[0, piece], recv_ref[0, piece])
-
-
-def own_kernel(keep_ref, recv_ref, cross_ref, *own_refs, piece):
-    for q, own_ref in enumerate(own_refs):
-        own_ref[...] = add(keep_ref[1, piece, q], recv_ref[1, piece, q], cross_ref[q])
-
-
-def final_kernel(*refs):
-    pieces, out_ref = refs[:-1], refs[-1]
-    rows = pieces[0].shape[1]
-    for h in range(out_ref.shape[1] // rows):
-        out_ref[:, h * rows : (h + 1) * rows, :] = add(
-            *[piece[...] for piece in pieces[4 * h : 4 * h + 4]]
-        )
-
-
-def add(*arrays):
-    total = arrays[0].astype(jnp.float32)
-    for array in arrays[1:]:
-        total = total + array.astype(jnp.float32)
-    return total.astype(jnp.bfloat16)
-
-
-def swap(array, axis, mask):
-    return lax.ppermute(array, axis, [(i, i ^ mask) for i in range(lax.axis_size(axis))])
 
 
 def by_targets(
@@ -170,80 +133,37 @@
     terms = left_env.shape[1]
     targets = block_dims.shape[0]
     strip = width // 4
-    share = strip // CALLS
-    rows = share // SPLIT
     vmem = pl.BlockSpec(memory_space=pltpu.VMEM)
     hbm = pl.BlockSpec(memory_space=pltpu.HBM)
-    anywhere = pl.BlockSpec(memory_space=pl.ANY)
-    block = jax.ShapeDtypeStruct((4, targets, rows, strip), jnp.bfloat16)
-    part = jax.ShapeDtypeStruct((targets, rows, strip), jnp.bfloat16)
-    pair_out = jax.ShapeDtypeStruct((2, SPLIT) + block.shape, jnp.bfloat16)
     scalars = (term_class, term_id, pair_table, block_dims.T, mpo_coef)
     operands = [
         pltpu.with_memory_space_constraint(x, pltpu.HBM)
         for x in (*scalars, wave_blocks, left_env, right_env)
     ]
-    kept, received = [], []
-    for call in range(CALLS):
-        send, keep = pl.pallas_call(
-            functools.partial(term_kernel, call=call),
-            out_shape=[pair_out] * 2,
-            in_specs=[hbm] * 8,
-            out_specs=[vmem] * 2,
-            scratch_shapes=[pltpu.SMEM(scalar.shape, scalar.dtype) for scalar in scalars]
-            + [
-                pltpu.VMEM((width, width), jnp.bfloat16),
-                pltpu.VMEM((terms, 4 * share, width), jnp.bfloat16),
-                pltpu.VMEM((terms, width, width), jnp.bfloat16),
-                pltpu.VMEM((targets, 4 * share, width), jnp.float32),
-                pltpu.SemaphoreType.DMA((len(scalars),)),
-                pltpu.SemaphoreType.DMA,
-                pltpu.SemaphoreType.DMA((terms,)),
-                pltpu.SemaphoreType.DMA((terms,)),
-            ],
-            compiler_params=pltpu.CompilerParams(vmem_limit_bytes=20 * 1024 * 1024),
-            cost_estimate=pl.CostEstimate(
-                flops=4 * terms * width**3 // CALLS,
-                bytes_accessed=4 * 1024 * 1024,
-                transcendentals=0,
-            ),
-            name=f"terms_{call}",
-        )(*operands)
-        kept.append(keep)
-        received.append(swap(send, "mpo", 1))
-    pieces = []
-    after = []
-    for h in range(CALLS * SPLIT):
-        keep, recv = kept[h // SPLIT], received[h // SPLIT]
-        far = pl.pallas_call(
-            functools.partial(far_kernel, piece=h % SPLIT),
-            out_shape=block,
-            in_specs=[vmem, vmem] + [anywhere] * len(after),
-            out_specs=vmem,
-            compiler_params=SMALL,
-            name=f"far_{h}",
-        )(keep, recv, *after)
-        crossed = swap(far, "mpo", 2)
-        after = [crossed]
-        own = pl.pallas_call(
-            functools.partial(own_kernel, piece=h % SPLIT),
-            out_shape=[part] * 4,
-            in_specs=[vmem] * 3,
-            out_specs=[vmem] * 4,
-            compiler_params=SMALL,
-            name=f"own_{h}",
-        )(keep, recv, crossed)
-        pieces.append(own[0])
-        for q in (1, 2, 3):
-            pieces.append(swap(own[q], "sec", q))
-    return pl.pallas_call(
-        final_kernel,
-        out_shape=jax.ShapeDtypeStruct((targets, strip, strip), jnp.bfloat16),
-        in_specs=[vmem] * len(pieces),
+    out = pl.pallas_call(
+        functools.partial(term_kernel, call=0),
+        out_shape=jax.ShapeDtypeStruct((4, 4, targets, strip, strip), jnp.bfloat16),
+        in_specs=[hbm] * 8,
         out_specs=vmem,
-        compiler_params=SMALL,
-        name="final",
-    )(*pieces)
+        scratch_shapes=[pltpu.SMEM(scalar.shape, scalar.dtype) for scalar in scalars]
+        + [
+            pltpu.VMEM((width, width), jnp.bfloat16),
+            pltpu.VMEM((terms, width, width), jnp.bfloat16),
+            pltpu.VMEM((terms, width, width), jnp.bfloat16),
+            pltpu.VMEM((targets, width, width), jnp.float32),
+            pltpu.SemaphoreType.DMA((len(scalars),)),
+            pltpu.SemaphoreType.DMA,
+            pltpu.SemaphoreType.DMA((terms,)),
+            pltpu.SemaphoreType.DMA((terms,)),
+        ],
+        compiler_params=pltpu.CompilerParams(vmem_limit_bytes=20 * 1024 * 1024),
+        cost_estimate=pl.CostEstimate(
+            flops=4 * terms * width**3, bytes_accessed=4 * 1024 * 1024, transcendentals=0
+        ),
+        name="terms",
+    )(*operands)
+    out = lax.psum_scatter(out, "mpo", scatter_dimension=0, tiled=False)
+    return lax.psum_scatter(out, "sec", scatter_dimension=0, tiled=False)
 
 
 def by_classes(

time: 51.3 us -> 78 us (1.52)
  waiting for transfers between devices: 16.2 us -> 58.3 us
  starting transfers between devices: 26.8 us -> 0.04 us
  between operations: 0.06 us -> 13.4 us
  Pallas kernels: 8.18 us -> 6.06 us
    reduce_scatter x0 -> x2, waiting for transfers between devices: none -> 58.3 us  [the longest x1 34.2 us: by_targets(): out = lax.psum_scatter(out, 'mpo', scatter_dimension=0, tiled=False)]
    ppermute x18 -> x0, starting transfers between devices: 26.8 us -> none  [swap(): lax.ppermute(array, axis, [(i, i ^ mask) for i in range(lax.axis_size(axi...]
    ppermute x18 -> x0, waiting for transfers between devices: 16.2 us -> none  [swap(): lax.ppermute(array, axis, [(i, i ^ mask) for i in range(lax.axis_size(axi...]
    pallas_call x11 -> x1, Pallas kernels: 8.18 us -> 6.06 us  [by_targets(): pl.pallas_call(functools.partial(term_kernel, call=0), out_shape=jax.Shap...]
  transfers between devices with their start and end apart: 18 -> 2, of which waited for: 8 -> 2; matrix products, arithmetic and copies ran while one was open for 0% -> 0% of each run, Pallas kernels for 7% -> 0%
where the time goes in v3:
time: 78 us; the launch traced here: 77.8 us
  waiting for transfers between devices  58.3 us (75%)
  between operations  13.4 us (17%)
  Pallas kernels  6.06 us (8%)
    reduce_scatter x1, waiting for transfers between devices, by_targets(): out = lax.psum_scatter(out, 'mpo', scatter_dimension=0, tiled=False)  34.2 us
    reduce_scatter x1, waiting for transfers between devices, by_targets(): return lax.psum_scatter(out, 'sec', scatter_dimension=0, tiled=False)  24 us
    pallas_call x1, Pallas kernels, by_targets(): pl.pallas_call(functools.partial(term_kernel, call=0), out_shape=jax.Shap...  6.06 us
  transfers between devices with their start and end apart: 2, of which 2 were waited for; matrix products, arithmetic and copies ran while one was open for 0% of the time, Pallas kernels for 0%

profile of v3, /device:TPU:0, one launch (start us, length us, event | category | flops | bytes accessed | tf_op | source)
XLA Modules:
  0.0 77.8 jit_solution(15598920411018046536)
XLA Ops:
  6.5 0.0 reduce-scatter.3.cloned.1.call-start
  6.5 6.1 %terms.1 = bf16[4,4,4,128,128]{4,3,2,1,0:T(8,128)(2,1)} custom-call(s32[1,3]{1,0:T(1,128)} %cls_hbm.1, s32[1,3]{1,0:T(1,128)} %tid_hbm.1, s32[4,5]{1,0:T(4,128)} %pair_hbm.1, s32[2,4]{1,0:T(2,128)} %bitcast.4, f32[50]{0:T(128)} %coef_hbm.1, bf16[1,512,512]{2,1,0:T(8,128)(2,1)} %wave_hbm.1, bf16[1,3,512,512]{3,2,1,0:T(8,128)(2,1)} %left_hbm.1, ...), custom_call_target="tpu_custom_call" | custom-call | flops 1610612736 | bytes 4194304 | tf_op jit(solution)/shard_map/terms/pallas_call | solution.py:143
  12.6 0.0 reduce-scatter.3.cloned.1.call-update
  12.6 0.0 reduce-scatter.5.cloned.1.call-start
  12.7 34.2 %reduce-scatter.3.cloned.1.call-done = bf16[1,4,4,128,128]{4,3,2,1,0:T(8,128)(2,1)} async-done(((bf16[4,4,4,128,128]{4,3,2,1,0:T(8,128)(2,1)}), bf16[1,4,4,128,128]{4,3,2,1,0:T(8,128)(2,1)}) %reduce-scatter.3.cloned.1.call-update) | async-done | bytes 524304 | tf_op jit(solution)/shard_map/reduce_scatter | solution.py:165
  46.9 0.0 reduce-scatter.5.cloned.1.call-update
  46.9 24.0 %reduce-scatter.5.cloned.1.call-done = bf16[1,4,128,128]{3,2,1,0:T(8,128)(2,1)} async-done(((bf16[4,4,128,128]{3,2,1,0:T(8,128)(2,1)}), bf16[1,4,128,128]{3,2,1,0:T(8,128)(2,1)}) %reduce-scatter.5.cloned.1.call-update) | async-done | bytes 131088 | tf_op jit(solution)/shard_map/reduce_scatter | solution.py:166
Async XLA Ops:
  6.5 40.4 %reduce-scatter.3.cloned.1.call-start = ((), (), s32[]{:S(2)}) async-start(), calls=%async_computation.2 | async-start | bytes 2621440 | tf_op jit(solution)/shard_map/reduce_scatter | solution.py:165
  12.6 58.3 %reduce-scatter.5.cloned.1.call-start = ((), (), s32[]{:S(2)}) async-start(), calls=%async_computation.3 | async-start | bytes 655360 | tf_op jit(solution)/shard_map/reduce_scatter | solution.py:166
Sparse Core Ops, SparseCore 0:
  12.7 34.1 reduce-scatter.2
  49.3 21.6 reduce-scatter.4

commit v4 on v3

--- a/solution.py
+++ b/solution.py
@@ -6,6 +6,10 @@
 from jax.experimental import pallas as pl
 from jax.experimental.pallas import tpu as pltpu
 from jax.sharding import PartitionSpec as P
+
+SPLIT = 2
+COLUMN_ORDER = (3, 1, 2, 0)
+SMALL = pltpu.CompilerParams(vmem_limit_bytes=4 * 1024 * 1024)
 
 
 def term_kernel(
@@ -17,7 +21,10 @@
     wave_hbm,
     left_hbm,
     right_hbm,
-    out_ref,
+    far_send,
+    near_send,
+    far_keep,
+    near_keep,
     cls,
     tid,
     pair,
@@ -31,16 +38,12 @@
     wave_sem,
     left_sems,
     right_sems,
-    *,
-    call,
 ):
     width = wave.shape[0]
     terms = left.shape[0]
     targets = total.shape[0]
     strip = width // 4
-    share = left.shape[1] // 4
-    split = 1
-    rows = share // split
+    split, _, _, rows, _ = far_send.shape
     unit = width // 8
     sec = lax.axis_index("sec")
     mpo = lax.axis_index("mpo")
@@ -57,15 +60,9 @@
     wave_copy.start()
 
     def fetch(j, carry):
-        for q in range(4):
-            src = q * strip + call * share
-            pltpu.make_async_copy(
-                left_hbm.at[0, j, pl.ds(src, share)],
-                left.at[j, pl.ds(q * share, share)],
-                left_sems.at[j],
-            ).start()
-        for p in range(4):
-            src = p * strip
+        pltpu.make_async_copy(left_hbm.at[0, j], left.at[j], left_sems.at[j]).start()
+        for p, r in enumerate(COLUMN_ORDER):
+            src = pl.multiple_of((mpo ^ r) * strip, strip)
             pltpu.make_async_copy(
                 right_hbm.at[0, j, pl.ds(src, strip)],
                 right.at[j, pl.ds(p * strip, strip)],
@@ -93,9 +90,7 @@
     lax.fori_loop(0, width // 64, mask, 0)
 
     def term(j, carry):
-        pltpu.make_async_copy(
-            left_hbm.at[0, j, pl.ds(0, 4 * share)], left.at[j], left_sems.at[j]
-        ).wait()
+        pltpu.make_async_copy(left_hbm.at[0, j], left.at[j], left_sems.at[j]).wait()
         half = jnp.dot(left[j], wave[...], preferred_element_type=jnp.float32)
         half = half.astype(jnp.bfloat16)
         pltpu.make_async_copy(right_hbm.at[0, j], right.at[j], right_sems.at[j]).wait()
@@ -112,18 +107,44 @@
     line = lax.broadcasted_iota(jnp.int32, (rows, strip), 0)
 
     def store(t, carry):
-        for p in range(4):
-            cols_in = p * strip + lane < dims[1, t] * unit
+        for p, r in enumerate(COLUMN_ORDER):
+            out_ref = (far_send, near_send, far_keep, near_keep)[p]
+            cols_in = (mpo ^ r) * strip + lane < dims[1, t] * unit
             for q in range(4):
                 for g in range(split):
-                    first = q * strip + call * share + g * rows
-                    inside = cols_in & (first + line < dims[0, t] * unit)
-                    at = q * share + g * rows
+                    at = q * strip + g * rows
+                    inside = cols_in & (at + line < dims[0, t] * unit)
                     value = total[t, at : at + rows, p * strip : (p + 1) * strip]
-                    out_ref[p, q, t] = jnp.where(inside, value, 0.0).astype(jnp.bfloat16)
+                    out_ref[g, q, t] = jnp.where(inside, value, 0.0).astype(jnp.bfloat16)
         return carry
 
     lax.fori_loop(0, targets, store, 0)
+
+
+def far_kernel(keep_ref, recv_ref, far_ref, *, piece):
+    far_ref[...] = add(keep_ref[piece], recv_ref[piece])
+
+
+def own_kernel(keep_ref, recv_ref, cross_ref, own_ref, *, piece):
+    own_ref[...] = add(keep_ref[piece], recv_ref[piece], cross_ref[...])
+
+
+def final_kernel(*refs):
+    pieces, out_ref = refs[:-1], refs[-1]
+    rows = pieces[0].shape[2]
+    for h, piece in enumerate(pieces):
+        out_ref[:, h * rows : (h + 1) * rows, :] = add(*[piece[k] for k in range(4)])
+
+
+def add(*arrays):
+    total = arrays[0].astype(jnp.float32)
+    for array in arrays[1:]:
+        total = total + array.astype(jnp.float32)
+    return total.astype(jnp.bfloat16)
+
+
+def swap(array, axis, mask):
+    return lax.ppermute(array, axis, [(i, i ^ mask) for i in range(lax.axis_size(axis))])
 
 
 def by_targets(
@@ -133,18 +154,21 @@
     terms = left_env.shape[1]
     targets = block_dims.shape[0]
     strip = width // 4
+    rows = strip // SPLIT
     vmem = pl.BlockSpec(memory_space=pltpu.VMEM)
     hbm = pl.BlockSpec(memory_space=pltpu.HBM)
+    piece = jax.ShapeDtypeStruct((4, targets, rows, strip), jnp.bfloat16)
+    pieces = jax.ShapeDtypeStruct((SPLIT,) + piece.shape, jnp.bfloat16)
     scalars = (term_class, term_id, pair_table, block_dims.T, mpo_coef)
     operands = [
         pltpu.with_memory_space_constraint(x, pltpu.HBM)
         for x in (*scalars, wave_blocks, left_env, right_env)
     ]
-    out = pl.pallas_call(
-        functools.partial(term_kernel, call=0),
-        out_shape=jax.ShapeDtypeStruct((4, 4, targets, strip, strip), jnp.bfloat16),
+    far_send, near_send, far_keep, near_keep = pl.pallas_call(
+        term_kernel,
+        out_shape=[pieces] * 4,
         in_specs=[hbm] * 8,
-        out_specs=vmem,
+        out_specs=[vmem] * 4,
         scratch_shapes=[pltpu.SMEM(scalar.shape, scalar.dtype) for scalar in scalars]
         + [
             pltpu.VMEM((width, width), jnp.bfloat16),
@@ -162,8 +186,36 @@
         ),
         name="terms",
     )(*operands)
-    out = lax.psum_scatter(out, "mpo", scatter_dimension=0, tiled=False)
-    return lax.psum_scatter(out, "sec", scatter_dimension=0, tiled=False)
+    far_recv = swap(far_send, "mpo", 1)
+    near_recv = swap(near_send, "mpo", 1)
+    arrived = []
+    for h in range(SPLIT):
+        far = pl.pallas_call(
+            functools.partial(far_kernel, piece=h),
+            out_shape=piece,
+            in_specs=[vmem] * 2,
+            out_specs=vmem,
+            compiler_params=SMALL,
+            name=f"far_{h}",
+        )(far_keep, far_recv)
+        crossed = swap(far, "mpo", 2)
+        own = pl.pallas_call(
+            functools.partial(own_kernel, piece=h),
+            out_shape=piece,
+            in_specs=[vmem] * 3,
+            out_specs=vmem,
+            compiler_params=SMALL,
+            name=f"own_{h}",
+        )(near_keep, near_recv, crossed)
+        arrived.append(lax.all_to_all(own, "sec", split_axis=0, concat_axis=0, tiled=True))
+    return pl.pallas_call(
+        final_kernel,
+        out_shape=jax.ShapeDtypeStruct((targets, strip, strip), jnp.bfloat16),
+        in_specs=[vmem] * SPLIT,
+        out_specs=vmem,
+        compiler_params=SMALL,
+        name="final",
+    )(*arrived)
 
 
 def by_classes(

time: 78 us -> 42.5 us (0.54)
  waiting for transfers between devices: 58.3 us -> 14.7 us
  between operations: 13.4 us -> 0.02 us
  blocking collectives: 0 us -> 10.9 us
  starting transfers between devices: 0.04 us -> 10.2 us
    reduce_scatter x2 -> x0, waiting for transfers between devices: 58.3 us -> none  [the longest x1 34.2 us: by_targets(): out = lax.psum_scatter(out, 'mpo', scatter_dimension=0, tiled=False)]
    ppermute x0 -> x4, waiting for transfers between devices: none -> 13.8 us  [swap(): lax.ppermute(array, axis, [(i, i ^ mask) for i in range(lax.axis_size(axi...]
    all_to_all x0 -> x1, blocking collectives: none -> 10.9 us  [by_targets(): lax.all_to_all(own, 'sec', split_axis=0, concat_axis=0, tiled=True)]
    all_to_all x0 -> x1, starting transfers between devices: none -> 5.12 us  [by_targets(): lax.all_to_all(own, 'sec', split_axis=0, concat_axis=0, tiled=True)]
    ppermute x0 -> x4, starting transfers between devices: none -> 5.08 us  [swap(): lax.ppermute(array, axis, [(i, i ^ mask) for i in range(lax.axis_size(axi...]
    all_to_all x0 -> x1, waiting for transfers between devices: none -> 0.88 us  [by_targets(): lax.all_to_all(own, 'sec', split_axis=0, concat_axis=0, tiled=True)]
    pallas_call x1 -> x6, Pallas kernels: 6.06 us -> 6.5 us  [the longest x1 4.76 us: by_targets(): pl.pallas_call(term_kernel, out_shape=[pieces] * 4, in_specs=[hbm] * 8, o...]
  transfers between devices with their start and end apart: 2 -> 5, of which waited for: 2 -> 4; matrix products, arithmetic and copies ran while one was open for 0% -> 0% of each run, Pallas kernels for 0% -> 1%
where the time goes in v4:
time: 42.5 us; the launch traced here: 42.3 us
  waiting for transfers between devices  14.7 us (35%)
  blocking collectives  10.9 us (26%)
  starting transfers between devices  10.2 us (24%)
  Pallas kernels  6.5 us (15%)
    ppermute x4, waiting for transfers between devices, swap(): lax.ppermute(array, axis, [(i, i ^ mask) for i in range(lax.axis_size(axi...  13.8 us
    all_to_all x1, blocking collectives, by_targets(): lax.all_to_all(own, 'sec', split_axis=0, concat_axis=0, tiled=True)  10.9 us
    all_to_all x1, starting transfers between devices, by_targets(): lax.all_to_all(own, 'sec', split_axis=0, concat_axis=0, tiled=True)  5.12 us
    ppermute x4, starting transfers between devices, swap(): lax.ppermute(array, axis, [(i, i ^ mask) for i in range(lax.axis_size(axi...  5.08 us
    pallas_call x1, Pallas kernels, by_targets(): pl.pallas_call(term_kernel, out_shape=[pieces] * 4, in_specs=[hbm] * 8, o...  4.76 us
    pallas_call x2, Pallas kernels, by_targets(): pl.pallas_call(functools.partial(own_kernel, piece=h), out_shape=piece, i...  0.89 us
    all_to_all x1, waiting for transfers between devices, by_targets(): lax.all_to_all(own, 'sec', split_axis=0, concat_axis=0, tiled=True)  0.88 us
  transfers between devices with their start and end apart: 5, of which 4 were waited for; matrix products, arithmetic and copies ran while one was open for 0% of the time, Pallas kernels for 1%

profile of v4, /device:TPU:0, one launch (start us, length us, event | category | flops | bytes accessed | tf_op | source)
XLA Modules:
  0.0 42.3 jit_solution(8162950714308839212)
XLA Ops:
  0.0 4.8 %terms.1 = (bf16[2,4,4,64,128]{4,3,2,1,0:T(8,128)(2,1)S(1)}, bf16[2,4,4,64,128]{4,3,2,1,0:T(8,128)(2,1)S(1)}, bf16[2,4,4,64,128]{4,3,2,1,0:T(8,128)(2,1)S(1)}, bf16[2,4,4,64,128]{4,3,2,1,0:T(8,128)(2,1)S(1)}) custom-call(s32[1,3]{1,0:T(1,128)} %cls_hbm.1, s32[1,3]{1,0:T(1,128)} %tid_hbm.1, s32[4,5]{1,0:T(4,128)} %pair_hbm.1, s32[2,4]{1,0:T(2,128)} %bitcast.1, ...), custom_call_target="tpu_custom_call" | custom-call | flops 1610612736 | bytes 4194304 | tf_op jit(solution)/shard_map/terms/pallas_call | solution.py:167
  4.8 0.5 %collective-permute-start.1 = (bf16[2,4,4,64,128]{4,3,2,1,0:T(8,128)(2,1)S(1)}, bf16[2,4,4,64,128]{4,3,2,1,0:T(8,128)(2,1)S(1)}, u32[]{:S(2)}, u32[]{:S(2)}) collective-permute-start(bf16[2,4,4,64,128]{4,3,2,1,0:T(8,128)(2,1)S(1)} %get-tuple-element.12), channel_id=1, source_target_pairs={{0,1},{1,0},{2,3},{3,2},{4,5},{5,4},{6,7},{7,6},{8,9},{9,8},{10,11... | collective-permute-start | bytes 1572872 | tf_op jit(solution)/shard_map/ppermute | solution.py:147
  5.3 0.1 collective-permute-start
  5.4 1.5 %collective-permute-done.1.recv_ref = bf16[2,4,4,64,128]{4,3,2,1,0:T(8,128)(2,1)S(1)} collective-permute-done((bf16[2,4,4,64,128]{4,3,2,1,0:T(8,128)(2,1)S(1)}, bf16[2,4,4,64,128]{4,3,2,1,0:T(8,128)(2,1)S(1)}, u32[]{:S(2)}, u32[]{:S(2)}) %collective-permute-start.1) | collective-permute-done | bytes 524320 | tf_op jit(solution)/shard_map/ppermute | solution.py:147
  6.8 0.1 far_0.1
  6.9 2.9 %collective-permute-start.2 = (bf16[4,4,64,128]{3,2,1,0:T(8,128)(2,1)S(1)}, bf16[4,4,64,128]{3,2,1,0:T(8,128)(2,1)S(1)}, u32[]{:S(2)}, u32[]{:S(2)}) collective-permute-start(bf16[4,4,64,128]{3,2,1,0:T(8,128)(2,1)S(1)} %far_0.1), channel_id=1, source_target_pairs={{0,2},{1,3},{2,0},{3,1},{4,6},{5,7},{6,4},{7,5},{8,10},{9,11},{10,... | collective-permute-start | bytes 786440 | tf_op jit(solution)/shard_map/ppermute | solution.py:147
  9.8 0.0 collective-permute-done.recv_ref
  9.8 6.6 %collective-permute-done.2.cross_ref = bf16[4,4,64,128]{3,2,1,0:T(8,128)(2,1)S(1)} collective-permute-done((bf16[4,4,64,128]{3,2,1,0:T(8,128)(2,1)S(1)}, bf16[4,4,64,128]{3,2,1,0:T(8,128)(2,1)S(1)}, u32[]{:S(2)}, u32[]{:S(2)}) %collective-permute-start.2) | collective-permute-done | bytes 262176 | tf_op jit(solution)/shard_map/ppermute | solution.py:147
  16.4 0.8 %own_0.1 = bf16[4,4,64,128]{3,2,1,0:T(8,128)(2,1)} custom-call(bf16[2,4,4,64,128]{4,3,2,1,0:T(8,128)(2,1)S(1)} %get-tuple-element.9.keep_ref, bf16[2,4,4,64,128]{4,3,2,1,0:T(8,128)(2,1)S(1)} %collective-permute-done.recv_ref, bf16[4,4,64,128]{3,2,1,0:T(8,128)(2,1)S(1)} %collective-permute-done.2.cross_ref), custom_call_target="tpu_custom_call" | custom-call | tf_op jit(solution)/shard_map/own_0/pallas_call | solution.py:202
  17.2 5.1 %all-to-all-start = ((bf16[4,4,64,128]{3,2,1,0:T(8,128)(2,1)}), bf16[4,4,64,128]{3,2,1,0:T(8,128)(2,1)S(1)}, u32[]{:S(2)}, u32[]{:S(2)}) async-start(bf16[4,4,64,128]{3,2,1,0:T(8,128)(2,1)} %own_0.1), calls=%async_computation | async-start | bytes 524288 | tf_op jit(solution)/shard_map/all_to_all | solution.py:210
  22.3 0.1 far_1.1
  22.4 1.6 %collective-permute-start.3 = (bf16[4,4,64,128]{3,2,1,0:T(8,128)(2,1)S(1)}, bf16[4,4,64,128]{3,2,1,0:T(8,128)(2,1)S(1)}, u32[]{:S(2)}, u32[]{:S(2)}) collective-permute-start(bf16[4,4,64,128]{3,2,1,0:T(8,128)(2,1)S(1)} %far_1.1), channel_id=1, source_target_pairs={{0,2},{1,3},{2,0},{3,1},{4,6},{5,7},{6,4},{7,5},{8,10},{9,11},{10,... | collective-permute-start | bytes 786440 | tf_op jit(solution)/shard_map/ppermute | solution.py:147
  24.0 5.7 %collective-permute-done.3.cross_ref = bf16[4,4,64,128]{3,2,1,0:T(8,128)(2,1)S(1)} collective-permute-done((bf16[4,4,64,128]{3,2,1,0:T(8,128)(2,1)S(1)}, bf16[4,4,64,128]{3,2,1,0:T(8,128)(2,1)S(1)}, u32[]{:S(2)}, u32[]{:S(2)}) %collective-permute-start.3) | collective-permute-done | bytes 262176 | tf_op jit(solution)/shard_map/ppermute | solution.py:147
  29.7 0.1 own_1.1
  29.8 0.9 %all-to-all-done.refs_0_ = bf16[4,4,64,128]{3,2,1,0:T(8,128)(2,1)S(1)} async-done(((bf16[4,4,64,128]{3,2,1,0:T(8,128)(2,1)}), bf16[4,4,64,128]{3,2,1,0:T(8,128)(2,1)S(1)}, u32[]{:S(2)}, u32[]{:S(2)}) %all-to-all-start) | async-done | bytes 262176 | tf_op jit(solution)/shard_map/all_to_all | solution.py:210
  30.7 10.9 %all_to_all.10.refs_1_ = bf16[4,4,64,128]{3,2,1,0:T(8,128)(2,1)S(1)} all-to-all(bf16[4,4,64,128]{3,2,1,0:T(8,128)(2,1)S(1)} %own_1.1), channel_id=1, replica_groups=mesh['grp'=2,'sec'=4,'mpo'=4] {'sec'}, dimensions={0} | all-to-all | bytes 524288 | tf_op jit(solution)/shard_map/all_to_all | solution.py:210
  41.6 0.7 %final.1 = bf16[4,128,128]{2,1,0:T(8,128)(2,1)} custom-call(bf16[4,4,64,128]{3,2,1,0:T(8,128)(2,1)S(1)} %all-to-all-done.refs_0_, bf16[4,4,64,128]{3,2,1,0:T(8,128)(2,1)S(1)} %all_to_all.10.refs_1_), custom_call_target="tpu_custom_call" | custom-call | tf_op jit(solution)/shard_map/final/pallas_call | solution.py:211
Async XLA Ops:
  4.8 2.1 %collective-permute-start.1 = (bf16[2,4,4,64,128]{4,3,2,1,0:T(8,128)(2,1)S(1)}, bf16[2,4,4,64,128]{4,3,2,1,0:T(8,128)(2,1)S(1)}, u32[]{:S(2)}, u32[]{:S(2)}) collective-permute-start(bf16[2,4,4,64,128]{4,3,2,1,0:T(8,128)(2,1)S(1)} %get-tuple-element.12), channel_id=1, source_target_pairs={{0,1},{1,0},{2,3},{3,2},{4,5},{5,4},{6,7},{7,6},{8,9},{9,8},{10,11... | collective-permute-start | bytes 1572872 | tf_op jit(solution)/shard_map/ppermute | solution.py:147
  5.3 4.5 %collective-permute-start = (bf16[2,4,4,64,128]{4,3,2,1,0:T(8,128)(2,1)S(1)}, bf16[2,4,4,64,128]{4,3,2,1,0:T(8,128)(2,1)S(1)}, u32[]{:S(2)}, u32[]{:S(2)}) collective-permute-start(bf16[2,4,4,64,128]{4,3,2,1,0:T(8,128)(2,1)S(1)} %get-tuple-element.10), channel_id=1, source_target_pairs={{0,1},{1,0},{2,3},{3,2},{4,5},{5,4},{6,7},{7,6},{8,9},{9,8},{10,11... | collective-permute-start | bytes 1572872 | tf_op jit(solution)/shard_map/ppermute | solution.py:147
  6.9 9.5 %collective-permute-start.2 = (bf16[4,4,64,128]{3,2,1,0:T(8,128)(2,1)S(1)}, bf16[4,4,64,128]{3,2,1,0:T(8,128)(2,1)S(1)}, u32[]{:S(2)}, u32[]{:S(2)}) collective-permute-start(bf16[4,4,64,128]{3,2,1,0:T(8,128)(2,1)S(1)} %far_0.1), channel_id=1, source_target_pairs={{0,2},{1,3},{2,0},{3,1},{4,6},{5,7},{6,4},{7,5},{8,10},{9,11},{10,... | collective-permute-start | bytes 786440 | tf_op jit(solution)/shard_map/ppermute | solution.py:147
  17.2 13.5 %all-to-all-start = ((bf16[4,4,64,128]{3,2,1,0:T(8,128)(2,1)}), bf16[4,4,64,128]{3,2,1,0:T(8,128)(2,1)S(1)}, u32[]{:S(2)}, u32[]{:S(2)}) async-start(bf16[4,4,64,128]{3,2,1,0:T(8,128)(2,1)} %own_0.1), calls=%async_computation | async-start | bytes 524288 | tf_op jit(solution)/shard_map/all_to_all | solution.py:210
  22.4 7.3 %collective-permute-start.3 = (bf16[4,4,64,128]{3,2,1,0:T(8,128)(2,1)S(1)}, bf16[4,4,64,128]{3,2,1,0:T(8,128)(2,1)S(1)}, u32[]{:S(2)}, u32[]{:S(2)}) collective-permute-start(bf16[4,4,64,128]{3,2,1,0:T(8,128)(2,1)S(1)} %far_1.1), channel_id=1, source_target_pairs={{0,2},{1,3},{2,0},{3,1},{4,6},{5,7},{6,4},{7,5},{8,10},{9,11},{10,... | collective-permute-start | bytes 786440 | tf_op jit(solution)/shard_map/ppermute | solution.py:147

commit v5 on v3

--- a/solution.py
+++ b/solution.py
@@ -6,6 +6,9 @@
 from jax.experimental import pallas as pl
 from jax.experimental.pallas import tpu as pltpu
 from jax.sharding import PartitionSpec as P
+
+COLUMN_ORDER = (3, 1, 2, 0)
+SMALL = pltpu.CompilerParams(vmem_limit_bytes=4 * 1024 * 1024)
 
 
 def term_kernel(
@@ -17,7 +20,12 @@
     wave_hbm,
     left_hbm,
     right_hbm,
-    out_ref,
+    a_far_send,
+    a_near_send,
+    a_far_keep,
+    a_near_keep,
+    b_send,
+    b_keep,
     cls,
     tid,
     pair,
@@ -31,16 +39,11 @@
     wave_sem,
     left_sems,
     right_sems,
-    *,
-    call,
 ):
     width = wave.shape[0]
     terms = left.shape[0]
     targets = total.shape[0]
     strip = width // 4
-    share = left.shape[1] // 4
-    split = 1
-    rows = share // split
     unit = width // 8
     sec = lax.axis_index("sec")
     mpo = lax.axis_index("mpo")
@@ -58,14 +61,14 @@
 
     def fetch(j, carry):
         for q in range(4):
-            src = q * strip + call * share
+            src = pl.multiple_of((sec ^ q) * strip, strip)
             pltpu.make_async_copy(
-                left_hbm.at[0, j, pl.ds(src, share)],
-                left.at[j, pl.ds(q * share, share)],
+                left_hbm.at[0, j, pl.ds(src, strip)],
+                left.at[j, pl.ds(q * strip, strip)],
                 left_sems.at[j],
             ).start()
-        for p in range(4):
-            src = p * strip
+        for p, r in enumerate(COLUMN_ORDER):
+            src = pl.multiple_of((mpo ^ r) * strip, strip)
             pltpu.make_async_copy(
                 right_hbm.at[0, j, pl.ds(src, strip)],
                 right.at[j, pl.ds(p * strip, strip)],
@@ -93,9 +96,7 @@
     lax.fori_loop(0, width // 64, mask, 0)
 
     def term(j, carry):
-        pltpu.make_async_copy(
-            left_hbm.at[0, j, pl.ds(0, 4 * share)], left.at[j], left_sems.at[j]
-        ).wait()
+        pltpu.make_async_copy(left_hbm.at[0, j], left.at[j], left_sems.at[j]).wait()
         half = jnp.dot(left[j], wave[...], preferred_element_type=jnp.float32)
         half = half.astype(jnp.bfloat16)
         pltpu.make_async_copy(right_hbm.at[0, j], right.at[j], right_sems.at[j]).wait()
@@ -108,22 +109,62 @@
 
     lax.fori_loop(0, terms, term, 0)
 
-    lane = lax.broadcasted_iota(jnp.int32, (rows, strip), 1)
-    line = lax.broadcasted_iota(jnp.int32, (rows, strip), 0)
+    a_rows = a_far_send.shape[2]
+    lane = lax.broadcasted_iota(jnp.int32, (strip, strip), 1)
+    line = lax.broadcasted_iota(jnp.int32, (strip, strip), 0)
 
     def store(t, carry):
-        for p in range(4):
-            cols_in = p * strip + lane < dims[1, t] * unit
+        for p, r in enumerate(COLUMN_ORDER):
+            a_ref = (a_far_send, a_near_send, a_far_keep, a_near_keep)[p]
+            b_ref = b_send if p < 2 else b_keep
+            cols_in = (mpo ^ r) * strip + lane < dims[1, t] * unit
             for q in range(4):
-                for g in range(split):
-                    first = q * strip + call * share + g * rows
-                    inside = cols_in & (first + line < dims[0, t] * unit)
-                    at = q * share + g * rows
-                    value = total[t, at : at + rows, p * strip : (p + 1) * strip]
-                    out_ref[p, q, t] = jnp.where(inside, value, 0.0).astype(jnp.bfloat16)
+                inside = cols_in & ((sec ^ q) * strip + line < dims[0, t] * unit)
+                value = total[t, q * strip : (q + 1) * strip, p * strip : (p + 1) * strip]
+                value = jnp.where(inside, value, 0.0).astype(jnp.bfloat16)
+                a_ref[q, t] = value[:a_rows]
+                b_ref[p % 2, q, t] = value[a_rows:]
         return carry
 
     lax.fori_loop(0, targets, store, 0)
+
+
+def far_kernel(keep_ref, recv_ref, far_ref):
+    far_ref[...] = add(keep_ref[...], recv_ref[...])
+
+
+def a_kernel(keep_ref, recv_ref, cross_ref, *own_refs):
+    for q, own_ref in enumerate(own_refs):
+        own_ref[...] = add(keep_ref[q], recv_ref[q], cross_ref[q])
+
+
+def b_kernel(keep_ref, recv_ref, *own_refs):
+    for q, own_ref in enumerate(own_refs):
+        own_ref[...] = add(keep_ref[:, q], recv_ref[:, q])
+
+
+def b_sum_kernel(*refs):
+    pieces, (far_ref, near_ref) = refs[:-2], refs[-2:]
+    far_ref[...] = add(*[piece[0] for piece in pieces])
+    near_ref[...] = add(*[piece[1] for piece in pieces])
+
+
+def final_kernel(near_ref, cross_ref, *refs):
+    pieces, out_ref = refs[:-1], refs[-1]
+    a_rows = pieces[0].shape[1]
+    out_ref[:, :a_rows, :] = add(*[piece[...] for piece in pieces])
+    out_ref[:, a_rows:, :] = add(near_ref[...], cross_ref[...])
+
+
+def add(*arrays):
+    total = arrays[0].astype(jnp.float32)
+    for array in arrays[1:]:
+        total = total + array.astype(jnp.float32)
+    return total.astype(jnp.bfloat16)
+
+
+def swap(array, axis, mask):
+    return lax.ppermute(array, axis, [(i, i ^ mask) for i in range(lax.axis_size(axis))])
 
 
 def by_targets(
@@ -133,18 +174,34 @@
     terms = left_env.shape[1]
     targets = block_dims.shape[0]
     strip = width // 4
+    a_rows = strip * 5 // 8
+    b_rows = strip - a_rows
     vmem = pl.BlockSpec(memory_space=pltpu.VMEM)
     hbm = pl.BlockSpec(memory_space=pltpu.HBM)
+
+    def like(*shape):
+        return jax.ShapeDtypeStruct(shape + (strip,), jnp.bfloat16)
+
+    def call(kernel, out_shape, *args):
+        return pl.pallas_call(
+            kernel,
+            out_shape=out_shape,
+            in_specs=[vmem] * len(args),
+            out_specs=jax.tree.map(lambda _: vmem, out_shape),
+            compiler_params=SMALL,
+            name=kernel.__name__,
+        )(*args)
+
     scalars = (term_class, term_id, pair_table, block_dims.T, mpo_coef)
     operands = [
         pltpu.with_memory_space_constraint(x, pltpu.HBM)
         for x in (*scalars, wave_blocks, left_env, right_env)
     ]
-    out = pl.pallas_call(
-        functools.partial(term_kernel, call=0),
-        out_shape=jax.ShapeDtypeStruct((4, 4, targets, strip, strip), jnp.bfloat16),
+    a_far_send, a_near_send, a_far_keep, a_near_keep, b_send, b_keep = pl.pallas_call(
+        term_kernel,
+        out_shape=[like(4, targets, a_rows)] * 4 + [like(2, 4, targets, b_rows)] * 2,
         in_specs=[hbm] * 8,
-        out_specs=vmem,
+        out_specs=[vmem] * 6,
         scratch_shapes=[pltpu.SMEM(scalar.shape, scalar.dtype) for scalar in scalars]
         + [
             pltpu.VMEM((width, width), jnp.bfloat16),
@@ -162,8 +219,18 @@
         ),
         name="terms",
     )(*operands)
-    out = lax.psum_scatter(out, "mpo", scatter_dimension=0, tiled=False)
-    return lax.psum_scatter(out, "sec", scatter_dimension=0, tiled=False)
+    a_far_recv = swap(a_far_send, "mpo", 1)
+    b_recv = swap(b_send, "mpo", 1)
+    a_near_recv = swap(a_near_send, "mpo", 1)
+    a_far = call(far_kernel, like(4, targets, a_rows), a_far_keep, a_far_recv)
+    a_cross = swap(a_far, "mpo", 2)
+    b_own = call(b_kernel, [like(2, targets, b_rows)] * 4, b_keep, b_recv)
+    b_pieces = [b_own[0]] + [swap(b_own[q], "sec", q) for q in (1, 2, 3)]
+    a_own = call(a_kernel, [like(targets, a_rows)] * 4, a_near_keep, a_near_recv, a_cross)
+    a_pieces = [a_own[0]] + [swap(a_own[q], "sec", q) for q in (1, 2, 3)]
+    b_far, b_near = call(b_sum_kernel, [like(targets, b_rows)] * 2, *b_pieces)
+    b_cross = swap(b_far, "mpo", 2)
+    return call(final_kernel, like(targets, strip), b_near, b_cross, *a_pieces)
 
 
 def by_classes(

time: 78 us -> 29.5 us (0.38)
  waiting for transfers between devices: 58.3 us -> 8.88 us
  starting transfers between devices: 0.04 us -> 14.6 us
  between operations: 13.4 us -> 0.05 us
    reduce_scatter x2 -> x0, waiting for transfers between devices: 58.3 us -> none  [the longest x1 34.2 us: by_targets(): out = lax.psum_scatter(out, 'mpo', scatter_dimension=0, tiled=False)]
    ppermute x0 -> x11, starting transfers between devices: none -> 14.6 us  [swap(): lax.ppermute(array, axis, [(i, i ^ mask) for i in range(lax.axis_size(axi...]
    ppermute x0 -> x11, waiting for transfers between devices: none -> 8.88 us  [swap(): lax.ppermute(array, axis, [(i, i ^ mask) for i in range(lax.axis_size(axi...]
    pallas_call x1 -> x6, Pallas kernels: 6.06 us -> 5.8 us  [the longest x1 4.74 us: by_targets(): pl.pallas_call(term_kernel, out_shape=[like(4, targets, a_rows)] * 4 + [l...]
  transfers between devices with their start and end apart: 2 -> 11, of which waited for: 2 -> 4; matrix products, arithmetic and copies ran while one was open for 0% -> 0% of each run, Pallas kernels for 0% -> 1%
where the time goes in v5:
time: 29.5 us; the launch traced here: 29.4 us
  starting transfers between devices  14.6 us (49%)
  waiting for transfers between devices  8.88 us (30%)
  Pallas kernels  5.8 us (20%)
    ppermute x11, starting transfers between devices, swap(): lax.ppermute(array, axis, [(i, i ^ mask) for i in range(lax.axis_size(axi...  14.6 us
    ppermute x11, waiting for transfers between devices, swap(): lax.ppermute(array, axis, [(i, i ^ mask) for i in range(lax.axis_size(axi...  8.88 us
    pallas_call x1, Pallas kernels, by_targets(): pl.pallas_call(term_kernel, out_shape=[like(4, targets, a_rows)] * 4 + [l...  4.74 us
    pallas_call x5, Pallas kernels, call(): pl.pallas_call(kernel, out_shape=out_shape, in_specs=[vmem] * len(args),...  1.05 us
  transfers between devices with their start and end apart: 11, of which 4 were waited for; matrix products, arithmetic and copies ran while one was open for 0% of the time, Pallas kernels for 1%

profile of v5, /device:TPU:0, one launch (start us, length us, event | category | flops | bytes accessed | tf_op | source)
XLA Modules:
  0.0 29.4 jit_solution(12684632582056900048)
XLA Ops:
  0.0 4.7 %terms.1 = (bf16[4,4,80,128]{3,2,1,0:T(8,128)(2,1)S(1)}, bf16[4,4,80,128]{3,2,1,0:T(8,128)(2,1)S(1)}, bf16[4,4,80,128]{3,2,1,0:T(8,128)(2,1)S(1)}, bf16[4,4,80,1...) custom-call(s32[1,3]{1,0:T(1,128)} %cls_hbm.1, ...), custom_call_target="tpu_custom_call" | custom-call | flops 1610612736 | bytes 4194304 | tf_op jit(solution)/shard_map/terms/pallas_call | solution.py:200
  4.8 0.5 %collective-permute-start.6 = (bf16[4,4,80,128]{3,2,1,0:T(8,128)(2,1)S(1)}, bf16[4,4,80,128]{3,2,1,0:T(8,128)(2,1)S(1)}, u32[]{:S(2)}, u32[]{:S(2)}) collective-permute-start(bf16[4,4,80,128]{3,2,1,0:T(8,128)(2,1)S(1)} %get-tuple-element.32), channel_id=1, source_target_pairs={{0,1},{1,0},{2,3},{3,2},{4,5},{5,4},{6,7},{7,6},{8,9},{9,8},{10,11... | collective-permute-start | bytes 983048 | tf_op jit(solution)/shard_map/ppermute | solution.py:167
  5.3 0.1 collective-permute-start
  5.4 0.4 %collective-permute-start.5 = (bf16[4,4,80,128]{3,2,1,0:T(8,128)(2,1)S(1)}, bf16[4,4,80,128]{3,2,1,0:T(8,128)(2,1)S(1)}, u32[]{:S(2)}, u32[]{:S(2)}) collective-permute-start(bf16[4,4,80,128]{3,2,1,0:T(8,128)(2,1)S(1)} %get-tuple-element.30), channel_id=1, source_target_pairs={{0,1},{1,0},{2,3},{3,2},{4,5},{5,4},{6,7},{7,6},{8,9},{9,8},{10,11... | collective-permute-start | bytes 983048 | tf_op jit(solution)/shard_map/ppermute | solution.py:167
  5.8 0.7 %collective-permute-done.6.recv_ref = bf16[4,4,80,128]{3,2,1,0:T(8,128)(2,1)S(1)} collective-permute-done((bf16[4,4,80,128]{3,2,1,0:T(8,128)(2,1)S(1)}, bf16[4,4,80,128]{3,2,1,0:T(8,128)(2,1)S(1)}, u32[]{:S(2)}, u32[]{:S(2)}) %collective-permute-start.6) | collective-permute-done | bytes 327712 | tf_op jit(solution)/shard_map/ppermute | solution.py:167
  6.5 0.1 far_kernel.1
  6.6 2.9 %collective-permute-start.7 = (bf16[4,4,80,128]{3,2,1,0:T(8,128)(2,1)S(1)}, bf16[4,4,80,128]{3,2,1,0:T(8,128)(2,1)S(1)}, u32[]{:S(2)}, u32[]{:S(2)}) collective-permute-start(bf16[4,4,80,128]{3,2,1,0:T(8,128)(2,1)S(1)} %far_kernel.1), channel_id=1, source_target_pairs={{0,2},{1,3},{2,0},{3,1},{4,6},{5,7},{6,4},{7,5},{8,10},{9,11},{10,... | collective-permute-start | bytes 983048 | tf_op jit(solution)/shard_map/ppermute | solution.py:167
  9.5 0.0 collective-permute-done.recv_ref
  9.5 0.1 b_kernel.1
  9.6 1.6 %collective-permute-start.1 = (bf16[2,4,48,128]{3,2,1,0:T(8,128)(2,1)S(1)}, bf16[2,4,48,128]{3,2,1,0:T(8,128)(2,1)S(1)}, u32[]{:S(2)}, u32[]{:S(2)}) collective-permute-start(bf16[2,4,48,128]{3,2,1,0:T(8,128)(2,1)S(1)} %get-tuple-element.24), channel_id=1, source_target_pairs={{0,4},{4,0},{8,12},{12,8},{1,5},{5,1},{9,13},{13,9},{2,6},{6,2},{1... | collective-permute-start | bytes 294920 | tf_op jit(solution)/shard_map/ppermute | solution.py:167
  11.3 2.6 %collective-permute-start.2 = (bf16[2,4,48,128]{3,2,1,0:T(8,128)(2,1)S(1)}, bf16[2,4,48,128]{3,2,1,0:T(8,128)(2,1)S(1)}, u32[]{:S(2)}, u32[]{:S(2)}) collective-permute-start(bf16[2,4,48,128]{3,2,1,0:T(8,128)(2,1)S(1)} %get-tuple-element.25), channel_id=1, source_target_pairs={{0,8},{4,12},{8,0},{12,4},{1,9},{5,13},{9,1},{13,5},{2,10},{6,14},... | collective-permute-start | bytes 294920 | tf_op jit(solution)/shard_map/ppermute | solution.py:167
  13.9 0.2 collective-permute-start.3
  14.1 0.0 collective-permute-done.5.recv_ref
  14.1 3.5 %collective-permute-done.7.cross_ref = bf16[4,4,80,128]{3,2,1,0:T(8,128)(2,1)S(1)} collective-permute-done((bf16[4,4,80,128]{3,2,1,0:T(8,128)(2,1)S(1)}, bf16[4,4,80,128]{3,2,1,0:T(8,128)(2,1)S(1)}, u32[]{:S(2)}, u32[]{:S(2)}) %collective-permute-start.7) | collective-permute-done | bytes 327712 | tf_op jit(solution)/shard_map/ppermute | solution.py:167
  17.5 0.1 a_kernel.1
  17.7 1.9 %collective-permute-start.8 = (bf16[4,80,128]{2,1,0:T(8,128)(2,1)S(1)}, bf16[4,80,128]{2,1,0:T(8,128)(2,1)S(1)}, u32[]{:S(2)}, u32[]{:S(2)}) collective-permute-start(bf16[4,80,128]{2,1,0:T(8,128)(2,1)S(1)} %get-tuple-element.34), channel_id=1, source_target_pairs={{0,4},{4,0},{8,12},{12,8},{1,5},{5,1},{9,13},{13,9},{2,6},{6,2},{1... | collective-permute-start | bytes 245768 | tf_op jit(solution)/shard_map/ppermute | solution.py:167
  19.6 2.6 %collective-permute-start.9 = (bf16[4,80,128]{2,1,0:T(8,128)(2,1)S(1)}, bf16[4,80,128]{2,1,0:T(8,128)(2,1)S(1)}, u32[]{:S(2)}, u32[]{:S(2)}) collective-permute-start(bf16[4,80,128]{2,1,0:T(8,128)(2,1)S(1)} %get-tuple-element.35), channel_id=1, source_target_pairs={{0,8},{4,12},{8,0},{12,4},{1,9},{5,13},{9,1},{13,5},{2,10},{6,14},... | collective-permute-start | bytes 245768 | tf_op jit(solution)/shard_map/ppermute | solution.py:167
  22.2 0.0 collective-permute-done.1.refs_1_
  22.2 0.0 collective-permute-start.10
  22.2 0.0 collective-permute-done.2.refs_2_
  22.2 0.0 collective-permute-done.3.refs_3_
  22.2 0.1 b_sum_kernel.1
  22.2 1.8 %collective-permute-start.4 = (bf16[4,48,128]{2,1,0:T(8,128)(2,1)S(1)}, bf16[4,48,128]{2,1,0:T(8,128)(2,1)S(1)}, u32[]{:S(2)}, u32[]{:S(2)}) collective-permute-start(bf16[4,48,128]{2,1,0:T(8,128)(2,1)S(1)} %get-tuple-element.28), channel_id=1, source_target_pairs={{0,2},{1,3},{2,0},{3,1},{4,6},{5,7},{6,4},{7,5},{8,10},{9,11},{10,... | collective-permute-start | bytes 147464 | tf_op jit(solution)/shard_map/ppermute | solution.py:167
  24.0 2.4 %collective-permute-done.4.cross_ref = bf16[4,48,128]{2,1,0:T(8,128)(2,1)S(1)} collective-permute-done((bf16[4,48,128]{2,1,0:T(8,128)(2,1)S(1)}, bf16[4,48,128]{2,1,0:T(8,128)(2,1)S(1)}, u32[]{:S(2)}, u32[]{:S(2)}) %collective-permute-start.4) | collective-permute-done | bytes 49184 | tf_op jit(solution)/shard_map/ppermute | solution.py:167
  26.4 0.0 collective-permute-done.8.refs_1_
  26.4 2.3 %collective-permute-done.9.refs_2_ = bf16[4,80,128]{2,1,0:T(8,128)(2,1)S(1)} collective-permute-done((bf16[4,80,128]{2,1,0:T(8,128)(2,1)S(1)}, bf16[4,80,128]{2,1,0:T(8,128)(2,1)S(1)}, u32[]{:S(2)}, u32[]{:S(2)}) %collective-permute-start.9) | collective-permute-done | bytes 81952 | tf_op jit(solution)/shard_map/ppermute | solution.py:167
  28.7 0.0 collective-permute-done.10.refs_3_
  28.7 0.7 %final_kernel.1 = bf16[4,128,128]{2,1,0:T(8,128)(2,1)} custom-call(bf16[4,48,128]{2,1,0:T(8,128)(2,1)S(1)} %get-tuple-element.27.near_ref, bf16[4,48,128]{2,1,0:T(8,128)(2,1)S(1)} %collective-permute-done.4.cross_ref, bf16[4,80,128]{2,1,0:T(8,128)(2,1)S(1)} %get-tuple-element.33.refs_0_, bf16[4,80,128]{2,1,0:T(8,128)(2,1)S(1)} %collective-permute-done.8.refs_1_, ...), custom_call_target="tpu_custom_call" | custom-call | tf_op jit(solution)/shard_map/final_kernel/pallas_call | solution.py:186
Async XLA Ops:
  4.8 1.8 %collective-permute-start.6 = (bf16[4,4,80,128]{3,2,1,0:T(8,128)(2,1)S(1)}, bf16[4,4,80,128]{3,2,1,0:T(8,128)(2,1)S(1)}, u32[]{:S(2)}, u32[]{:S(2)}) collective-permute-start(bf16[4,4,80,128]{3,2,1,0:T(8,128)(2,1)S(1)} %get-tuple-element.32), channel_id=1, source_target_pairs={{0,1},{1,0},{2,3},{3,2},{4,5},{5,4},{6,7},{7,6},{8,9},{9,8},{10,11... | collective-permute-start | bytes 983048 | tf_op jit(solution)/shard_map/ppermute | solution.py:167
  5.3 4.3 %collective-permute-start = (bf16[2,4,4,48,128]{4,3,2,1,0:T(8,128)(2,1)S(1)}, bf16[2,4,4,48,128]{4,3,2,1,0:T(8,128)(2,1)S(1)}, u32[]{:S(2)}, u32[]{:S(2)}) collective-permute-start(bf16[2,4,4,48,128]{4,3,2,1,0:T(8,128)(2,1)S(1)} %get-tuple-element.22), channel_id=1, source_target_pairs={{0,1},{1,0},{2,3},{3,2},{4,5},{5,4},{6,7},{7,6},{8,9},{9,8},{10,11... | collective-permute-start | bytes 1179656 | tf_op jit(solution)/shard_map/ppermute | solution.py:167
  5.4 8.7 %collective-permute-start.5 = (bf16[4,4,80,128]{3,2,1,0:T(8,128)(2,1)S(1)}, bf16[4,4,80,128]{3,2,1,0:T(8,128)(2,1)S(1)}, u32[]{:S(2)}, u32[]{:S(2)}) collective-permute-start(bf16[4,4,80,128]{3,2,1,0:T(8,128)(2,1)S(1)} %get-tuple-element.30), channel_id=1, source_target_pairs={{0,1},{1,0},{2,3},{3,2},{4,5},{5,4},{6,7},{7,6},{8,9},{9,8},{10,11... | collective-permute-start | bytes 983048 | tf_op jit(solution)/shard_map/ppermute | solution.py:167
  6.6 10.9 %collective-permute-start.7 = (bf16[4,4,80,128]{3,2,1,0:T(8,128)(2,1)S(1)}, bf16[4,4,80,128]{3,2,1,0:T(8,128)(2,1)S(1)}, u32[]{:S(2)}, u32[]{:S(2)}) collective-permute-start(bf16[4,4,80,128]{3,2,1,0:T(8,128)(2,1)S(1)} %far_kernel.1), channel_id=1, source_target_pairs={{0,2},{1,3},{2,0},{3,1},{4,6},{5,7},{6,4},{7,5},{8,10},{9,11},{10,... | collective-permute-start | bytes 983048 | tf_op jit(solution)/shard_map/ppermute | solution.py:167
  9.6 12.5 %collective-permute-start.1 = (bf16[2,4,48,128]{3,2,1,0:T(8,128)(2,1)S(1)}, bf16[2,4,48,128]{3,2,1,0:T(8,128)(2,1)S(1)}, u32[]{:S(2)}, u32[]{:S(2)}) collective-permute-start(bf16[2,4,48,128]{3,2,1,0:T(8,128)(2,1)S(1)} %get-tuple-element.24), channel_id=1, source_target_pairs={{0,4},{4,0},{8,12},{12,8},{1,5},{5,1},{9,13},{13,9},{2,6},{6,2},{1... | collective-permute-start | bytes 294920 | tf_op jit(solution)/shard_map/ppermute | solution.py:167
  11.3 10.9 %collective-permute-start.2 = (bf16[2,4,48,128]{3,2,1,0:T(8,128)(2,1)S(1)}, bf16[2,4,48,128]{3,2,1,0:T(8,128)(2,1)S(1)}, u32[]{:S(2)}, u32[]{:S(2)}) collective-permute-start(bf16[2,4,48,128]{3,2,1,0:T(8,128)(2,1)S(1)} %get-tuple-element.25), channel_id=1, source_target_pairs={{0,8},{4,12},{8,0},{12,4},{1,9},{5,13},{9,1},{13,5},{2,10},{6,14},... | collective-permute-start | bytes 294920 | tf_op jit(solution)/shard_map/ppermute | solution.py:167
  13.9 8.3 %collective-permute-start.3 = (bf16[2,4,48,128]{3,2,1,0:T(8,128)(2,1)S(1)}, bf16[2,4,48,128]{3,2,1,0:T(8,128)(2,1)S(1)}, u32[]{:S(2)}, u32[]{:S(2)}) collective-permute-start(bf16[2,4,48,128]{3,2,1,0:T(8,128)(2,1)S(1)} %get-tuple-element.26), channel_id=1, source_target_pairs={{0,12},{4,8},{8,4},{12,0},{1,13},{5,9},{9,5},{13,1},{2,14},{6,10},... | collective-permute-start | bytes 294920 | tf_op jit(solution)/shard_map/ppermute | solution.py:167
  17.7 8.7 %collective-permute-start.8 = (bf16[4,80,128]{2,1,0:T(8,128)(2,1)S(1)}, bf16[4,80,128]{2,1,0:T(8,128)(2,1)S(1)}, u32[]{:S(2)}, u32[]{:S(2)}) collective-permute-start(bf16[4,80,128]{2,1,0:T(8,128)(2,1)S(1)} %get-tuple-element.34), channel_id=1, source_target_pairs={{0,4},{4,0},{8,12},{12,8},{1,5},{5,1},{9,13},{13,9},{2,6},{6,2},{1... | collective-permute-start | bytes 245768 | tf_op jit(solution)/shard_map/ppermute | solution.py:167
  19.6 9.1 %collective-permute-start.9 = (bf16[4,80,128]{2,1,0:T(8,128)(2,1)S(1)}, bf16[4,80,128]{2,1,0:T(8,128)(2,1)S(1)}, u32[]{:S(2)}, u32[]{:S(2)}) collective-permute-start(bf16[4,80,128]{2,1,0:T(8,128)(2,1)S(1)} %get-tuple-element.35), channel_id=1, source_target_pairs={{0,8},{4,12},{8,0},{12,4},{1,9},{5,13},{9,1},{13,5},{2,10},{6,14},... | collective-permute-start | bytes 245768 | tf_op jit(solution)/shard_map/ppermute | solution.py:167
  22.2 6.5 %collective-permute-start.10 = (bf16[4,80,128]{2,1,0:T(8,128)(2,1)S(1)}, bf16[4,80,128]{2,1,0:T(8,128)(2,1)S(1)}, u32[]{:S(2)}, u32[]{:S(2)}) collective-permute-start(bf16[4,80,128]{2,1,0:T(8,128)(2,1)S(1)} %get-tuple-element.36), channel_id=1, source_target_pairs={{0,12},{4,8},{8,4},{12,0},{1,13},{5,9},{9,5},{13,1},{2,14},{6,10},... | collective-permute-start | bytes 245768 | tf_op jit(solution)/shard_map/ppermute | solution.py:167
  22.2 4.2 %collective-permute-start.4 = (bf16[4,48,128]{2,1,0:T(8,128)(2,1)S(1)}, bf16[4,48,128]{2,1,0:T(8,128)(2,1)S(1)}, u32[]{:S(2)}, u32[]{:S(2)}) collective-permute-start(bf16[4,48,128]{2,1,0:T(8,128)(2,1)S(1)} %get-tuple-element.28), channel_id=1, source_target_pairs={{0,2},{1,3},{2,0},{3,1},{4,6},{5,7},{6,4},{7,5},{8,10},{9,11},{10,... | collective-permute-start | bytes 147464 | tf_op jit(solution)/shard_map/ppermute | solution.py:167

commit v6 on v5

--- a/solution.py
+++ b/solution.py
@@ -20,12 +20,13 @@
     wave_hbm,
     left_hbm,
     right_hbm,
-    a_far_send,
-    a_near_send,
-    a_far_keep,
-    a_near_keep,
+    first_send,
+    first_keep,
     b_send,
     b_keep,
+    rest_send,
+    rest_keep,
+    mask_ref,
     cls,
     tid,
     pair,
@@ -34,7 +35,6 @@
     wave,
     left,
     right,
-    total,
     scalar_sems,
     wave_sem,
     left_sems,
@@ -42,8 +42,8 @@
 ):
     width = wave.shape[0]
     terms = left.shape[0]
-    targets = total.shape[0]
-    strip = width // 4
+    targets, strip, _ = mask_ref.shape
+    a_rows = first_send.shape[2]
     unit = width // 8
     sec = lax.axis_index("sec")
     mpo = lax.axis_index("mpo")
@@ -54,10 +54,10 @@
             ((cls_hbm, cls), (tid_hbm, tid), (pair_hbm, pair), (dims_hbm, dims), (coef_hbm, coef))
         )
     ]
+    wave_copy = pltpu.make_async_copy(wave_hbm.at[0], wave, wave_sem)
+    wave_copy.start()
     for copy in scalars:
         copy.start()
-    wave_copy = pltpu.make_async_copy(wave_hbm.at[0], wave, wave_sem)
-    wave_copy.start()
 
     def fetch(j, carry):
         for q in range(4):
@@ -77,9 +77,28 @@
         return carry
 
     lax.fori_loop(0, terms, fetch, 0)
-    total[...] = jnp.zeros_like(total)
+    for ref in (first_send, first_keep, b_send, b_keep, rest_send, rest_keep):
+
+        def clear(q, carry, ref=ref):
+            if len(ref.shape) == 4:
+                ref[q] = jnp.zeros(ref.shape[1:], ref.dtype)
+            else:
+                for n in range(ref.shape[0]):
+                    ref[n, q] = jnp.zeros(ref.shape[2:], ref.dtype)
+            return carry
+
+        lax.fori_loop(0, 4, clear, 0)
     for copy in scalars:
         copy.wait()
+    lane = mpo * strip + lax.broadcasted_iota(jnp.int32, (strip, strip), 1)
+    line = sec * strip + lax.broadcasted_iota(jnp.int32, (strip, strip), 0)
+
+    def target_mask(t, carry):
+        inside = (line < dims[0, t] * unit) & (lane < dims[1, t] * unit)
+        mask_ref[t] = jnp.where(inside, 1.0, 0.0).astype(jnp.bfloat16)
+        return carry
+
+    lax.fori_loop(0, targets, target_mask, 0)
     wave_copy.wait()
     row_limit = dims[0, sec] * unit
     col_limit = dims[1, sec] * unit
@@ -100,45 +119,59 @@
         half = jnp.dot(left[j], wave[...], preferred_element_type=jnp.float32)
         half = half.astype(jnp.bfloat16)
         pltpu.make_async_copy(right_hbm.at[0, j], right.at[j], right_sems.at[j]).wait()
-        contrib = lax.dot_general(
-            half, right[j], (((1,), (1,)), ((), ())), preferred_element_type=jnp.float32
-        )
-        target = pair[sec, cls[0, j]]
-        total[target] += coef[tid[0, j]] * contrib
+        t = pair[sec, cls[0, j]]
+        weight = coef[tid[0, j]]
+        for side in range(2):
+            contrib = lax.dot_general(
+                half,
+                right[j, 2 * side * strip : 2 * (side + 1) * strip, :],
+                (((1,), (1,)), ((), ())),
+                preferred_element_type=jnp.float32,
+            )
+            first, b_part, rest = (
+                (first_send, b_send, rest_send) if side == 0 else (first_keep, b_keep, rest_keep)
+            )
+            for q in range(4):
+                for n in range(2):
+                    value = weight * contrib[
+                        q * strip : (q + 1) * strip, n * strip : (n + 1) * strip
+                    ]
+                    if n == 0:
+                        put(first, (q, t), value[:a_rows])
+                        put(rest, (0, q, t), value[a_rows : 2 * a_rows])
+                    else:
+                        put(rest, (1, q, t), value[:a_rows])
+                        put(rest, (2, q, t), value[a_rows : 2 * a_rows])
+                    put(b_part, (n, q, t), value[2 * a_rows :])
         return carry
 
     lax.fori_loop(0, terms, term, 0)
 
-    a_rows = a_far_send.shape[2]
-    lane = lax.broadcasted_iota(jnp.int32, (strip, strip), 1)
-    line = lax.broadcasted_iota(jnp.int32, (strip, strip), 0)
-
-    def store(t, carry):
-        for p, r in enumerate(COLUMN_ORDER):
-            a_ref = (a_far_send, a_near_send, a_far_keep, a_near_keep)[p]
-            b_ref = b_send if p < 2 else b_keep
-            cols_in = (mpo ^ r) * strip + lane < dims[1, t] * unit
-            for q in range(4):
-                inside = cols_in & ((sec ^ q) * strip + line < dims[0, t] * unit)
-                value = total[t, q * strip : (q + 1) * strip, p * strip : (p + 1) * strip]
-                value = jnp.where(inside, value, 0.0).astype(jnp.bfloat16)
-                a_ref[q, t] = value[:a_rows]
-                b_ref[p % 2, q, t] = value[a_rows:]
-        return carry
-
-    lax.fori_loop(0, targets, store, 0)
-
-
-def far_kernel(keep_ref, recv_ref, far_ref):
+
+def put(ref, at, value):
+    ref[at] = (ref[at].astype(jnp.float32) + value).astype(jnp.bfloat16)
+
+
+def far_first(keep_ref, recv_ref, far_ref):
     far_ref[...] = add(keep_ref[...], recv_ref[...])
 
 
-def a_kernel(keep_ref, recv_ref, cross_ref, *own_refs):
+def far_second(keep_ref, recv_ref, after_ref, far_ref):
+    far_ref[...] = add(keep_ref[0], recv_ref[0])
+
+
+def own_first(keep_ref, recv_ref, cross_ref, *own_refs):
     for q, own_ref in enumerate(own_refs):
-        own_ref[...] = add(keep_ref[q], recv_ref[q], cross_ref[q])
-
-
-def b_kernel(keep_ref, recv_ref, *own_refs):
+        own_ref[...] = add(keep_ref[1, q], recv_ref[1, q], cross_ref[q])
+
+
+def own_second(keep_ref, recv_ref, cross_ref, *own_refs):
+    for q, own_ref in enumerate(own_refs):
+        own_ref[...] = add(keep_ref[2, q], recv_ref[2, q], cross_ref[q])
+
+
+def b_kernel(keep_ref, recv_ref, rest_in, after_ref, rest_out, *own_refs):
+    del rest_in, rest_out
     for q, own_ref in enumerate(own_refs):
         own_ref[...] = add(keep_ref[:, q], recv_ref[:, q])
 
@@ -149,11 +182,24 @@
     near_ref[...] = add(*[piece[1] for piece in pieces])
 
 
-def final_kernel(near_ref, cross_ref, *refs):
+def sum_first(*refs):
+    pieces, sum_ref = refs[:-1], refs[-1]
+    total = pieces[0][...].astype(jnp.float32)
+    for piece in pieces[1:]:
+        total = total + piece[...].astype(jnp.float32)
+    sum_ref[...] = total
+
+
+def final_kernel(mask_ref, near_ref, cross_ref, sum_ref, *refs):
     pieces, out_ref = refs[:-1], refs[-1]
-    a_rows = pieces[0].shape[1]
-    out_ref[:, :a_rows, :] = add(*[piece[...] for piece in pieces])
-    out_ref[:, a_rows:, :] = add(near_ref[...], cross_ref[...])
+    rows = sum_ref.shape[1]
+    for first, group in ((0, (sum_ref,)), (rows, pieces), (2 * rows, (near_ref, cross_ref))):
+        last = first + group[0].shape[1]
+        total = group[0][...].astype(jnp.float32)
+        for piece in group[1:]:
+            total = total + piece[...].astype(jnp.float32)
+        inside = mask_ref[:, first:last, :].astype(jnp.float32) > 0.0
+        out_ref[:, first:last, :] = jnp.where(inside, total, 0.0).astype(jnp.bfloat16)
 
 
 def add(*arrays):
@@ -174,20 +220,24 @@
     terms = left_env.shape[1]
     targets = block_dims.shape[0]
     strip = width // 4
-    a_rows = strip * 5 // 8
-    b_rows = strip - a_rows
+    a_rows = strip * 3 // 8
+    b_rows = strip - 2 * a_rows
     vmem = pl.BlockSpec(memory_space=pltpu.VMEM)
     hbm = pl.BlockSpec(memory_space=pltpu.HBM)
 
     def like(*shape):
         return jax.ShapeDtypeStruct(shape + (strip,), jnp.bfloat16)
 
-    def call(kernel, out_shape, *args):
+    def call(kernel, out_shape, *args, aliases={}, span=0.1):
         return pl.pallas_call(
             kernel,
             out_shape=out_shape,
             in_specs=[vmem] * len(args),
             out_specs=jax.tree.map(lambda _: vmem, out_shape),
+            input_output_aliases=aliases,
+            cost_estimate=pl.CostEstimate(
+                flops=round(span * 1e9), bytes_accessed=0, transcendentals=0
+            ),
             compiler_params=SMALL,
             name=kernel.__name__,
         )(*args)
@@ -197,17 +247,19 @@
         pltpu.with_memory_space_constraint(x, pltpu.HBM)
         for x in (*scalars, wave_blocks, left_env, right_env)
     ]
-    a_far_send, a_near_send, a_far_keep, a_near_keep, b_send, b_keep = pl.pallas_call(
+    across = like(4, targets, a_rows)
+    b_shape = like(2, 4, targets, b_rows)
+    rest_shape = like(3, 4, targets, a_rows)
+    first_send, first_keep, b_send, b_keep, rest_send, rest_keep, mask = pl.pallas_call(
         term_kernel,
-        out_shape=[like(4, targets, a_rows)] * 4 + [like(2, 4, targets, b_rows)] * 2,
+        out_shape=[across] * 2 + [b_shape] * 2 + [rest_shape] * 2 + [like(targets, strip)],
         in_specs=[hbm] * 8,
-        out_specs=[vmem] * 6,
+        out_specs=[vmem] * 7,
         scratch_shapes=[pltpu.SMEM(scalar.shape, scalar.dtype) for scalar in scalars]
         + [
             pltpu.VMEM((width, width), jnp.bfloat16),
             pltpu.VMEM((terms, width, width), jnp.bfloat16),
             pltpu.VMEM((terms, width, width), jnp.bfloat16),
-            pltpu.VMEM((targets, width, width), jnp.float32),
             pltpu.SemaphoreType.DMA((len(scalars),)),
             pltpu.SemaphoreType.DMA,
             pltpu.SemaphoreType.DMA((terms,)),
@@ -219,18 +271,34 @@
         ),
         name="terms",
     )(*operands)
-    a_far_recv = swap(a_far_send, "mpo", 1)
+    first_recv = swap(first_send, "mpo", 1)
     b_recv = swap(b_send, "mpo", 1)
-    a_near_recv = swap(a_near_send, "mpo", 1)
-    a_far = call(far_kernel, like(4, targets, a_rows), a_far_keep, a_far_recv)
-    a_cross = swap(a_far, "mpo", 2)
-    b_own = call(b_kernel, [like(2, targets, b_rows)] * 4, b_keep, b_recv)
-    b_pieces = [b_own[0]] + [swap(b_own[q], "sec", q) for q in (1, 2, 3)]
-    a_own = call(a_kernel, [like(targets, a_rows)] * 4, a_near_keep, a_near_recv, a_cross)
-    a_pieces = [a_own[0]] + [swap(a_own[q], "sec", q) for q in (1, 2, 3)]
-    b_far, b_near = call(b_sum_kernel, [like(targets, b_rows)] * 2, *b_pieces)
+    first_far = call(far_first, across, first_keep, first_recv, span=3)
+    first_cross = swap(first_far, "mpo", 2)
+    rest_send, *b_own = call(
+        b_kernel,
+        [rest_shape] + [like(2, targets, b_rows)] * 4,
+        b_keep,
+        b_recv,
+        rest_send,
+        first_far,
+        aliases={2: 0},
+    )
+    b_pieces = [b_own[0]] + [swap(b_own[q], "sec", q) for q in (2, 3, 1)]
+    rest_recv = swap(rest_send, "mpo", 1)
+    second_far = call(far_second, across, rest_keep, rest_recv, first_cross, span=3)
+    second_cross = swap(second_far, "mpo", 2)
+    pieces = []
+    for kernel, cross in ((own_first, first_cross), (own_second, second_cross)):
+        own = call(kernel, [like(targets, a_rows)] * 4, rest_keep, rest_recv, cross)
+        pieces += [own[0]] + [swap(own[q], "sec", q) for q in (2, 3, 1)]
+    b_far, b_near = call(b_sum_kernel, [like(targets, b_rows)] * 2, *b_pieces, span=3)
     b_cross = swap(b_far, "mpo", 2)
-    return call(final_kernel, like(targets, strip), b_near, b_cross, *a_pieces)
+    first_sum = jax.ShapeDtypeStruct((targets, a_rows, strip), jnp.float32)
+    first_sum = call(sum_first, first_sum, *pieces[:4], span=3)
+    return call(
+        final_kernel, like(targets, strip), mask, b_near, b_cross, first_sum, *pieces[4:]
+    )
 
 
 def by_classes(

time: 29.5 us -> 31 us (1.051)
  starting transfers between devices: 14.6 us -> 19 us
  waiting for transfers between devices: 8.88 us -> 6.63 us
  Pallas kernels: 5.8 us -> 5.23 us
    ppermute x11 -> x15, starting transfers between devices: 14.6 us -> 19 us  [swap(): lax.ppermute(array, axis, [(i, i ^ mask) for i in range(lax.axis_size(axi...]
    ppermute x11 -> x15, waiting for transfers between devices: 8.88 us -> 6.63 us  [swap(): lax.ppermute(array, axis, [(i, i ^ mask) for i in range(lax.axis_size(axi...]
    pallas_call x1, Pallas kernels: 4.74 us -> 4.14 us  [by_targets(): pl.pallas_call(term_kernel, out_shape=[across] * 2 + [b_shape] * 2 + [res...]
    pallas_call x5 -> x8, Pallas kernels: 1.05 us -> 1.08 us  [call(): pl.pallas_call(kernel, out_shape=out_shape, in_specs=[vmem] * len(args),...]
  transfers between devices with their start and end apart: 11 -> 15, of which waited for: 4 -> 7; matrix products, arithmetic and copies ran while one was open for 0% -> 0% of each run, Pallas kernels for 1% -> 1%
where the time goes in v6:
time: 31 us; the launch traced here: 30.9 us
  starting transfers between devices  19 us (61%)
  waiting for transfers between devices  6.63 us (21%)
  Pallas kernels  5.23 us (17%)
    ppermute x15, starting transfers between devices, swap(): lax.ppermute(array, axis, [(i, i ^ mask) for i in range(lax.axis_size(axi...  19 us
    ppermute x15, waiting for transfers between devices, swap(): lax.ppermute(array, axis, [(i, i ^ mask) for i in range(lax.axis_size(axi...  6.63 us
    pallas_call x1, Pallas kernels, by_targets(): pl.pallas_call(term_kernel, out_shape=[across] * 2 + [b_shape] * 2 + [res...  4.14 us
    pallas_call x8, Pallas kernels, call(): pl.pallas_call(kernel, out_shape=out_shape, in_specs=[vmem] * len(args),...  1.08 us
  transfers between devices with their start and end apart: 15, of which 7 were waited for; matrix products, arithmetic and copies ran while one was open for 0% of the time, Pallas kernels for 1%

profile of v6, /device:TPU:0, one launch (start us, length us, event | category | flops | bytes accessed | tf_op | source)
XLA Modules:
  0.0 30.9 jit_solution(13788534411458930322)
XLA Ops:
  0.0 4.1 %terms.1 = (bf16[4,4,48,128]{3,2,1,0:T(8,128)(2,1)S(1)}, bf16[4,4,48,128]{3,2,1,0:T(8,128)(2,1)S(1)}, bf16[2,4,4,32,128]{4,3,2,1,0:T(8,128)(2,1)S(1)}, bf16[2,4,...) custom-call(s32[1,3]{1,0:T(1,128)} %cls_hbm.1, ...), custom_call_target="tpu_custom_call" | custom-call | flops 1610612736 | bytes 4194304 | tf_op jit(solution)/shard_map/terms/pallas_call | solution.py:253
  4.1 0.5 %collective-permute-start.1 = (bf16[4,4,48,128]{3,2,1,0:T(8,128)(2,1)S(1)}, bf16[4,4,48,128]{3,2,1,0:T(8,128)(2,1)S(1)}, u32[]{:S(2)}, u32[]{:S(2)}) collective-permute-start(bf16[4,4,48,128]{3,2,1,0:T(8,128)(2,1)S(1)} %get-tuple-element.32), channel_id=1, source_target_pairs={{0,1},{1,0},{2,3},{3,2},{4,5},{5,4},{6,7},{7,6},{8,9},{9,8},{10,11... | collective-permute-start | bytes 589832 | tf_op jit(solution)/shard_map/ppermute | solution.py:213
  4.7 0.1 collective-permute-start
  4.7 1.0 %collective-permute-done.1.recv_ref = bf16[4,4,48,128]{3,2,1,0:T(8,128)(2,1)S(1)} collective-permute-done((bf16[4,4,48,128]{3,2,1,0:T(8,128)(2,1)S(1)}, bf16[4,4,48,128]{3,2,1,0:T(8,128)(2,1)S(1)}, u32[]{:S(2)}, u32[]{:S(2)}) %collective-permute-start.1) | collective-permute-done | bytes 196640 | tf_op jit(solution)/shard_map/ppermute | solution.py:213
  5.8 0.4 %collective-permute-done.recv_ref = bf16[2,4,4,32,128]{4,3,2,1,0:T(8,128)(2,1)S(1)} collective-permute-done((bf16[2,4,4,32,128]{4,3,2,1,0:T(8,128)(2,1)S(1)}, bf16[2,4,4,32,128]{4,3,2,1,0:T(8,128)(2,1)S(1)}, u32[]{:S(2)}, u32[]{:S(2)}) %collective-permute-start) | collective-permute-done | bytes 262176 | tf_op jit(solution)/shard_map/ppermute | solution.py:213
  6.2 0.1 b_kernel.1
  6.3 0.3 %collective-permute-start.6 = (bf16[3,4,4,48,128]{4,3,2,1,0:T(8,128)(2,1)S(1)}, bf16[3,4,4,48,128]{4,3,2,1,0:T(8,128)(2,1)S(1)}, u32[]{:S(2)}, u32[]{:S(2)}) collective-permute-start(bf16[3,4,4,48,128]{4,3,2,1,0:T(8,128)(2,1)S(1)} %get-tuple-element.40), channel_id=1, source_target_pairs={{0,1},{1,0},{2,3},{3,2},{4,5},{5,4},{6,7},{7,6},{8,9},{9,8},{10,11... | collective-permute-start | bytes 1769480 | tf_op jit(solution)/shard_map/ppermute | solution.py:213
  6.6 2.7 %collective-permute-start.7 = (bf16[4,4,48,128]{3,2,1,0:T(8,128)(2,1)S(1)}, bf16[4,4,48,128]{3,2,1,0:T(8,128)(2,1)S(1)}, u32[]{:S(2)}, u32[]{:S(2)}) collective-permute-start(bf16[4,4,48,128]{3,2,1,0:T(8,128)(2,1)S(1)} %far_first.1.after_ref), channel_id=1, source_target_pairs={{0,2},{1,3},{2,0},{3,1},{4,6},{5,7},{6,4},{7,5},{8,10},{9,11},{10,... | collective-permute-start | bytes 589832 | tf_op jit(solution)/shard_map/ppermute | solution.py:213
  9.3 2.6 %collective-permute-start.2 = (bf16[2,4,32,128]{3,2,1,0:T(8,128)(2,1)S(1)}, bf16[2,4,32,128]{3,2,1,0:T(8,128)(2,1)S(1)}, u32[]{:S(2)}, u32[]{:S(2)}) collective-permute-start(bf16[2,4,32,128]{3,2,1,0:T(8,128)(2,1)S(1)} %get-tuple-element.34), channel_id=1, source_target_pairs={{0,8},{4,12},{8,0},{12,4},{1,9},{5,13},{9,1},{13,5},{2,10},{6,14},... | collective-permute-start | bytes 196616 | tf_op jit(solution)/shard_map/ppermute | solution.py:213
  11.9 1.3 %collective-permute-start.3 = (bf16[2,4,32,128]{3,2,1,0:T(8,128)(2,1)S(1)}, bf16[2,4,32,128]{3,2,1,0:T(8,128)(2,1)S(1)}, u32[]{:S(2)}, u32[]{:S(2)}) collective-permute-start(bf16[2,4,32,128]{3,2,1,0:T(8,128)(2,1)S(1)} %get-tuple-element.35), channel_id=1, source_target_pairs={{0,12},{4,8},{8,4},{12,0},{1,13},{5,9},{9,5},{13,1},{2,14},{6,10},... | collective-permute-start | bytes 196616 | tf_op jit(solution)/shard_map/ppermute | solution.py:213
  13.3 0.2 collective-permute-start.4
  13.5 1.2 %collective-permute-done.7.cross_ref.after_ref = bf16[4,4,48,128]{3,2,1,0:T(8,128)(2,1)S(1)} collective-permute-done((bf16[4,4,48,128]{3,2,1,0:T(8,128)(2,1)S(1)}, bf16[4,4,48,128]{3,2,1,0:T(8,128)(2,1)S(1)}, u32[]{:S(2)}, u32[]{:S(2)}) %collective-permute-start.7) | collective-permute-done | bytes 196640 | tf_op jit(solution)/shard_map/ppermute | solution.py:213
  14.7 0.0 collective-permute-done.6.recv_ref
  14.7 1.8 %collective-permute-start.11 = (bf16[4,4,48,128]{3,2,1,0:T(8,128)(2,1)S(1)}, bf16[4,4,48,128]{3,2,1,0:T(8,128)(2,1)S(1)}, u32[]{:S(2)}, u32[]{:S(2)}) collective-permute-start(bf16[4,4,48,128]{3,2,1,0:T(8,128)(2,1)S(1)} %far_second.1), channel_id=1, source_target_pairs={{0,2},{1,3},{2,0},{3,1},{4,6},{5,7},{6,4},{7,5},{8,10},{9,11},{10,... | collective-permute-start | bytes 589832 | tf_op jit(solution)/shard_map/ppermute | solution.py:213
  16.5 0.1 own_first.1
  16.6 1.6 %collective-permute-start.10 = (bf16[4,48,128]{2,1,0:T(8,128)(2,1)S(1)}, bf16[4,48,128]{2,1,0:T(8,128)(2,1)S(1)}, u32[]{:S(2)}, u32[]{:S(2)}) collective-permute-start(bf16[4,48,128]{2,1,0:T(8,128)(2,1)S(1)} %get-tuple-element.44), channel_id=1, source_target_pairs={{0,4},{4,0},{8,12},{12,8},{1,5},{5,1},{9,13},{13,9},{2,6},{6,2},{1... | collective-permute-start | bytes 147464 | tf_op jit(solution)/shard_map/ppermute | solution.py:213
  18.3 0.0 collective-permute-done.2.refs_1_
  18.3 2.6 %collective-permute-start.8 = (bf16[4,48,128]{2,1,0:T(8,128)(2,1)S(1)}, bf16[4,48,128]{2,1,0:T(8,128)(2,1)S(1)}, u32[]{:S(2)}, u32[]{:S(2)}) collective-permute-start(bf16[4,48,128]{2,1,0:T(8,128)(2,1)S(1)} %get-tuple-element.42), channel_id=1, source_target_pairs={{0,8},{4,12},{8,0},{12,4},{1,9},{5,13},{9,1},{13,5},{2,10},{6,14},... | collective-permute-start | bytes 147464 | tf_op jit(solution)/shard_map/ppermute | solution.py:213
  20.9 0.0 collective-permute-done.3.refs_2_
  20.9 0.2 collective-permute-start.9
  21.1 0.0 collective-permute-done.4.refs_3_
  21.1 0.4 %collective-permute-start.5 = (bf16[4,32,128]{2,1,0:T(8,128)(2,1)S(1)}, bf16[4,32,128]{2,1,0:T(8,128)(2,1)S(1)}, u32[]{:S(2)}, u32[]{:S(2)}) collective-permute-start(bf16[4,32,128]{2,1,0:T(8,128)(2,1)S(1)} %get-tuple-element.38), channel_id=1, source_target_pairs={{0,2},{1,3},{2,0},{3,1},{4,6},{5,7},{6,4},{7,5},{8,10},{9,11},{10,... | collective-permute-start | bytes 98312 | tf_op jit(solution)/shard_map/ppermute | solution.py:213
  21.5 0.0 collective-permute-done.11.cross_ref
  21.5 0.1 own_second.1
  21.6 2.5 %collective-permute-start.12 = (bf16[4,48,128]{2,1,0:T(8,128)(2,1)S(1)}, bf16[4,48,128]{2,1,0:T(8,128)(2,1)S(1)}, u32[]{:S(2)}, u32[]{:S(2)}) collective-permute-start(bf16[4,48,128]{2,1,0:T(8,128)(2,1)S(1)} %get-tuple-element.46), channel_id=1, source_target_pairs={{0,8},{4,12},{8,0},{12,4},{1,9},{5,13},{9,1},{13,5},{2,10},{6,14},... | collective-permute-start | bytes 147464 | tf_op jit(solution)/shard_map/ppermute | solution.py:213
  24.1 0.0 collective-permute-done.10.refs_3_
  24.1 1.5 %collective-permute-start.13 = (bf16[4,48,128]{2,1,0:T(8,128)(2,1)S(1)}, bf16[4,48,128]{2,1,0:T(8,128)(2,1)S(1)}, u32[]{:S(2)}, u32[]{:S(2)}) collective-permute-start(bf16[4,48,128]{2,1,0:T(8,128)(2,1)S(1)} %get-tuple-element.47), channel_id=1, source_target_pairs={{0,12},{4,8},{8,4},{12,0},{1,13},{5,9},{9,5},{13,1},{2,14},{6,10},... | collective-permute-start | bytes 147464 | tf_op jit(solution)/shard_map/ppermute | solution.py:213
  25.6 0.0 collective-permute-done.8.refs_1_
  25.6 0.5 %collective-permute-start.14 = (bf16[4,48,128]{2,1,0:T(8,128)(2,1)S(1)}, bf16[4,48,128]{2,1,0:T(8,128)(2,1)S(1)}, u32[]{:S(2)}, u32[]{:S(2)}) collective-permute-start(bf16[4,48,128]{2,1,0:T(8,128)(2,1)S(1)} %get-tuple-element.48), channel_id=1, source_target_pairs={{0,4},{4,0},{8,12},{12,8},{1,5},{5,1},{9,13},{13,9},{2,6},{6,2},{1... | collective-permute-start | bytes 147464 | tf_op jit(solution)/shard_map/ppermute | solution.py:213
  26.1 0.9 %collective-permute-done.9.refs_2_ = bf16[4,48,128]{2,1,0:T(8,128)(2,1)S(1)} collective-permute-done((bf16[4,48,128]{2,1,0:T(8,128)(2,1)S(1)}, bf16[4,48,128]{2,1,0:T(8,128)(2,1)S(1)}, u32[]{:S(2)}, u32[]{:S(2)}) %collective-permute-start.9) | collective-permute-done | bytes 49184 | tf_op jit(solution)/shard_map/ppermute | solution.py:213
  27.0 0.0 collective-permute-done.5.cross_ref
  27.0 2.0 %collective-permute-done.12.refs_1_ = bf16[4,48,128]{2,1,0:T(8,128)(2,1)S(1)} collective-permute-done((bf16[4,48,128]{2,1,0:T(8,128)(2,1)S(1)}, bf16[4,48,128]{2,1,0:T(8,128)(2,1)S(1)}, u32[]{:S(2)}, u32[]{:S(2)}) %collective-permute-start.12) | collective-permute-done | bytes 49184 | tf_op jit(solution)/shard_map/ppermute | solution.py:213
  29.0 1.1 %collective-permute-done.13.refs_2_ = bf16[4,48,128]{2,1,0:T(8,128)(2,1)S(1)} collective-permute-done((bf16[4,48,128]{2,1,0:T(8,128)(2,1)S(1)}, bf16[4,48,128]{2,1,0:T(8,128)(2,1)S(1)}, u32[]{:S(2)}, u32[]{:S(2)}) %collective-permute-start.13) | collective-permute-done | bytes 49184 | tf_op jit(solution)/shard_map/ppermute | solution.py:213
  30.1 0.1 collective-permute-done.14.refs_3_
  30.2 0.7 %final_kernel.1 = bf16[4,128,128]{2,1,0:T(8,128)(2,1)} custom-call(bf16[4,128,128]{2,1,0:T(8,128)(2,1)S(1)} %get-tuple-element.27.mask_ref, bf16[4,32,128]{2,1,0:T(8,128)(2,1)S(1)} %get-tuple-element.37.near_ref, bf16[4,32,128]{2,1,0:T(8,128)(2,1)S(1)} %collective-permute-done.5.cross_ref, f32[4,48,128]{2,1,0:T(8,128)S(1)} %sum_first.1.sum_ref, ...), custom_call_target="tpu_custom_call" | custom-call | flops 100000000 | tf_op jit(solution)/shard_map/final_kernel/pallas_call | solution.py:232
  (4 shorter events, 0.2 us)
Async XLA Ops:
  4.1 1.6 %collective-permute-start.1 = (bf16[4,4,48,128]{3,2,1,0:T(8,128)(2,1)S(1)}, bf16[4,4,48,128]{3,2,1,0:T(8,128)(2,1)S(1)}, u32[]{:S(2)}, u32[]{:S(2)}) collective-permute-start(bf16[4,4,48,128]{3,2,1,0:T(8,128)(2,1)S(1)} %get-tuple-element.32), channel_id=1, source_target_pairs={{0,1},{1,0},{2,3},{3,2},{4,5},{5,4},{6,7},{7,6},{8,9},{9,8},{10,11... | collective-permute-start | bytes 589832 | tf_op jit(solution)/shard_map/ppermute | solution.py:213
  4.7 1.5 %collective-permute-start = (bf16[2,4,4,32,128]{4,3,2,1,0:T(8,128)(2,1)S(1)}, bf16[2,4,4,32,128]{4,3,2,1,0:T(8,128)(2,1)S(1)}, u32[]{:S(2)}, u32[]{:S(2)}) collective-permute-start(bf16[2,4,4,32,128]{4,3,2,1,0:T(8,128)(2,1)S(1)} %get-tuple-element.29), channel_id=1, source_target_pairs={{0,1},{1,0},{2,3},{3,2},{4,5},{5,4},{6,7},{7,6},{8,9},{9,8},{10,11... | collective-permute-start | bytes 786440 | tf_op jit(solution)/shard_map/ppermute | solution.py:213
  6.3 8.4 %collective-permute-start.6 = (bf16[3,4,4,48,128]{4,3,2,1,0:T(8,128)(2,1)S(1)}, bf16[3,4,4,48,128]{4,3,2,1,0:T(8,128)(2,1)S(1)}, u32[]{:S(2)}, u32[]{:S(2)}) collective-permute-start(bf16[3,4,4,48,128]{4,3,2,1,0:T(8,128)(2,1)S(1)} %get-tuple-element.40), channel_id=1, source_target_pairs={{0,1},{1,0},{2,3},{3,2},{4,5},{5,4},{6,7},{7,6},{8,9},{9,8},{10,11... | collective-permute-start | bytes 1769480 | tf_op jit(solution)/shard_map/ppermute | solution.py:213
  6.6 8.1 %collective-permute-start.7 = (bf16[4,4,48,128]{3,2,1,0:T(8,128)(2,1)S(1)}, bf16[4,4,48,128]{3,2,1,0:T(8,128)(2,1)S(1)}, u32[]{:S(2)}, u32[]{:S(2)}) collective-permute-start(bf16[4,4,48,128]{3,2,1,0:T(8,128)(2,1)S(1)} %far_first.1.after_ref), channel_id=1, source_target_pairs={{0,2},{1,3},{2,0},{3,1},{4,6},{5,7},{6,4},{7,5},{8,10},{9,11},{10,... | collective-permute-start | bytes 589832 | tf_op jit(solution)/shard_map/ppermute | solution.py:213
  9.3 8.9 %collective-permute-start.2 = (bf16[2,4,32,128]{3,2,1,0:T(8,128)(2,1)S(1)}, bf16[2,4,32,128]{3,2,1,0:T(8,128)(2,1)S(1)}, u32[]{:S(2)}, u32[]{:S(2)}) collective-permute-start(bf16[2,4,32,128]{3,2,1,0:T(8,128)(2,1)S(1)} %get-tuple-element.34), channel_id=1, source_target_pairs={{0,8},{4,12},{8,0},{12,4},{1,9},{5,13},{9,1},{13,5},{2,10},{6,14},... | collective-permute-start | bytes 196616 | tf_op jit(solution)/shard_map/ppermute | solution.py:213
  11.9 8.9 %collective-permute-start.3 = (bf16[2,4,32,128]{3,2,1,0:T(8,128)(2,1)S(1)}, bf16[2,4,32,128]{3,2,1,0:T(8,128)(2,1)S(1)}, u32[]{:S(2)}, u32[]{:S(2)}) collective-permute-start(bf16[2,4,32,128]{3,2,1,0:T(8,128)(2,1)S(1)} %get-tuple-element.35), channel_id=1, source_target_pairs={{0,12},{4,8},{8,4},{12,0},{1,13},{5,9},{9,5},{13,1},{2,14},{6,10},... | collective-permute-start | bytes 196616 | tf_op jit(solution)/shard_map/ppermute | solution.py:213
  13.3 7.8 %collective-permute-start.4 = (bf16[2,4,32,128]{3,2,1,0:T(8,128)(2,1)S(1)}, bf16[2,4,32,128]{3,2,1,0:T(8,128)(2,1)S(1)}, u32[]{:S(2)}, u32[]{:S(2)}) collective-permute-start(bf16[2,4,32,128]{3,2,1,0:T(8,128)(2,1)S(1)} %get-tuple-element.36), channel_id=1, source_target_pairs={{0,4},{4,0},{8,12},{12,8},{1,5},{5,1},{9,13},{13,9},{2,6},{6,2},{1... | collective-permute-start | bytes 196616 | tf_op jit(solution)/shard_map/ppermute | solution.py:213
  14.7 6.8 %collective-permute-start.11 = (bf16[4,4,48,128]{3,2,1,0:T(8,128)(2,1)S(1)}, bf16[4,4,48,128]{3,2,1,0:T(8,128)(2,1)S(1)}, u32[]{:S(2)}, u32[]{:S(2)}) collective-permute-start(bf16[4,4,48,128]{3,2,1,0:T(8,128)(2,1)S(1)} %far_second.1), channel_id=1, source_target_pairs={{0,2},{1,3},{2,0},{3,1},{4,6},{5,7},{6,4},{7,5},{8,10},{9,11},{10,... | collective-permute-start | bytes 589832 | tf_op jit(solution)/shard_map/ppermute | solution.py:213
  16.6 7.4 %collective-permute-start.10 = (bf16[4,48,128]{2,1,0:T(8,128)(2,1)S(1)}, bf16[4,48,128]{2,1,0:T(8,128)(2,1)S(1)}, u32[]{:S(2)}, u32[]{:S(2)}) collective-permute-start(bf16[4,48,128]{2,1,0:T(8,128)(2,1)S(1)} %get-tuple-element.44), channel_id=1, source_target_pairs={{0,4},{4,0},{8,12},{12,8},{1,5},{5,1},{9,13},{13,9},{2,6},{6,2},{1... | collective-permute-start | bytes 147464 | tf_op jit(solution)/shard_map/ppermute | solution.py:213
  18.3 7.3 %collective-permute-start.8 = (bf16[4,48,128]{2,1,0:T(8,128)(2,1)S(1)}, bf16[4,48,128]{2,1,0:T(8,128)(2,1)S(1)}, u32[]{:S(2)}, u32[]{:S(2)}) collective-permute-start(bf16[4,48,128]{2,1,0:T(8,128)(2,1)S(1)} %get-tuple-element.42), channel_id=1, source_target_pairs={{0,8},{4,12},{8,0},{12,4},{1,9},{5,13},{9,1},{13,5},{2,10},{6,14},... | collective-permute-start | bytes 147464 | tf_op jit(solution)/shard_map/ppermute | solution.py:213
  20.9 6.1 %collective-permute-start.9 = (bf16[4,48,128]{2,1,0:T(8,128)(2,1)S(1)}, bf16[4,48,128]{2,1,0:T(8,128)(2,1)S(1)}, u32[]{:S(2)}, u32[]{:S(2)}) collective-permute-start(bf16[4,48,128]{2,1,0:T(8,128)(2,1)S(1)} %get-tuple-element.43), channel_id=1, source_target_pairs={{0,12},{4,8},{8,4},{12,0},{1,13},{5,9},{9,5},{13,1},{2,14},{6,10},... | collective-permute-start | bytes 147464 | tf_op jit(solution)/shard_map/ppermute | solution.py:213
  21.1 5.9 %collective-permute-start.5 = (bf16[4,32,128]{2,1,0:T(8,128)(2,1)S(1)}, bf16[4,32,128]{2,1,0:T(8,128)(2,1)S(1)}, u32[]{:S(2)}, u32[]{:S(2)}) collective-permute-start(bf16[4,32,128]{2,1,0:T(8,128)(2,1)S(1)} %get-tuple-element.38), channel_id=1, source_target_pairs={{0,2},{1,3},{2,0},{3,1},{4,6},{5,7},{6,4},{7,5},{8,10},{9,11},{10,... | collective-permute-start | bytes 98312 | tf_op jit(solution)/shard_map/ppermute | solution.py:213
  21.6 7.4 %collective-permute-start.12 = (bf16[4,48,128]{2,1,0:T(8,128)(2,1)S(1)}, bf16[4,48,128]{2,1,0:T(8,128)(2,1)S(1)}, u32[]{:S(2)}, u32[]{:S(2)}) collective-permute-start(bf16[4,48,128]{2,1,0:T(8,128)(2,1)S(1)} %get-tuple-element.46), channel_id=1, source_target_pairs={{0,8},{4,12},{8,0},{12,4},{1,9},{5,13},{9,1},{13,5},{2,10},{6,14},... | collective-permute-start | bytes 147464 | tf_op jit(solution)/shard_map/ppermute | solution.py:213
  24.1 6.0 %collective-permute-start.13 = (bf16[4,48,128]{2,1,0:T(8,128)(2,1)S(1)}, bf16[4,48,128]{2,1,0:T(8,128)(2,1)S(1)}, u32[]{:S(2)}, u32[]{:S(2)}) collective-permute-start(bf16[4,48,128]{2,1,0:T(8,128)(2,1)S(1)} %get-tuple-element.47), channel_id=1, source_target_pairs={{0,12},{4,8},{8,4},{12,0},{1,13},{5,9},{9,5},{13,1},{2,14},{6,10},... | collective-permute-start | bytes 147464 | tf_op jit(solution)/shard_map/ppermute | solution.py:213
  25.6 4.6 %collective-permute-start.14 = (bf16[4,48,128]{2,1,0:T(8,128)(2,1)S(1)}, bf16[4,48,128]{2,1,0:T(8,128)(2,1)S(1)}, u32[]{:S(2)}, u32[]{:S(2)}) collective-permute-start(bf16[4,48,128]{2,1,0:T(8,128)(2,1)S(1)} %get-tuple-element.48), channel_id=1, source_target_pairs={{0,4},{4,0},{8,12},{12,8},{1,5},{5,1},{9,13},{13,9},{2,6},{6,2},{1... | collective-permute-start | bytes 147464 | tf_op jit(solution)/shard_map/ppermute | solution.py:213

commit v7 on v6

--- a/solution.py
+++ b/solution.py
@@ -22,8 +22,8 @@
     right_hbm,
     first_send,
     first_keep,
-    b_send,
-    b_keep,
+    soon_send,
+    soon_keep,
     rest_send,
     rest_keep,
     mask_ref,
@@ -43,7 +43,8 @@
     width = wave.shape[0]
     terms = left.shape[0]
     targets, strip, _ = mask_ref.shape
-    a_rows = first_send.shape[2]
+    a_rows = first_send.shape[1] // 2
+    b_rows = strip - a_rows
     unit = width // 8
     sec = lax.axis_index("sec")
     mpo = lax.axis_index("mpo")
@@ -77,17 +78,15 @@
         return carry
 
     lax.fori_loop(0, terms, fetch, 0)
-    for ref in (first_send, first_keep, b_send, b_keep, rest_send, rest_keep):
-
-        def clear(q, carry, ref=ref):
-            if len(ref.shape) == 4:
-                ref[q] = jnp.zeros(ref.shape[1:], ref.dtype)
-            else:
-                for n in range(ref.shape[0]):
-                    ref[n, q] = jnp.zeros(ref.shape[2:], ref.dtype)
-            return carry
-
-        lax.fori_loop(0, 4, clear, 0)
+    def clear(t, carry):
+        for ref in (first_send, first_keep, rest_send, rest_keep):
+            ref[t] = jnp.zeros(ref.shape[1:], ref.dtype)
+        for ref in (soon_send, soon_keep):
+            for n in range(2):
+                ref[n, t] = jnp.zeros(ref.shape[2:], ref.dtype)
+        return carry
+
+    lax.fori_loop(0, targets, clear, 0)
     for copy in scalars:
         copy.wait()
     lane = mpo * strip + lax.broadcasted_iota(jnp.int32, (strip, strip), 1)
@@ -128,85 +127,95 @@
                 (((1,), (1,)), ((), ())),
                 preferred_element_type=jnp.float32,
             )
-            first, b_part, rest = (
-                (first_send, b_send, rest_send) if side == 0 else (first_keep, b_keep, rest_keep)
+            first, soon, rest = (
+                (first_send, soon_send, rest_send)
+                if side == 0
+                else (first_keep, soon_keep, rest_keep)
             )
             for q in range(4):
                 for n in range(2):
                     value = weight * contrib[
                         q * strip : (q + 1) * strip, n * strip : (n + 1) * strip
                     ]
-                    if n == 0:
-                        put(first, (q, t), value[:a_rows])
-                        put(rest, (0, q, t), value[a_rows : 2 * a_rows])
+                    if q == 0:
+                        put(rest, (t,), n * strip, value)
+                    elif q == 1:
+                        put(soon, (n, t), 0, value)
                     else:
-                        put(rest, (1, q, t), value[:a_rows])
-                        put(rest, (2, q, t), value[a_rows : 2 * a_rows])
-                    put(b_part, (n, q, t), value[2 * a_rows :])
+                        if n == 0:
+                            put(first, (t,), (q - 2) * a_rows, value[:a_rows])
+                        else:
+                            put(rest, (t,), 2 * strip + (q - 2) * a_rows, value[:a_rows])
+                        put(soon, (n, t), strip + (q - 2) * b_rows, value[a_rows:])
         return carry
 
     lax.fori_loop(0, terms, term, 0)
 
 
-def put(ref, at, value):
+def put(ref, at, row, value):
+    at = at + (slice(row, row + value.shape[0]), slice(None))
     ref[at] = (ref[at].astype(jnp.float32) + value).astype(jnp.bfloat16)
 
 
-def far_first(keep_ref, recv_ref, far_ref):
+def far_kernel(keep_ref, recv_ref, far_ref):
     far_ref[...] = add(keep_ref[...], recv_ref[...])
 
 
-def far_second(keep_ref, recv_ref, after_ref, far_ref):
-    far_ref[...] = add(keep_ref[0], recv_ref[0])
-
-
-def own_first(keep_ref, recv_ref, cross_ref, *own_refs):
-    for q, own_ref in enumerate(own_refs):
-        own_ref[...] = add(keep_ref[1, q], recv_ref[1, q], cross_ref[q])
-
-
-def own_second(keep_ref, recv_ref, cross_ref, *own_refs):
-    for q, own_ref in enumerate(own_refs):
-        own_ref[...] = add(keep_ref[2, q], recv_ref[2, q], cross_ref[q])
-
-
-def b_kernel(keep_ref, recv_ref, rest_in, after_ref, rest_out, *own_refs):
-    del rest_in, rest_out
-    for q, own_ref in enumerate(own_refs):
-        own_ref[...] = add(keep_ref[:, q], recv_ref[:, q])
-
-
-def b_sum_kernel(*refs):
-    pieces, (far_ref, near_ref) = refs[:-2], refs[-2:]
-    far_ref[...] = add(*[piece[0] for piece in pieces])
-    near_ref[...] = add(*[piece[1] for piece in pieces])
-
-
-def sum_first(*refs):
-    pieces, sum_ref = refs[:-1], refs[-1]
-    total = pieces[0][...].astype(jnp.float32)
-    for piece in pieces[1:]:
-        total = total + piece[...].astype(jnp.float32)
-    sum_ref[...] = total
-
-
-def final_kernel(mask_ref, near_ref, cross_ref, sum_ref, *refs):
-    pieces, out_ref = refs[:-1], refs[-1]
-    rows = sum_ref.shape[1]
-    for first, group in ((0, (sum_ref,)), (rows, pieces), (2 * rows, (near_ref, cross_ref))):
-        last = first + group[0].shape[1]
-        total = group[0][...].astype(jnp.float32)
-        for piece in group[1:]:
-            total = total + piece[...].astype(jnp.float32)
+def soon_kernel(keep_ref, recv_ref, rest_in, after_ref, rest_out, *own_refs):
+    del rest_in, after_ref, rest_out
+    row = 0
+    for own_ref in own_refs:
+        rows = own_ref.shape[2]
+        own_ref[...] = add(keep_ref[:, :, row : row + rows, :], recv_ref[:, :, row : row + rows, :])
+        row += rows
+
+
+def own_kernel(keep_ref, recv_ref, cross_ref, *own_refs):
+    rows = own_refs[0].shape[1]
+    row = keep_ref.shape[1] - 2 * rows
+    for n, own_ref in enumerate(own_refs):
+        at = slice(row + n * rows, row + (n + 1) * rows)
+        own_ref[...] = add(
+            keep_ref[:, at, :], recv_ref[:, at, :], cross_ref[:, n * rows : (n + 1) * rows, :]
+        )
+
+
+def here_kernel(keep_ref, recv_ref, next_ref, two_ref, three_ref, after_ref, far_ref, near_ref):
+    del after_ref
+    strip = far_ref.shape[1]
+    a_rows = strip - two_ref.shape[2]
+    for n, out_ref in enumerate((far_ref, near_ref)):
+        for first, last in ((0, a_rows), (a_rows, strip)):
+            at = slice(n * strip + first, n * strip + last)
+            parts = [keep_ref[:, at, :], recv_ref[:, at, :], next_ref[n, :, first:last, :]]
+            if first:
+                parts += [two_ref[n], three_ref[n]]
+            out_ref[:, first:last, :] = total(*parts).astype(out_ref.dtype)
+
+
+def far_sum_kernel(two_ref, three_ref, sum_ref):
+    sum_ref[...] = total(two_ref[...], three_ref[...])
+
+
+def final_kernel(mask_ref, near_ref, cross_ref, sum_ref, out_ref):
+    a_rows, strip = sum_ref.shape[1], out_ref.shape[1]
+    for first, last in ((0, a_rows), (a_rows, strip)):
+        parts = [near_ref[:, first:last, :], cross_ref[:, first:last, :]]
+        if not first:
+            parts += [sum_ref[...]]
         inside = mask_ref[:, first:last, :].astype(jnp.float32) > 0.0
-        out_ref[:, first:last, :] = jnp.where(inside, total, 0.0).astype(jnp.bfloat16)
+        out_ref[:, first:last, :] = jnp.where(inside, total(*parts), 0.0).astype(jnp.bfloat16)
+
+
+def total(*arrays):
+    result = arrays[0].astype(jnp.float32)
+    for array in arrays[1:]:
+        result = result + array.astype(jnp.float32)
+    return result
 
 
 def add(*arrays):
-    total = arrays[0].astype(jnp.float32)
-    for array in arrays[1:]:
-        total = total + array.astype(jnp.float32)
-    return total.astype(jnp.bfloat16)
+    return total(*arrays).astype(jnp.bfloat16)
 
 
 def swap(array, axis, mask):
@@ -220,8 +229,8 @@
     terms = left_env.shape[1]
     targets = block_dims.shape[0]
     strip = width // 4
-    a_rows = strip * 3 // 8
-    b_rows = strip - 2 * a_rows
+    a_rows = strip * 3 // 4
+    b_rows = strip - a_rows
     vmem = pl.BlockSpec(memory_space=pltpu.VMEM)
     hbm = pl.BlockSpec(memory_space=pltpu.HBM)
 
@@ -247,12 +256,15 @@
         pltpu.with_memory_space_constraint(x, pltpu.HBM)
         for x in (*scalars, wave_blocks, left_env, right_env)
     ]
-    across = like(4, targets, a_rows)
-    b_shape = like(2, 4, targets, b_rows)
-    rest_shape = like(3, 4, targets, a_rows)
-    first_send, first_keep, b_send, b_keep, rest_send, rest_keep, mask = pl.pallas_call(
+    first_shape = like(targets, 2 * a_rows)
+    soon_shape = like(2, targets, strip + 2 * b_rows)
+    rest_shape = like(targets, 2 * strip + 2 * a_rows)
+    first_send, first_keep, soon_send, soon_keep, rest_send, rest_keep, mask = pl.pallas_call(
         term_kernel,
-        out_shape=[across] * 2 + [b_shape] * 2 + [rest_shape] * 2 + [like(targets, strip)],
+        out_shape=[first_shape] * 2
+        + [soon_shape] * 2
+        + [rest_shape] * 2
+        + [like(targets, strip)],
         in_specs=[hbm] * 8,
         out_specs=[vmem] * 7,
         scratch_shapes=[pltpu.SMEM(scalar.shape, scalar.dtype) for scalar in scalars]
@@ -272,33 +284,40 @@
         name="terms",
     )(*operands)
     first_recv = swap(first_send, "mpo", 1)
-    b_recv = swap(b_send, "mpo", 1)
-    first_far = call(far_first, across, first_keep, first_recv, span=3)
-    first_cross = swap(first_far, "mpo", 2)
-    rest_send, *b_own = call(
-        b_kernel,
-        [rest_shape] + [like(2, targets, b_rows)] * 4,
-        b_keep,
-        b_recv,
+    soon_recv = swap(soon_send, "mpo", 1)
+    far = call(far_kernel, first_shape, first_keep, first_recv, span=3)
+    cross = swap(far, "mpo", 2)
+    part = like(2, targets, b_rows)
+    rest_send, *soon = call(
+        soon_kernel,
+        [rest_shape, like(2, targets, strip), part, part],
+        soon_keep,
+        soon_recv,
         rest_send,
-        first_far,
+        far,
         aliases={2: 0},
-    )
-    b_pieces = [b_own[0]] + [swap(b_own[q], "sec", q) for q in (2, 3, 1)]
+        span=3,
+    )
+    two, three, one = [swap(soon[q - 1], "sec", q) for q in (2, 3, 1)]
     rest_recv = swap(rest_send, "mpo", 1)
-    second_far = call(far_second, across, rest_keep, rest_recv, first_cross, span=3)
-    second_cross = swap(second_far, "mpo", 2)
-    pieces = []
-    for kernel, cross in ((own_first, first_cross), (own_second, second_cross)):
-        own = call(kernel, [like(targets, a_rows)] * 4, rest_keep, rest_recv, cross)
-        pieces += [own[0]] + [swap(own[q], "sec", q) for q in (2, 3, 1)]
-    b_far, b_near = call(b_sum_kernel, [like(targets, b_rows)] * 2, *b_pieces, span=3)
-    b_cross = swap(b_far, "mpo", 2)
-    first_sum = jax.ShapeDtypeStruct((targets, a_rows, strip), jnp.float32)
-    first_sum = call(sum_first, first_sum, *pieces[:4], span=3)
-    return call(
-        final_kernel, like(targets, strip), mask, b_near, b_cross, first_sum, *pieces[4:]
-    )
+    own = call(own_kernel, [like(targets, a_rows)] * 2, rest_keep, rest_recv, cross, span=3)
+    near = jax.ShapeDtypeStruct((targets, strip, strip), jnp.float32)
+    here, near = call(
+        here_kernel,
+        [like(targets, strip), near],
+        rest_keep,
+        rest_recv,
+        one,
+        two,
+        three,
+        own[0],
+        span=3,
+    )
+    own = [swap(array, "sec", q) for array, q in zip(own, (2, 3))]
+    here = swap(here, "mpo", 2)
+    far_sum = jax.ShapeDtypeStruct((targets, a_rows, strip), jnp.float32)
+    far_sum = call(far_sum_kernel, far_sum, *own, span=3)
+    return call(final_kernel, like(targets, strip), mask, near, here, far_sum)
 
 
 def by_classes(

time: 31 us -> 29.7 us (0.958)
  starting transfers between devices: 19 us -> 12.9 us
  waiting for transfers between devices: 6.63 us -> 11.4 us
    ppermute x15 -> x10, starting transfers between devices: 19 us -> 12.9 us  [swap(): lax.ppermute(array, axis, [(i, i ^ mask) for i in range(lax.axis_size(axi...]
    ppermute x15 -> x10, waiting for transfers between devices: 6.63 us -> 11.4 us  [swap(): lax.ppermute(array, axis, [(i, i ^ mask) for i in range(lax.axis_size(axi...]
    pallas_call x8 -> x6, Pallas kernels: 1.08 us -> 1.06 us  [call(): pl.pallas_call(kernel, out_shape=out_shape, in_specs=[vmem] * len(args),...]
  transfers between devices with their start and end apart: 15 -> 10, of which waited for: 7 -> 6; matrix products, arithmetic and copies ran while one was open for 0% -> 0% of each run, Pallas kernels for 1% -> 1%
where the time goes in v7:
time: 29.7 us; the launch traced here: 29.5 us
  starting transfers between devices  12.9 us (43%)
  waiting for transfers between devices  11.4 us (38%)
  Pallas kernels  5.2 us (18%)
    ppermute x10, starting transfers between devices, swap(): lax.ppermute(array, axis, [(i, i ^ mask) for i in range(lax.axis_size(axi...  12.9 us
    ppermute x10, waiting for transfers between devices, swap(): lax.ppermute(array, axis, [(i, i ^ mask) for i in range(lax.axis_size(axi...  11.4 us
    pallas_call x1, Pallas kernels, by_targets(): pl.pallas_call(term_kernel, out_shape=[first_shape] * 2 + [soon_shape] *...  4.14 us
    pallas_call x6, Pallas kernels, call(): pl.pallas_call(kernel, out_shape=out_shape, in_specs=[vmem] * len(args),...  1.06 us
  transfers between devices with their start and end apart: 10, of which 6 were waited for; matrix products, arithmetic and copies ran while one was open for 0% of the time, Pallas kernels for 1%

profile of v7, /device:TPU:0, one launch (start us, length us, event | category | flops | bytes accessed | tf_op | source)
XLA Modules:
  0.0 29.5 jit_solution(85539531072328229)
XLA Ops:
  0.0 4.1 %terms.1 = (bf16[4,192,128]{2,1,0:T(8,128)(2,1)S(1)}, bf16[4,192,128]{2,1,0:T(8,128)(2,1)S(1)}, bf16[2,4,192,128]{3,2,1,0:T(8,128)(2,1)S(1)}, bf16[2,4,192,128]{...) custom-call(s32[1,3]{1,0:T(1,128)} %cls_hbm.1, ...), custom_call_target="tpu_custom_call" | custom-call | flops 1610612736 | bytes 4194304 | tf_op jit(solution)/shard_map/terms/pallas_call | solution.py:262
  4.1 0.5 %collective-permute-start.1 = (bf16[4,192,128]{2,1,0:T(8,128)(2,1)S(1)}, bf16[4,192,128]{2,1,0:T(8,128)(2,1)S(1)}, u32[]{:S(2)}, u32[]{:S(2)}) collective-permute-start(bf16[4,192,128]{2,1,0:T(8,128)(2,1)S(1)} %get-tuple-element.26), channel_id=1, source_target_pairs={{0,1},{1,0},{2,3},{3,2},{4,5},{5,4},{6,7},{7,6},{8,9},{9,8},{10,11... | collective-permute-start | bytes 589832 | tf_op jit(solution)/shard_map/ppermute | solution.py:222
  4.7 0.1 collective-permute-start
  4.7 1.0 %collective-permute-done.1.recv_ref = bf16[4,192,128]{2,1,0:T(8,128)(2,1)S(1)} collective-permute-done((bf16[4,192,128]{2,1,0:T(8,128)(2,1)S(1)}, bf16[4,192,128]{2,1,0:T(8,128)(2,1)S(1)}, u32[]{:S(2)}, u32[]{:S(2)}) %collective-permute-start.1) | collective-permute-done | bytes 196640 | tf_op jit(solution)/shard_map/ppermute | solution.py:222
  5.8 0.6 %collective-permute-done.recv_ref = bf16[2,4,192,128]{3,2,1,0:T(8,128)(2,1)S(1)} collective-permute-done((bf16[2,4,192,128]{3,2,1,0:T(8,128)(2,1)S(1)}, bf16[2,4,192,128]{3,2,1,0:T(8,128)(2,1)S(1)}, u32[]{:S(2)}, u32[]{:S(2)}) %collective-permute-start) | collective-permute-done | bytes 393248 | tf_op jit(solution)/shard_map/ppermute | solution.py:222
  6.4 0.1 soon_kernel.1
  6.5 0.3 %collective-permute-start.2 = (bf16[4,448,128]{2,1,0:T(8,128)(2,1)S(1)}, bf16[4,448,128]{2,1,0:T(8,128)(2,1)S(1)}, u32[]{:S(2)}, u32[]{:S(2)}) collective-permute-start(bf16[4,448,128]{2,1,0:T(8,128)(2,1)S(1)} %get-tuple-element.27), channel_id=1, source_target_pairs={{0,1},{1,0},{2,3},{3,2},{4,5},{5,4},{6,7},{7,6},{8,9},{9,8},{10,11... | collective-permute-start | bytes 1376264 | tf_op jit(solution)/shard_map/ppermute | solution.py:222
  6.8 2.7 %collective-permute-start.6 = (bf16[4,192,128]{2,1,0:T(8,128)(2,1)S(1)}, bf16[4,192,128]{2,1,0:T(8,128)(2,1)S(1)}, u32[]{:S(2)}, u32[]{:S(2)}) collective-permute-start(bf16[4,192,128]{2,1,0:T(8,128)(2,1)S(1)} %far_kernel.1.after_ref), channel_id=1, source_target_pairs={{0,2},{1,3},{2,0},{3,1},{4,6},{5,7},{6,4},{7,5},{8,10},{9,11},{10,... | collective-permute-start | bytes 589832 | tf_op jit(solution)/shard_map/ppermute | solution.py:222
  9.5 1.6 %collective-permute-start.3 = (bf16[2,4,128,128]{3,2,1,0:T(8,128)(2,1)S(1)}, bf16[2,4,128,128]{3,2,1,0:T(8,128)(2,1)S(1)}, u32[]{:S(2)}, u32[]{:S(2)}) collective-permute-start(bf16[2,4,128,128]{3,2,1,0:T(8,128)(2,1)S(1)} %get-tuple-element.28), channel_id=1, source_target_pairs={{0,4},{4,0},{8,12},{12,8},{1,5},{5,1},{9,13},{13,9},{2,6},{6,2},{1... | collective-permute-start | bytes 786440 | tf_op jit(solution)/shard_map/ppermute | solution.py:222
  11.1 2.6 %collective-permute-start.4 = (bf16[2,4,32,128]{3,2,1,0:T(8,128)(2,1)S(1)}, bf16[2,4,32,128]{3,2,1,0:T(8,128)(2,1)S(1)}, u32[]{:S(2)}, u32[]{:S(2)}) collective-permute-start(bf16[2,4,32,128]{3,2,1,0:T(8,128)(2,1)S(1)} %get-tuple-element.29), channel_id=1, source_target_pairs={{0,8},{4,12},{8,0},{12,4},{1,9},{5,13},{9,1},{13,5},{2,10},{6,14},... | collective-permute-start | bytes 196616 | tf_op jit(solution)/shard_map/ppermute | solution.py:222
  13.7 0.2 collective-permute-start.5
  13.9 1.0 %collective-permute-done.6.cross_ref = bf16[4,192,128]{2,1,0:T(8,128)(2,1)S(1)} collective-permute-done((bf16[4,192,128]{2,1,0:T(8,128)(2,1)S(1)}, bf16[4,192,128]{2,1,0:T(8,128)(2,1)S(1)}, u32[]{:S(2)}, u32[]{:S(2)}) %collective-permute-start.6) | collective-permute-done | bytes 196640 | tf_op jit(solution)/shard_map/ppermute | solution.py:222
  14.9 0.0 collective-permute-done.2.recv_ref
  14.9 0.1 own_kernel.1
  15.0 2.9 %collective-permute-start.8 = (bf16[4,96,128]{2,1,0:T(8,128)(2,1)S(1)}, bf16[4,96,128]{2,1,0:T(8,128)(2,1)S(1)}, u32[]{:S(2)}, u32[]{:S(2)}) collective-permute-start(bf16[4,96,128]{2,1,0:T(8,128)(2,1)S(1)} %get-tuple-element.31.after_ref), channel_id=1, source_target_pairs={{0,8},{4,12},{8,0},{12,4},{1,9},{5,13},{9,1},{13,5},{2,10},{6,14},... | collective-permute-start | bytes 294920 | tf_op jit(solution)/shard_map/ppermute | solution.py:222
  17.9 1.3 %collective-permute-start.9 = (bf16[4,96,128]{2,1,0:T(8,128)(2,1)S(1)}, bf16[4,96,128]{2,1,0:T(8,128)(2,1)S(1)}, u32[]{:S(2)}, u32[]{:S(2)}) collective-permute-start(bf16[4,96,128]{2,1,0:T(8,128)(2,1)S(1)} %get-tuple-element.34), channel_id=1, source_target_pairs={{0,12},{4,8},{8,4},{12,0},{1,13},{5,9},{9,5},{13,1},{2,14},{6,10},... | collective-permute-start | bytes 294920 | tf_op jit(solution)/shard_map/ppermute | solution.py:222
  19.2 0.0 collective-permute-done.4.two_ref
  19.3 4.4 %collective-permute-done.5.three_ref = bf16[2,4,32,128]{3,2,1,0:T(8,128)(2,1)S(1)} collective-permute-done((bf16[2,4,32,128]{3,2,1,0:T(8,128)(2,1)S(1)}, bf16[2,4,32,128]{3,2,1,0:T(8,128)(2,1)S(1)}, u32[]{:S(2)}, u32[]{:S(2)}) %collective-permute-start.5) | collective-permute-done | bytes 65568 | tf_op jit(solution)/shard_map/ppermute | solution.py:222
  23.7 0.0 collective-permute-done.3.next_ref
  23.7 0.1 here_kernel.1
  23.8 0.6 %collective-permute-start.7 = (bf16[4,128,128]{2,1,0:T(8,128)(2,1)S(1)}, bf16[4,128,128]{2,1,0:T(8,128)(2,1)S(1)}, u32[]{:S(2)}, u32[]{:S(2)}) collective-permute-start(bf16[4,128,128]{2,1,0:T(8,128)(2,1)S(1)} %get-tuple-element.33), channel_id=1, source_target_pairs={{0,2},{1,3},{2,0},{3,1},{4,6},{5,7},{6,4},{7,5},{8,10},{9,11},{10,... | collective-permute-start | bytes 393224 | tf_op jit(solution)/shard_map/ppermute | solution.py:222
  24.4 3.7 %collective-permute-done.8.two_ref = bf16[4,96,128]{2,1,0:T(8,128)(2,1)S(1)} collective-permute-done((bf16[4,96,128]{2,1,0:T(8,128)(2,1)S(1)}, bf16[4,96,128]{2,1,0:T(8,128)(2,1)S(1)}, u32[]{:S(2)}, u32[]{:S(2)}) %collective-permute-start.8) | collective-permute-done | bytes 98336 | tf_op jit(solution)/shard_map/ppermute | solution.py:222
  28.1 0.0 collective-permute-done.9.three_ref
  28.1 0.7 %collective-permute-done.7.cross_ref = bf16[4,128,128]{2,1,0:T(8,128)(2,1)S(1)} collective-permute-done((bf16[4,128,128]{2,1,0:T(8,128)(2,1)S(1)}, bf16[4,128,128]{2,1,0:T(8,128)(2,1)S(1)}, u32[]{:S(2)}, u32[]{:S(2)}) %collective-permute-start.7) | collective-permute-done | bytes 131104 | tf_op jit(solution)/shard_map/ppermute | solution.py:222
  28.8 0.7 %final_kernel.1 = bf16[4,128,128]{2,1,0:T(8,128)(2,1)} custom-call(bf16[4,128,128]{2,1,0:T(8,128)(2,1)S(1)} %get-tuple-element.20.mask_ref, f32[4,128,128]{2,1,0:T(8,128)S(1)} %get-tuple-element.32.near_ref, bf16[4,128,128]{2,1,0:T(8,128)(2,1)S(1)} %collective-permute-done.7.cross_ref, f32[4,96,128]{2,1,0:T(8,128)S(1)} %far_sum_kernel.1.sum_ref), custom_call_target="tpu_custom_call" | custom-call | flops 100000000 | tf_op jit(solution)/shard_map/final_kernel/pallas_call | solution.py:241
  (2 shorter events, 0.1 us)
Async XLA Ops:
  4.1 1.6 %collective-permute-start.1 = (bf16[4,192,128]{2,1,0:T(8,128)(2,1)S(1)}, bf16[4,192,128]{2,1,0:T(8,128)(2,1)S(1)}, u32[]{:S(2)}, u32[]{:S(2)}) collective-permute-start(bf16[4,192,128]{2,1,0:T(8,128)(2,1)S(1)} %get-tuple-element.26), channel_id=1, source_target_pairs={{0,1},{1,0},{2,3},{3,2},{4,5},{5,4},{6,7},{7,6},{8,9},{9,8},{10,11... | collective-permute-start | bytes 589832 | tf_op jit(solution)/shard_map/ppermute | solution.py:222
  4.7 1.7 %collective-permute-start = (bf16[2,4,192,128]{3,2,1,0:T(8,128)(2,1)S(1)}, bf16[2,4,192,128]{3,2,1,0:T(8,128)(2,1)S(1)}, u32[]{:S(2)}, u32[]{:S(2)}) collective-permute-start(bf16[2,4,192,128]{3,2,1,0:T(8,128)(2,1)S(1)} %get-tuple-element.23), channel_id=1, source_target_pairs={{0,1},{1,0},{2,3},{3,2},{4,5},{5,4},{6,7},{7,6},{8,9},{9,8},{10,11... | collective-permute-start | bytes 1179656 | tf_op jit(solution)/shard_map/ppermute | solution.py:222
  6.5 8.4 %collective-permute-start.2 = (bf16[4,448,128]{2,1,0:T(8,128)(2,1)S(1)}, bf16[4,448,128]{2,1,0:T(8,128)(2,1)S(1)}, u32[]{:S(2)}, u32[]{:S(2)}) collective-permute-start(bf16[4,448,128]{2,1,0:T(8,128)(2,1)S(1)} %get-tuple-element.27), channel_id=1, source_target_pairs={{0,1},{1,0},{2,3},{3,2},{4,5},{5,4},{6,7},{7,6},{8,9},{9,8},{10,11... | collective-permute-start | bytes 1376264 | tf_op jit(solution)/shard_map/ppermute | solution.py:222
  6.8 8.1 %collective-permute-start.6 = (bf16[4,192,128]{2,1,0:T(8,128)(2,1)S(1)}, bf16[4,192,128]{2,1,0:T(8,128)(2,1)S(1)}, u32[]{:S(2)}, u32[]{:S(2)}) collective-permute-start(bf16[4,192,128]{2,1,0:T(8,128)(2,1)S(1)} %far_kernel.1.after_ref), channel_id=1, source_target_pairs={{0,2},{1,3},{2,0},{3,1},{4,6},{5,7},{6,4},{7,5},{8,10},{9,11},{10,... | collective-permute-start | bytes 589832 | tf_op jit(solution)/shard_map/ppermute | solution.py:222
  9.5 14.1 %collective-permute-start.3 = (bf16[2,4,128,128]{3,2,1,0:T(8,128)(2,1)S(1)}, bf16[2,4,128,128]{3,2,1,0:T(8,128)(2,1)S(1)}, u32[]{:S(2)}, u32[]{:S(2)}) collective-permute-start(bf16[2,4,128,128]{3,2,1,0:T(8,128)(2,1)S(1)} %get-tuple-element.28), channel_id=1, source_target_pairs={{0,4},{4,0},{8,12},{12,8},{1,5},{5,1},{9,13},{13,9},{2,6},{6,2},{1... | collective-permute-start | bytes 786440 | tf_op jit(solution)/shard_map/ppermute | solution.py:222
  11.1 8.1 %collective-permute-start.4 = (bf16[2,4,32,128]{3,2,1,0:T(8,128)(2,1)S(1)}, bf16[2,4,32,128]{3,2,1,0:T(8,128)(2,1)S(1)}, u32[]{:S(2)}, u32[]{:S(2)}) collective-permute-start(bf16[2,4,32,128]{3,2,1,0:T(8,128)(2,1)S(1)} %get-tuple-element.29), channel_id=1, source_target_pairs={{0,8},{4,12},{8,0},{12,4},{1,9},{5,13},{9,1},{13,5},{2,10},{6,14},... | collective-permute-start | bytes 196616 | tf_op jit(solution)/shard_map/ppermute | solution.py:222
  13.7 9.9 %collective-permute-start.5 = (bf16[2,4,32,128]{3,2,1,0:T(8,128)(2,1)S(1)}, bf16[2,4,32,128]{3,2,1,0:T(8,128)(2,1)S(1)}, u32[]{:S(2)}, u32[]{:S(2)}) collective-permute-start(bf16[2,4,32,128]{3,2,1,0:T(8,128)(2,1)S(1)} %get-tuple-element.30), channel_id=1, source_target_pairs={{0,12},{4,8},{8,4},{12,0},{1,13},{5,9},{9,5},{13,1},{2,14},{6,10},... | collective-permute-start | bytes 196616 | tf_op jit(solution)/shard_map/ppermute | solution.py:222
  15.0 13.1 %collective-permute-start.8 = (bf16[4,96,128]{2,1,0:T(8,128)(2,1)S(1)}, bf16[4,96,128]{2,1,0:T(8,128)(2,1)S(1)}, u32[]{:S(2)}, u32[]{:S(2)}) collective-permute-start(bf16[4,96,128]{2,1,0:T(8,128)(2,1)S(1)} %get-tuple-element.31.after_ref), channel_id=1, source_target_pairs={{0,8},{4,12},{8,0},{12,4},{1,9},{5,13},{9,1},{13,5},{2,10},{6,14},... | collective-permute-start | bytes 294920 | tf_op jit(solution)/shard_map/ppermute | solution.py:222
  17.9 10.2 %collective-permute-start.9 = (bf16[4,96,128]{2,1,0:T(8,128)(2,1)S(1)}, bf16[4,96,128]{2,1,0:T(8,128)(2,1)S(1)}, u32[]{:S(2)}, u32[]{:S(2)}) collective-permute-start(bf16[4,96,128]{2,1,0:T(8,128)(2,1)S(1)} %get-tuple-element.34), channel_id=1, source_target_pairs={{0,12},{4,8},{8,4},{12,0},{1,13},{5,9},{9,5},{13,1},{2,14},{6,10},... | collective-permute-start | bytes 294920 | tf_op jit(solution)/shard_map/ppermute | solution.py:222
  23.8 5.0 %collective-permute-start.7 = (bf16[4,128,128]{2,1,0:T(8,128)(2,1)S(1)}, bf16[4,128,128]{2,1,0:T(8,128)(2,1)S(1)}, u32[]{:S(2)}, u32[]{:S(2)}) collective-permute-start(bf16[4,128,128]{2,1,0:T(8,128)(2,1)S(1)} %get-tuple-element.33), channel_id=1, source_target_pairs={{0,2},{1,3},{2,0},{3,1},{4,6},{5,7},{6,4},{7,5},{8,10},{9,11},{10,... | collective-permute-start | bytes 393224 | tf_op jit(solution)/shard_map/ppermute | solution.py:222

commit v8 on v7

--- a/solution.py
+++ b/solution.py
@@ -20,10 +20,8 @@
     wave_hbm,
     left_hbm,
     right_hbm,
-    first_send,
-    first_keep,
-    soon_send,
-    soon_keep,
+    lead_send,
+    lead_keep,
     rest_send,
     rest_keep,
     mask_ref,
@@ -43,8 +41,9 @@
     width = wave.shape[0]
     terms = left.shape[0]
     targets, strip, _ = mask_ref.shape
-    a_rows = first_send.shape[1] // 2
+    a_rows = (rest_send.shape[1] - 2 * strip) // 2
     b_rows = strip - a_rows
+    soon = (2 * a_rows, 2 * a_rows + strip + 2 * b_rows)
     unit = width // 8
     sec = lax.axis_index("sec")
     mpo = lax.axis_index("mpo")
@@ -79,11 +78,8 @@
 
     lax.fori_loop(0, terms, fetch, 0)
     def clear(t, carry):
-        for ref in (first_send, first_keep, rest_send, rest_keep):
+        for ref in (lead_send, lead_keep, rest_send, rest_keep):
             ref[t] = jnp.zeros(ref.shape[1:], ref.dtype)
-        for ref in (soon_send, soon_keep):
-            for n in range(2):
-                ref[n, t] = jnp.zeros(ref.shape[2:], ref.dtype)
         return carry
 
     lax.fori_loop(0, targets, clear, 0)
@@ -113,7 +109,7 @@
 
     lax.fori_loop(0, width // 64, mask, 0)
 
-    def term(j, carry):
+    def term(j):
         pltpu.make_async_copy(left_hbm.at[0, j], left.at[j], left_sems.at[j]).wait()
         half = jnp.dot(left[j], wave[...], preferred_element_type=jnp.float32)
         half = half.astype(jnp.bfloat16)
@@ -127,47 +123,41 @@
                 (((1,), (1,)), ((), ())),
                 preferred_element_type=jnp.float32,
             )
-            first, soon, rest = (
-                (first_send, soon_send, rest_send)
-                if side == 0
-                else (first_keep, soon_keep, rest_keep)
-            )
+            lead, rest = (lead_send, rest_send) if side == 0 else (lead_keep, rest_keep)
             for q in range(4):
                 for n in range(2):
                     value = weight * contrib[
                         q * strip : (q + 1) * strip, n * strip : (n + 1) * strip
                     ]
                     if q == 0:
-                        put(rest, (t,), n * strip, value)
+                        put(rest, t, n * strip, value)
                     elif q == 1:
-                        put(soon, (n, t), 0, value)
+                        put(lead, t, soon[n], value)
                     else:
                         if n == 0:
-                            put(first, (t,), (q - 2) * a_rows, value[:a_rows])
+                            put(lead, t, (q - 2) * a_rows, value[:a_rows])
                         else:
-                            put(rest, (t,), 2 * strip + (q - 2) * a_rows, value[:a_rows])
-                        put(soon, (n, t), strip + (q - 2) * b_rows, value[a_rows:])
-        return carry
-
-    lax.fori_loop(0, terms, term, 0)
-
-
-def put(ref, at, row, value):
-    at = at + (slice(row, row + value.shape[0]), slice(None))
-    ref[at] = (ref[at].astype(jnp.float32) + value).astype(jnp.bfloat16)
-
-
-def far_kernel(keep_ref, recv_ref, far_ref):
-    far_ref[...] = add(keep_ref[...], recv_ref[...])
-
-
-def soon_kernel(keep_ref, recv_ref, rest_in, after_ref, rest_out, *own_refs):
-    del rest_in, after_ref, rest_out
-    row = 0
-    for own_ref in own_refs:
-        rows = own_ref.shape[2]
-        own_ref[...] = add(keep_ref[:, :, row : row + rows, :], recv_ref[:, :, row : row + rows, :])
-        row += rows
+                            put(rest, t, 2 * strip + (q - 2) * a_rows, value[:a_rows])
+                        put(lead, t, soon[n] + strip + (q - 2) * b_rows, value[a_rows:])
+
+    for j in range(terms):
+        term(j)
+
+
+def put(ref, t, row, value):
+    at = slice(row, row + value.shape[0])
+    ref[t, at, :] = (ref[t, at, :].astype(jnp.float32) + value).astype(jnp.bfloat16)
+
+
+def lead_kernel(keep_ref, recv_ref, rest_in, rest_out, far_ref, *own_refs):
+    del rest_in, rest_out
+    row = far_ref.shape[1]
+    far_ref[...] = add(keep_ref[:, :row, :], recv_ref[:, :row, :])
+    for n in range(2):
+        for own_ref in own_refs:
+            at = slice(row, row + own_ref.shape[2])
+            own_ref[n] = add(keep_ref[:, at, :], recv_ref[:, at, :])
+            row += own_ref.shape[2]
 
 
 def own_kernel(keep_ref, recv_ref, cross_ref, *own_refs):
@@ -180,16 +170,20 @@
         )
 
 
-def here_kernel(keep_ref, recv_ref, next_ref, two_ref, three_ref, after_ref, far_ref, near_ref):
+def middle_kernel(two_ref, three_ref, after_ref, sum_ref):
     del after_ref
+    sum_ref[...] = total(two_ref[...], three_ref[...])
+
+
+def here_kernel(keep_ref, recv_ref, one_ref, middle_ref, far_ref, near_ref):
     strip = far_ref.shape[1]
-    a_rows = strip - two_ref.shape[2]
+    a_rows = strip - middle_ref.shape[2]
     for n, out_ref in enumerate((far_ref, near_ref)):
         for first, last in ((0, a_rows), (a_rows, strip)):
             at = slice(n * strip + first, n * strip + last)
-            parts = [keep_ref[:, at, :], recv_ref[:, at, :], next_ref[n, :, first:last, :]]
+            parts = [keep_ref[:, at, :], recv_ref[:, at, :], one_ref[n, :, first:last, :]]
             if first:
-                parts += [two_ref[n], three_ref[n]]
+                parts += [middle_ref[n]]
             out_ref[:, first:last, :] = total(*parts).astype(out_ref.dtype)
 
 
@@ -256,17 +250,13 @@
         pltpu.with_memory_space_constraint(x, pltpu.HBM)
         for x in (*scalars, wave_blocks, left_env, right_env)
     ]
-    first_shape = like(targets, 2 * a_rows)
-    soon_shape = like(2, targets, strip + 2 * b_rows)
+    lead_shape = like(targets, 2 * a_rows + 2 * (strip + 2 * b_rows))
     rest_shape = like(targets, 2 * strip + 2 * a_rows)
-    first_send, first_keep, soon_send, soon_keep, rest_send, rest_keep, mask = pl.pallas_call(
+    lead_send, lead_keep, rest_send, rest_keep, mask = pl.pallas_call(
         term_kernel,
-        out_shape=[first_shape] * 2
-        + [soon_shape] * 2
-        + [rest_shape] * 2
-        + [like(targets, strip)],
+        out_shape=[lead_shape] * 2 + [rest_shape] * 2 + [like(targets, strip)],
         in_specs=[hbm] * 8,
-        out_specs=[vmem] * 7,
+        out_specs=[vmem] * 5,
         scratch_shapes=[pltpu.SMEM(scalar.shape, scalar.dtype) for scalar in scalars]
         + [
             pltpu.VMEM((width, width), jnp.bfloat16),
@@ -283,35 +273,26 @@
         ),
         name="terms",
     )(*operands)
-    first_recv = swap(first_send, "mpo", 1)
-    soon_recv = swap(soon_send, "mpo", 1)
-    far = call(far_kernel, first_shape, first_keep, first_recv, span=3)
-    cross = swap(far, "mpo", 2)
+    lead_recv = swap(lead_send, "mpo", 1)
     part = like(2, targets, b_rows)
-    rest_send, *soon = call(
-        soon_kernel,
-        [rest_shape, like(2, targets, strip), part, part],
-        soon_keep,
-        soon_recv,
+    rest_send, far, one, two, three = call(
+        lead_kernel,
+        [rest_shape, like(targets, 2 * a_rows), like(2, targets, strip), part, part],
+        lead_keep,
+        lead_recv,
         rest_send,
-        far,
         aliases={2: 0},
         span=3,
     )
-    two, three, one = [swap(soon[q - 1], "sec", q) for q in (2, 3, 1)]
+    cross = swap(far, "mpo", 2)
+    two, three, one = [swap(x, "sec", q) for x, q in ((two, 2), (three, 3), (one, 1))]
     rest_recv = swap(rest_send, "mpo", 1)
     own = call(own_kernel, [like(targets, a_rows)] * 2, rest_keep, rest_recv, cross, span=3)
+    middle = jax.ShapeDtypeStruct(part.shape, jnp.float32)
+    middle = call(middle_kernel, middle, two, three, own[0], span=3)
     near = jax.ShapeDtypeStruct((targets, strip, strip), jnp.float32)
     here, near = call(
-        here_kernel,
-        [like(targets, strip), near],
-        rest_keep,
-        rest_recv,
-        one,
-        two,
-        three,
-        own[0],
-        span=3,
+        here_kernel, [like(targets, strip), near], rest_keep, rest_recv, one, middle, span=3
     )
     own = [swap(array, "sec", q) for array, q in zip(own, (2, 3))]
     here = swap(here, "mpo", 2)

time: 29.7 us -> 32.6 us (1.098)
  waiting for transfers between devices: 11.4 us -> 15.5 us
  starting transfers between devices: 12.9 us -> 11.8 us
    ppermute x10 -> x9, waiting for transfers between devices: 11.4 us -> 15.5 us  [swap(): lax.ppermute(array, axis, [(i, i ^ mask) for i in range(lax.axis_size(axi...]
    ppermute x10 -> x9, starting transfers between devices: 12.9 us -> 11.8 us  [swap(): lax.ppermute(array, axis, [(i, i ^ mask) for i in range(lax.axis_size(axi...]
  transfers between devices with their start and end apart: 10 -> 9, of which waited for: 6 -> 5; matrix products, arithmetic and copies ran while one was open for 0% -> 0% of each run, Pallas kernels for 1% -> 1%
where the time goes in v8:
time: 32.6 us; the launch traced here: 32.5 us
  waiting for transfers between devices  15.5 us (48%)
  starting transfers between devices  11.8 us (36%)
  Pallas kernels  5.19 us (16%)
    ppermute x9, waiting for transfers between devices, swap(): lax.ppermute(array, axis, [(i, i ^ mask) for i in range(lax.axis_size(axi...  15.5 us
    ppermute x9, starting transfers between devices, swap(): lax.ppermute(array, axis, [(i, i ^ mask) for i in range(lax.axis_size(axi...  11.8 us
    pallas_call x1, Pallas kernels, by_targets(): pl.pallas_call(term_kernel, out_shape=[lead_shape] * 2 + [rest_shape] * 2...  4.13 us
    pallas_call x6, Pallas kernels, call(): pl.pallas_call(kernel, out_shape=out_shape, in_specs=[vmem] * len(args),...  1.06 us
  transfers between devices with their start and end apart: 9, of which 5 were waited for; matrix products, arithmetic and copies ran while one was open for 0% of the time, Pallas kernels for 1%

profile of v8, /device:TPU:0, one launch (start us, length us, event | category | flops | bytes accessed | tf_op | source)
XLA Modules:
  0.0 32.5 jit_solution(12823204924868744516)
XLA Ops:
  0.0 4.1 %terms.1 = (bf16[4,576,128]{2,1,0:T(8,128)(2,1)S(1)}, bf16[4,576,128]{2,1,0:T(8,128)(2,1)S(1)}, bf16[4,448,128]{2,1,0:T(8,128)(2,1)S(1)}, bf16[4,448,128]{2,1,0:T(8,128)(2,1)S(1)}, bf16[4,128,128]{2,1,0:T(8,128)(2,1)S(1)}) custom-call(s32[1,3]{1,0:T(1,128)} %cls_hbm.1, s32[1,3]{1,0:T(1,128)} %tid_hbm.1, s32[4,5]{1,0:T(4,128)} %pair_hbm.1, s32[2,4]{1,0:T(2,128)} %bitcast.1, ...), custom_call_target="tpu_custom_call" | custom-call | flops 1610612736 | bytes 4194304 | tf_op jit(solution)/shard_map/terms/pallas_call | solution.py:255
  4.1 0.5 %collective-permute-start = (bf16[4,576,128]{2,1,0:T(8,128)(2,1)S(1)}, bf16[4,576,128]{2,1,0:T(8,128)(2,1)S(1)}, u32[]{:S(2)}, u32[]{:S(2)}) collective-permute-start(bf16[4,576,128]{2,1,0:T(8,128)(2,1)S(1)} %get-tuple-element.22), channel_id=1, source_target_pairs={{0,1},{1,0},{2,3},{3,2},{4,5},{5,4},{6,7},{7,6},{8,9},{9,8},{10,11... | collective-permute-start | bytes 1769480 | tf_op jit(solution)/shard_map/ppermute | solution.py:216
  4.7 1.6 %collective-permute-done.recv_ref = bf16[4,576,128]{2,1,0:T(8,128)(2,1)S(1)} collective-permute-done((bf16[4,576,128]{2,1,0:T(8,128)(2,1)S(1)}, bf16[4,576,128]{2,1,0:T(8,128)(2,1)S(1)}, u32[]{:S(2)}, u32[]{:S(2)}) %collective-permute-start) | collective-permute-done | bytes 589856 | tf_op jit(solution)/shard_map/ppermute | solution.py:216
  6.3 0.1 lead_kernel.1
  6.4 0.4 %collective-permute-start.1 = (bf16[4,448,128]{2,1,0:T(8,128)(2,1)S(1)}, bf16[4,448,128]{2,1,0:T(8,128)(2,1)S(1)}, u32[]{:S(2)}, u32[]{:S(2)}) collective-permute-start(bf16[4,448,128]{2,1,0:T(8,128)(2,1)S(1)} %get-tuple-element.24), channel_id=1, source_target_pairs={{0,1},{1,0},{2,3},{3,2},{4,5},{5,4},{6,7},{7,6},{8,9},{9,8},{10,11... | collective-permute-start | bytes 1376264 | tf_op jit(solution)/shard_map/ppermute | solution.py:216
  6.9 2.6 %collective-permute-start.5 = (bf16[4,192,128]{2,1,0:T(8,128)(2,1)S(1)}, bf16[4,192,128]{2,1,0:T(8,128)(2,1)S(1)}, u32[]{:S(2)}, u32[]{:S(2)}) collective-permute-start(bf16[4,192,128]{2,1,0:T(8,128)(2,1)S(1)} %get-tuple-element.28), channel_id=1, source_target_pairs={{0,2},{1,3},{2,0},{3,1},{4,6},{5,7},{6,4},{7,5},{8,10},{9,11},{10,... | collective-permute-start | bytes 589832 | tf_op jit(solution)/shard_map/ppermute | solution.py:216
  9.5 2.6 %collective-permute-start.3 = (bf16[2,4,32,128]{3,2,1,0:T(8,128)(2,1)S(1)}, bf16[2,4,32,128]{3,2,1,0:T(8,128)(2,1)S(1)}, u32[]{:S(2)}, u32[]{:S(2)}) collective-permute-start(bf16[2,4,32,128]{3,2,1,0:T(8,128)(2,1)S(1)} %get-tuple-element.26), channel_id=1, source_target_pairs={{0,8},{4,12},{8,0},{12,4},{1,9},{5,13},{9,1},{13,5},{2,10},{6,14},... | collective-permute-start | bytes 196616 | tf_op jit(solution)/shard_map/ppermute | solution.py:216
  12.1 1.3 %collective-permute-start.4 = (bf16[2,4,32,128]{3,2,1,0:T(8,128)(2,1)S(1)}, bf16[2,4,32,128]{3,2,1,0:T(8,128)(2,1)S(1)}, u32[]{:S(2)}, u32[]{:S(2)}) collective-permute-start(bf16[2,4,32,128]{3,2,1,0:T(8,128)(2,1)S(1)} %get-tuple-element.27), channel_id=1, source_target_pairs={{0,12},{4,8},{8,4},{12,0},{1,13},{5,9},{9,5},{13,1},{2,14},{6,10},... | collective-permute-start | bytes 196616 | tf_op jit(solution)/shard_map/ppermute | solution.py:216
  13.4 0.2 collective-permute-start.2
  13.7 1.2 %collective-permute-done.5.cross_ref = bf16[4,192,128]{2,1,0:T(8,128)(2,1)S(1)} collective-permute-done((bf16[4,192,128]{2,1,0:T(8,128)(2,1)S(1)}, bf16[4,192,128]{2,1,0:T(8,128)(2,1)S(1)}, u32[]{:S(2)}, u32[]{:S(2)}) %collective-permute-start.5) | collective-permute-done | bytes 196640 | tf_op jit(solution)/shard_map/ppermute | solution.py:216
  14.9 0.0 collective-permute-done.1.recv_ref
  14.9 0.1 own_kernel.1
  15.0 3.9 %collective-permute-start.8 = (bf16[4,96,128]{2,1,0:T(8,128)(2,1)S(1)}, bf16[4,96,128]{2,1,0:T(8,128)(2,1)S(1)}, u32[]{:S(2)}, u32[]{:S(2)}) collective-permute-start(bf16[4,96,128]{2,1,0:T(8,128)(2,1)S(1)} %get-tuple-element.32), channel_id=1, source_target_pairs={{0,12},{4,8},{8,4},{12,0},{1,13},{5,9},{9,5},{13,1},{2,14},{6,10},... | collective-permute-start | bytes 294920 | tf_op jit(solution)/shard_map/ppermute | solution.py:216
  18.9 0.0 collective-permute-start.7
  18.9 0.0 collective-permute-done.3.two_ref
  18.9 0.0 collective-permute-done.4.three_ref
  19.0 7.7 %collective-permute-done.2.one_ref = bf16[2,4,128,128]{3,2,1,0:T(8,128)(2,1)S(1)} collective-permute-done((bf16[2,4,128,128]{3,2,1,0:T(8,128)(2,1)S(1)}, bf16[2,4,128,128]{3,2,1,0:T(8,128)(2,1)S(1)}, u32[]{:S(2)}, u32[]{:S(2)}) %collective-permute-start.2) | collective-permute-done | bytes 262176 | tf_op jit(solution)/shard_map/ppermute | solution.py:216
  26.6 0.1 here_kernel.1
  26.7 0.1 collective-permute-start.6
  26.8 0.0 collective-permute-done.8.three_ref
  26.8 1.2 %collective-permute-done.7.two_ref = bf16[4,96,128]{2,1,0:T(8,128)(2,1)S(1)} collective-permute-done((bf16[4,96,128]{2,1,0:T(8,128)(2,1)S(1)}, bf16[4,96,128]{2,1,0:T(8,128)(2,1)S(1)}, u32[]{:S(2)}, u32[]{:S(2)}) %collective-permute-start.7) | collective-permute-done | bytes 98336 | tf_op jit(solution)/shard_map/ppermute | solution.py:216
  28.1 3.7 %collective-permute-done.6.cross_ref = bf16[4,128,128]{2,1,0:T(8,128)(2,1)S(1)} collective-permute-done((bf16[4,128,128]{2,1,0:T(8,128)(2,1)S(1)}, bf16[4,128,128]{2,1,0:T(8,128)(2,1)S(1)}, u32[]{:S(2)}, u32[]{:S(2)}) %collective-permute-start.6) | collective-permute-done | bytes 131104 | tf_op jit(solution)/shard_map/ppermute | solution.py:216
  31.8 0.7 %final_kernel.1 = bf16[4,128,128]{2,1,0:T(8,128)(2,1)} custom-call(bf16[4,128,128]{2,1,0:T(8,128)(2,1)S(1)} %get-tuple-element.19.mask_ref, f32[4,128,128]{2,1,0:T(8,128)S(1)} %get-tuple-element.30.near_ref, bf16[4,128,128]{2,1,0:T(8,128)(2,1)S(1)} %collective-permute-done.6.cross_ref, f32[4,96,128]{2,1,0:T(8,128)S(1)} %far_sum_kernel.1.sum_ref), custom_call_target="tpu_custom_call" | custom-call | flops 100000000 | tf_op jit(solution)/shard_map/final_kernel/pallas_call | solution.py:235
  (2 shorter events, 0.0 us)
Async XLA Ops:
  4.1 2.1 %collective-permute-start = (bf16[4,576,128]{2,1,0:T(8,128)(2,1)S(1)}, bf16[4,576,128]{2,1,0:T(8,128)(2,1)S(1)}, u32[]{:S(2)}, u32[]{:S(2)}) collective-permute-start(bf16[4,576,128]{2,1,0:T(8,128)(2,1)S(1)} %get-tuple-element.22), channel_id=1, source_target_pairs={{0,1},{1,0},{2,3},{3,2},{4,5},{5,4},{6,7},{7,6},{8,9},{9,8},{10,11... | collective-permute-start | bytes 1769480 | tf_op jit(solution)/shard_map/ppermute | solution.py:216
  6.4 8.5 %collective-permute-start.1 = (bf16[4,448,128]{2,1,0:T(8,128)(2,1)S(1)}, bf16[4,448,128]{2,1,0:T(8,128)(2,1)S(1)}, u32[]{:S(2)}, u32[]{:S(2)}) collective-permute-start(bf16[4,448,128]{2,1,0:T(8,128)(2,1)S(1)} %get-tuple-element.24), channel_id=1, source_target_pairs={{0,1},{1,0},{2,3},{3,2},{4,5},{5,4},{6,7},{7,6},{8,9},{9,8},{10,11... | collective-permute-start | bytes 1376264 | tf_op jit(solution)/shard_map/ppermute | solution.py:216
  6.9 8.1 %collective-permute-start.5 = (bf16[4,192,128]{2,1,0:T(8,128)(2,1)S(1)}, bf16[4,192,128]{2,1,0:T(8,128)(2,1)S(1)}, u32[]{:S(2)}, u32[]{:S(2)}) collective-permute-start(bf16[4,192,128]{2,1,0:T(8,128)(2,1)S(1)} %get-tuple-element.28), channel_id=1, source_target_pairs={{0,2},{1,3},{2,0},{3,1},{4,6},{5,7},{6,4},{7,5},{8,10},{9,11},{10,... | collective-permute-start | bytes 589832 | tf_op jit(solution)/shard_map/ppermute | solution.py:216
  9.5 9.4 %collective-permute-start.3 = (bf16[2,4,32,128]{3,2,1,0:T(8,128)(2,1)S(1)}, bf16[2,4,32,128]{3,2,1,0:T(8,128)(2,1)S(1)}, u32[]{:S(2)}, u32[]{:S(2)}) collective-permute-start(bf16[2,4,32,128]{3,2,1,0:T(8,128)(2,1)S(1)} %get-tuple-element.26), channel_id=1, source_target_pairs={{0,8},{4,12},{8,0},{12,4},{1,9},{5,13},{9,1},{13,5},{2,10},{6,14},... | collective-permute-start | bytes 196616 | tf_op jit(solution)/shard_map/ppermute | solution.py:216
  12.1 6.8 %collective-permute-start.4 = (bf16[2,4,32,128]{3,2,1,0:T(8,128)(2,1)S(1)}, bf16[2,4,32,128]{3,2,1,0:T(8,128)(2,1)S(1)}, u32[]{:S(2)}, u32[]{:S(2)}) collective-permute-start(bf16[2,4,32,128]{3,2,1,0:T(8,128)(2,1)S(1)} %get-tuple-element.27), channel_id=1, source_target_pairs={{0,12},{4,8},{8,4},{12,0},{1,13},{5,9},{9,5},{13,1},{2,14},{6,10},... | collective-permute-start | bytes 196616 | tf_op jit(solution)/shard_map/ppermute | solution.py:216
  13.4 13.2 %collective-permute-start.2 = (bf16[2,4,128,128]{3,2,1,0:T(8,128)(2,1)S(1)}, bf16[2,4,128,128]{3,2,1,0:T(8,128)(2,1)S(1)}, u32[]{:S(2)}, u32[]{:S(2)}) collective-permute-start(bf16[2,4,128,128]{3,2,1,0:T(8,128)(2,1)S(1)} %get-tuple-element.25), channel_id=1, source_target_pairs={{0,4},{4,0},{8,12},{12,8},{1,5},{5,1},{9,13},{13,9},{2,6},{6,2},{1... | collective-permute-start | bytes 786440 | tf_op jit(solution)/shard_map/ppermute | solution.py:216
  15.0 11.8 %collective-permute-start.8 = (bf16[4,96,128]{2,1,0:T(8,128)(2,1)S(1)}, bf16[4,96,128]{2,1,0:T(8,128)(2,1)S(1)}, u32[]{:S(2)}, u32[]{:S(2)}) collective-permute-start(bf16[4,96,128]{2,1,0:T(8,128)(2,1)S(1)} %get-tuple-element.32), channel_id=1, source_target_pairs={{0,12},{4,8},{8,4},{12,0},{1,13},{5,9},{9,5},{13,1},{2,14},{6,10},... | collective-permute-start | bytes 294920 | tf_op jit(solution)/shard_map/ppermute | solution.py:216
  18.9 9.1 %collective-permute-start.7 = (bf16[4,96,128]{2,1,0:T(8,128)(2,1)S(1)}, bf16[4,96,128]{2,1,0:T(8,128)(2,1)S(1)}, u32[]{:S(2)}, u32[]{:S(2)}) collective-permute-start(bf16[4,96,128]{2,1,0:T(8,128)(2,1)S(1)} %get-tuple-element.29.after_ref), channel_id=1, source_target_pairs={{0,8},{4,12},{8,0},{12,4},{1,9},{5,13},{9,1},{13,5},{2,10},{6,14},... | collective-permute-start | bytes 294920 | tf_op jit(solution)/shard_map/ppermute | solution.py:216
  26.7 5.0 %collective-permute-start.6 = (bf16[4,128,128]{2,1,0:T(8,128)(2,1)S(1)}, bf16[4,128,128]{2,1,0:T(8,128)(2,1)S(1)}, u32[]{:S(2)}, u32[]{:S(2)}) collective-permute-start(bf16[4,128,128]{2,1,0:T(8,128)(2,1)S(1)} %get-tuple-element.31), channel_id=1, source_target_pairs={{0,2},{1,3},{2,0},{3,1},{4,6},{5,7},{6,4},{7,5},{8,10},{9,11},{10,... | collective-permute-start | bytes 393224 | tf_op jit(solution)/shard_map/ppermute | solution.py:216

commit v9 on v8

--- a/solution.py
+++ b/solution.py
@@ -11,7 +11,7 @@
 SMALL = pltpu.CompilerParams(vmem_limit_bytes=4 * 1024 * 1024)
 
 
-def term_kernel(
+def send_kernel(
     cls_hbm,
     tid_hbm,
     pair_hbm,
@@ -20,11 +20,10 @@
     wave_hbm,
     left_hbm,
     right_hbm,
-    lead_send,
-    lead_keep,
-    rest_send,
-    rest_keep,
-    mask_ref,
+    lead_ref,
+    rest_ref,
+    half_ref,
+    keep_right,
     cls,
     tid,
     pair,
@@ -37,13 +36,11 @@
     wave_sem,
     left_sems,
     right_sems,
+    keep_sem,
 ):
     width = wave.shape[0]
     terms = left.shape[0]
-    targets, strip, _ = mask_ref.shape
-    a_rows = (rest_send.shape[1] - 2 * strip) // 2
-    b_rows = strip - a_rows
-    soon = (2 * a_rows, 2 * a_rows + strip + 2 * b_rows)
+    strip = width // 4
     unit = width // 8
     sec = lax.axis_index("sec")
     mpo = lax.axis_index("mpo")
@@ -67,7 +64,7 @@
                 left.at[j, pl.ds(q * strip, strip)],
                 left_sems.at[j],
             ).start()
-        for p, r in enumerate(COLUMN_ORDER):
+        for p, r in enumerate(COLUMN_ORDER[:2]):
             src = pl.multiple_of((mpo ^ r) * strip, strip)
             pltpu.make_async_copy(
                 right_hbm.at[0, j, pl.ds(src, strip)],
@@ -76,24 +73,21 @@
             ).start()
         return carry
 
+    def fetch_keep(j, carry):
+        for p, r in enumerate(COLUMN_ORDER[2:]):
+            src = pl.multiple_of((mpo ^ r) * strip, strip)
+            pltpu.make_async_copy(
+                right_hbm.at[0, j, pl.ds(src, strip)],
+                keep_right.at[j, pl.ds(p * strip, strip)],
+                keep_sem,
+            ).start()
+        return carry
+
     lax.fori_loop(0, terms, fetch, 0)
-    def clear(t, carry):
-        for ref in (lead_send, lead_keep, rest_send, rest_keep):
-            ref[t] = jnp.zeros(ref.shape[1:], ref.dtype)
-        return carry
-
-    lax.fori_loop(0, targets, clear, 0)
+    lax.fori_loop(0, terms, fetch_keep, 0)
+    clear(lead_ref, rest_ref)
     for copy in scalars:
         copy.wait()
-    lane = mpo * strip + lax.broadcasted_iota(jnp.int32, (strip, strip), 1)
-    line = sec * strip + lax.broadcasted_iota(jnp.int32, (strip, strip), 0)
-
-    def target_mask(t, carry):
-        inside = (line < dims[0, t] * unit) & (lane < dims[1, t] * unit)
-        mask_ref[t] = jnp.where(inside, 1.0, 0.0).astype(jnp.bfloat16)
-        return carry
-
-    lax.fori_loop(0, targets, target_mask, 0)
     wave_copy.wait()
     row_limit = dims[0, sec] * unit
     col_limit = dims[1, sec] * unit
@@ -108,40 +102,99 @@
         return carry
 
     lax.fori_loop(0, width // 64, mask, 0)
-
-    def term(j):
+    for j in range(terms):
         pltpu.make_async_copy(left_hbm.at[0, j], left.at[j], left_sems.at[j]).wait()
         half = jnp.dot(left[j], wave[...], preferred_element_type=jnp.float32)
         half = half.astype(jnp.bfloat16)
-        pltpu.make_async_copy(right_hbm.at[0, j], right.at[j], right_sems.at[j]).wait()
-        t = pair[sec, cls[0, j]]
-        weight = coef[tid[0, j]]
-        for side in range(2):
-            contrib = lax.dot_general(
-                half,
-                right[j, 2 * side * strip : 2 * (side + 1) * strip, :],
-                (((1,), (1,)), ((), ())),
-                preferred_element_type=jnp.float32,
-            )
-            lead, rest = (lead_send, rest_send) if side == 0 else (lead_keep, rest_keep)
-            for q in range(4):
-                for n in range(2):
-                    value = weight * contrib[
-                        q * strip : (q + 1) * strip, n * strip : (n + 1) * strip
-                    ]
-                    if q == 0:
-                        put(rest, t, n * strip, value)
-                    elif q == 1:
-                        put(lead, t, soon[n], value)
-                    else:
-                        if n == 0:
-                            put(lead, t, (q - 2) * a_rows, value[:a_rows])
-                        else:
-                            put(rest, t, 2 * strip + (q - 2) * a_rows, value[:a_rows])
-                        put(lead, t, soon[n] + strip + (q - 2) * b_rows, value[a_rows:])
-
+        half_ref[j] = half
+        pltpu.make_async_copy(
+            right_hbm.at[0, j, pl.ds(0, 2 * strip)], right.at[j], right_sems.at[j]
+        ).wait()
+        spread(lead_ref, rest_ref, half, right[j], pair[sec, cls[0, j]], coef[tid[0, j]])
+    pltpu.make_async_copy(
+        right_hbm.at[0, pl.ds(0, terms), pl.ds(0, 2 * strip)], keep_right, keep_sem
+    ).wait()
+
+
+def keep_kernel(
+    cls_hbm,
+    tid_hbm,
+    pair_hbm,
+    dims_hbm,
+    coef_hbm,
+    half_ref,
+    right_ref,
+    lead_ref,
+    rest_ref,
+    mask_ref,
+    cls,
+    tid,
+    pair,
+    dims,
+    coef,
+    scalar_sems,
+):
+    terms, width, _ = half_ref.shape
+    targets, strip, _ = mask_ref.shape
+    unit = width // 8
+    sec = lax.axis_index("sec")
+    mpo = lax.axis_index("mpo")
+    scalars = [
+        pltpu.make_async_copy(src, dst, scalar_sems.at[n])
+        for n, (src, dst) in enumerate(
+            ((cls_hbm, cls), (tid_hbm, tid), (pair_hbm, pair), (dims_hbm, dims), (coef_hbm, coef))
+        )
+    ]
+    for copy in scalars:
+        copy.start()
+    clear(lead_ref, rest_ref)
+    for copy in scalars:
+        copy.wait()
     for j in range(terms):
-        term(j)
+        spread(
+            lead_ref, rest_ref, half_ref[j], right_ref[j], pair[sec, cls[0, j]], coef[tid[0, j]]
+        )
+    lane = mpo * strip + lax.broadcasted_iota(jnp.int32, (strip, strip), 1)
+    line = sec * strip + lax.broadcasted_iota(jnp.int32, (strip, strip), 0)
+
+    def target_mask(t, carry):
+        inside = (line < dims[0, t] * unit) & (lane < dims[1, t] * unit)
+        mask_ref[t] = jnp.where(inside, 1.0, 0.0).astype(jnp.bfloat16)
+        return carry
+
+    lax.fori_loop(0, targets, target_mask, 0)
+
+
+def clear(*refs):
+    def one(t, carry):
+        for ref in refs:
+            ref[t] = jnp.zeros(ref.shape[1:], ref.dtype)
+        return carry
+
+    lax.fori_loop(0, refs[0].shape[0], one, 0)
+
+
+def spread(lead, rest, half, right, t, weight):
+    contrib = lax.dot_general(
+        half, right, (((1,), (1,)), ((), ())), preferred_element_type=jnp.float32
+    )
+    strip = contrib.shape[1] // 2
+    a_rows = (rest.shape[1] - 2 * strip) // 2
+    b_rows = strip - a_rows
+    soon = (2 * a_rows, 2 * a_rows + strip + 2 * b_rows)
+    for q in range(4):
+        for n in range(2):
+            value = weight * contrib[q * strip : (q + 1) * strip, n * strip : (n + 1) * strip]
+            if q == 0:
+                put(rest, t, n * strip, value)
+            elif q == 1:
+                put(lead, t, soon[n], value)
+            else:
+                if n == 0:
+                    put(lead, t, (q - 2) * a_rows, value[:a_rows])
+                else:
+                    put(rest, t, 2 * strip + (q - 2) * a_rows, value[:a_rows])
+                put(lead, t, soon[n] + strip + (q - 2) * b_rows, value[a_rows:])
 
 
 def put(ref, t, row, value):
@@ -149,11 +202,14 @@
     ref[t, at, :] = (ref[t, at, :].astype(jnp.float32) + value).astype(jnp.bfloat16)
 
 
-def lead_kernel(keep_ref, recv_ref, rest_in, rest_out, far_ref, *own_refs):
+def lead_kernel(keep_ref, recv_ref, rest_in, rest_out, far_ref, one_far, one_near, *own_refs):
     del rest_in, rest_out
     row = far_ref.shape[1]
     far_ref[...] = add(keep_ref[:, :row, :], recv_ref[:, :row, :])
-    for n in range(2):
+    for n, one_ref in enumerate((one_far, one_near)):
+        at = slice(row, row + one_ref.shape[1])
+        one_ref[...] = add(keep_ref[:, at, :], recv_ref[:, at, :])
+        row += one_ref.shape[1]
         for own_ref in own_refs:
             at = slice(row, row + own_ref.shape[2])
             own_ref[n] = add(keep_ref[:, at, :], recv_ref[:, at, :])
@@ -170,20 +226,18 @@
         )
 
 
-def middle_kernel(two_ref, three_ref, after_ref, sum_ref):
+def here_kernel(keep_ref, recv_ref, one_ref, two_ref, three_ref, after_ref, far_ref, near_ref):
     del after_ref
-    sum_ref[...] = total(two_ref[...], three_ref[...])
-
-
-def here_kernel(keep_ref, recv_ref, one_ref, middle_ref, far_ref, near_ref):
     strip = far_ref.shape[1]
-    a_rows = strip - middle_ref.shape[2]
+    a_rows = strip - two_ref.shape[2]
     for n, out_ref in enumerate((far_ref, near_ref)):
         for first, last in ((0, a_rows), (a_rows, strip)):
             at = slice(n * strip + first, n * strip + last)
-            parts = [keep_ref[:, at, :], recv_ref[:, at, :], one_ref[n, :, first:last, :]]
+            parts = [keep_ref[:, at, :], recv_ref[:, at, :]]
+            if n == 0:
+                parts += [one_ref[:, first:last, :]]
             if first:
-                parts += [middle_ref[n]]
+                parts += [two_ref[n], three_ref[n]]
             out_ref[:, first:last, :] = total(*parts).astype(out_ref.dtype)
 
 
@@ -191,10 +245,10 @@
     sum_ref[...] = total(two_ref[...], three_ref[...])
 
 
-def final_kernel(mask_ref, near_ref, cross_ref, sum_ref, out_ref):
+def final_kernel(mask_ref, near_ref, one_ref, cross_ref, sum_ref, out_ref):
     a_rows, strip = sum_ref.shape[1], out_ref.shape[1]
     for first, last in ((0, a_rows), (a_rows, strip)):
-        parts = [near_ref[:, first:last, :], cross_ref[:, first:last, :]]
+        parts = [ref[:, first:last, :] for ref in (near_ref, one_ref, cross_ref)]
         if not first:
             parts += [sum_ref[...]]
         inside = mask_ref[:, first:last, :].astype(jnp.float32) > 0.0
@@ -252,32 +306,49 @@
     ]
     lead_shape = like(targets, 2 * a_rows + 2 * (strip + 2 * b_rows))
     rest_shape = like(targets, 2 * strip + 2 * a_rows)
-    lead_send, lead_keep, rest_send, rest_keep, mask = pl.pallas_call(
-        term_kernel,
-        out_shape=[lead_shape] * 2 + [rest_shape] * 2 + [like(targets, strip)],
+    scalar_room = [pltpu.SMEM(scalar.shape, scalar.dtype) for scalar in scalars]
+    limit = pltpu.CompilerParams(vmem_limit_bytes=16 * 1024 * 1024)
+    half_shape = jax.ShapeDtypeStruct((terms, width, width), jnp.bfloat16)
+    right_shape = jax.ShapeDtypeStruct((terms, 2 * strip, width), jnp.bfloat16)
+    lead_send, rest_send, half, keep_right = pl.pallas_call(
+        send_kernel,
+        out_shape=[lead_shape, rest_shape, half_shape, right_shape],
         in_specs=[hbm] * 8,
-        out_specs=[vmem] * 5,
-        scratch_shapes=[pltpu.SMEM(scalar.shape, scalar.dtype) for scalar in scalars]
+        out_specs=[vmem] * 4,
+        scratch_shapes=scalar_room
         + [
             pltpu.VMEM((width, width), jnp.bfloat16),
             pltpu.VMEM((terms, width, width), jnp.bfloat16),
-            pltpu.VMEM((terms, width, width), jnp.bfloat16),
+            pltpu.VMEM((terms, 2 * strip, width), jnp.bfloat16),
             pltpu.SemaphoreType.DMA((len(scalars),)),
             pltpu.SemaphoreType.DMA,
             pltpu.SemaphoreType.DMA((terms,)),
             pltpu.SemaphoreType.DMA((terms,)),
+            pltpu.SemaphoreType.DMA,
         ],
-        compiler_params=pltpu.CompilerParams(vmem_limit_bytes=20 * 1024 * 1024),
+        compiler_params=limit,
         cost_estimate=pl.CostEstimate(
-            flops=4 * terms * width**3, bytes_accessed=4 * 1024 * 1024, transcendentals=0
+            flops=3 * terms * width**3, bytes_accessed=4 * 1024 * 1024, transcendentals=0
         ),
-        name="terms",
+        name="send_kernel",
     )(*operands)
+    lead_keep, rest_keep, mask = pl.pallas_call(
+        keep_kernel,
+        out_shape=[lead_shape, rest_shape, like(targets, strip)],
+        in_specs=[hbm] * len(scalars) + [vmem] * 2,
+        out_specs=[vmem] * 3,
+        scratch_shapes=scalar_room + [pltpu.SemaphoreType.DMA((len(scalars),))],
+        compiler_params=limit,
+        cost_estimate=pl.CostEstimate(
+            flops=3 * terms * width**3, bytes_accessed=0, transcendentals=0
+        ),
+        name="keep_kernel",
+    )(*operands[: len(scalars)], half, keep_right)
     lead_recv = swap(lead_send, "mpo", 1)
     part = like(2, targets, b_rows)
-    rest_send, far, one, two, three = call(
+    rest_send, far, one, one_near, two, three = call(
         lead_kernel,
-        [rest_shape, like(targets, 2 * a_rows), like(2, targets, strip), part, part],
+        [rest_shape, like(targets, 2 * a_rows)] + [like(targets, strip)] * 2 + [part] * 2,
         lead_keep,
         lead_recv,
         rest_send,
@@ -285,20 +356,27 @@
         span=3,
     )
     cross = swap(far, "mpo", 2)
-    two, three, one = [swap(x, "sec", q) for x, q in ((two, 2), (three, 3), (one, 1))]
+    one, two, three = [swap(x, "sec", q) for x, q in ((one, 1), (two, 2), (three, 3))]
+    one_near = swap(one_near, "sec", 1)
     rest_recv = swap(rest_send, "mpo", 1)
     own = call(own_kernel, [like(targets, a_rows)] * 2, rest_keep, rest_recv, cross, span=3)
-    middle = jax.ShapeDtypeStruct(part.shape, jnp.float32)
-    middle = call(middle_kernel, middle, two, three, own[0], span=3)
     near = jax.ShapeDtypeStruct((targets, strip, strip), jnp.float32)
     here, near = call(
-        here_kernel, [like(targets, strip), near], rest_keep, rest_recv, one, middle, span=3
+        here_kernel,
+        [like(targets, strip), near],
+        rest_keep,
+        rest_recv,
+        one,
+        two,
+        three,
+        own[0],
+        span=3,
     )
     own = [swap(array, "sec", q) for array, q in zip(own, (2, 3))]
     here = swap(here, "mpo", 2)
     far_sum = jax.ShapeDtypeStruct((targets, a_rows, strip), jnp.float32)
     far_sum = call(far_sum_kernel, far_sum, *own, span=3)
-    return call(final_kernel, like(targets, strip), mask, near, here, far_sum)
+    return call(final_kernel, like(targets, strip), mask, near, one_near, here, far_sum)
 
 
 def by_classes(

time: 32.6 us -> 29.4 us (0.902)
  waiting for transfers between devices: 15.5 us -> 9.56 us
  Pallas kernels: 5.19 us -> 6.73 us
  starting transfers between devices: 11.8 us -> 12.9 us
    ppermute x9 -> x10, waiting for transfers between devices: 15.5 us -> 9.56 us  [swap(): lax.ppermute(array, axis, [(i, i ^ mask) for i in range(lax.axis_size(axi...]
    pallas_call x1 -> x2, Pallas kernels: 4.13 us -> 5.67 us  [the longest x1 4.17 us: by_targets(): pl.pallas_call(send_kernel, out_shape=[lead_shape, rest_shape, half_shape...]
    ppermute x9 -> x10, starting transfers between devices: 11.8 us -> 12.9 us  [swap(): lax.ppermute(array, axis, [(i, i ^ mask) for i in range(lax.axis_size(axi...]
    pallas_call x6 -> x5, Pallas kernels: 1.06 us -> 1.05 us  [call(): pl.pallas_call(kernel, out_shape=out_shape, in_specs=[vmem] * len(args),...]
  transfers between devices with their start and end apart: 9 -> 10, of which waited for: 5 -> 5; matrix products, arithmetic and copies ran while one was open for 0% -> 0% of each run, Pallas kernels for 1% -> 6%
where the time goes in v9:
time: 29.4 us; the launch traced here: 29.2 us
  starting transfers between devices  12.9 us (44%)
  waiting for transfers between devices  9.56 us (33%)
  Pallas kernels  6.73 us (23%)
    ppermute x10, starting transfers between devices, swap(): lax.ppermute(array, axis, [(i, i ^ mask) for i in range(lax.axis_size(axi...  12.9 us
    ppermute x10, waiting for transfers between devices, swap(): lax.ppermute(array, axis, [(i, i ^ mask) for i in range(lax.axis_size(axi...  9.56 us
    pallas_call x1, Pallas kernels, by_targets(): pl.pallas_call(send_kernel, out_shape=[lead_shape, rest_shape, half_shape...  4.17 us
    pallas_call x1, Pallas kernels, by_targets(): pl.pallas_call(keep_kernel, out_shape=[lead_shape, rest_shape, like(targe...  1.5 us
    pallas_call x5, Pallas kernels, call(): pl.pallas_call(kernel, out_shape=out_shape, in_specs=[vmem] * len(args),...  1.05 us
  transfers between devices with their start and end apart: 10, of which 5 were waited for; matrix products, arithmetic and copies ran while one was open for 0% of the time, Pallas kernels for 6%

profile of v9, /device:TPU:0, one launch (start us, length us, event | category | flops | bytes accessed | tf_op | source)
XLA Modules:
  0.0 29.2 jit_solution(5899579466933867082)
XLA Ops:
  0.0 4.2 %send_kernel.1 = (bf16[4,576,128]{2,1,0:T(8,128)(2,1)S(1)}, bf16[4,448,128]{2,1,0:T(8,128)(2,1)S(1)}, bf16[3,512,512]{2,1,0:T(8,128)(2,1)S(1)}, bf16[3,256,512]{2,1,0:T(8,128)(2,1)S(1)}) custom-call(s32[1,3]{1,0:T(1,128)} %cls_hbm.3, s32[1,3]{1,0:T(1,128)} %tid_hbm.3, s32[4,5]{1,0:T(4,128)} %pair_hbm.3, s32[2,4]{1,0:T(2,128)} %bitcast.1, f32[50]{0:T(128)} %coef_hbm.3, ...), custom_call_target="tpu_custom_call" | custom-call | flops 1207959552 | bytes 4194304 | tf_op jit(solution)/shard_map/send_kernel/pallas_call | solution.py:313
  4.2 0.5 %collective-permute-start = (bf16[4,576,128]{2,1,0:T(8,128)(2,1)S(1)}, bf16[4,576,128]{2,1,0:T(8,128)(2,1)S(1)}, u32[]{:S(2)}, u32[]{:S(2)}) collective-permute-start(bf16[4,576,128]{2,1,0:T(8,128)(2,1)S(1)} %get-tuple-element.27), channel_id=1, source_target_pairs={{0,1},{1,0},{2,3},{3,2},{4,5},{5,4},{6,7},{7,6},{8,9},{9,8},{10,11... | collective-permute-start | bytes 1769480 | tf_op jit(solution)/shard_map/ppermute | solution.py:270
  4.7 1.5 %keep_kernel.1 = (bf16[4,576,128]{2,1,0:T(8,128)(2,1)S(1)}, bf16[4,448,128]{2,1,0:T(8,128)(2,1)S(1)}, bf16[4,128,128]{2,1,0:T(8,128)(2,1)S(1)}) custom-call(s32[1,3]{1,0:T(1,128)} %cls_hbm.3, s32[1,3]{1,0:T(1,128)} %tid_hbm.3, s32[4,5]{1,0:T(4,128)} %pair_hbm.3, s32[2,4]{1,0:T(2,128)} %bitcast.2, f32[50]{0:T(128)} %coef_hbm.3, ...), custom_call_target="tpu_custom_call" | custom-call | flops 1207959552 | tf_op jit(solution)/shard_map/keep_kernel/pallas_call | solution.py:335
  6.2 0.1 collective-permute-done.recv_ref
  6.3 0.1 lead_kernel.1
  6.5 0.4 %collective-permute-start.1 = (bf16[4,448,128]{2,1,0:T(8,128)(2,1)S(1)}, bf16[4,448,128]{2,1,0:T(8,128)(2,1)S(1)}, u32[]{:S(2)}, u32[]{:S(2)}) collective-permute-start(bf16[4,448,128]{2,1,0:T(8,128)(2,1)S(1)} %get-tuple-element.29), channel_id=1, source_target_pairs={{0,1},{1,0},{2,3},{3,2},{4,5},{5,4},{6,7},{7,6},{8,9},{9,8},{10,11... | collective-permute-start | bytes 1376264 | tf_op jit(solution)/shard_map/ppermute | solution.py:270
  6.9 2.6 %collective-permute-start.5 = (bf16[4,192,128]{2,1,0:T(8,128)(2,1)S(1)}, bf16[4,192,128]{2,1,0:T(8,128)(2,1)S(1)}, u32[]{:S(2)}, u32[]{:S(2)}) collective-permute-start(bf16[4,192,128]{2,1,0:T(8,128)(2,1)S(1)} %get-tuple-element.33), channel_id=1, source_target_pairs={{0,2},{1,3},{2,0},{3,1},{4,6},{5,7},{6,4},{7,5},{8,10},{9,11},{10,... | collective-permute-start | bytes 589832 | tf_op jit(solution)/shard_map/ppermute | solution.py:270
  9.5 2.6 %collective-permute-start.3 = (bf16[2,4,32,128]{3,2,1,0:T(8,128)(2,1)S(1)}, bf16[2,4,32,128]{3,2,1,0:T(8,128)(2,1)S(1)}, u32[]{:S(2)}, u32[]{:S(2)}) collective-permute-start(bf16[2,4,32,128]{3,2,1,0:T(8,128)(2,1)S(1)} %get-tuple-element.31), channel_id=1, source_target_pairs={{0,8},{4,12},{8,0},{12,4},{1,9},{5,13},{9,1},{13,5},{2,10},{6,14},... | collective-permute-start | bytes 196616 | tf_op jit(solution)/shard_map/ppermute | solution.py:270
  12.1 1.3 %collective-permute-start.4 = (bf16[2,4,32,128]{3,2,1,0:T(8,128)(2,1)S(1)}, bf16[2,4,32,128]{3,2,1,0:T(8,128)(2,1)S(1)}, u32[]{:S(2)}, u32[]{:S(2)}) collective-permute-start(bf16[2,4,32,128]{3,2,1,0:T(8,128)(2,1)S(1)} %get-tuple-element.32), channel_id=1, source_target_pairs={{0,12},{4,8},{8,4},{12,0},{1,13},{5,9},{9,5},{13,1},{2,14},{6,10},... | collective-permute-start | bytes 196616 | tf_op jit(solution)/shard_map/ppermute | solution.py:270
  13.5 0.2 collective-permute-start.2
  13.7 1.3 %collective-permute-done.5.cross_ref = bf16[4,192,128]{2,1,0:T(8,128)(2,1)S(1)} collective-permute-done((bf16[4,192,128]{2,1,0:T(8,128)(2,1)S(1)}, bf16[4,192,128]{2,1,0:T(8,128)(2,1)S(1)}, u32[]{:S(2)}, u32[]{:S(2)}) %collective-permute-start.5) | collective-permute-done | bytes 196640 | tf_op jit(solution)/shard_map/ppermute | solution.py:270
  15.0 1.8 %collective-permute-start.6 = (bf16[4,128,128]{2,1,0:T(8,128)(2,1)S(1)}, bf16[4,128,128]{2,1,0:T(8,128)(2,1)S(1)}, u32[]{:S(2)}, u32[]{:S(2)}) collective-permute-start(bf16[4,128,128]{2,1,0:T(8,128)(2,1)S(1)} %get-tuple-element.36), channel_id=1, source_target_pairs={{0,4},{4,0},{8,12},{12,8},{1,5},{5,1},{9,13},{13,9},{2,6},{6,2},{1... | collective-permute-start | bytes 393224 | tf_op jit(solution)/shard_map/ppermute | solution.py:270
  16.8 0.0 collective-permute-done.1.recv_ref
  16.8 0.1 own_kernel.1
  16.9 2.5 %collective-permute-start.9 = (bf16[4,96,128]{2,1,0:T(8,128)(2,1)S(1)}, bf16[4,96,128]{2,1,0:T(8,128)(2,1)S(1)}, u32[]{:S(2)}, u32[]{:S(2)}) collective-permute-start(bf16[4,96,128]{2,1,0:T(8,128)(2,1)S(1)} %get-tuple-element.38), channel_id=1, source_target_pairs={{0,12},{4,8},{8,4},{12,0},{1,13},{5,9},{9,5},{13,1},{2,14},{6,10},... | collective-permute-start | bytes 294920 | tf_op jit(solution)/shard_map/ppermute | solution.py:270
  19.4 0.0 collective-permute-done.3.two_ref
  19.4 0.2 collective-permute-start.8
  19.6 0.0 collective-permute-done.4.three_ref
  19.6 1.2 %collective-permute-done.2.one_ref = bf16[4,128,128]{2,1,0:T(8,128)(2,1)S(1)} collective-permute-done((bf16[4,128,128]{2,1,0:T(8,128)(2,1)S(1)}, bf16[4,128,128]{2,1,0:T(8,128)(2,1)S(1)}, u32[]{:S(2)}, u32[]{:S(2)}) %collective-permute-start.2) | collective-permute-done | bytes 131104 | tf_op jit(solution)/shard_map/ppermute | solution.py:270
  20.8 0.1 here_kernel.1
  20.9 0.6 %collective-permute-start.7 = (bf16[4,128,128]{2,1,0:T(8,128)(2,1)S(1)}, bf16[4,128,128]{2,1,0:T(8,128)(2,1)S(1)}, u32[]{:S(2)}, u32[]{:S(2)}) collective-permute-start(bf16[4,128,128]{2,1,0:T(8,128)(2,1)S(1)} %get-tuple-element.37), channel_id=1, source_target_pairs={{0,2},{1,3},{2,0},{3,1},{4,6},{5,7},{6,4},{7,5},{8,10},{9,11},{10,... | collective-permute-start | bytes 393224 | tf_op jit(solution)/shard_map/ppermute | solution.py:270
  21.4 5.2 %collective-permute-done.9.three_ref = bf16[4,96,128]{2,1,0:T(8,128)(2,1)S(1)} collective-permute-done((bf16[4,96,128]{2,1,0:T(8,128)(2,1)S(1)}, bf16[4,96,128]{2,1,0:T(8,128)(2,1)S(1)}, u32[]{:S(2)}, u32[]{:S(2)}) %collective-permute-start.9) | collective-permute-done | bytes 98336 | tf_op jit(solution)/shard_map/ppermute | solution.py:270
  26.6 1.8 %collective-permute-done.8.two_ref = bf16[4,96,128]{2,1,0:T(8,128)(2,1)S(1)} collective-permute-done((bf16[4,96,128]{2,1,0:T(8,128)(2,1)S(1)}, bf16[4,96,128]{2,1,0:T(8,128)(2,1)S(1)}, u32[]{:S(2)}, u32[]{:S(2)}) %collective-permute-start.8) | collective-permute-done | bytes 98336 | tf_op jit(solution)/shard_map/ppermute | solution.py:270
  28.5 0.0 collective-permute-done.6.one_ref
  28.5 0.0 collective-permute-done.7.cross_ref
  28.5 0.7 %final_kernel.1 = bf16[4,128,128]{2,1,0:T(8,128)(2,1)} custom-call(bf16[4,128,128]{2,1,0:T(8,128)(2,1)S(1)} %get-tuple-element.24.mask_ref, f32[4,128,128]{2,1,0:T(8,128)S(1)} %get-tuple-element.35.near_ref, bf16[4,128,128]{2,1,0:T(8,128)(2,1)S(1)} %collective-permute-done.6.one_ref, bf16[4,128,128]{2,1,0:T(8,128)(2,1)S(1)} %collective-permute-done.7.cross_ref, ...), custom_call_target="tpu_custom_call" | custom-call | flops 100000000 | tf_op jit(solution)/shard_map/final_kernel/pallas_call | solution.py:289
  (1 shorter events, 0.0 us)
Async XLA Ops:
  4.2 2.2 %collective-permute-start = (bf16[4,576,128]{2,1,0:T(8,128)(2,1)S(1)}, bf16[4,576,128]{2,1,0:T(8,128)(2,1)S(1)}, u32[]{:S(2)}, u32[]{:S(2)}) collective-permute-start(bf16[4,576,128]{2,1,0:T(8,128)(2,1)S(1)} %get-tuple-element.27), channel_id=1, source_target_pairs={{0,1},{1,0},{2,3},{3,2},{4,5},{5,4},{6,7},{7,6},{8,9},{9,8},{10,11... | collective-permute-start | bytes 1769480 | tf_op jit(solution)/shard_map/ppermute | solution.py:270
  6.5 10.3 %collective-permute-start.1 = (bf16[4,448,128]{2,1,0:T(8,128)(2,1)S(1)}, bf16[4,448,128]{2,1,0:T(8,128)(2,1)S(1)}, u32[]{:S(2)}, u32[]{:S(2)}) collective-permute-start(bf16[4,448,128]{2,1,0:T(8,128)(2,1)S(1)} %get-tuple-element.29), channel_id=1, source_target_pairs={{0,1},{1,0},{2,3},{3,2},{4,5},{5,4},{6,7},{7,6},{8,9},{9,8},{10,11... | collective-permute-start | bytes 1376264 | tf_op jit(solution)/shard_map/ppermute | solution.py:270
  6.9 8.1 %collective-permute-start.5 = (bf16[4,192,128]{2,1,0:T(8,128)(2,1)S(1)}, bf16[4,192,128]{2,1,0:T(8,128)(2,1)S(1)}, u32[]{:S(2)}, u32[]{:S(2)}) collective-permute-start(bf16[4,192,128]{2,1,0:T(8,128)(2,1)S(1)} %get-tuple-element.33), channel_id=1, source_target_pairs={{0,2},{1,3},{2,0},{3,1},{4,6},{5,7},{6,4},{7,5},{8,10},{9,11},{10,... | collective-permute-start | bytes 589832 | tf_op jit(solution)/shard_map/ppermute | solution.py:270
  9.5 9.9 %collective-permute-start.3 = (bf16[2,4,32,128]{3,2,1,0:T(8,128)(2,1)S(1)}, bf16[2,4,32,128]{3,2,1,0:T(8,128)(2,1)S(1)}, u32[]{:S(2)}, u32[]{:S(2)}) collective-permute-start(bf16[2,4,32,128]{3,2,1,0:T(8,128)(2,1)S(1)} %get-tuple-element.31), channel_id=1, source_target_pairs={{0,8},{4,12},{8,0},{12,4},{1,9},{5,13},{9,1},{13,5},{2,10},{6,14},... | collective-permute-start | bytes 196616 | tf_op jit(solution)/shard_map/ppermute | solution.py:270
  12.1 7.5 %collective-permute-start.4 = (bf16[2,4,32,128]{3,2,1,0:T(8,128)(2,1)S(1)}, bf16[2,4,32,128]{3,2,1,0:T(8,128)(2,1)S(1)}, u32[]{:S(2)}, u32[]{:S(2)}) collective-permute-start(bf16[2,4,32,128]{3,2,1,0:T(8,128)(2,1)S(1)} %get-tuple-element.32), channel_id=1, source_target_pairs={{0,12},{4,8},{8,4},{12,0},{1,13},{5,9},{9,5},{13,1},{2,14},{6,10},... | collective-permute-start | bytes 196616 | tf_op jit(solution)/shard_map/ppermute | solution.py:270
  13.5 7.3 %collective-permute-start.2 = (bf16[4,128,128]{2,1,0:T(8,128)(2,1)S(1)}, bf16[4,128,128]{2,1,0:T(8,128)(2,1)S(1)}, u32[]{:S(2)}, u32[]{:S(2)}) collective-permute-start(bf16[4,128,128]{2,1,0:T(8,128)(2,1)S(1)} %get-tuple-element.30), channel_id=1, source_target_pairs={{0,4},{4,0},{8,12},{12,8},{1,5},{5,1},{9,13},{13,9},{2,6},{6,2},{1... | collective-permute-start | bytes 393224 | tf_op jit(solution)/shard_map/ppermute | solution.py:270
  15.0 13.5 %collective-permute-start.6 = (bf16[4,128,128]{2,1,0:T(8,128)(2,1)S(1)}, bf16[4,128,128]{2,1,0:T(8,128)(2,1)S(1)}, u32[]{:S(2)}, u32[]{:S(2)}) collective-permute-start(bf16[4,128,128]{2,1,0:T(8,128)(2,1)S(1)} %get-tuple-element.36), channel_id=1, source_target_pairs={{0,4},{4,0},{8,12},{12,8},{1,5},{5,1},{9,13},{13,9},{2,6},{6,2},{1... | collective-permute-start | bytes 393224 | tf_op jit(solution)/shard_map/ppermute | solution.py:270
  16.9 9.7 %collective-permute-start.9 = (bf16[4,96,128]{2,1,0:T(8,128)(2,1)S(1)}, bf16[4,96,128]{2,1,0:T(8,128)(2,1)S(1)}, u32[]{:S(2)}, u32[]{:S(2)}) collective-permute-start(bf16[4,96,128]{2,1,0:T(8,128)(2,1)S(1)} %get-tuple-element.38), channel_id=1, source_target_pairs={{0,12},{4,8},{8,4},{12,0},{1,13},{5,9},{9,5},{13,1},{2,14},{6,10},... | collective-permute-start | bytes 294920 | tf_op jit(solution)/shard_map/ppermute | solution.py:270
  19.4 9.0 %collective-permute-start.8 = (bf16[4,96,128]{2,1,0:T(8,128)(2,1)S(1)}, bf16[4,96,128]{2,1,0:T(8,128)(2,1)S(1)}, u32[]{:S(2)}, u32[]{:S(2)}) collective-permute-start(bf16[4,96,128]{2,1,0:T(8,128)(2,1)S(1)} %get-tuple-element.34.after_ref), channel_id=1, source_target_pairs={{0,8},{4,12},{8,0},{12,4},{1,9},{5,13},{9,1},{13,5},{2,10},{6,14},... | collective-permute-start | bytes 294920 | tf_op jit(solution)/shard_map/ppermute | solution.py:270
  20.9 7.6 %collective-permute-start.7 = (bf16[4,128,128]{2,1,0:T(8,128)(2,1)S(1)}, bf16[4,128,128]{2,1,0:T(8,128)(2,1)S(1)}, u32[]{:S(2)}, u32[]{:S(2)}) collective-permute-start(bf16[4,128,128]{2,1,0:T(8,128)(2,1)S(1)} %get-tuple-element.37), channel_id=1, source_target_pairs={{0,2},{1,3},{2,0},{3,1},{4,6},{5,7},{6,4},{7,5},{8,10},{9,11},{10,... | collective-permute-start | bytes 393224 | tf_op jit(solution)/shard_map/ppermute | solution.py:270

commit v10 on v9

--- a/solution.py
+++ b/solution.py
@@ -23,7 +23,6 @@
     lead_ref,
     rest_ref,
     half_ref,
-    keep_right,
     cls,
     tid,
     pair,
@@ -36,7 +35,6 @@
     wave_sem,
     left_sems,
     right_sems,
-    keep_sem,
 ):
     width = wave.shape[0]
     terms = left.shape[0]
@@ -70,21 +68,10 @@
                 right_hbm.at[0, j, pl.ds(src, strip)],
                 right.at[j, pl.ds(p * strip, strip)],
                 right_sems.at[j],
-            ).start()
+            ).start(priority=1)
         return carry
 
-    def fetch_keep(j, carry):
-        for p, r in enumerate(COLUMN_ORDER[2:]):
-            src = pl.multiple_of((mpo ^ r) * strip, strip)
-            pltpu.make_async_copy(
-                right_hbm.at[0, j, pl.ds(src, strip)],
-                keep_right.at[j, pl.ds(p * strip, strip)],
-                keep_sem,
-            ).start()
-        return carry
-
     lax.fori_loop(0, terms, fetch, 0)
-    lax.fori_loop(0, terms, fetch_keep, 0)
     clear(lead_ref, rest_ref)
     for copy in scalars:
         copy.wait()
@@ -111,9 +98,6 @@
             right_hbm.at[0, j, pl.ds(0, 2 * strip)], right.at[j], right_sems.at[j]
         ).wait()
         spread(lead_ref, rest_ref, half, right[j], pair[sec, cls[0, j]], coef[tid[0, j]])
-    pltpu.make_async_copy(
-        right_hbm.at[0, pl.ds(0, terms), pl.ds(0, 2 * strip)], keep_right, keep_sem
-    ).wait()
 
 
 def keep_kernel(
@@ -122,8 +106,8 @@
     pair_hbm,
     dims_hbm,
     coef_hbm,
+    right_hbm,
     half_ref,
-    right_ref,
     lead_ref,
     rest_ref,
     mask_ref,
@@ -132,7 +116,9 @@
     pair,
     dims,
     coef,
+    right,
     scalar_sems,
+    right_sems,
 ):
     terms, width, _ = half_ref.shape
     targets, strip, _ = mask_ref.shape
@@ -147,13 +133,21 @@
     ]
     for copy in scalars:
         copy.start()
+
+    def fetch(j, carry):
+        for p, r in enumerate(COLUMN_ORDER[2:]):
+            src = pl.multiple_of((mpo ^ r) * strip, strip)
+            pltpu.make_async_copy(
+                right_hbm.at[0, j, pl.ds(src, strip)],
+                right.at[j, pl.ds(p * strip, strip)],
+                right_sems.at[j],
+            ).start(priority=p)
+        return carry
+
+    lax.fori_loop(0, terms, fetch, 0)
     clear(lead_ref, rest_ref)
     for copy in scalars:
         copy.wait()
-    for j in range(terms):
-        spread(
-            lead_ref, rest_ref, half_ref[j], right_ref[j], pair[sec, cls[0, j]], coef[tid[0, j]]
-        )
     lane = mpo * strip + lax.broadcasted_iota(jnp.int32, (strip, strip), 1)
     line = sec * strip + lax.broadcasted_iota(jnp.int32, (strip, strip), 0)
 
@@ -163,6 +157,11 @@
         return carry
 
     lax.fori_loop(0, targets, target_mask, 0)
+    for j in range(terms):
+        pltpu.make_async_copy(
+            right_hbm.at[0, j, pl.ds(0, 2 * strip)], right.at[j], right_sems.at[j]
+        ).wait()
+        spread(lead_ref, rest_ref, half_ref[j], right[j], pair[sec, cls[0, j]], coef[tid[0, j]])
 
 
 def clear(*refs):
@@ -216,7 +215,8 @@
             row += own_ref.shape[2]
 
 
-def own_kernel(keep_ref, recv_ref, cross_ref, *own_refs):
+def own_kernel(keep_ref, recv_ref, cross_ref, later_in, later_out, *own_refs):
+    del later_in, later_out
     rows = own_refs[0].shape[1]
     row = keep_ref.shape[1] - 2 * rows
     for n, own_ref in enumerate(own_refs):
@@ -309,22 +309,21 @@
     scalar_room = [pltpu.SMEM(scalar.shape, scalar.dtype) for scalar in scalars]
     limit = pltpu.CompilerParams(vmem_limit_bytes=16 * 1024 * 1024)
     half_shape = jax.ShapeDtypeStruct((terms, width, width), jnp.bfloat16)
-    right_shape = jax.ShapeDtypeStruct((terms, 2 * strip, width), jnp.bfloat16)
-    lead_send, rest_send, half, keep_right = pl.pallas_call(
+    right_room = pltpu.VMEM((terms, 2 * strip, width), jnp.bfloat16)
+    lead_send, rest_send, half = pl.pallas_call(
         send_kernel,
-        out_shape=[lead_shape, rest_shape, half_shape, right_shape],
+        out_shape=[lead_shape, rest_shape, half_shape],
         in_specs=[hbm] * 8,
-        out_specs=[vmem] * 4,
+        out_specs=[vmem] * 3,
         scratch_shapes=scalar_room
         + [
             pltpu.VMEM((width, width), jnp.bfloat16),
             pltpu.VMEM((terms, width, width), jnp.bfloat16),
-            pltpu.VMEM((terms, 2 * strip, width), jnp.bfloat16),
+            right_room,
             pltpu.SemaphoreType.DMA((len(scalars),)),
             pltpu.SemaphoreType.DMA,
             pltpu.SemaphoreType.DMA((terms,)),
             pltpu.SemaphoreType.DMA((terms,)),
-            pltpu.SemaphoreType.DMA,
         ],
         compiler_params=limit,
         cost_estimate=pl.CostEstimate(
@@ -335,15 +334,20 @@
     lead_keep, rest_keep, mask = pl.pallas_call(
         keep_kernel,
         out_shape=[lead_shape, rest_shape, like(targets, strip)],
-        in_specs=[hbm] * len(scalars) + [vmem] * 2,
+        in_specs=[hbm] * (len(scalars) + 1) + [vmem],
         out_specs=[vmem] * 3,
-        scratch_shapes=scalar_room + [pltpu.SemaphoreType.DMA((len(scalars),))],
+        scratch_shapes=scalar_room
+        + [
+            right_room,
+            pltpu.SemaphoreType.DMA((len(scalars),)),
+            pltpu.SemaphoreType.DMA((terms,)),
+        ],
         compiler_params=limit,
         cost_estimate=pl.CostEstimate(
             flops=3 * terms * width**3, bytes_accessed=0, transcendentals=0
         ),
         name="keep_kernel",
-    )(*operands[: len(scalars)], half, keep_right)
+    )(*operands[: len(scalars)], operands[-1], half)
     lead_recv = swap(lead_send, "mpo", 1)
     part = like(2, targets, b_rows)
     rest_send, far, one, one_near, two, three = call(
@@ -357,9 +361,17 @@
     )
     cross = swap(far, "mpo", 2)
     one, two, three = [swap(x, "sec", q) for x, q in ((one, 1), (two, 2), (three, 3))]
-    one_near = swap(one_near, "sec", 1)
     rest_recv = swap(rest_send, "mpo", 1)
-    own = call(own_kernel, [like(targets, a_rows)] * 2, rest_keep, rest_recv, cross, span=3)
+    one_near, *own = call(
+        own_kernel,
+        [like(targets, strip)] + [like(targets, a_rows)] * 2,
+        rest_keep,
+        rest_recv,
+        cross,
+        one_near,
+        aliases={3: 0},
+        span=3,
+    )
     near = jax.ShapeDtypeStruct((targets, strip, strip), jnp.float32)
     here, near = call(
         here_kernel,
@@ -373,6 +385,7 @@
         span=3,
     )
     own = [swap(array, "sec", q) for array, q in zip(own, (2, 3))]
+    one_near = swap(one_near, "sec", 1)
     here = swap(here, "mpo", 2)
     far_sum = jax.ShapeDtypeStruct((targets, a_rows, strip), jnp.float32)
     far_sum = call(far_sum_kernel, far_sum, *own, span=3)

time: 29.4 us -> 28.9 us (0.983)
  waiting for transfers between devices: 9.56 us -> 8.66 us
  Pallas kernels: 6.73 us -> 7.63 us
  starting transfers between devices: 12.9 us -> 12.4 us
    pallas_call x1, Pallas kernels: 1.5 us -> 2.41 us  [by_targets(): pl.pallas_call(keep_kernel, out_shape=[lead_shape, rest_shape, like(targe...]
    ppermute x10, waiting for transfers between devices: 9.56 us -> 8.66 us  [swap(): lax.ppermute(array, axis, [(i, i ^ mask) for i in range(lax.axis_size(axi...]
    ppermute x10, starting transfers between devices: 12.9 us -> 12.4 us  [swap(): lax.ppermute(array, axis, [(i, i ^ mask) for i in range(lax.axis_size(axi...]
  transfers between devices with their start and end apart: 10 -> 10, of which waited for: 5 -> 4; matrix products, arithmetic and copies ran while one was open for 0% -> 0% of each run, Pallas kernels for 6% -> 9%
where the time goes in v10:
time: 28.9 us; the launch traced here: 28.7 us
  starting transfers between devices  12.4 us (43%)
  waiting for transfers between devices  8.66 us (30%)
  Pallas kernels  7.63 us (26%)
    ppermute x10, starting transfers between devices, swap(): lax.ppermute(array, axis, [(i, i ^ mask) for i in range(lax.axis_size(axi...  12.4 us
    ppermute x10, waiting for transfers between devices, swap(): lax.ppermute(array, axis, [(i, i ^ mask) for i in range(lax.axis_size(axi...  8.66 us
    pallas_call x1, Pallas kernels, by_targets(): pl.pallas_call(send_kernel, out_shape=[lead_shape, rest_shape, half_shape...  4.16 us
    pallas_call x1, Pallas kernels, by_targets(): pl.pallas_call(keep_kernel, out_shape=[lead_shape, rest_shape, like(targe...  2.41 us
    pallas_call x5, Pallas kernels, call(): pl.pallas_call(kernel, out_shape=out_shape, in_specs=[vmem] * len(args),...  1.06 us
  transfers between devices with their start and end apart: 10, of which 4 were waited for; matrix products, arithmetic and copies ran while one was open for 0% of the time, Pallas kernels for 9%

profile of v10, /device:TPU:0, one launch (start us, length us, event | category | flops | bytes accessed | tf_op | source)
XLA Modules:
  0.0 28.7 jit_solution(6549944173978849249)
XLA Ops:
  0.0 4.2 %send_kernel.1 = (bf16[4,576,128]{2,1,0:T(8,128)(2,1)S(1)}, bf16[4,448,128]{2,1,0:T(8,128)(2,1)S(1)}, bf16[3,512,512]{2,1,0:T(8,128)(2,1)S(1)}) custom-call(s32[1,3]{1,0:T(1,128)} %cls_hbm.3, s32[1,3]{1,0:T(1,128)} %tid_hbm.3, s32[4,5]{1,0:T(4,128)} %pair_hbm.3, s32[2,4]{1,0:T(2,128)} %bitcast.1, f32[50]{0:T(128)} %coef_hbm.3, ...), custom_call_target="tpu_custom_call" | custom-call | flops 1207959552 | bytes 4194304 | tf_op jit(solution)/shard_map/send_kernel/pallas_call | solution.py:313
  4.2 0.5 %collective-permute-start = (bf16[4,576,128]{2,1,0:T(8,128)(2,1)S(1)}, bf16[4,576,128]{2,1,0:T(8,128)(2,1)S(1)}, u32[]{:S(2)}, u32[]{:S(2)}) collective-permute-start(bf16[4,576,128]{2,1,0:T(8,128)(2,1)S(1)} %get-tuple-element.26), channel_id=1, source_target_pairs={{0,1},{1,0},{2,3},{3,2},{4,5},{5,4},{6,7},{7,6},{8,9},{9,8},{10,11... | collective-permute-start | bytes 1769480 | tf_op jit(solution)/shard_map/ppermute | solution.py:270
  4.7 2.4 %keep_kernel.1 = (bf16[4,576,128]{2,1,0:T(8,128)(2,1)S(1)}, bf16[4,448,128]{2,1,0:T(8,128)(2,1)S(1)}, bf16[4,128,128]{2,1,0:T(8,128)(2,1)S(1)}) custom-call(s32[1,3]{1,0:T(1,128)} %cls_hbm.3, s32[1,3]{1,0:T(1,128)} %tid_hbm.3, s32[4,5]{1,0:T(4,128)} %pair_hbm.3, s32[2,4]{1,0:T(2,128)} %bitcast.2, f32[50]{0:T(128)} %coef_hbm.3, ...), custom_call_target="tpu_custom_call" | custom-call | flops 1207959552 | tf_op jit(solution)/shard_map/keep_kernel/pallas_call | solution.py:334
  7.1 0.0 collective-permute-done.recv_ref
  7.1 0.1 lead_kernel.1
  7.3 0.1 collective-permute-start.1
  7.4 2.9 %collective-permute-start.5 = (bf16[4,192,128]{2,1,0:T(8,128)(2,1)S(1)}, bf16[4,192,128]{2,1,0:T(8,128)(2,1)S(1)}, u32[]{:S(2)}, u32[]{:S(2)}) collective-permute-start(bf16[4,192,128]{2,1,0:T(8,128)(2,1)S(1)} %get-tuple-element.32), channel_id=1, source_target_pairs={{0,2},{1,3},{2,0},{3,1},{4,6},{5,7},{6,4},{7,5},{8,10},{9,11},{10,... | collective-permute-start | bytes 589832 | tf_op jit(solution)/shard_map/ppermute | solution.py:270
  10.3 2.6 %collective-permute-start.3 = (bf16[2,4,32,128]{3,2,1,0:T(8,128)(2,1)S(1)}, bf16[2,4,32,128]{3,2,1,0:T(8,128)(2,1)S(1)}, u32[]{:S(2)}, u32[]{:S(2)}) collective-permute-start(bf16[2,4,32,128]{3,2,1,0:T(8,128)(2,1)S(1)} %get-tuple-element.30), channel_id=1, source_target_pairs={{0,8},{4,12},{8,0},{12,4},{1,9},{5,13},{9,1},{13,5},{2,10},{6,14},... | collective-permute-start | bytes 196616 | tf_op jit(solution)/shard_map/ppermute | solution.py:270
  12.9 1.3 %collective-permute-start.4 = (bf16[2,4,32,128]{3,2,1,0:T(8,128)(2,1)S(1)}, bf16[2,4,32,128]{3,2,1,0:T(8,128)(2,1)S(1)}, u32[]{:S(2)}, u32[]{:S(2)}) collective-permute-start(bf16[2,4,32,128]{3,2,1,0:T(8,128)(2,1)S(1)} %get-tuple-element.31), channel_id=1, source_target_pairs={{0,12},{4,8},{8,4},{12,0},{1,13},{5,9},{9,5},{13,1},{2,14},{6,10},... | collective-permute-start | bytes 196616 | tf_op jit(solution)/shard_map/ppermute | solution.py:270
  14.3 0.2 collective-permute-start.2
  14.5 1.0 %collective-permute-done.5.cross_ref = bf16[4,192,128]{2,1,0:T(8,128)(2,1)S(1)} collective-permute-done((bf16[4,192,128]{2,1,0:T(8,128)(2,1)S(1)}, bf16[4,192,128]{2,1,0:T(8,128)(2,1)S(1)}, u32[]{:S(2)}, u32[]{:S(2)}) %collective-permute-start.5) | collective-permute-done | bytes 196640 | tf_op jit(solution)/shard_map/ppermute | solution.py:270
  15.5 0.0 collective-permute-done.1.recv_ref
  15.5 0.1 own_kernel.1
  15.5 3.9 %collective-permute-start.9 = (bf16[4,96,128]{2,1,0:T(8,128)(2,1)S(1)}, bf16[4,96,128]{2,1,0:T(8,128)(2,1)S(1)}, u32[]{:S(2)}, u32[]{:S(2)}) collective-permute-start(bf16[4,96,128]{2,1,0:T(8,128)(2,1)S(1)} %get-tuple-element.38), channel_id=1, source_target_pairs={{0,12},{4,8},{8,4},{12,0},{1,13},{5,9},{9,5},{13,1},{2,14},{6,10},... | collective-permute-start | bytes 294920 | tf_op jit(solution)/shard_map/ppermute | solution.py:270
  19.5 0.0 collective-permute-start.8
  19.5 0.0 collective-permute-done.3.two_ref
  19.5 0.6 %collective-permute-start.6 = (bf16[4,128,128]{2,1,0:T(8,128)(2,1)S(1)}, bf16[4,128,128]{2,1,0:T(8,128)(2,1)S(1)}, u32[]{:S(2)}, u32[]{:S(2)}) collective-permute-start(bf16[4,128,128]{2,1,0:T(8,128)(2,1)S(1)} %get-tuple-element.36), channel_id=1, source_target_pairs={{0,4},{4,0},{8,12},{12,8},{1,5},{5,1},{9,13},{13,9},{2,6},{6,2},{1... | collective-permute-start | bytes 393224 | tf_op jit(solution)/shard_map/ppermute | solution.py:270
  20.1 0.0 collective-permute-done.4.three_ref
  20.1 1.6 %collective-permute-done.2.one_ref = bf16[4,128,128]{2,1,0:T(8,128)(2,1)S(1)} collective-permute-done((bf16[4,128,128]{2,1,0:T(8,128)(2,1)S(1)}, bf16[4,128,128]{2,1,0:T(8,128)(2,1)S(1)}, u32[]{:S(2)}, u32[]{:S(2)}) %collective-permute-start.2) | collective-permute-done | bytes 131104 | tf_op jit(solution)/shard_map/ppermute | solution.py:270
  21.7 0.1 here_kernel.1
  21.8 0.1 collective-permute-start.7
  21.9 2.7 %collective-permute-done.9.three_ref = bf16[4,96,128]{2,1,0:T(8,128)(2,1)S(1)} collective-permute-done((bf16[4,96,128]{2,1,0:T(8,128)(2,1)S(1)}, bf16[4,96,128]{2,1,0:T(8,128)(2,1)S(1)}, u32[]{:S(2)}, u32[]{:S(2)}) %collective-permute-start.9) | collective-permute-done | bytes 98336 | tf_op jit(solution)/shard_map/ppermute | solution.py:270
  24.6 3.4 %collective-permute-done.8.two_ref = bf16[4,96,128]{2,1,0:T(8,128)(2,1)S(1)} collective-permute-done((bf16[4,96,128]{2,1,0:T(8,128)(2,1)S(1)}, bf16[4,96,128]{2,1,0:T(8,128)(2,1)S(1)}, u32[]{:S(2)}, u32[]{:S(2)}) %collective-permute-start.8) | collective-permute-done | bytes 98336 | tf_op jit(solution)/shard_map/ppermute | solution.py:270
  28.0 0.0 collective-permute-done.6.one_ref
  28.0 0.0 collective-permute-done.7.cross_ref
  28.0 0.7 %final_kernel.1 = bf16[4,128,128]{2,1,0:T(8,128)(2,1)} custom-call(bf16[4,128,128]{2,1,0:T(8,128)(2,1)S(1)} %get-tuple-element.23.mask_ref, f32[4,128,128]{2,1,0:T(8,128)S(1)} %get-tuple-element.35.near_ref, bf16[4,128,128]{2,1,0:T(8,128)(2,1)S(1)} %collective-permute-done.6.one_ref, bf16[4,128,128]{2,1,0:T(8,128)(2,1)S(1)} %collective-permute-done.7.cross_ref, ...), custom_call_target="tpu_custom_call" | custom-call | flops 100000000 | tf_op jit(solution)/shard_map/final_kernel/pallas_call | solution.py:289
  (1 shorter events, 0.0 us)
Async XLA Ops:
  4.2 2.9 %collective-permute-start = (bf16[4,576,128]{2,1,0:T(8,128)(2,1)S(1)}, bf16[4,576,128]{2,1,0:T(8,128)(2,1)S(1)}, u32[]{:S(2)}, u32[]{:S(2)}) collective-permute-start(bf16[4,576,128]{2,1,0:T(8,128)(2,1)S(1)} %get-tuple-element.26), channel_id=1, source_target_pairs={{0,1},{1,0},{2,3},{3,2},{4,5},{5,4},{6,7},{7,6},{8,9},{9,8},{10,11... | collective-permute-start | bytes 1769480 | tf_op jit(solution)/shard_map/ppermute | solution.py:270
  7.3 8.2 %collective-permute-start.1 = (bf16[4,448,128]{2,1,0:T(8,128)(2,1)S(1)}, bf16[4,448,128]{2,1,0:T(8,128)(2,1)S(1)}, u32[]{:S(2)}, u32[]{:S(2)}) collective-permute-start(bf16[4,448,128]{2,1,0:T(8,128)(2,1)S(1)} %get-tuple-element.28), channel_id=1, source_target_pairs={{0,1},{1,0},{2,3},{3,2},{4,5},{5,4},{6,7},{7,6},{8,9},{9,8},{10,11... | collective-permute-start | bytes 1376264 | tf_op jit(solution)/shard_map/ppermute | solution.py:270
  7.4 8.1 %collective-permute-start.5 = (bf16[4,192,128]{2,1,0:T(8,128)(2,1)S(1)}, bf16[4,192,128]{2,1,0:T(8,128)(2,1)S(1)}, u32[]{:S(2)}, u32[]{:S(2)}) collective-permute-start(bf16[4,192,128]{2,1,0:T(8,128)(2,1)S(1)} %get-tuple-element.32), channel_id=1, source_target_pairs={{0,2},{1,3},{2,0},{3,1},{4,6},{5,7},{6,4},{7,5},{8,10},{9,11},{10,... | collective-permute-start | bytes 589832 | tf_op jit(solution)/shard_map/ppermute | solution.py:270
  10.3 9.2 %collective-permute-start.3 = (bf16[2,4,32,128]{3,2,1,0:T(8,128)(2,1)S(1)}, bf16[2,4,32,128]{3,2,1,0:T(8,128)(2,1)S(1)}, u32[]{:S(2)}, u32[]{:S(2)}) collective-permute-start(bf16[2,4,32,128]{3,2,1,0:T(8,128)(2,1)S(1)} %get-tuple-element.30), channel_id=1, source_target_pairs={{0,8},{4,12},{8,0},{12,4},{1,9},{5,13},{9,1},{13,5},{2,10},{6,14},... | collective-permute-start | bytes 196616 | tf_op jit(solution)/shard_map/ppermute | solution.py:270
  12.9 7.2 %collective-permute-start.4 = (bf16[2,4,32,128]{3,2,1,0:T(8,128)(2,1)S(1)}, bf16[2,4,32,128]{3,2,1,0:T(8,128)(2,1)S(1)}, u32[]{:S(2)}, u32[]{:S(2)}) collective-permute-start(bf16[2,4,32,128]{3,2,1,0:T(8,128)(2,1)S(1)} %get-tuple-element.31), channel_id=1, source_target_pairs={{0,12},{4,8},{8,4},{12,0},{1,13},{5,9},{9,5},{13,1},{2,14},{6,10},... | collective-permute-start | bytes 196616 | tf_op jit(solution)/shard_map/ppermute | solution.py:270
  14.3 7.5 %collective-permute-start.2 = (bf16[4,128,128]{2,1,0:T(8,128)(2,1)S(1)}, bf16[4,128,128]{2,1,0:T(8,128)(2,1)S(1)}, u32[]{:S(2)}, u32[]{:S(2)}) collective-permute-start(bf16[4,128,128]{2,1,0:T(8,128)(2,1)S(1)} %get-tuple-element.29), channel_id=1, source_target_pairs={{0,4},{4,0},{8,12},{12,8},{1,5},{5,1},{9,13},{13,9},{2,6},{6,2},{1... | collective-permute-start | bytes 393224 | tf_op jit(solution)/shard_map/ppermute | solution.py:270
  15.5 9.0 %collective-permute-start.9 = (bf16[4,96,128]{2,1,0:T(8,128)(2,1)S(1)}, bf16[4,96,128]{2,1,0:T(8,128)(2,1)S(1)}, u32[]{:S(2)}, u32[]{:S(2)}) collective-permute-start(bf16[4,96,128]{2,1,0:T(8,128)(2,1)S(1)} %get-tuple-element.38), channel_id=1, source_target_pairs={{0,12},{4,8},{8,4},{12,0},{1,13},{5,9},{9,5},{13,1},{2,14},{6,10},... | collective-permute-start | bytes 294920 | tf_op jit(solution)/shard_map/ppermute | solution.py:270
  19.5 8.5 %collective-permute-start.8 = (bf16[4,96,128]{2,1,0:T(8,128)(2,1)S(1)}, bf16[4,96,128]{2,1,0:T(8,128)(2,1)S(1)}, u32[]{:S(2)}, u32[]{:S(2)}) collective-permute-start(bf16[4,96,128]{2,1,0:T(8,128)(2,1)S(1)} %get-tuple-element.34.after_ref), channel_id=1, source_target_pairs={{0,8},{4,12},{8,0},{12,4},{1,9},{5,13},{9,1},{13,5},{2,10},{6,14},... | collective-permute-start | bytes 294920 | tf_op jit(solution)/shard_map/ppermute | solution.py:270
  19.5 8.5 %collective-permute-start.6 = (bf16[4,128,128]{2,1,0:T(8,128)(2,1)S(1)}, bf16[4,128,128]{2,1,0:T(8,128)(2,1)S(1)}, u32[]{:S(2)}, u32[]{:S(2)}) collective-permute-start(bf16[4,128,128]{2,1,0:T(8,128)(2,1)S(1)} %get-tuple-element.36), channel_id=1, source_target_pairs={{0,4},{4,0},{8,12},{12,8},{1,5},{5,1},{9,13},{13,9},{2,6},{6,2},{1... | collective-permute-start | bytes 393224 | tf_op jit(solution)/shard_map/ppermute | solution.py:270
  21.8 6.2 %collective-permute-start.7 = (bf16[4,128,128]{2,1,0:T(8,128)(2,1)S(1)}, bf16[4,128,128]{2,1,0:T(8,128)(2,1)S(1)}, u32[]{:S(2)}, u32[]{:S(2)}) collective-permute-start(bf16[4,128,128]{2,1,0:T(8,128)(2,1)S(1)} %get-tuple-element.37), channel_id=1, source_target_pairs={{0,2},{1,3},{2,0},{3,1},{4,6},{5,7},{6,4},{7,5},{8,10},{9,11},{10,... | collective-permute-start | bytes 393224 | tf_op jit(solution)/shard_map/ppermute | solution.py:270

commit v11 on v9

--- a/solution.py
+++ b/solution.py
@@ -216,7 +216,8 @@
             row += own_ref.shape[2]
 
 
-def own_kernel(keep_ref, recv_ref, cross_ref, *own_refs):
+def own_kernel(keep_ref, recv_ref, cross_ref, later_in, later_out, *own_refs):
+    del later_in, later_out
     rows = own_refs[0].shape[1]
     row = keep_ref.shape[1] - 2 * rows
     for n, own_ref in enumerate(own_refs):
@@ -357,9 +358,17 @@
     )
     cross = swap(far, "mpo", 2)
     one, two, three = [swap(x, "sec", q) for x, q in ((one, 1), (two, 2), (three, 3))]
-    one_near = swap(one_near, "sec", 1)
     rest_recv = swap(rest_send, "mpo", 1)
-    own = call(own_kernel, [like(targets, a_rows)] * 2, rest_keep, rest_recv, cross, span=3)
+    one_near, *own = call(
+        own_kernel,
+        [like(targets, strip)] + [like(targets, a_rows)] * 2,
+        rest_keep,
+        rest_recv,
+        cross,
+        one_near,
+        aliases={3: 0},
+        span=3,
+    )
     near = jax.ShapeDtypeStruct((targets, strip, strip), jnp.float32)
     here, near = call(
         here_kernel,
@@ -373,6 +382,7 @@
         span=3,
     )
     own = [swap(array, "sec", q) for array, q in zip(own, (2, 3))]
+    one_near = swap(one_near, "sec", 1)
     here = swap(here, "mpo", 2)
     far_sum = jax.ShapeDtypeStruct((targets, a_rows, strip), jnp.float32)
     far_sum = call(far_sum_kernel, far_sum, *own, span=3)

time: 29.4 us -> 28.3 us (0.963)
  waiting for transfers between devices: 9.56 us -> 8.64 us
    ppermute x10, waiting for transfers between devices: 9.56 us -> 8.64 us  [swap(): lax.ppermute(array, axis, [(i, i ^ mask) for i in range(lax.axis_size(axi...]
where the time goes in v11:
time: 28.3 us; the launch traced here: 28.1 us
  starting transfers between devices  12.7 us (45%)
  waiting for transfers between devices  8.64 us (31%)
  Pallas kernels  6.73 us (24%)
    ppermute x10, starting transfers between devices, swap(): lax.ppermute(array, axis, [(i, i ^ mask) for i in range(lax.axis_size(axi...  12.7 us
    ppermute x10, waiting for transfers between devices, swap(): lax.ppermute(array, axis, [(i, i ^ mask) for i in range(lax.axis_size(axi...  8.64 us
    pallas_call x1, Pallas kernels, by_targets(): pl.pallas_call(send_kernel, out_shape=[lead_shape, rest_shape, half_shape...  4.17 us
    pallas_call x1, Pallas kernels, by_targets(): pl.pallas_call(keep_kernel, out_shape=[lead_shape, rest_shape, like(targe...  1.5 us
    pallas_call x5, Pallas kernels, call(): pl.pallas_call(kernel, out_shape=out_shape, in_specs=[vmem] * len(args),...  1.05 us
  transfers between devices with their start and end apart: 10, of which 5 were waited for; matrix products, arithmetic and copies ran while one was open for 0% of the time, Pallas kernels for 6%

profile of v11, /device:TPU:0, one launch (start us, length us, event | category | flops | bytes accessed | tf_op | source)
XLA Modules:
  0.0 28.1 jit_solution(1472666429809133030)
XLA Ops:
  0.0 4.2 %send_kernel.1 = (bf16[4,576,128]{2,1,0:T(8,128)(2,1)S(1)}, bf16[4,448,128]{2,1,0:T(8,128)(2,1)S(1)}, bf16[3,512,512]{2,1,0:T(8,128)(2,1)S(1)}, bf16[3,256,512]{2,1,0:T(8,128)(2,1)S(1)}) custom-call(s32[1,3]{1,0:T(1,128)} %cls_hbm.3, s32[1,3]{1,0:T(1,128)} %tid_hbm.3, s32[4,5]{1,0:T(4,128)} %pair_hbm.3, s32[2,4]{1,0:T(2,128)} %bitcast.1, f32[50]{0:T(128)} %coef_hbm.3, ...), custom_call_target="tpu_custom_call" | custom-call | flops 1207959552 | bytes 4194304 | tf_op jit(solution)/shard_map/send_kernel/pallas_call | solution.py:314
  4.2 0.5 %collective-permute-start = (bf16[4,576,128]{2,1,0:T(8,128)(2,1)S(1)}, bf16[4,576,128]{2,1,0:T(8,128)(2,1)S(1)}, u32[]{:S(2)}, u32[]{:S(2)}) collective-permute-start(bf16[4,576,128]{2,1,0:T(8,128)(2,1)S(1)} %get-tuple-element.28), channel_id=1, source_target_pairs={{0,1},{1,0},{2,3},{3,2},{4,5},{5,4},{6,7},{7,6},{8,9},{9,8},{10,11... | collective-permute-start | bytes 1769480 | tf_op jit(solution)/shard_map/ppermute | solution.py:271
  4.7 1.5 %keep_kernel.1 = (bf16[4,576,128]{2,1,0:T(8,128)(2,1)S(1)}, bf16[4,448,128]{2,1,0:T(8,128)(2,1)S(1)}, bf16[4,128,128]{2,1,0:T(8,128)(2,1)S(1)}) custom-call(s32[1,3]{1,0:T(1,128)} %cls_hbm.3, s32[1,3]{1,0:T(1,128)} %tid_hbm.3, s32[4,5]{1,0:T(4,128)} %pair_hbm.3, s32[2,4]{1,0:T(2,128)} %bitcast.2, f32[50]{0:T(128)} %coef_hbm.3, ...), custom_call_target="tpu_custom_call" | custom-call | flops 1207959552 | tf_op jit(solution)/shard_map/keep_kernel/pallas_call | solution.py:336
  6.2 0.1 collective-permute-done.recv_ref
  6.3 0.1 lead_kernel.1
  6.5 0.4 %collective-permute-start.1 = (bf16[4,448,128]{2,1,0:T(8,128)(2,1)S(1)}, bf16[4,448,128]{2,1,0:T(8,128)(2,1)S(1)}, u32[]{:S(2)}, u32[]{:S(2)}) collective-permute-start(bf16[4,448,128]{2,1,0:T(8,128)(2,1)S(1)} %get-tuple-element.30), channel_id=1, source_target_pairs={{0,1},{1,0},{2,3},{3,2},{4,5},{5,4},{6,7},{7,6},{8,9},{9,8},{10,11... | collective-permute-start | bytes 1376264 | tf_op jit(solution)/shard_map/ppermute | solution.py:271
  6.9 2.6 %collective-permute-start.5 = (bf16[4,192,128]{2,1,0:T(8,128)(2,1)S(1)}, bf16[4,192,128]{2,1,0:T(8,128)(2,1)S(1)}, u32[]{:S(2)}, u32[]{:S(2)}) collective-permute-start(bf16[4,192,128]{2,1,0:T(8,128)(2,1)S(1)} %get-tuple-element.34), channel_id=1, source_target_pairs={{0,2},{1,3},{2,0},{3,1},{4,6},{5,7},{6,4},{7,5},{8,10},{9,11},{10,... | collective-permute-start | bytes 589832 | tf_op jit(solution)/shard_map/ppermute | solution.py:271
  9.5 2.6 %collective-permute-start.3 = (bf16[2,4,32,128]{3,2,1,0:T(8,128)(2,1)S(1)}, bf16[2,4,32,128]{3,2,1,0:T(8,128)(2,1)S(1)}, u32[]{:S(2)}, u32[]{:S(2)}) collective-permute-start(bf16[2,4,32,128]{3,2,1,0:T(8,128)(2,1)S(1)} %get-tuple-element.32), channel_id=1, source_target_pairs={{0,8},{4,12},{8,0},{12,4},{1,9},{5,13},{9,1},{13,5},{2,10},{6,14},... | collective-permute-start | bytes 196616 | tf_op jit(solution)/shard_map/ppermute | solution.py:271
  12.1 1.3 %collective-permute-start.4 = (bf16[2,4,32,128]{3,2,1,0:T(8,128)(2,1)S(1)}, bf16[2,4,32,128]{3,2,1,0:T(8,128)(2,1)S(1)}, u32[]{:S(2)}, u32[]{:S(2)}) collective-permute-start(bf16[2,4,32,128]{3,2,1,0:T(8,128)(2,1)S(1)} %get-tuple-element.33), channel_id=1, source_target_pairs={{0,12},{4,8},{8,4},{12,0},{1,13},{5,9},{9,5},{13,1},{2,14},{6,10},... | collective-permute-start | bytes 196616 | tf_op jit(solution)/shard_map/ppermute | solution.py:271
  13.5 0.2 collective-permute-start.2
  13.7 1.3 %collective-permute-done.5.cross_ref = bf16[4,192,128]{2,1,0:T(8,128)(2,1)S(1)} collective-permute-done((bf16[4,192,128]{2,1,0:T(8,128)(2,1)S(1)}, bf16[4,192,128]{2,1,0:T(8,128)(2,1)S(1)}, u32[]{:S(2)}, u32[]{:S(2)}) %collective-permute-start.5) | collective-permute-done | bytes 196640 | tf_op jit(solution)/shard_map/ppermute | solution.py:271
  15.0 0.0 collective-permute-done.1.recv_ref
  15.0 0.1 own_kernel.1
  15.1 3.9 %collective-permute-start.9 = (bf16[4,96,128]{2,1,0:T(8,128)(2,1)S(1)}, bf16[4,96,128]{2,1,0:T(8,128)(2,1)S(1)}, u32[]{:S(2)}, u32[]{:S(2)}) collective-permute-start(bf16[4,96,128]{2,1,0:T(8,128)(2,1)S(1)} %get-tuple-element.40), channel_id=1, source_target_pairs={{0,12},{4,8},{8,4},{12,0},{1,13},{5,9},{9,5},{13,1},{2,14},{6,10},... | collective-permute-start | bytes 294920 | tf_op jit(solution)/shard_map/ppermute | solution.py:271
  19.0 0.0 collective-permute-start.8
  19.0 0.0 collective-permute-done.3.two_ref
  19.0 0.6 %collective-permute-start.6 = (bf16[4,128,128]{2,1,0:T(8,128)(2,1)S(1)}, bf16[4,128,128]{2,1,0:T(8,128)(2,1)S(1)}, u32[]{:S(2)}, u32[]{:S(2)}) collective-permute-start(bf16[4,128,128]{2,1,0:T(8,128)(2,1)S(1)} %get-tuple-element.38), channel_id=1, source_target_pairs={{0,4},{4,0},{8,12},{12,8},{1,5},{5,1},{9,13},{13,9},{2,6},{6,2},{1... | collective-permute-start | bytes 393224 | tf_op jit(solution)/shard_map/ppermute | solution.py:271
  19.6 0.0 collective-permute-done.4.three_ref
  19.6 1.3 %collective-permute-done.2.one_ref = bf16[4,128,128]{2,1,0:T(8,128)(2,1)S(1)} collective-permute-done((bf16[4,128,128]{2,1,0:T(8,128)(2,1)S(1)}, bf16[4,128,128]{2,1,0:T(8,128)(2,1)S(1)}, u32[]{:S(2)}, u32[]{:S(2)}) %collective-permute-start.2) | collective-permute-done | bytes 131104 | tf_op jit(solution)/shard_map/ppermute | solution.py:271
  20.9 0.1 here_kernel.1
  21.0 0.4 %collective-permute-start.7 = (bf16[4,128,128]{2,1,0:T(8,128)(2,1)S(1)}, bf16[4,128,128]{2,1,0:T(8,128)(2,1)S(1)}, u32[]{:S(2)}, u32[]{:S(2)}) collective-permute-start(bf16[4,128,128]{2,1,0:T(8,128)(2,1)S(1)} %get-tuple-element.39), channel_id=1, source_target_pairs={{0,2},{1,3},{2,0},{3,1},{4,6},{5,7},{6,4},{7,5},{8,10},{9,11},{10,... | collective-permute-start | bytes 393224 | tf_op jit(solution)/shard_map/ppermute | solution.py:271
  21.4 2.5 %collective-permute-done.9.three_ref = bf16[4,96,128]{2,1,0:T(8,128)(2,1)S(1)} collective-permute-done((bf16[4,96,128]{2,1,0:T(8,128)(2,1)S(1)}, bf16[4,96,128]{2,1,0:T(8,128)(2,1)S(1)}, u32[]{:S(2)}, u32[]{:S(2)}) %collective-permute-start.9) | collective-permute-done | bytes 98336 | tf_op jit(solution)/shard_map/ppermute | solution.py:271
  23.9 3.4 %collective-permute-done.8.two_ref = bf16[4,96,128]{2,1,0:T(8,128)(2,1)S(1)} collective-permute-done((bf16[4,96,128]{2,1,0:T(8,128)(2,1)S(1)}, bf16[4,96,128]{2,1,0:T(8,128)(2,1)S(1)}, u32[]{:S(2)}, u32[]{:S(2)}) %collective-permute-start.8) | collective-permute-done | bytes 98336 | tf_op jit(solution)/shard_map/ppermute | solution.py:271
  27.4 0.0 collective-permute-done.6.one_ref
  27.4 0.0 collective-permute-done.7.cross_ref
  27.4 0.7 %final_kernel.1 = bf16[4,128,128]{2,1,0:T(8,128)(2,1)} custom-call(bf16[4,128,128]{2,1,0:T(8,128)(2,1)S(1)} %get-tuple-element.25.mask_ref, f32[4,128,128]{2,1,0:T(8,128)S(1)} %get-tuple-element.37.near_ref, bf16[4,128,128]{2,1,0:T(8,128)(2,1)S(1)} %collective-permute-done.6.one_ref, bf16[4,128,128]{2,1,0:T(8,128)(2,1)S(1)} %collective-permute-done.7.cross_ref, ...), custom_call_target="tpu_custom_call" | custom-call | flops 100000000 | tf_op jit(solution)/shard_map/final_kernel/pallas_call | solution.py:290
  (1 shorter events, 0.0 us)
Async XLA Ops:
  4.2 2.2 %collective-permute-start = (bf16[4,576,128]{2,1,0:T(8,128)(2,1)S(1)}, bf16[4,576,128]{2,1,0:T(8,128)(2,1)S(1)}, u32[]{:S(2)}, u32[]{:S(2)}) collective-permute-start(bf16[4,576,128]{2,1,0:T(8,128)(2,1)S(1)} %get-tuple-element.28), channel_id=1, source_target_pairs={{0,1},{1,0},{2,3},{3,2},{4,5},{5,4},{6,7},{7,6},{8,9},{9,8},{10,11... | collective-permute-start | bytes 1769480 | tf_op jit(solution)/shard_map/ppermute | solution.py:271
  6.5 8.5 %collective-permute-start.1 = (bf16[4,448,128]{2,1,0:T(8,128)(2,1)S(1)}, bf16[4,448,128]{2,1,0:T(8,128)(2,1)S(1)}, u32[]{:S(2)}, u32[]{:S(2)}) collective-permute-start(bf16[4,448,128]{2,1,0:T(8,128)(2,1)S(1)} %get-tuple-element.30), channel_id=1, source_target_pairs={{0,1},{1,0},{2,3},{3,2},{4,5},{5,4},{6,7},{7,6},{8,9},{9,8},{10,11... | collective-permute-start | bytes 1376264 | tf_op jit(solution)/shard_map/ppermute | solution.py:271
  6.9 8.1 %collective-permute-start.5 = (bf16[4,192,128]{2,1,0:T(8,128)(2,1)S(1)}, bf16[4,192,128]{2,1,0:T(8,128)(2,1)S(1)}, u32[]{:S(2)}, u32[]{:S(2)}) collective-permute-start(bf16[4,192,128]{2,1,0:T(8,128)(2,1)S(1)} %get-tuple-element.34), channel_id=1, source_target_pairs={{0,2},{1,3},{2,0},{3,1},{4,6},{5,7},{6,4},{7,5},{8,10},{9,11},{10,... | collective-permute-start | bytes 589832 | tf_op jit(solution)/shard_map/ppermute | solution.py:271
  9.5 9.4 %collective-permute-start.3 = (bf16[2,4,32,128]{3,2,1,0:T(8,128)(2,1)S(1)}, bf16[2,4,32,128]{3,2,1,0:T(8,128)(2,1)S(1)}, u32[]{:S(2)}, u32[]{:S(2)}) collective-permute-start(bf16[2,4,32,128]{3,2,1,0:T(8,128)(2,1)S(1)} %get-tuple-element.32), channel_id=1, source_target_pairs={{0,8},{4,12},{8,0},{12,4},{1,9},{5,13},{9,1},{13,5},{2,10},{6,14},... | collective-permute-start | bytes 196616 | tf_op jit(solution)/shard_map/ppermute | solution.py:271
  12.1 7.5 %collective-permute-start.4 = (bf16[2,4,32,128]{3,2,1,0:T(8,128)(2,1)S(1)}, bf16[2,4,32,128]{3,2,1,0:T(8,128)(2,1)S(1)}, u32[]{:S(2)}, u32[]{:S(2)}) collective-permute-start(bf16[2,4,32,128]{3,2,1,0:T(8,128)(2,1)S(1)} %get-tuple-element.33), channel_id=1, source_target_pairs={{0,12},{4,8},{8,4},{12,0},{1,13},{5,9},{9,5},{13,1},{2,14},{6,10},... | collective-permute-start | bytes 196616 | tf_op jit(solution)/shard_map/ppermute | solution.py:271
  13.5 7.5 %collective-permute-start.2 = (bf16[4,128,128]{2,1,0:T(8,128)(2,1)S(1)}, bf16[4,128,128]{2,1,0:T(8,128)(2,1)S(1)}, u32[]{:S(2)}, u32[]{:S(2)}) collective-permute-start(bf16[4,128,128]{2,1,0:T(8,128)(2,1)S(1)} %get-tuple-element.31), channel_id=1, source_target_pairs={{0,4},{4,0},{8,12},{12,8},{1,5},{5,1},{9,13},{13,9},{2,6},{6,2},{1... | collective-permute-start | bytes 393224 | tf_op jit(solution)/shard_map/ppermute | solution.py:271
  15.1 8.9 %collective-permute-start.9 = (bf16[4,96,128]{2,1,0:T(8,128)(2,1)S(1)}, bf16[4,96,128]{2,1,0:T(8,128)(2,1)S(1)}, u32[]{:S(2)}, u32[]{:S(2)}) collective-permute-start(bf16[4,96,128]{2,1,0:T(8,128)(2,1)S(1)} %get-tuple-element.40), channel_id=1, source_target_pairs={{0,12},{4,8},{8,4},{12,0},{1,13},{5,9},{9,5},{13,1},{2,14},{6,10},... | collective-permute-start | bytes 294920 | tf_op jit(solution)/shard_map/ppermute | solution.py:271
  19.0 8.4 %collective-permute-start.8 = (bf16[4,96,128]{2,1,0:T(8,128)(2,1)S(1)}, bf16[4,96,128]{2,1,0:T(8,128)(2,1)S(1)}, u32[]{:S(2)}, u32[]{:S(2)}) collective-permute-start(bf16[4,96,128]{2,1,0:T(8,128)(2,1)S(1)} %get-tuple-element.36.after_ref), channel_id=1, source_target_pairs={{0,8},{4,12},{8,0},{12,4},{1,9},{5,13},{9,1},{13,5},{2,10},{6,14},... | collective-permute-start | bytes 294920 | tf_op jit(solution)/shard_map/ppermute | solution.py:271
  19.0 8.4 %collective-permute-start.6 = (bf16[4,128,128]{2,1,0:T(8,128)(2,1)S(1)}, bf16[4,128,128]{2,1,0:T(8,128)(2,1)S(1)}, u32[]{:S(2)}, u32[]{:S(2)}) collective-permute-start(bf16[4,128,128]{2,1,0:T(8,128)(2,1)S(1)} %get-tuple-element.38), channel_id=1, source_target_pairs={{0,4},{4,0},{8,12},{12,8},{1,5},{5,1},{9,13},{13,9},{2,6},{6,2},{1... | collective-permute-start | bytes 393224 | tf_op jit(solution)/shard_map/ppermute | solution.py:271
  21.0 6.4 %collective-permute-start.7 = (bf16[4,128,128]{2,1,0:T(8,128)(2,1)S(1)}, bf16[4,128,128]{2,1,0:T(8,128)(2,1)S(1)}, u32[]{:S(2)}, u32[]{:S(2)}) collective-permute-start(bf16[4,128,128]{2,1,0:T(8,128)(2,1)S(1)} %get-tuple-element.39), channel_id=1, source_target_pairs={{0,2},{1,3},{2,0},{3,1},{4,6},{5,7},{6,4},{7,5},{8,10},{9,11},{10,... | collective-permute-start | bytes 393224 | tf_op jit(solution)/shard_map/ppermute | solution.py:271

commit v12 on v11

--- a/solution.py
+++ b/solution.py
@@ -220,7 +220,7 @@
     del later_in, later_out
     rows = own_refs[0].shape[1]
     row = keep_ref.shape[1] - 2 * rows
-    for n, own_ref in enumerate(own_refs):
+    for n, own_ref in enumerate(own_refs[::-1]):
         at = slice(row + n * rows, row + (n + 1) * rows)
         own_ref[...] = add(
             keep_ref[:, at, :], recv_ref[:, at, :], cross_ref[:, n * rows : (n + 1) * rows, :]
@@ -381,7 +381,7 @@
         own[0],
         span=3,
     )
-    own = [swap(array, "sec", q) for array, q in zip(own, (2, 3))]
+    own = [swap(array, "sec", q) for array, q in zip(own[::-1], (2, 3))]
     one_near = swap(one_near, "sec", 1)
     here = swap(here, "mpo", 2)
     far_sum = jax.ShapeDtypeStruct((targets, a_rows, strip), jnp.float32)

time: 28.3 us -> 28.8 us (1.018)
  waiting for transfers between devices: 8.64 us -> 9.55 us
  starting transfers between devices: 12.7 us -> 12.3 us
    ppermute x10, waiting for transfers between devices: 8.64 us -> 9.55 us  [swap(): lax.ppermute(array, axis, [(i, i ^ mask) for i in range(lax.axis_size(axi...]
    ppermute x10, starting transfers between devices: 12.7 us -> 12.3 us  [swap(): lax.ppermute(array, axis, [(i, i ^ mask) for i in range(lax.axis_size(axi...]
  transfers between devices with their start and end apart: 10 -> 10, of which waited for: 5 -> 6; matrix products, arithmetic and copies ran while one was open for 0% -> 0% of each run, Pallas kernels for 6% -> 6%
where the time goes in v12:
time: 28.8 us; the launch traced here: 28.6 us
  starting transfers between devices  12.3 us (43%)
  waiting for transfers between devices  9.55 us (33%)
  Pallas kernels  6.73 us (23%)
    ppermute x10, starting transfers between devices, swap(): lax.ppermute(array, axis, [(i, i ^ mask) for i in range(lax.axis_size(axi...  12.3 us
    ppermute x10, waiting for transfers between devices, swap(): lax.ppermute(array, axis, [(i, i ^ mask) for i in range(lax.axis_size(axi...  9.55 us
    pallas_call x1, Pallas kernels, by_targets(): pl.pallas_call(send_kernel, out_shape=[lead_shape, rest_shape, half_shape...  4.17 us
    pallas_call x1, Pallas kernels, by_targets(): pl.pallas_call(keep_kernel, out_shape=[lead_shape, rest_shape, like(targe...  1.5 us
    pallas_call x5, Pallas kernels, call(): pl.pallas_call(kernel, out_shape=out_shape, in_specs=[vmem] * len(args),...  1.05 us
  transfers between devices with their start and end apart: 10, of which 6 were waited for; matrix products, arithmetic and copies ran while one was open for 0% of the time, Pallas kernels for 6%

profile of v12, /device:TPU:0, one launch (start us, length us, event | category | flops | bytes accessed | tf_op | source)
XLA Modules:
  0.0 28.6 jit_solution(2698431263142873895)
XLA Ops:
  0.0 4.2 %send_kernel.1 = (bf16[4,576,128]{2,1,0:T(8,128)(2,1)S(1)}, bf16[4,448,128]{2,1,0:T(8,128)(2,1)S(1)}, bf16[3,512,512]{2,1,0:T(8,128)(2,1)S(1)}, bf16[3,256,512]{2,1,0:T(8,128)(2,1)S(1)}) custom-call(s32[1,3]{1,0:T(1,128)} %cls_hbm.3, s32[1,3]{1,0:T(1,128)} %tid_hbm.3, s32[4,5]{1,0:T(4,128)} %pair_hbm.3, s32[2,4]{1,0:T(2,128)} %bitcast.1, f32[50]{0:T(128)} %coef_hbm.3, ...), custom_call_target="tpu_custom_call" | custom-call | flops 1207959552 | bytes 4194304 | tf_op jit(solution)/shard_map/send_kernel/pallas_call | solution.py:314
  4.2 0.5 %collective-permute-start = (bf16[4,576,128]{2,1,0:T(8,128)(2,1)S(1)}, bf16[4,576,128]{2,1,0:T(8,128)(2,1)S(1)}, u32[]{:S(2)}, u32[]{:S(2)}) collective-permute-start(bf16[4,576,128]{2,1,0:T(8,128)(2,1)S(1)} %get-tuple-element.28), channel_id=1, source_target_pairs={{0,1},{1,0},{2,3},{3,2},{4,5},{5,4},{6,7},{7,6},{8,9},{9,8},{10,11... | collective-permute-start | bytes 1769480 | tf_op jit(solution)/shard_map/ppermute | solution.py:271
  4.7 1.5 %keep_kernel.1 = (bf16[4,576,128]{2,1,0:T(8,128)(2,1)S(1)}, bf16[4,448,128]{2,1,0:T(8,128)(2,1)S(1)}, bf16[4,128,128]{2,1,0:T(8,128)(2,1)S(1)}) custom-call(s32[1,3]{1,0:T(1,128)} %cls_hbm.3, s32[1,3]{1,0:T(1,128)} %tid_hbm.3, s32[4,5]{1,0:T(4,128)} %pair_hbm.3, s32[2,4]{1,0:T(2,128)} %bitcast.2, f32[50]{0:T(128)} %coef_hbm.3, ...), custom_call_target="tpu_custom_call" | custom-call | flops 1207959552 | tf_op jit(solution)/shard_map/keep_kernel/pallas_call | solution.py:336
  6.2 0.1 collective-permute-done.recv_ref
  6.3 0.1 lead_kernel.1
  6.5 0.4 %collective-permute-start.1 = (bf16[4,448,128]{2,1,0:T(8,128)(2,1)S(1)}, bf16[4,448,128]{2,1,0:T(8,128)(2,1)S(1)}, u32[]{:S(2)}, u32[]{:S(2)}) collective-permute-start(bf16[4,448,128]{2,1,0:T(8,128)(2,1)S(1)} %get-tuple-element.30), channel_id=1, source_target_pairs={{0,1},{1,0},{2,3},{3,2},{4,5},{5,4},{6,7},{7,6},{8,9},{9,8},{10,11... | collective-permute-start | bytes 1376264 | tf_op jit(solution)/shard_map/ppermute | solution.py:271
  6.9 2.6 %collective-permute-start.5 = (bf16[4,192,128]{2,1,0:T(8,128)(2,1)S(1)}, bf16[4,192,128]{2,1,0:T(8,128)(2,1)S(1)}, u32[]{:S(2)}, u32[]{:S(2)}) collective-permute-start(bf16[4,192,128]{2,1,0:T(8,128)(2,1)S(1)} %get-tuple-element.34), channel_id=1, source_target_pairs={{0,2},{1,3},{2,0},{3,1},{4,6},{5,7},{6,4},{7,5},{8,10},{9,11},{10,... | collective-permute-start | bytes 589832 | tf_op jit(solution)/shard_map/ppermute | solution.py:271
  9.5 2.6 %collective-permute-start.3 = (bf16[2,4,32,128]{3,2,1,0:T(8,128)(2,1)S(1)}, bf16[2,4,32,128]{3,2,1,0:T(8,128)(2,1)S(1)}, u32[]{:S(2)}, u32[]{:S(2)}) collective-permute-start(bf16[2,4,32,128]{3,2,1,0:T(8,128)(2,1)S(1)} %get-tuple-element.32), channel_id=1, source_target_pairs={{0,8},{4,12},{8,0},{12,4},{1,9},{5,13},{9,1},{13,5},{2,10},{6,14},... | collective-permute-start | bytes 196616 | tf_op jit(solution)/shard_map/ppermute | solution.py:271
  12.1 1.3 %collective-permute-start.4 = (bf16[2,4,32,128]{3,2,1,0:T(8,128)(2,1)S(1)}, bf16[2,4,32,128]{3,2,1,0:T(8,128)(2,1)S(1)}, u32[]{:S(2)}, u32[]{:S(2)}) collective-permute-start(bf16[2,4,32,128]{3,2,1,0:T(8,128)(2,1)S(1)} %get-tuple-element.33), channel_id=1, source_target_pairs={{0,12},{4,8},{8,4},{12,0},{1,13},{5,9},{9,5},{13,1},{2,14},{6,10},... | collective-permute-start | bytes 196616 | tf_op jit(solution)/shard_map/ppermute | solution.py:271
  13.5 0.2 collective-permute-start.2
  13.7 1.3 %collective-permute-done.5.cross_ref = bf16[4,192,128]{2,1,0:T(8,128)(2,1)S(1)} collective-permute-done((bf16[4,192,128]{2,1,0:T(8,128)(2,1)S(1)}, bf16[4,192,128]{2,1,0:T(8,128)(2,1)S(1)}, u32[]{:S(2)}, u32[]{:S(2)}) %collective-permute-start.5) | collective-permute-done | bytes 196640 | tf_op jit(solution)/shard_map/ppermute | solution.py:271
  15.0 0.0 collective-permute-done.1.recv_ref
  15.0 0.1 own_kernel.1
  15.1 2.9 %collective-permute-start.8 = (bf16[4,96,128]{2,1,0:T(8,128)(2,1)S(1)}, bf16[4,96,128]{2,1,0:T(8,128)(2,1)S(1)}, u32[]{:S(2)}, u32[]{:S(2)}) collective-permute-start(bf16[4,96,128]{2,1,0:T(8,128)(2,1)S(1)} %get-tuple-element.40), channel_id=1, source_target_pairs={{0,8},{4,12},{8,0},{12,4},{1,9},{5,13},{9,1},{13,5},{2,10},{6,14},... | collective-permute-start | bytes 294920 | tf_op jit(solution)/shard_map/ppermute | solution.py:271
  18.0 1.4 %collective-permute-start.9 = (bf16[4,96,128]{2,1,0:T(8,128)(2,1)S(1)}, bf16[4,96,128]{2,1,0:T(8,128)(2,1)S(1)}, u32[]{:S(2)}, u32[]{:S(2)}) collective-permute-start(bf16[4,96,128]{2,1,0:T(8,128)(2,1)S(1)} %get-tuple-element.36.after_ref), channel_id=1, source_target_pairs={{0,12},{4,8},{8,4},{12,0},{1,13},{5,9},{9,5},{13,1},{2,14},{6,10},... | collective-permute-start | bytes 294920 | tf_op jit(solution)/shard_map/ppermute | solution.py:271
  19.3 0.0 collective-permute-done.3.two_ref
  19.3 0.2 collective-permute-start.6
  19.5 0.0 collective-permute-done.4.three_ref
  19.5 3.2 %collective-permute-done.2.one_ref = bf16[4,128,128]{2,1,0:T(8,128)(2,1)S(1)} collective-permute-done((bf16[4,128,128]{2,1,0:T(8,128)(2,1)S(1)}, bf16[4,128,128]{2,1,0:T(8,128)(2,1)S(1)}, u32[]{:S(2)}, u32[]{:S(2)}) %collective-permute-start.2) | collective-permute-done | bytes 131104 | tf_op jit(solution)/shard_map/ppermute | solution.py:271
  22.8 0.1 here_kernel.1
  22.9 0.1 collective-permute-start.7
  23.0 2.9 %collective-permute-done.8.two_ref = bf16[4,96,128]{2,1,0:T(8,128)(2,1)S(1)} collective-permute-done((bf16[4,96,128]{2,1,0:T(8,128)(2,1)S(1)}, bf16[4,96,128]{2,1,0:T(8,128)(2,1)S(1)}, u32[]{:S(2)}, u32[]{:S(2)}) %collective-permute-start.8) | collective-permute-done | bytes 98336 | tf_op jit(solution)/shard_map/ppermute | solution.py:271
  25.9 0.0 collective-permute-done.9.three_ref
  25.9 1.3 %collective-permute-done.6.one_ref = bf16[4,128,128]{2,1,0:T(8,128)(2,1)S(1)} collective-permute-done((bf16[4,128,128]{2,1,0:T(8,128)(2,1)S(1)}, bf16[4,128,128]{2,1,0:T(8,128)(2,1)S(1)}, u32[]{:S(2)}, u32[]{:S(2)}) %collective-permute-start.6) | collective-permute-done | bytes 131104 | tf_op jit(solution)/shard_map/ppermute | solution.py:271
  27.2 0.7 %collective-permute-done.7.cross_ref = bf16[4,128,128]{2,1,0:T(8,128)(2,1)S(1)} collective-permute-done((bf16[4,128,128]{2,1,0:T(8,128)(2,1)S(1)}, bf16[4,128,128]{2,1,0:T(8,128)(2,1)S(1)}, u32[]{:S(2)}, u32[]{:S(2)}) %collective-permute-start.7) | collective-permute-done | bytes 131104 | tf_op jit(solution)/shard_map/ppermute | solution.py:271
  27.9 0.7 %final_kernel.1 = bf16[4,128,128]{2,1,0:T(8,128)(2,1)} custom-call(bf16[4,128,128]{2,1,0:T(8,128)(2,1)S(1)} %get-tuple-element.25.mask_ref, f32[4,128,128]{2,1,0:T(8,128)S(1)} %get-tuple-element.37.near_ref, bf16[4,128,128]{2,1,0:T(8,128)(2,1)S(1)} %collective-permute-done.6.one_ref, bf16[4,128,128]{2,1,0:T(8,128)(2,1)S(1)} %collective-permute-done.7.cross_ref, ...), custom_call_target="tpu_custom_call" | custom-call | flops 100000000 | tf_op jit(solution)/shard_map/final_kernel/pallas_call | solution.py:290
  (1 shorter events, 0.0 us)
Async XLA Ops:
  4.2 2.2 %collective-permute-start = (bf16[4,576,128]{2,1,0:T(8,128)(2,1)S(1)}, bf16[4,576,128]{2,1,0:T(8,128)(2,1)S(1)}, u32[]{:S(2)}, u32[]{:S(2)}) collective-permute-start(bf16[4,576,128]{2,1,0:T(8,128)(2,1)S(1)} %get-tuple-element.28), channel_id=1, source_target_pairs={{0,1},{1,0},{2,3},{3,2},{4,5},{5,4},{6,7},{7,6},{8,9},{9,8},{10,11... | collective-permute-start | bytes 1769480 | tf_op jit(solution)/shard_map/ppermute | solution.py:271
  6.5 8.5 %collective-permute-start.1 = (bf16[4,448,128]{2,1,0:T(8,128)(2,1)S(1)}, bf16[4,448,128]{2,1,0:T(8,128)(2,1)S(1)}, u32[]{:S(2)}, u32[]{:S(2)}) collective-permute-start(bf16[4,448,128]{2,1,0:T(8,128)(2,1)S(1)} %get-tuple-element.30), channel_id=1, source_target_pairs={{0,1},{1,0},{2,3},{3,2},{4,5},{5,4},{6,7},{7,6},{8,9},{9,8},{10,11... | collective-permute-start | bytes 1376264 | tf_op jit(solution)/shard_map/ppermute | solution.py:271
  6.9 8.1 %collective-permute-start.5 = (bf16[4,192,128]{2,1,0:T(8,128)(2,1)S(1)}, bf16[4,192,128]{2,1,0:T(8,128)(2,1)S(1)}, u32[]{:S(2)}, u32[]{:S(2)}) collective-permute-start(bf16[4,192,128]{2,1,0:T(8,128)(2,1)S(1)} %get-tuple-element.34), channel_id=1, source_target_pairs={{0,2},{1,3},{2,0},{3,1},{4,6},{5,7},{6,4},{7,5},{8,10},{9,11},{10,... | collective-permute-start | bytes 589832 | tf_op jit(solution)/shard_map/ppermute | solution.py:271
  9.5 9.8 %collective-permute-start.3 = (bf16[2,4,32,128]{3,2,1,0:T(8,128)(2,1)S(1)}, bf16[2,4,32,128]{3,2,1,0:T(8,128)(2,1)S(1)}, u32[]{:S(2)}, u32[]{:S(2)}) collective-permute-start(bf16[2,4,32,128]{3,2,1,0:T(8,128)(2,1)S(1)} %get-tuple-element.32), channel_id=1, source_target_pairs={{0,8},{4,12},{8,0},{12,4},{1,9},{5,13},{9,1},{13,5},{2,10},{6,14},... | collective-permute-start | bytes 196616 | tf_op jit(solution)/shard_map/ppermute | solution.py:271
  12.1 7.4 %collective-permute-start.4 = (bf16[2,4,32,128]{3,2,1,0:T(8,128)(2,1)S(1)}, bf16[2,4,32,128]{3,2,1,0:T(8,128)(2,1)S(1)}, u32[]{:S(2)}, u32[]{:S(2)}) collective-permute-start(bf16[2,4,32,128]{3,2,1,0:T(8,128)(2,1)S(1)} %get-tuple-element.33), channel_id=1, source_target_pairs={{0,12},{4,8},{8,4},{12,0},{1,13},{5,9},{9,5},{13,1},{2,14},{6,10},... | collective-permute-start | bytes 196616 | tf_op jit(solution)/shard_map/ppermute | solution.py:271
  13.5 9.3 %collective-permute-start.2 = (bf16[4,128,128]{2,1,0:T(8,128)(2,1)S(1)}, bf16[4,128,128]{2,1,0:T(8,128)(2,1)S(1)}, u32[]{:S(2)}, u32[]{:S(2)}) collective-permute-start(bf16[4,128,128]{2,1,0:T(8,128)(2,1)S(1)} %get-tuple-element.31), channel_id=1, source_target_pairs={{0,4},{4,0},{8,12},{12,8},{1,5},{5,1},{9,13},{13,9},{2,6},{6,2},{1... | collective-permute-start | bytes 393224 | tf_op jit(solution)/shard_map/ppermute | solution.py:271
  15.1 10.8 %collective-permute-start.8 = (bf16[4,96,128]{2,1,0:T(8,128)(2,1)S(1)}, bf16[4,96,128]{2,1,0:T(8,128)(2,1)S(1)}, u32[]{:S(2)}, u32[]{:S(2)}) collective-permute-start(bf16[4,96,128]{2,1,0:T(8,128)(2,1)S(1)} %get-tuple-element.40), channel_id=1, source_target_pairs={{0,8},{4,12},{8,0},{12,4},{1,9},{5,13},{9,1},{13,5},{2,10},{6,14},... | collective-permute-start | bytes 294920 | tf_op jit(solution)/shard_map/ppermute | solution.py:271
  18.0 7.9 %collective-permute-start.9 = (bf16[4,96,128]{2,1,0:T(8,128)(2,1)S(1)}, bf16[4,96,128]{2,1,0:T(8,128)(2,1)S(1)}, u32[]{:S(2)}, u32[]{:S(2)}) collective-permute-start(bf16[4,96,128]{2,1,0:T(8,128)(2,1)S(1)} %get-tuple-element.36.after_ref), channel_id=1, source_target_pairs={{0,12},{4,8},{8,4},{12,0},{1,13},{5,9},{9,5},{13,1},{2,14},{6,10},... | collective-permute-start | bytes 294920 | tf_op jit(solution)/shard_map/ppermute | solution.py:271
  19.3 7.9 %collective-permute-start.6 = (bf16[4,128,128]{2,1,0:T(8,128)(2,1)S(1)}, bf16[4,128,128]{2,1,0:T(8,128)(2,1)S(1)}, u32[]{:S(2)}, u32[]{:S(2)}) collective-permute-start(bf16[4,128,128]{2,1,0:T(8,128)(2,1)S(1)} %get-tuple-element.38), channel_id=1, source_target_pairs={{0,4},{4,0},{8,12},{12,8},{1,5},{5,1},{9,13},{13,9},{2,6},{6,2},{1... | collective-permute-start | bytes 393224 | tf_op jit(solution)/shard_map/ppermute | solution.py:271
  22.9 5.0 %collective-permute-start.7 = (bf16[4,128,128]{2,1,0:T(8,128)(2,1)S(1)}, bf16[4,128,128]{2,1,0:T(8,128)(2,1)S(1)}, u32[]{:S(2)}, u32[]{:S(2)}) collective-permute-start(bf16[4,128,128]{2,1,0:T(8,128)(2,1)S(1)} %get-tuple-element.39), channel_id=1, source_target_pairs={{0,2},{1,3},{2,0},{3,1},{4,6},{5,7},{6,4},{7,5},{8,10},{9,11},{10,... | collective-permute-start | bytes 393224 | tf_op jit(solution)/shard_map/ppermute | solution.py:271

commit v13 on v12

--- a/solution.py
+++ b/solution.py
@@ -240,6 +240,11 @@
             if first:
                 parts += [two_ref[n], three_ref[n]]
             out_ref[:, first:last, :] = total(*parts).astype(out_ref.dtype)
+
+
+def widen_kernel(one_ref, after_ref, sum_ref):
+    del after_ref
+    sum_ref[...] = one_ref[...].astype(jnp.float32)
 
 
 def far_sum_kernel(two_ref, three_ref, sum_ref):
@@ -370,6 +375,8 @@
         span=3,
     )
     near = jax.ShapeDtypeStruct((targets, strip, strip), jnp.float32)
+    one_wide = jax.ShapeDtypeStruct(one.shape, jnp.float32)
+    one = call(widen_kernel, one_wide, one, own[0], span=3)
     here, near = call(
         here_kernel,
         [like(targets, strip), near],

time: 28.8 us -> 29.1 us (1.010)
  waiting for transfers between devices: 9.55 us -> 9.93 us
    ppermute x10, waiting for transfers between devices: 9.55 us -> 9.93 us  [swap(): lax.ppermute(array, axis, [(i, i ^ mask) for i in range(lax.axis_size(axi...]
    pallas_call x5 -> x6, Pallas kernels: 1.05 us -> 1.07 us  [call(): pl.pallas_call(kernel, out_shape=out_shape, in_specs=[vmem] * len(args),...]
where the time goes in v13:
time: 29.1 us; the launch traced here: 28.9 us
  starting transfers between devices  12.2 us (42%)
  waiting for transfers between devices  9.93 us (34%)
  Pallas kernels  6.74 us (23%)
    ppermute x10, starting transfers between devices, swap(): lax.ppermute(array, axis, [(i, i ^ mask) for i in range(lax.axis_size(axi...  12.2 us
    ppermute x10, waiting for transfers between devices, swap(): lax.ppermute(array, axis, [(i, i ^ mask) for i in range(lax.axis_size(axi...  9.93 us
    pallas_call x1, Pallas kernels, by_targets(): pl.pallas_call(send_kernel, out_shape=[lead_shape, rest_shape, half_shape...  4.17 us
    pallas_call x1, Pallas kernels, by_targets(): pl.pallas_call(keep_kernel, out_shape=[lead_shape, rest_shape, like(targe...  1.5 us
    pallas_call x6, Pallas kernels, call(): pl.pallas_call(kernel, out_shape=out_shape, in_specs=[vmem] * len(args),...  1.07 us
  transfers between devices with their start and end apart: 10, of which 6 were waited for; matrix products, arithmetic and copies ran while one was open for 0% of the time, Pallas kernels for 6%

profile of v13, /device:TPU:0, one launch (start us, length us, event | category | flops | bytes accessed | tf_op | source)
XLA Modules:
  0.0 28.9 jit_solution(17811980769884811838)
XLA Ops:
  0.0 4.2 %send_kernel.1 = (bf16[4,576,128]{2,1,0:T(8,128)(2,1)S(1)}, bf16[4,448,128]{2,1,0:T(8,128)(2,1)S(1)}, bf16[3,512,512]{2,1,0:T(8,128)(2,1)S(1)}, bf16[3,256,512]{2,1,0:T(8,128)(2,1)S(1)}) custom-call(s32[1,3]{1,0:T(1,128)} %cls_hbm.3, s32[1,3]{1,0:T(1,128)} %tid_hbm.3, s32[4,5]{1,0:T(4,128)} %pair_hbm.3, s32[2,4]{1,0:T(2,128)} %bitcast.1, f32[50]{0:T(128)} %coef_hbm.3, ...), custom_call_target="tpu_custom_call" | custom-call | flops 1207959552 | bytes 4194304 | tf_op jit(solution)/shard_map/send_kernel/pallas_call | solution.py:319
  4.2 0.5 %collective-permute-start = (bf16[4,576,128]{2,1,0:T(8,128)(2,1)S(1)}, bf16[4,576,128]{2,1,0:T(8,128)(2,1)S(1)}, u32[]{:S(2)}, u32[]{:S(2)}) collective-permute-start(bf16[4,576,128]{2,1,0:T(8,128)(2,1)S(1)} %get-tuple-element.28), channel_id=1, source_target_pairs={{0,1},{1,0},{2,3},{3,2},{4,5},{5,4},{6,7},{7,6},{8,9},{9,8},{10,11... | collective-permute-start | bytes 1769480 | tf_op jit(solution)/shard_map/ppermute | solution.py:276
  4.7 1.5 %keep_kernel.1 = (bf16[4,576,128]{2,1,0:T(8,128)(2,1)S(1)}, bf16[4,448,128]{2,1,0:T(8,128)(2,1)S(1)}, bf16[4,128,128]{2,1,0:T(8,128)(2,1)S(1)}) custom-call(s32[1,3]{1,0:T(1,128)} %cls_hbm.3, s32[1,3]{1,0:T(1,128)} %tid_hbm.3, s32[4,5]{1,0:T(4,128)} %pair_hbm.3, s32[2,4]{1,0:T(2,128)} %bitcast.2, f32[50]{0:T(128)} %coef_hbm.3, ...), custom_call_target="tpu_custom_call" | custom-call | flops 1207959552 | tf_op jit(solution)/shard_map/keep_kernel/pallas_call | solution.py:341
  6.2 0.1 collective-permute-done.recv_ref
  6.3 0.1 lead_kernel.1
  6.5 0.4 %collective-permute-start.1 = (bf16[4,448,128]{2,1,0:T(8,128)(2,1)S(1)}, bf16[4,448,128]{2,1,0:T(8,128)(2,1)S(1)}, u32[]{:S(2)}, u32[]{:S(2)}) collective-permute-start(bf16[4,448,128]{2,1,0:T(8,128)(2,1)S(1)} %get-tuple-element.30), channel_id=1, source_target_pairs={{0,1},{1,0},{2,3},{3,2},{4,5},{5,4},{6,7},{7,6},{8,9},{9,8},{10,11... | collective-permute-start | bytes 1376264 | tf_op jit(solution)/shard_map/ppermute | solution.py:276
  6.9 2.6 %collective-permute-start.3 = (bf16[4,192,128]{2,1,0:T(8,128)(2,1)S(1)}, bf16[4,192,128]{2,1,0:T(8,128)(2,1)S(1)}, u32[]{:S(2)}, u32[]{:S(2)}) collective-permute-start(bf16[4,192,128]{2,1,0:T(8,128)(2,1)S(1)} %get-tuple-element.32), channel_id=1, source_target_pairs={{0,2},{1,3},{2,0},{3,1},{4,6},{5,7},{6,4},{7,5},{8,10},{9,11},{10,... | collective-permute-start | bytes 589832 | tf_op jit(solution)/shard_map/ppermute | solution.py:276
  9.5 2.6 %collective-permute-start.4 = (bf16[2,4,32,128]{3,2,1,0:T(8,128)(2,1)S(1)}, bf16[2,4,32,128]{3,2,1,0:T(8,128)(2,1)S(1)}, u32[]{:S(2)}, u32[]{:S(2)}) collective-permute-start(bf16[2,4,32,128]{3,2,1,0:T(8,128)(2,1)S(1)} %get-tuple-element.35), channel_id=1, source_target_pairs={{0,8},{4,12},{8,0},{12,4},{1,9},{5,13},{9,1},{13,5},{2,10},{6,14},... | collective-permute-start | bytes 196616 | tf_op jit(solution)/shard_map/ppermute | solution.py:276
  12.1 1.3 %collective-permute-start.5 = (bf16[2,4,32,128]{3,2,1,0:T(8,128)(2,1)S(1)}, bf16[2,4,32,128]{3,2,1,0:T(8,128)(2,1)S(1)}, u32[]{:S(2)}, u32[]{:S(2)}) collective-permute-start(bf16[2,4,32,128]{3,2,1,0:T(8,128)(2,1)S(1)} %get-tuple-element.36), channel_id=1, source_target_pairs={{0,12},{4,8},{8,4},{12,0},{1,13},{5,9},{9,5},{13,1},{2,14},{6,10},... | collective-permute-start | bytes 196616 | tf_op jit(solution)/shard_map/ppermute | solution.py:276
  13.5 0.2 collective-permute-start.2
  13.7 1.3 %collective-permute-done.3.cross_ref = bf16[4,192,128]{2,1,0:T(8,128)(2,1)S(1)} collective-permute-done((bf16[4,192,128]{2,1,0:T(8,128)(2,1)S(1)}, bf16[4,192,128]{2,1,0:T(8,128)(2,1)S(1)}, u32[]{:S(2)}, u32[]{:S(2)}) %collective-permute-start.3) | collective-permute-done | bytes 196640 | tf_op jit(solution)/shard_map/ppermute | solution.py:276
  15.0 0.0 collective-permute-done.1.recv_ref
  15.0 0.1 own_kernel.1
  15.1 2.9 %collective-permute-start.8 = (bf16[4,96,128]{2,1,0:T(8,128)(2,1)S(1)}, bf16[4,96,128]{2,1,0:T(8,128)(2,1)S(1)}, u32[]{:S(2)}, u32[]{:S(2)}) collective-permute-start(bf16[4,96,128]{2,1,0:T(8,128)(2,1)S(1)} %get-tuple-element.40), channel_id=1, source_target_pairs={{0,8},{4,12},{8,0},{12,4},{1,9},{5,13},{9,1},{13,5},{2,10},{6,14},... | collective-permute-start | bytes 294920 | tf_op jit(solution)/shard_map/ppermute | solution.py:276
  18.0 1.4 %collective-permute-start.9 = (bf16[4,96,128]{2,1,0:T(8,128)(2,1)S(1)}, bf16[4,96,128]{2,1,0:T(8,128)(2,1)S(1)}, u32[]{:S(2)}, u32[]{:S(2)}) collective-permute-start(bf16[4,96,128]{2,1,0:T(8,128)(2,1)S(1)} %get-tuple-element.34.after_ref), channel_id=1, source_target_pairs={{0,12},{4,8},{8,4},{12,0},{1,13},{5,9},{9,5},{13,1},{2,14},{6,10},... | collective-permute-start | bytes 294920 | tf_op jit(solution)/shard_map/ppermute | solution.py:276
  19.3 2.5 %collective-permute-done.2.one_ref = bf16[4,128,128]{2,1,0:T(8,128)(2,1)S(1)} collective-permute-done((bf16[4,128,128]{2,1,0:T(8,128)(2,1)S(1)}, bf16[4,128,128]{2,1,0:T(8,128)(2,1)S(1)}, u32[]{:S(2)}, u32[]{:S(2)}) %collective-permute-start.2) | collective-permute-done | bytes 131104 | tf_op jit(solution)/shard_map/ppermute | solution.py:276
  21.8 0.0 collective-permute-done.4.two_ref
  21.8 0.0 collective-permute-done.5.three_ref
  21.8 0.1 here_kernel.1
  21.9 0.1 collective-permute-start.7
  22.0 0.1 collective-permute-start.6
  22.1 3.8 %collective-permute-done.8.two_ref = bf16[4,96,128]{2,1,0:T(8,128)(2,1)S(1)} collective-permute-done((bf16[4,96,128]{2,1,0:T(8,128)(2,1)S(1)}, bf16[4,96,128]{2,1,0:T(8,128)(2,1)S(1)}, u32[]{:S(2)}, u32[]{:S(2)}) %collective-permute-start.8) | collective-permute-done | bytes 98336 | tf_op jit(solution)/shard_map/ppermute | solution.py:276
  25.9 0.0 collective-permute-done.9.three_ref
  25.9 1.1 %collective-permute-done.7.cross_ref = bf16[4,128,128]{2,1,0:T(8,128)(2,1)S(1)} collective-permute-done((bf16[4,128,128]{2,1,0:T(8,128)(2,1)S(1)}, bf16[4,128,128]{2,1,0:T(8,128)(2,1)S(1)}, u32[]{:S(2)}, u32[]{:S(2)}) %collective-permute-start.7) | collective-permute-done | bytes 131104 | tf_op jit(solution)/shard_map/ppermute | solution.py:276
  27.0 1.2 %collective-permute-done.6.one_ref = bf16[4,128,128]{2,1,0:T(8,128)(2,1)S(1)} collective-permute-done((bf16[4,128,128]{2,1,0:T(8,128)(2,1)S(1)}, bf16[4,128,128]{2,1,0:T(8,128)(2,1)S(1)}, u32[]{:S(2)}, u32[]{:S(2)}) %collective-permute-start.6) | collective-permute-done | bytes 131104 | tf_op jit(solution)/shard_map/ppermute | solution.py:276
  28.2 0.7 %final_kernel.1 = bf16[4,128,128]{2,1,0:T(8,128)(2,1)} custom-call(bf16[4,128,128]{2,1,0:T(8,128)(2,1)S(1)} %get-tuple-element.25.mask_ref, f32[4,128,128]{2,1,0:T(8,128)S(1)} %get-tuple-element.37.near_ref, bf16[4,128,128]{2,1,0:T(8,128)(2,1)S(1)} %collective-permute-done.6.one_ref, bf16[4,128,128]{2,1,0:T(8,128)(2,1)S(1)} %collective-permute-done.7.cross_ref, ...), custom_call_target="tpu_custom_call" | custom-call | flops 100000000 | tf_op jit(solution)/shard_map/final_kernel/pallas_call | solution.py:295
  (2 shorter events, 0.0 us)
Async XLA Ops:
  4.2 2.2 %collective-permute-start = (bf16[4,576,128]{2,1,0:T(8,128)(2,1)S(1)}, bf16[4,576,128]{2,1,0:T(8,128)(2,1)S(1)}, u32[]{:S(2)}, u32[]{:S(2)}) collective-permute-start(bf16[4,576,128]{2,1,0:T(8,128)(2,1)S(1)} %get-tuple-element.28), channel_id=1, source_target_pairs={{0,1},{1,0},{2,3},{3,2},{4,5},{5,4},{6,7},{7,6},{8,9},{9,8},{10,11... | collective-permute-start | bytes 1769480 | tf_op jit(solution)/shard_map/ppermute | solution.py:276
  6.5 8.5 %collective-permute-start.1 = (bf16[4,448,128]{2,1,0:T(8,128)(2,1)S(1)}, bf16[4,448,128]{2,1,0:T(8,128)(2,1)S(1)}, u32[]{:S(2)}, u32[]{:S(2)}) collective-permute-start(bf16[4,448,128]{2,1,0:T(8,128)(2,1)S(1)} %get-tuple-element.30), channel_id=1, source_target_pairs={{0,1},{1,0},{2,3},{3,2},{4,5},{5,4},{6,7},{7,6},{8,9},{9,8},{10,11... | collective-permute-start | bytes 1376264 | tf_op jit(solution)/shard_map/ppermute | solution.py:276
  6.9 8.1 %collective-permute-start.3 = (bf16[4,192,128]{2,1,0:T(8,128)(2,1)S(1)}, bf16[4,192,128]{2,1,0:T(8,128)(2,1)S(1)}, u32[]{:S(2)}, u32[]{:S(2)}) collective-permute-start(bf16[4,192,128]{2,1,0:T(8,128)(2,1)S(1)} %get-tuple-element.32), channel_id=1, source_target_pairs={{0,2},{1,3},{2,0},{3,1},{4,6},{5,7},{6,4},{7,5},{8,10},{9,11},{10,... | collective-permute-start | bytes 589832 | tf_op jit(solution)/shard_map/ppermute | solution.py:276
  9.5 12.3 %collective-permute-start.4 = (bf16[2,4,32,128]{3,2,1,0:T(8,128)(2,1)S(1)}, bf16[2,4,32,128]{3,2,1,0:T(8,128)(2,1)S(1)}, u32[]{:S(2)}, u32[]{:S(2)}) collective-permute-start(bf16[2,4,32,128]{3,2,1,0:T(8,128)(2,1)S(1)} %get-tuple-element.35), channel_id=1, source_target_pairs={{0,8},{4,12},{8,0},{12,4},{1,9},{5,13},{9,1},{13,5},{2,10},{6,14},... | collective-permute-start | bytes 196616 | tf_op jit(solution)/shard_map/ppermute | solution.py:276
  12.1 9.7 %collective-permute-start.5 = (bf16[2,4,32,128]{3,2,1,0:T(8,128)(2,1)S(1)}, bf16[2,4,32,128]{3,2,1,0:T(8,128)(2,1)S(1)}, u32[]{:S(2)}, u32[]{:S(2)}) collective-permute-start(bf16[2,4,32,128]{3,2,1,0:T(8,128)(2,1)S(1)} %get-tuple-element.36), channel_id=1, source_target_pairs={{0,12},{4,8},{8,4},{12,0},{1,13},{5,9},{9,5},{13,1},{2,14},{6,10},... | collective-permute-start | bytes 196616 | tf_op jit(solution)/shard_map/ppermute | solution.py:276
  13.5 8.3 %collective-permute-start.2 = (bf16[4,128,128]{2,1,0:T(8,128)(2,1)S(1)}, bf16[4,128,128]{2,1,0:T(8,128)(2,1)S(1)}, u32[]{:S(2)}, u32[]{:S(2)}) collective-permute-start(bf16[4,128,128]{2,1,0:T(8,128)(2,1)S(1)} %get-tuple-element.31), channel_id=1, source_target_pairs={{0,4},{4,0},{8,12},{12,8},{1,5},{5,1},{9,13},{13,9},{2,6},{6,2},{1... | collective-permute-start | bytes 393224 | tf_op jit(solution)/shard_map/ppermute | solution.py:276
  15.1 10.8 %collective-permute-start.8 = (bf16[4,96,128]{2,1,0:T(8,128)(2,1)S(1)}, bf16[4,96,128]{2,1,0:T(8,128)(2,1)S(1)}, u32[]{:S(2)}, u32[]{:S(2)}) collective-permute-start(bf16[4,96,128]{2,1,0:T(8,128)(2,1)S(1)} %get-tuple-element.40), channel_id=1, source_target_pairs={{0,8},{4,12},{8,0},{12,4},{1,9},{5,13},{9,1},{13,5},{2,10},{6,14},... | collective-permute-start | bytes 294920 | tf_op jit(solution)/shard_map/ppermute | solution.py:276
  18.0 7.9 %collective-permute-start.9 = (bf16[4,96,128]{2,1,0:T(8,128)(2,1)S(1)}, bf16[4,96,128]{2,1,0:T(8,128)(2,1)S(1)}, u32[]{:S(2)}, u32[]{:S(2)}) collective-permute-start(bf16[4,96,128]{2,1,0:T(8,128)(2,1)S(1)} %get-tuple-element.34.after_ref), channel_id=1, source_target_pairs={{0,12},{4,8},{8,4},{12,0},{1,13},{5,9},{9,5},{13,1},{2,14},{6,10},... | collective-permute-start | bytes 294920 | tf_op jit(solution)/shard_map/ppermute | solution.py:276
  21.9 5.0 %collective-permute-start.7 = (bf16[4,128,128]{2,1,0:T(8,128)(2,1)S(1)}, bf16[4,128,128]{2,1,0:T(8,128)(2,1)S(1)}, u32[]{:S(2)}, u32[]{:S(2)}) collective-permute-start(bf16[4,128,128]{2,1,0:T(8,128)(2,1)S(1)} %get-tuple-element.39), channel_id=1, source_target_pairs={{0,2},{1,3},{2,0},{3,1},{4,6},{5,7},{6,4},{7,5},{8,10},{9,11},{10,... | collective-permute-start | bytes 393224 | tf_op jit(solution)/shard_map/ppermute | solution.py:276
  22.0 6.2 %collective-permute-start.6 = (bf16[4,128,128]{2,1,0:T(8,128)(2,1)S(1)}, bf16[4,128,128]{2,1,0:T(8,128)(2,1)S(1)}, u32[]{:S(2)}, u32[]{:S(2)}) collective-permute-start(bf16[4,128,128]{2,1,0:T(8,128)(2,1)S(1)} %get-tuple-element.38), channel_id=1, source_target_pairs={{0,4},{4,0},{8,12},{12,8},{1,5},{5,1},{9,13},{13,9},{2,6},{6,2},{1... | collective-permute-start | bytes 393224 | tf_op jit(solution)/shard_map/ppermute | solution.py:276

commit v14 on v12

--- a/solution.py
+++ b/solution.py
@@ -240,6 +240,10 @@
             if first:
                 parts += [two_ref[n], three_ref[n]]
             out_ref[:, first:last, :] = total(*parts).astype(out_ref.dtype)
+
+
+def widen_kernel(one_ref, sum_ref):
+    sum_ref[...] = one_ref[...].astype(jnp.float32)
 
 
 def far_sum_kernel(two_ref, three_ref, sum_ref):
@@ -370,6 +374,8 @@
         span=3,
     )
     near = jax.ShapeDtypeStruct((targets, strip, strip), jnp.float32)
+    one_wide = jax.ShapeDtypeStruct(one.shape, jnp.float32)
+    one = call(widen_kernel, one_wide, one, span=.1)
     here, near = call(
         here_kernel,
         [like(targets, strip), near],

time: 28.8 us -> 29.1 us (1.010)
  starting transfers between devices: 12.3 us -> 13.1 us
  waiting for transfers between devices: 9.55 us -> 9 us
    ppermute x10, starting transfers between devices: 12.3 us -> 13.1 us  [swap(): lax.ppermute(array, axis, [(i, i ^ mask) for i in range(lax.axis_size(axi...]
    ppermute x10, waiting for transfers between devices: 9.55 us -> 9 us  [swap(): lax.ppermute(array, axis, [(i, i ^ mask) for i in range(lax.axis_size(axi...]
    pallas_call x5 -> x6, Pallas kernels: 1.05 us -> 1.07 us  [call(): pl.pallas_call(kernel, out_shape=out_shape, in_specs=[vmem] * len(args),...]
  transfers between devices with their start and end apart: 10 -> 10, of which waited for: 6 -> 4; matrix products, arithmetic and copies ran while one was open for 0% -> 0% of each run, Pallas kernels for 6% -> 6%
where the time goes in v14:
time: 29.1 us; the launch traced here: 28.9 us
  starting transfers between devices  13.1 us (45%)
  waiting for transfers between devices  9 us (31%)
  Pallas kernels  6.74 us (23%)
    ppermute x10, starting transfers between devices, swap(): lax.ppermute(array, axis, [(i, i ^ mask) for i in range(lax.axis_size(axi...  13.1 us
    ppermute x10, waiting for transfers between devices, swap(): lax.ppermute(array, axis, [(i, i ^ mask) for i in range(lax.axis_size(axi...  9 us
    pallas_call x1, Pallas kernels, by_targets(): pl.pallas_call(send_kernel, out_shape=[lead_shape, rest_shape, half_shape...  4.17 us
    pallas_call x1, Pallas kernels, by_targets(): pl.pallas_call(keep_kernel, out_shape=[lead_shape, rest_shape, like(targe...  1.5 us
    pallas_call x6, Pallas kernels, call(): pl.pallas_call(kernel, out_shape=out_shape, in_specs=[vmem] * len(args),...  1.07 us
  transfers between devices with their start and end apart: 10, of which 4 were waited for; matrix products, arithmetic and copies ran while one was open for 0% of the time, Pallas kernels for 6%

profile of v14, /device:TPU:0, one launch (start us, length us, event | category | flops | bytes accessed | tf_op | source)
XLA Modules:
  0.0 28.9 jit_solution(6407886802709541935)
XLA Ops:
  0.0 4.2 %send_kernel.1 = (bf16[4,576,128]{2,1,0:T(8,128)(2,1)S(1)}, bf16[4,448,128]{2,1,0:T(8,128)(2,1)S(1)}, bf16[3,512,512]{2,1,0:T(8,128)(2,1)S(1)}, bf16[3,256,512]{2,1,0:T(8,128)(2,1)S(1)}) custom-call(s32[1,3]{1,0:T(1,128)} %cls_hbm.3, s32[1,3]{1,0:T(1,128)} %tid_hbm.3, s32[4,5]{1,0:T(4,128)} %pair_hbm.3, s32[2,4]{1,0:T(2,128)} %bitcast.1, f32[50]{0:T(128)} %coef_hbm.3, ...), custom_call_target="tpu_custom_call" | custom-call | flops 1207959552 | bytes 4194304 | tf_op jit(solution)/shard_map/send_kernel/pallas_call | solution.py:318
  4.2 0.5 %collective-permute-start = (bf16[4,576,128]{2,1,0:T(8,128)(2,1)S(1)}, bf16[4,576,128]{2,1,0:T(8,128)(2,1)S(1)}, u32[]{:S(2)}, u32[]{:S(2)}) collective-permute-start(bf16[4,576,128]{2,1,0:T(8,128)(2,1)S(1)} %get-tuple-element.28), channel_id=1, source_target_pairs={{0,1},{1,0},{2,3},{3,2},{4,5},{5,4},{6,7},{7,6},{8,9},{9,8},{10,11... | collective-permute-start | bytes 1769480 | tf_op jit(solution)/shard_map/ppermute | solution.py:275
  4.7 1.5 %keep_kernel.1 = (bf16[4,576,128]{2,1,0:T(8,128)(2,1)S(1)}, bf16[4,448,128]{2,1,0:T(8,128)(2,1)S(1)}, bf16[4,128,128]{2,1,0:T(8,128)(2,1)S(1)}) custom-call(s32[1,3]{1,0:T(1,128)} %cls_hbm.3, s32[1,3]{1,0:T(1,128)} %tid_hbm.3, s32[4,5]{1,0:T(4,128)} %pair_hbm.3, s32[2,4]{1,0:T(2,128)} %bitcast.2, f32[50]{0:T(128)} %coef_hbm.3, ...), custom_call_target="tpu_custom_call" | custom-call | flops 1207959552 | tf_op jit(solution)/shard_map/keep_kernel/pallas_call | solution.py:340
  6.2 0.1 collective-permute-done.recv_ref
  6.3 0.1 lead_kernel.1
  6.5 0.4 %collective-permute-start.1 = (bf16[4,448,128]{2,1,0:T(8,128)(2,1)S(1)}, bf16[4,448,128]{2,1,0:T(8,128)(2,1)S(1)}, u32[]{:S(2)}, u32[]{:S(2)}) collective-permute-start(bf16[4,448,128]{2,1,0:T(8,128)(2,1)S(1)} %get-tuple-element.30), channel_id=1, source_target_pairs={{0,1},{1,0},{2,3},{3,2},{4,5},{5,4},{6,7},{7,6},{8,9},{9,8},{10,11... | collective-permute-start | bytes 1376264 | tf_op jit(solution)/shard_map/ppermute | solution.py:275
  6.9 2.6 %collective-permute-start.5 = (bf16[4,192,128]{2,1,0:T(8,128)(2,1)S(1)}, bf16[4,192,128]{2,1,0:T(8,128)(2,1)S(1)}, u32[]{:S(2)}, u32[]{:S(2)}) collective-permute-start(bf16[4,192,128]{2,1,0:T(8,128)(2,1)S(1)} %get-tuple-element.34), channel_id=1, source_target_pairs={{0,2},{1,3},{2,0},{3,1},{4,6},{5,7},{6,4},{7,5},{8,10},{9,11},{10,... | collective-permute-start | bytes 589832 | tf_op jit(solution)/shard_map/ppermute | solution.py:275
  9.5 1.6 %collective-permute-start.2 = (bf16[4,128,128]{2,1,0:T(8,128)(2,1)S(1)}, bf16[4,128,128]{2,1,0:T(8,128)(2,1)S(1)}, u32[]{:S(2)}, u32[]{:S(2)}) collective-permute-start(bf16[4,128,128]{2,1,0:T(8,128)(2,1)S(1)} %get-tuple-element.31), channel_id=1, source_target_pairs={{0,4},{4,0},{8,12},{12,8},{1,5},{5,1},{9,13},{13,9},{2,6},{6,2},{1... | collective-permute-start | bytes 393224 | tf_op jit(solution)/shard_map/ppermute | solution.py:275
  11.1 2.6 %collective-permute-start.3 = (bf16[2,4,32,128]{3,2,1,0:T(8,128)(2,1)S(1)}, bf16[2,4,32,128]{3,2,1,0:T(8,128)(2,1)S(1)}, u32[]{:S(2)}, u32[]{:S(2)}) collective-permute-start(bf16[2,4,32,128]{3,2,1,0:T(8,128)(2,1)S(1)} %get-tuple-element.32), channel_id=1, source_target_pairs={{0,8},{4,12},{8,0},{12,4},{1,9},{5,13},{9,1},{13,5},{2,10},{6,14},... | collective-permute-start | bytes 196616 | tf_op jit(solution)/shard_map/ppermute | solution.py:275
  13.7 0.2 collective-permute-start.4
  13.9 2.1 %collective-permute-done.2.one_ref = bf16[4,128,128]{2,1,0:T(8,128)(2,1)S(1)} collective-permute-done((bf16[4,128,128]{2,1,0:T(8,128)(2,1)S(1)}, bf16[4,128,128]{2,1,0:T(8,128)(2,1)S(1)}, u32[]{:S(2)}, u32[]{:S(2)}) %collective-permute-start.2) | collective-permute-done | bytes 131104 | tf_op jit(solution)/shard_map/ppermute | solution.py:275
  16.0 0.0 collective-permute-done.5.cross_ref
  16.0 0.0 collective-permute-done.1.recv_ref
  16.0 0.1 own_kernel.1
  16.1 2.4 %collective-permute-start.8 = (bf16[4,96,128]{2,1,0:T(8,128)(2,1)S(1)}, bf16[4,96,128]{2,1,0:T(8,128)(2,1)S(1)}, u32[]{:S(2)}, u32[]{:S(2)}) collective-permute-start(bf16[4,96,128]{2,1,0:T(8,128)(2,1)S(1)} %get-tuple-element.40), channel_id=1, source_target_pairs={{0,8},{4,12},{8,0},{12,4},{1,9},{5,13},{9,1},{13,5},{2,10},{6,14},... | collective-permute-start | bytes 294920 | tf_op jit(solution)/shard_map/ppermute | solution.py:275
  18.6 1.6 %collective-permute-start.9 = (bf16[4,96,128]{2,1,0:T(8,128)(2,1)S(1)}, bf16[4,96,128]{2,1,0:T(8,128)(2,1)S(1)}, u32[]{:S(2)}, u32[]{:S(2)}) collective-permute-start(bf16[4,96,128]{2,1,0:T(8,128)(2,1)S(1)} %get-tuple-element.36.after_ref), channel_id=1, source_target_pairs={{0,12},{4,8},{8,4},{12,0},{1,13},{5,9},{9,5},{13,1},{2,14},{6,10},... | collective-permute-start | bytes 294920 | tf_op jit(solution)/shard_map/ppermute | solution.py:275
  20.2 0.5 %collective-permute-start.6 = (bf16[4,128,128]{2,1,0:T(8,128)(2,1)S(1)}, bf16[4,128,128]{2,1,0:T(8,128)(2,1)S(1)}, u32[]{:S(2)}, u32[]{:S(2)}) collective-permute-start(bf16[4,128,128]{2,1,0:T(8,128)(2,1)S(1)} %get-tuple-element.38), channel_id=1, source_target_pairs={{0,4},{4,0},{8,12},{12,8},{1,5},{5,1},{9,13},{13,9},{2,6},{6,2},{1... | collective-permute-start | bytes 393224 | tf_op jit(solution)/shard_map/ppermute | solution.py:275
  20.7 0.0 collective-permute-done.3.two_ref
  20.7 0.0 collective-permute-done.4.three_ref
  20.7 0.1 here_kernel.1
  20.8 0.6 %collective-permute-start.7 = (bf16[4,128,128]{2,1,0:T(8,128)(2,1)S(1)}, bf16[4,128,128]{2,1,0:T(8,128)(2,1)S(1)}, u32[]{:S(2)}, u32[]{:S(2)}) collective-permute-start(bf16[4,128,128]{2,1,0:T(8,128)(2,1)S(1)} %get-tuple-element.39), channel_id=1, source_target_pairs={{0,2},{1,3},{2,0},{3,1},{4,6},{5,7},{6,4},{7,5},{8,10},{9,11},{10,... | collective-permute-start | bytes 393224 | tf_op jit(solution)/shard_map/ppermute | solution.py:275
  21.4 5.9 %collective-permute-done.8.two_ref = bf16[4,96,128]{2,1,0:T(8,128)(2,1)S(1)} collective-permute-done((bf16[4,96,128]{2,1,0:T(8,128)(2,1)S(1)}, bf16[4,96,128]{2,1,0:T(8,128)(2,1)S(1)}, u32[]{:S(2)}, u32[]{:S(2)}) %collective-permute-start.8) | collective-permute-done | bytes 98336 | tf_op jit(solution)/shard_map/ppermute | solution.py:275
  27.3 0.0 collective-permute-done.9.three_ref
  27.3 0.9 %collective-permute-done.6.one_ref = bf16[4,128,128]{2,1,0:T(8,128)(2,1)S(1)} collective-permute-done((bf16[4,128,128]{2,1,0:T(8,128)(2,1)S(1)}, bf16[4,128,128]{2,1,0:T(8,128)(2,1)S(1)}, u32[]{:S(2)}, u32[]{:S(2)}) %collective-permute-start.6) | collective-permute-done | bytes 131104 | tf_op jit(solution)/shard_map/ppermute | solution.py:275
  28.2 0.0 collective-permute-done.7.cross_ref
  28.2 0.7 %final_kernel.1 = bf16[4,128,128]{2,1,0:T(8,128)(2,1)} custom-call(bf16[4,128,128]{2,1,0:T(8,128)(2,1)S(1)} %get-tuple-element.25.mask_ref, f32[4,128,128]{2,1,0:T(8,128)S(1)} %get-tuple-element.37.near_ref, bf16[4,128,128]{2,1,0:T(8,128)(2,1)S(1)} %collective-permute-done.6.one_ref, bf16[4,128,128]{2,1,0:T(8,128)(2,1)S(1)} %collective-permute-done.7.cross_ref, ...), custom_call_target="tpu_custom_call" | custom-call | flops 100000000 | tf_op jit(solution)/shard_map/final_kernel/pallas_call | solution.py:294
  (2 shorter events, 0.0 us)
Async XLA Ops:
  4.2 2.2 %collective-permute-start = (bf16[4,576,128]{2,1,0:T(8,128)(2,1)S(1)}, bf16[4,576,128]{2,1,0:T(8,128)(2,1)S(1)}, u32[]{:S(2)}, u32[]{:S(2)}) collective-permute-start(bf16[4,576,128]{2,1,0:T(8,128)(2,1)S(1)} %get-tuple-element.28), channel_id=1, source_target_pairs={{0,1},{1,0},{2,3},{3,2},{4,5},{5,4},{6,7},{7,6},{8,9},{9,8},{10,11... | collective-permute-start | bytes 1769480 | tf_op jit(solution)/shard_map/ppermute | solution.py:275
  6.5 9.6 %collective-permute-start.1 = (bf16[4,448,128]{2,1,0:T(8,128)(2,1)S(1)}, bf16[4,448,128]{2,1,0:T(8,128)(2,1)S(1)}, u32[]{:S(2)}, u32[]{:S(2)}) collective-permute-start(bf16[4,448,128]{2,1,0:T(8,128)(2,1)S(1)} %get-tuple-element.30), channel_id=1, source_target_pairs={{0,1},{1,0},{2,3},{3,2},{4,5},{5,4},{6,7},{7,6},{8,9},{9,8},{10,11... | collective-permute-start | bytes 1376264 | tf_op jit(solution)/shard_map/ppermute | solution.py:275
  6.9 9.1 %collective-permute-start.5 = (bf16[4,192,128]{2,1,0:T(8,128)(2,1)S(1)}, bf16[4,192,128]{2,1,0:T(8,128)(2,1)S(1)}, u32[]{:S(2)}, u32[]{:S(2)}) collective-permute-start(bf16[4,192,128]{2,1,0:T(8,128)(2,1)S(1)} %get-tuple-element.34), channel_id=1, source_target_pairs={{0,2},{1,3},{2,0},{3,1},{4,6},{5,7},{6,4},{7,5},{8,10},{9,11},{10,... | collective-permute-start | bytes 589832 | tf_op jit(solution)/shard_map/ppermute | solution.py:275
  9.5 6.5 %collective-permute-start.2 = (bf16[4,128,128]{2,1,0:T(8,128)(2,1)S(1)}, bf16[4,128,128]{2,1,0:T(8,128)(2,1)S(1)}, u32[]{:S(2)}, u32[]{:S(2)}) collective-permute-start(bf16[4,128,128]{2,1,0:T(8,128)(2,1)S(1)} %get-tuple-element.31), channel_id=1, source_target_pairs={{0,4},{4,0},{8,12},{12,8},{1,5},{5,1},{9,13},{13,9},{2,6},{6,2},{1... | collective-permute-start | bytes 393224 | tf_op jit(solution)/shard_map/ppermute | solution.py:275
  11.1 9.6 %collective-permute-start.3 = (bf16[2,4,32,128]{3,2,1,0:T(8,128)(2,1)S(1)}, bf16[2,4,32,128]{3,2,1,0:T(8,128)(2,1)S(1)}, u32[]{:S(2)}, u32[]{:S(2)}) collective-permute-start(bf16[2,4,32,128]{3,2,1,0:T(8,128)(2,1)S(1)} %get-tuple-element.32), channel_id=1, source_target_pairs={{0,8},{4,12},{8,0},{12,4},{1,9},{5,13},{9,1},{13,5},{2,10},{6,14},... | collective-permute-start | bytes 196616 | tf_op jit(solution)/shard_map/ppermute | solution.py:275
  13.7 7.0 %collective-permute-start.4 = (bf16[2,4,32,128]{3,2,1,0:T(8,128)(2,1)S(1)}, bf16[2,4,32,128]{3,2,1,0:T(8,128)(2,1)S(1)}, u32[]{:S(2)}, u32[]{:S(2)}) collective-permute-start(bf16[2,4,32,128]{3,2,1,0:T(8,128)(2,1)S(1)} %get-tuple-element.33), channel_id=1, source_target_pairs={{0,12},{4,8},{8,4},{12,0},{1,13},{5,9},{9,5},{13,1},{2,14},{6,10},... | collective-permute-start | bytes 196616 | tf_op jit(solution)/shard_map/ppermute | solution.py:275
  16.1 11.2 %collective-permute-start.8 = (bf16[4,96,128]{2,1,0:T(8,128)(2,1)S(1)}, bf16[4,96,128]{2,1,0:T(8,128)(2,1)S(1)}, u32[]{:S(2)}, u32[]{:S(2)}) collective-permute-start(bf16[4,96,128]{2,1,0:T(8,128)(2,1)S(1)} %get-tuple-element.40), channel_id=1, source_target_pairs={{0,8},{4,12},{8,0},{12,4},{1,9},{5,13},{9,1},{13,5},{2,10},{6,14},... | collective-permute-start | bytes 294920 | tf_op jit(solution)/shard_map/ppermute | solution.py:275
  18.6 8.7 %collective-permute-start.9 = (bf16[4,96,128]{2,1,0:T(8,128)(2,1)S(1)}, bf16[4,96,128]{2,1,0:T(8,128)(2,1)S(1)}, u32[]{:S(2)}, u32[]{:S(2)}) collective-permute-start(bf16[4,96,128]{2,1,0:T(8,128)(2,1)S(1)} %get-tuple-element.36.after_ref), channel_id=1, source_target_pairs={{0,12},{4,8},{8,4},{12,0},{1,13},{5,9},{9,5},{13,1},{2,14},{6,10},... | collective-permute-start | bytes 294920 | tf_op jit(solution)/shard_map/ppermute | solution.py:275
  20.2 8.0 %collective-permute-start.6 = (bf16[4,128,128]{2,1,0:T(8,128)(2,1)S(1)}, bf16[4,128,128]{2,1,0:T(8,128)(2,1)S(1)}, u32[]{:S(2)}, u32[]{:S(2)}) collective-permute-start(bf16[4,128,128]{2,1,0:T(8,128)(2,1)S(1)} %get-tuple-element.38), channel_id=1, source_target_pairs={{0,4},{4,0},{8,12},{12,8},{1,5},{5,1},{9,13},{13,9},{2,6},{6,2},{1... | collective-permute-start | bytes 393224 | tf_op jit(solution)/shard_map/ppermute | solution.py:275
  20.8 7.4 %collective-permute-start.7 = (bf16[4,128,128]{2,1,0:T(8,128)(2,1)S(1)}, bf16[4,128,128]{2,1,0:T(8,128)(2,1)S(1)}, u32[]{:S(2)}, u32[]{:S(2)}) collective-permute-start(bf16[4,128,128]{2,1,0:T(8,128)(2,1)S(1)} %get-tuple-element.39), channel_id=1, source_target_pairs={{0,2},{1,3},{2,0},{3,1},{4,6},{5,7},{6,4},{7,5},{8,10},{9,11},{10,... | collective-permute-start | bytes 393224 | tf_op jit(solution)/shard_map/ppermute | solution.py:275

commit v15 on v11

--- a/solution.py
+++ b/solution.py
@@ -278,7 +278,7 @@
     terms = left_env.shape[1]
     targets = block_dims.shape[0]
     strip = width // 4
-    a_rows = strip * 3 // 4
+    a_rows = strip * 7 // 8
     b_rows = strip - a_rows
     vmem = pl.BlockSpec(memory_space=pltpu.VMEM)
     hbm = pl.BlockSpec(memory_space=pltpu.HBM)

time: 28.3 us -> 30 us (1.060)
  starting transfers between devices: 12.7 us -> 14 us
  waiting for transfers between devices: 8.64 us -> 8.99 us
    ppermute x10, starting transfers between devices: 12.7 us -> 14 us  [swap(): lax.ppermute(array, axis, [(i, i ^ mask) for i in range(lax.axis_size(axi...]
    ppermute x10, waiting for transfers between devices: 8.64 us -> 8.99 us  [swap(): lax.ppermute(array, axis, [(i, i ^ mask) for i in range(lax.axis_size(axi...]
  transfers between devices with their start and end apart: 10 -> 10, of which waited for: 5 -> 4; matrix products, arithmetic and copies ran while one was open for 0% -> 0% of each run, Pallas kernels for 6% -> 6%
where the time goes in v15:
time: 30 us; the launch traced here: 29.8 us
  starting transfers between devices  14 us (47%)
  waiting for transfers between devices  8.99 us (30%)
  Pallas kernels  6.73 us (22%)
    ppermute x10, starting transfers between devices, swap(): lax.ppermute(array, axis, [(i, i ^ mask) for i in range(lax.axis_size(axi...  14 us
    ppermute x10, waiting for transfers between devices, swap(): lax.ppermute(array, axis, [(i, i ^ mask) for i in range(lax.axis_size(axi...  8.99 us
    pallas_call x1, Pallas kernels, by_targets(): pl.pallas_call(send_kernel, out_shape=[lead_shape, rest_shape, half_shape...  4.17 us
    pallas_call x1, Pallas kernels, by_targets(): pl.pallas_call(keep_kernel, out_shape=[lead_shape, rest_shape, like(targe...  1.5 us
    pallas_call x5, Pallas kernels, call(): pl.pallas_call(kernel, out_shape=out_shape, in_specs=[vmem] * len(args),...  1.05 us
  transfers between devices with their start and end apart: 10, of which 4 were waited for; matrix products, arithmetic and copies ran while one was open for 0% of the time, Pallas kernels for 6%

profile of v15, /device:TPU:0, one launch (start us, length us, event | category | flops | bytes accessed | tf_op | source)
XLA Modules:
  0.0 29.8 jit_solution(9907540033950796671)
XLA Ops:
  0.0 4.2 %send_kernel.1 = (bf16[4,544,128]{2,1,0:T(8,128)(2,1)S(1)}, bf16[4,480,128]{2,1,0:T(8,128)(2,1)S(1)}, bf16[3,512,512]{2,1,0:T(8,128)(2,1)S(1)}, bf16[3,256,512]{2,1,0:T(8,128)(2,1)S(1)}) custom-call(s32[1,3]{1,0:T(1,128)} %cls_hbm.3, s32[1,3]{1,0:T(1,128)} %tid_hbm.3, s32[4,5]{1,0:T(4,128)} %pair_hbm.3, s32[2,4]{1,0:T(2,128)} %bitcast.1, f32[50]{0:T(128)} %coef_hbm.3, ...), custom_call_target="tpu_custom_call" | custom-call | flops 1207959552 | bytes 4194304 | tf_op jit(solution)/shard_map/send_kernel/pallas_call | solution.py:314
  4.2 0.5 %collective-permute-start = (bf16[4,544,128]{2,1,0:T(8,128)(2,1)S(1)}, bf16[4,544,128]{2,1,0:T(8,128)(2,1)S(1)}, u32[]{:S(2)}, u32[]{:S(2)}) collective-permute-start(bf16[4,544,128]{2,1,0:T(8,128)(2,1)S(1)} %get-tuple-element.28), channel_id=1, source_target_pairs={{0,1},{1,0},{2,3},{3,2},{4,5},{5,4},{6,7},{7,6},{8,9},{9,8},{10,11... | collective-permute-start | bytes 1671176 | tf_op jit(solution)/shard_map/ppermute | solution.py:271
  4.7 1.5 %keep_kernel.1 = (bf16[4,544,128]{2,1,0:T(8,128)(2,1)S(1)}, bf16[4,480,128]{2,1,0:T(8,128)(2,1)S(1)}, bf16[4,128,128]{2,1,0:T(8,128)(2,1)S(1)}) custom-call(s32[1,3]{1,0:T(1,128)} %cls_hbm.3, s32[1,3]{1,0:T(1,128)} %tid_hbm.3, s32[4,5]{1,0:T(4,128)} %pair_hbm.3, s32[2,4]{1,0:T(2,128)} %bitcast.2, f32[50]{0:T(128)} %coef_hbm.3, ...), custom_call_target="tpu_custom_call" | custom-call | flops 1207959552 | tf_op jit(solution)/shard_map/keep_kernel/pallas_call | solution.py:336
  6.2 0.1 collective-permute-done.recv_ref
  6.3 0.1 lead_kernel.1
  6.4 0.4 %collective-permute-start.1 = (bf16[4,480,128]{2,1,0:T(8,128)(2,1)S(1)}, bf16[4,480,128]{2,1,0:T(8,128)(2,1)S(1)}, u32[]{:S(2)}, u32[]{:S(2)}) collective-permute-start(bf16[4,480,128]{2,1,0:T(8,128)(2,1)S(1)} %get-tuple-element.30), channel_id=1, source_target_pairs={{0,1},{1,0},{2,3},{3,2},{4,5},{5,4},{6,7},{7,6},{8,9},{9,8},{10,11... | collective-permute-start | bytes 1474568 | tf_op jit(solution)/shard_map/ppermute | solution.py:271
  6.9 2.6 %collective-permute-start.5 = (bf16[4,224,128]{2,1,0:T(8,128)(2,1)S(1)}, bf16[4,224,128]{2,1,0:T(8,128)(2,1)S(1)}, u32[]{:S(2)}, u32[]{:S(2)}) collective-permute-start(bf16[4,224,128]{2,1,0:T(8,128)(2,1)S(1)} %get-tuple-element.34), channel_id=1, source_target_pairs={{0,2},{1,3},{2,0},{3,1},{4,6},{5,7},{6,4},{7,5},{8,10},{9,11},{10,... | collective-permute-start | bytes 688136 | tf_op jit(solution)/shard_map/ppermute | solution.py:271
  9.5 2.6 %collective-permute-start.3 = (bf16[2,4,16,128]{3,2,1,0:T(8,128)(2,1)S(1)}, bf16[2,4,16,128]{3,2,1,0:T(8,128)(2,1)S(1)}, u32[]{:S(2)}, u32[]{:S(2)}) collective-permute-start(bf16[2,4,16,128]{3,2,1,0:T(8,128)(2,1)S(1)} %get-tuple-element.32), channel_id=1, source_target_pairs={{0,8},{4,12},{8,0},{12,4},{1,9},{5,13},{9,1},{13,5},{2,10},{6,14},... | collective-permute-start | bytes 98312 | tf_op jit(solution)/shard_map/ppermute | solution.py:271
  12.1 1.3 %collective-permute-start.4 = (bf16[2,4,16,128]{3,2,1,0:T(8,128)(2,1)S(1)}, bf16[2,4,16,128]{3,2,1,0:T(8,128)(2,1)S(1)}, u32[]{:S(2)}, u32[]{:S(2)}) collective-permute-start(bf16[2,4,16,128]{3,2,1,0:T(8,128)(2,1)S(1)} %get-tuple-element.33), channel_id=1, source_target_pairs={{0,12},{4,8},{8,4},{12,0},{1,13},{5,9},{9,5},{13,1},{2,14},{6,10},... | collective-permute-start | bytes 98312 | tf_op jit(solution)/shard_map/ppermute | solution.py:271
  13.4 0.2 collective-permute-start.2
  13.7 2.0 %collective-permute-done.5.cross_ref = bf16[4,224,128]{2,1,0:T(8,128)(2,1)S(1)} collective-permute-done((bf16[4,224,128]{2,1,0:T(8,128)(2,1)S(1)}, bf16[4,224,128]{2,1,0:T(8,128)(2,1)S(1)}, u32[]{:S(2)}, u32[]{:S(2)}) %collective-permute-start.5) | collective-permute-done | bytes 229408 | tf_op jit(solution)/shard_map/ppermute | solution.py:271
  15.6 0.0 collective-permute-done.1.recv_ref
  15.6 0.1 own_kernel.1
  15.7 3.9 %collective-permute-start.9 = (bf16[4,112,128]{2,1,0:T(8,128)(2,1)S(1)}, bf16[4,112,128]{2,1,0:T(8,128)(2,1)S(1)}, u32[]{:S(2)}, u32[]{:S(2)}) collective-permute-start(bf16[4,112,128]{2,1,0:T(8,128)(2,1)S(1)} %get-tuple-element.40), channel_id=1, source_target_pairs={{0,12},{4,8},{8,4},{12,0},{1,13},{5,9},{9,5},{13,1},{2,14},{6,10},... | collective-permute-start | bytes 344072 | tf_op jit(solution)/shard_map/ppermute | solution.py:271
  19.6 0.0 collective-permute-start.8
  19.6 0.0 collective-permute-done.3.two_ref
  19.6 0.6 %collective-permute-start.6 = (bf16[4,128,128]{2,1,0:T(8,128)(2,1)S(1)}, bf16[4,128,128]{2,1,0:T(8,128)(2,1)S(1)}, u32[]{:S(2)}, u32[]{:S(2)}) collective-permute-start(bf16[4,128,128]{2,1,0:T(8,128)(2,1)S(1)} %get-tuple-element.38), channel_id=1, source_target_pairs={{0,4},{4,0},{8,12},{12,8},{1,5},{5,1},{9,13},{13,9},{2,6},{6,2},{1... | collective-permute-start | bytes 393224 | tf_op jit(solution)/shard_map/ppermute | solution.py:271
  20.3 0.0 collective-permute-done.4.three_ref
  20.3 0.0 collective-permute-done.2.one_ref
  20.3 0.1 here_kernel.1
  20.4 1.7 %collective-permute-start.7 = (bf16[4,128,128]{2,1,0:T(8,128)(2,1)S(1)}, bf16[4,128,128]{2,1,0:T(8,128)(2,1)S(1)}, u32[]{:S(2)}, u32[]{:S(2)}) collective-permute-start(bf16[4,128,128]{2,1,0:T(8,128)(2,1)S(1)} %get-tuple-element.39), channel_id=1, source_target_pairs={{0,2},{1,3},{2,0},{3,1},{4,6},{5,7},{6,4},{7,5},{8,10},{9,11},{10,... | collective-permute-start | bytes 393224 | tf_op jit(solution)/shard_map/ppermute | solution.py:271
  22.1 1.6 %collective-permute-done.9.three_ref = bf16[4,112,128]{2,1,0:T(8,128)(2,1)S(1)} collective-permute-done((bf16[4,112,128]{2,1,0:T(8,128)(2,1)S(1)}, bf16[4,112,128]{2,1,0:T(8,128)(2,1)S(1)}, u32[]{:S(2)}, u32[]{:S(2)}) %collective-permute-start.9) | collective-permute-done | bytes 114720 | tf_op jit(solution)/shard_map/ppermute | solution.py:271
  23.7 5.3 %collective-permute-done.8.two_ref = bf16[4,112,128]{2,1,0:T(8,128)(2,1)S(1)} collective-permute-done((bf16[4,112,128]{2,1,0:T(8,128)(2,1)S(1)}, bf16[4,112,128]{2,1,0:T(8,128)(2,1)S(1)}, u32[]{:S(2)}, u32[]{:S(2)}) %collective-permute-start.8) | collective-permute-done | bytes 114720 | tf_op jit(solution)/shard_map/ppermute | solution.py:271
  29.0 0.0 collective-permute-done.6.one_ref
  29.1 0.0 collective-permute-done.7.cross_ref
  29.1 0.7 %final_kernel.1 = bf16[4,128,128]{2,1,0:T(8,128)(2,1)} custom-call(bf16[4,128,128]{2,1,0:T(8,128)(2,1)S(1)} %get-tuple-element.25.mask_ref, f32[4,128,128]{2,1,0:T(8,128)S(1)} %get-tuple-element.37.near_ref, bf16[4,128,128]{2,1,0:T(8,128)(2,1)S(1)} %collective-permute-done.6.one_ref, bf16[4,128,128]{2,1,0:T(8,128)(2,1)S(1)} %collective-permute-done.7.cross_ref, ...), custom_call_target="tpu_custom_call" | custom-call | flops 100000000 | tf_op jit(solution)/shard_map/final_kernel/pallas_call | solution.py:290
  (1 shorter events, 0.0 us)
Async XLA Ops:
  4.2 2.1 %collective-permute-start = (bf16[4,544,128]{2,1,0:T(8,128)(2,1)S(1)}, bf16[4,544,128]{2,1,0:T(8,128)(2,1)S(1)}, u32[]{:S(2)}, u32[]{:S(2)}) collective-permute-start(bf16[4,544,128]{2,1,0:T(8,128)(2,1)S(1)} %get-tuple-element.28), channel_id=1, source_target_pairs={{0,1},{1,0},{2,3},{3,2},{4,5},{5,4},{6,7},{7,6},{8,9},{9,8},{10,11... | collective-permute-start | bytes 1671176 | tf_op jit(solution)/shard_map/ppermute | solution.py:271
  6.4 9.2 %collective-permute-start.1 = (bf16[4,480,128]{2,1,0:T(8,128)(2,1)S(1)}, bf16[4,480,128]{2,1,0:T(8,128)(2,1)S(1)}, u32[]{:S(2)}, u32[]{:S(2)}) collective-permute-start(bf16[4,480,128]{2,1,0:T(8,128)(2,1)S(1)} %get-tuple-element.30), channel_id=1, source_target_pairs={{0,1},{1,0},{2,3},{3,2},{4,5},{5,4},{6,7},{7,6},{8,9},{9,8},{10,11... | collective-permute-start | bytes 1474568 | tf_op jit(solution)/shard_map/ppermute | solution.py:271
  6.9 8.8 %collective-permute-start.5 = (bf16[4,224,128]{2,1,0:T(8,128)(2,1)S(1)}, bf16[4,224,128]{2,1,0:T(8,128)(2,1)S(1)}, u32[]{:S(2)}, u32[]{:S(2)}) collective-permute-start(bf16[4,224,128]{2,1,0:T(8,128)(2,1)S(1)} %get-tuple-element.34), channel_id=1, source_target_pairs={{0,2},{1,3},{2,0},{3,1},{4,6},{5,7},{6,4},{7,5},{8,10},{9,11},{10,... | collective-permute-start | bytes 688136 | tf_op jit(solution)/shard_map/ppermute | solution.py:271
  9.5 10.1 %collective-permute-start.3 = (bf16[2,4,16,128]{3,2,1,0:T(8,128)(2,1)S(1)}, bf16[2,4,16,128]{3,2,1,0:T(8,128)(2,1)S(1)}, u32[]{:S(2)}, u32[]{:S(2)}) collective-permute-start(bf16[2,4,16,128]{3,2,1,0:T(8,128)(2,1)S(1)} %get-tuple-element.32), channel_id=1, source_target_pairs={{0,8},{4,12},{8,0},{12,4},{1,9},{5,13},{9,1},{13,5},{2,10},{6,14},... | collective-permute-start | bytes 98312 | tf_op jit(solution)/shard_map/ppermute | solution.py:271
  12.1 8.2 %collective-permute-start.4 = (bf16[2,4,16,128]{3,2,1,0:T(8,128)(2,1)S(1)}, bf16[2,4,16,128]{3,2,1,0:T(8,128)(2,1)S(1)}, u32[]{:S(2)}, u32[]{:S(2)}) collective-permute-start(bf16[2,4,16,128]{3,2,1,0:T(8,128)(2,1)S(1)} %get-tuple-element.33), channel_id=1, source_target_pairs={{0,12},{4,8},{8,4},{12,0},{1,13},{5,9},{9,5},{13,1},{2,14},{6,10},... | collective-permute-start | bytes 98312 | tf_op jit(solution)/shard_map/ppermute | solution.py:271
  13.4 6.9 %collective-permute-start.2 = (bf16[4,128,128]{2,1,0:T(8,128)(2,1)S(1)}, bf16[4,128,128]{2,1,0:T(8,128)(2,1)S(1)}, u32[]{:S(2)}, u32[]{:S(2)}) collective-permute-start(bf16[4,128,128]{2,1,0:T(8,128)(2,1)S(1)} %get-tuple-element.31), channel_id=1, source_target_pairs={{0,4},{4,0},{8,12},{12,8},{1,5},{5,1},{9,13},{13,9},{2,6},{6,2},{1... | collective-permute-start | bytes 393224 | tf_op jit(solution)/shard_map/ppermute | solution.py:271
  15.7 8.0 %collective-permute-start.9 = (bf16[4,112,128]{2,1,0:T(8,128)(2,1)S(1)}, bf16[4,112,128]{2,1,0:T(8,128)(2,1)S(1)}, u32[]{:S(2)}, u32[]{:S(2)}) collective-permute-start(bf16[4,112,128]{2,1,0:T(8,128)(2,1)S(1)} %get-tuple-element.40), channel_id=1, source_target_pairs={{0,12},{4,8},{8,4},{12,0},{1,13},{5,9},{9,5},{13,1},{2,14},{6,10},... | collective-permute-start | bytes 344072 | tf_op jit(solution)/shard_map/ppermute | solution.py:271
  19.6 9.4 %collective-permute-start.8 = (bf16[4,112,128]{2,1,0:T(8,128)(2,1)S(1)}, bf16[4,112,128]{2,1,0:T(8,128)(2,1)S(1)}, u32[]{:S(2)}, u32[]{:S(2)}) collective-permute-start(bf16[4,112,128]{2,1,0:T(8,128)(2,1)S(1)} %get-tuple-element.36.after_ref), channel_id=1, source_target_pairs={{0,8},{4,12},{8,0},{12,4},{1,9},{5,13},{9,1},{13,5},{2,10},{6,14},... | collective-permute-start | bytes 344072 | tf_op jit(solution)/shard_map/ppermute | solution.py:271
  19.6 9.4 %collective-permute-start.6 = (bf16[4,128,128]{2,1,0:T(8,128)(2,1)S(1)}, bf16[4,128,128]{2,1,0:T(8,128)(2,1)S(1)}, u32[]{:S(2)}, u32[]{:S(2)}) collective-permute-start(bf16[4,128,128]{2,1,0:T(8,128)(2,1)S(1)} %get-tuple-element.38), channel_id=1, source_target_pairs={{0,4},{4,0},{8,12},{12,8},{1,5},{5,1},{9,13},{13,9},{2,6},{6,2},{1... | collective-permute-start | bytes 393224 | tf_op jit(solution)/shard_map/ppermute | solution.py:271
  20.4 8.7 %collective-permute-start.7 = (bf16[4,128,128]{2,1,0:T(8,128)(2,1)S(1)}, bf16[4,128,128]{2,1,0:T(8,128)(2,1)S(1)}, u32[]{:S(2)}, u32[]{:S(2)}) collective-permute-start(bf16[4,128,128]{2,1,0:T(8,128)(2,1)S(1)} %get-tuple-element.39), channel_id=1, source_target_pairs={{0,2},{1,3},{2,0},{3,1},{4,6},{5,7},{6,4},{7,5},{8,10},{9,11},{10,... | collective-permute-start | bytes 393224 | tf_op jit(solution)/shard_map/ppermute | solution.py:271

commit v16 on v15

--- a/solution.py
+++ b/solution.py
@@ -278,7 +278,7 @@
     terms = left_env.shape[1]
     targets = block_dims.shape[0]
     strip = width // 4
-    a_rows = strip * 7 // 8
+    a_rows = strip * 5 // 8
     b_rows = strip - a_rows
     vmem = pl.BlockSpec(memory_space=pltpu.VMEM)
     hbm = pl.BlockSpec(memory_space=pltpu.HBM)

time: 30 us -> 30.2 us (level)
  waiting for transfers between devices: 8.99 us -> 11.5 us
  starting transfers between devices: 14 us -> 11.8 us
    ppermute x10, waiting for transfers between devices: 8.99 us -> 11.5 us  [swap(): lax.ppermute(array, axis, [(i, i ^ mask) for i in range(lax.axis_size(axi...]
    ppermute x10, starting transfers between devices: 14 us -> 11.8 us  [swap(): lax.ppermute(array, axis, [(i, i ^ mask) for i in range(lax.axis_size(axi...]
  transfers between devices with their start and end apart: 10 -> 10, of which waited for: 4 -> 6; matrix products, arithmetic and copies ran while one was open for 0% -> 0% of each run, Pallas kernels for 6% -> 6%
where the time goes in v16:
time: 30.2 us; the launch traced here: 30.1 us
  starting transfers between devices  11.8 us (39%)
  waiting for transfers between devices  11.5 us (38%)
  Pallas kernels  6.73 us (22%)
    ppermute x10, starting transfers between devices, swap(): lax.ppermute(array, axis, [(i, i ^ mask) for i in range(lax.axis_size(axi...  11.8 us
    ppermute x10, waiting for transfers between devices, swap(): lax.ppermute(array, axis, [(i, i ^ mask) for i in range(lax.axis_size(axi...  11.5 us
    pallas_call x1, Pallas kernels, by_targets(): pl.pallas_call(send_kernel, out_shape=[lead_shape, rest_shape, half_shape...  4.17 us
    pallas_call x1, Pallas kernels, by_targets(): pl.pallas_call(keep_kernel, out_shape=[lead_shape, rest_shape, like(targe...  1.5 us
    pallas_call x5, Pallas kernels, call(): pl.pallas_call(kernel, out_shape=out_shape, in_specs=[vmem] * len(args),...  1.05 us
  transfers between devices with their start and end apart: 10, of which 6 were waited for; matrix products, arithmetic and copies ran while one was open for 0% of the time, Pallas kernels for 6%

profile of v16, /device:TPU:0, one launch (start us, length us, event | category | flops | bytes accessed | tf_op | source)
XLA Modules:
  0.0 30.1 jit_solution(13537491475853628357)
XLA Ops:
  0.0 4.2 %send_kernel.1 = (bf16[4,608,128]{2,1,0:T(8,128)(2,1)S(1)}, bf16[4,416,128]{2,1,0:T(8,128)(2,1)S(1)}, bf16[3,512,512]{2,1,0:T(8,128)(2,1)S(1)}, bf16[3,256,512]{2,1,0:T(8,128)(2,1)S(1)}) custom-call(s32[1,3]{1,0:T(1,128)} %cls_hbm.3, s32[1,3]{1,0:T(1,128)} %tid_hbm.3, s32[4,5]{1,0:T(4,128)} %pair_hbm.3, s32[2,4]{1,0:T(2,128)} %bitcast.1, f32[50]{0:T(128)} %coef_hbm.3, ...), custom_call_target="tpu_custom_call" | custom-call | flops 1207959552 | bytes 4194304 | tf_op jit(solution)/shard_map/send_kernel/pallas_call | solution.py:314
  4.2 0.5 %collective-permute-start = (bf16[4,608,128]{2,1,0:T(8,128)(2,1)S(1)}, bf16[4,608,128]{2,1,0:T(8,128)(2,1)S(1)}, u32[]{:S(2)}, u32[]{:S(2)}) collective-permute-start(bf16[4,608,128]{2,1,0:T(8,128)(2,1)S(1)} %get-tuple-element.28), channel_id=1, source_target_pairs={{0,1},{1,0},{2,3},{3,2},{4,5},{5,4},{6,7},{7,6},{8,9},{9,8},{10,11... | collective-permute-start | bytes 1867784 | tf_op jit(solution)/shard_map/ppermute | solution.py:271
  4.7 1.5 %keep_kernel.1 = (bf16[4,608,128]{2,1,0:T(8,128)(2,1)S(1)}, bf16[4,416,128]{2,1,0:T(8,128)(2,1)S(1)}, bf16[4,128,128]{2,1,0:T(8,128)(2,1)S(1)}) custom-call(s32[1,3]{1,0:T(1,128)} %cls_hbm.3, s32[1,3]{1,0:T(1,128)} %tid_hbm.3, s32[4,5]{1,0:T(4,128)} %pair_hbm.3, s32[2,4]{1,0:T(2,128)} %bitcast.2, f32[50]{0:T(128)} %coef_hbm.3, ...), custom_call_target="tpu_custom_call" | custom-call | flops 1207959552 | tf_op jit(solution)/shard_map/keep_kernel/pallas_call | solution.py:336
  6.2 0.2 collective-permute-done.recv_ref
  6.4 0.1 lead_kernel.1
  6.5 0.4 %collective-permute-start.1 = (bf16[4,416,128]{2,1,0:T(8,128)(2,1)S(1)}, bf16[4,416,128]{2,1,0:T(8,128)(2,1)S(1)}, u32[]{:S(2)}, u32[]{:S(2)}) collective-permute-start(bf16[4,416,128]{2,1,0:T(8,128)(2,1)S(1)} %get-tuple-element.30), channel_id=1, source_target_pairs={{0,1},{1,0},{2,3},{3,2},{4,5},{5,4},{6,7},{7,6},{8,9},{9,8},{10,11... | collective-permute-start | bytes 1277960 | tf_op jit(solution)/shard_map/ppermute | solution.py:271
  7.0 2.6 %collective-permute-start.5 = (bf16[4,160,128]{2,1,0:T(8,128)(2,1)S(1)}, bf16[4,160,128]{2,1,0:T(8,128)(2,1)S(1)}, u32[]{:S(2)}, u32[]{:S(2)}) collective-permute-start(bf16[4,160,128]{2,1,0:T(8,128)(2,1)S(1)} %get-tuple-element.34), channel_id=1, source_target_pairs={{0,2},{1,3},{2,0},{3,1},{4,6},{5,7},{6,4},{7,5},{8,10},{9,11},{10,... | collective-permute-start | bytes 491528 | tf_op jit(solution)/shard_map/ppermute | solution.py:271
  9.6 2.6 %collective-permute-start.3 = (bf16[2,4,48,128]{3,2,1,0:T(8,128)(2,1)S(1)}, bf16[2,4,48,128]{3,2,1,0:T(8,128)(2,1)S(1)}, u32[]{:S(2)}, u32[]{:S(2)}) collective-permute-start(bf16[2,4,48,128]{3,2,1,0:T(8,128)(2,1)S(1)} %get-tuple-element.32), channel_id=1, source_target_pairs={{0,8},{4,12},{8,0},{12,4},{1,9},{5,13},{9,1},{13,5},{2,10},{6,14},... | collective-permute-start | bytes 294920 | tf_op jit(solution)/shard_map/ppermute | solution.py:271
  12.2 1.3 %collective-permute-start.4 = (bf16[2,4,48,128]{3,2,1,0:T(8,128)(2,1)S(1)}, bf16[2,4,48,128]{3,2,1,0:T(8,128)(2,1)S(1)}, u32[]{:S(2)}, u32[]{:S(2)}) collective-permute-start(bf16[2,4,48,128]{3,2,1,0:T(8,128)(2,1)S(1)} %get-tuple-element.33), channel_id=1, source_target_pairs={{0,12},{4,8},{8,4},{12,0},{1,13},{5,9},{9,5},{13,1},{2,14},{6,10},... | collective-permute-start | bytes 294920 | tf_op jit(solution)/shard_map/ppermute | solution.py:271
  13.5 0.2 collective-permute-start.2
  13.8 0.6 %collective-permute-done.5.cross_ref = bf16[4,160,128]{2,1,0:T(8,128)(2,1)S(1)} collective-permute-done((bf16[4,160,128]{2,1,0:T(8,128)(2,1)S(1)}, bf16[4,160,128]{2,1,0:T(8,128)(2,1)S(1)}, u32[]{:S(2)}, u32[]{:S(2)}) %collective-permute-start.5) | collective-permute-done | bytes 163872 | tf_op jit(solution)/shard_map/ppermute | solution.py:271
  14.3 0.0 collective-permute-done.1.recv_ref
  14.3 0.1 own_kernel.1
  14.4 3.9 %collective-permute-start.9 = (bf16[4,80,128]{2,1,0:T(8,128)(2,1)S(1)}, bf16[4,80,128]{2,1,0:T(8,128)(2,1)S(1)}, u32[]{:S(2)}, u32[]{:S(2)}) collective-permute-start(bf16[4,80,128]{2,1,0:T(8,128)(2,1)S(1)} %get-tuple-element.40), channel_id=1, source_target_pairs={{0,12},{4,8},{8,4},{12,0},{1,13},{5,9},{9,5},{13,1},{2,14},{6,10},... | collective-permute-start | bytes 245768 | tf_op jit(solution)/shard_map/ppermute | solution.py:271
  18.3 0.0 collective-permute-start.8
  18.3 2.4 %collective-permute-done.3.two_ref = bf16[2,4,48,128]{3,2,1,0:T(8,128)(2,1)S(1)} collective-permute-done((bf16[2,4,48,128]{3,2,1,0:T(8,128)(2,1)S(1)}, bf16[2,4,48,128]{3,2,1,0:T(8,128)(2,1)S(1)}, u32[]{:S(2)}, u32[]{:S(2)}) %collective-permute-start.3) | collective-permute-done | bytes 98336 | tf_op jit(solution)/shard_map/ppermute | solution.py:271
  20.7 0.0 collective-permute-start.6
  20.7 0.0 collective-permute-done.4.three_ref
  20.7 3.5 %collective-permute-done.2.one_ref = bf16[4,128,128]{2,1,0:T(8,128)(2,1)S(1)} collective-permute-done((bf16[4,128,128]{2,1,0:T(8,128)(2,1)S(1)}, bf16[4,128,128]{2,1,0:T(8,128)(2,1)S(1)}, u32[]{:S(2)}, u32[]{:S(2)}) %collective-permute-start.2) | collective-permute-done | bytes 131104 | tf_op jit(solution)/shard_map/ppermute | solution.py:271
  24.2 0.1 here_kernel.1
  24.3 0.2 collective-permute-start.7
  24.5 0.0 collective-permute-done.9.three_ref
  24.5 4.2 %collective-permute-done.8.two_ref = bf16[4,80,128]{2,1,0:T(8,128)(2,1)S(1)} collective-permute-done((bf16[4,80,128]{2,1,0:T(8,128)(2,1)S(1)}, bf16[4,80,128]{2,1,0:T(8,128)(2,1)S(1)}, u32[]{:S(2)}, u32[]{:S(2)}) %collective-permute-start.8) | collective-permute-done | bytes 81952 | tf_op jit(solution)/shard_map/ppermute | solution.py:271
  28.7 0.0 collective-permute-done.6.one_ref
  28.7 0.6 %collective-permute-done.7.cross_ref = bf16[4,128,128]{2,1,0:T(8,128)(2,1)S(1)} collective-permute-done((bf16[4,128,128]{2,1,0:T(8,128)(2,1)S(1)}, bf16[4,128,128]{2,1,0:T(8,128)(2,1)S(1)}, u32[]{:S(2)}, u32[]{:S(2)}) %collective-permute-start.7) | collective-permute-done | bytes 131104 | tf_op jit(solution)/shard_map/ppermute | solution.py:271
  29.4 0.7 %final_kernel.1 = bf16[4,128,128]{2,1,0:T(8,128)(2,1)} custom-call(bf16[4,128,128]{2,1,0:T(8,128)(2,1)S(1)} %get-tuple-element.25.mask_ref, f32[4,128,128]{2,1,0:T(8,128)S(1)} %get-tuple-element.37.near_ref, bf16[4,128,128]{2,1,0:T(8,128)(2,1)S(1)} %collective-permute-done.6.one_ref, bf16[4,128,128]{2,1,0:T(8,128)(2,1)S(1)} %collective-permute-done.7.cross_ref, ...), custom_call_target="tpu_custom_call" | custom-call | flops 100000000 | tf_op jit(solution)/shard_map/final_kernel/pallas_call | solution.py:290
  (1 shorter events, 0.0 us)
Async XLA Ops:
  4.2 2.2 %collective-permute-start = (bf16[4,608,128]{2,1,0:T(8,128)(2,1)S(1)}, bf16[4,608,128]{2,1,0:T(8,128)(2,1)S(1)}, u32[]{:S(2)}, u32[]{:S(2)}) collective-permute-start(bf16[4,608,128]{2,1,0:T(8,128)(2,1)S(1)} %get-tuple-element.28), channel_id=1, source_target_pairs={{0,1},{1,0},{2,3},{3,2},{4,5},{5,4},{6,7},{7,6},{8,9},{9,8},{10,11... | collective-permute-start | bytes 1867784 | tf_op jit(solution)/shard_map/ppermute | solution.py:271
  6.5 7.8 %collective-permute-start.1 = (bf16[4,416,128]{2,1,0:T(8,128)(2,1)S(1)}, bf16[4,416,128]{2,1,0:T(8,128)(2,1)S(1)}, u32[]{:S(2)}, u32[]{:S(2)}) collective-permute-start(bf16[4,416,128]{2,1,0:T(8,128)(2,1)S(1)} %get-tuple-element.30), channel_id=1, source_target_pairs={{0,1},{1,0},{2,3},{3,2},{4,5},{5,4},{6,7},{7,6},{8,9},{9,8},{10,11... | collective-permute-start | bytes 1277960 | tf_op jit(solution)/shard_map/ppermute | solution.py:271
  7.0 7.4 %collective-permute-start.5 = (bf16[4,160,128]{2,1,0:T(8,128)(2,1)S(1)}, bf16[4,160,128]{2,1,0:T(8,128)(2,1)S(1)}, u32[]{:S(2)}, u32[]{:S(2)}) collective-permute-start(bf16[4,160,128]{2,1,0:T(8,128)(2,1)S(1)} %get-tuple-element.34), channel_id=1, source_target_pairs={{0,2},{1,3},{2,0},{3,1},{4,6},{5,7},{6,4},{7,5},{8,10},{9,11},{10,... | collective-permute-start | bytes 491528 | tf_op jit(solution)/shard_map/ppermute | solution.py:271
  9.6 11.1 %collective-permute-start.3 = (bf16[2,4,48,128]{3,2,1,0:T(8,128)(2,1)S(1)}, bf16[2,4,48,128]{3,2,1,0:T(8,128)(2,1)S(1)}, u32[]{:S(2)}, u32[]{:S(2)}) collective-permute-start(bf16[2,4,48,128]{3,2,1,0:T(8,128)(2,1)S(1)} %get-tuple-element.32), channel_id=1, source_target_pairs={{0,8},{4,12},{8,0},{12,4},{1,9},{5,13},{9,1},{13,5},{2,10},{6,14},... | collective-permute-start | bytes 294920 | tf_op jit(solution)/shard_map/ppermute | solution.py:271
  12.2 8.5 %collective-permute-start.4 = (bf16[2,4,48,128]{3,2,1,0:T(8,128)(2,1)S(1)}, bf16[2,4,48,128]{3,2,1,0:T(8,128)(2,1)S(1)}, u32[]{:S(2)}, u32[]{:S(2)}) collective-permute-start(bf16[2,4,48,128]{3,2,1,0:T(8,128)(2,1)S(1)} %get-tuple-element.33), channel_id=1, source_target_pairs={{0,12},{4,8},{8,4},{12,0},{1,13},{5,9},{9,5},{13,1},{2,14},{6,10},... | collective-permute-start | bytes 294920 | tf_op jit(solution)/shard_map/ppermute | solution.py:271
  13.5 10.7 %collective-permute-start.2 = (bf16[4,128,128]{2,1,0:T(8,128)(2,1)S(1)}, bf16[4,128,128]{2,1,0:T(8,128)(2,1)S(1)}, u32[]{:S(2)}, u32[]{:S(2)}) collective-permute-start(bf16[4,128,128]{2,1,0:T(8,128)(2,1)S(1)} %get-tuple-element.31), channel_id=1, source_target_pairs={{0,4},{4,0},{8,12},{12,8},{1,5},{5,1},{9,13},{13,9},{2,6},{6,2},{1... | collective-permute-start | bytes 393224 | tf_op jit(solution)/shard_map/ppermute | solution.py:271
  14.4 10.1 %collective-permute-start.9 = (bf16[4,80,128]{2,1,0:T(8,128)(2,1)S(1)}, bf16[4,80,128]{2,1,0:T(8,128)(2,1)S(1)}, u32[]{:S(2)}, u32[]{:S(2)}) collective-permute-start(bf16[4,80,128]{2,1,0:T(8,128)(2,1)S(1)} %get-tuple-element.40), channel_id=1, source_target_pairs={{0,12},{4,8},{8,4},{12,0},{1,13},{5,9},{9,5},{13,1},{2,14},{6,10},... | collective-permute-start | bytes 245768 | tf_op jit(solution)/shard_map/ppermute | solution.py:271
  18.3 10.4 %collective-permute-start.8 = (bf16[4,80,128]{2,1,0:T(8,128)(2,1)S(1)}, bf16[4,80,128]{2,1,0:T(8,128)(2,1)S(1)}, u32[]{:S(2)}, u32[]{:S(2)}) collective-permute-start(bf16[4,80,128]{2,1,0:T(8,128)(2,1)S(1)} %get-tuple-element.36.after_ref), channel_id=1, source_target_pairs={{0,8},{4,12},{8,0},{12,4},{1,9},{5,13},{9,1},{13,5},{2,10},{6,14},... | collective-permute-start | bytes 245768 | tf_op jit(solution)/shard_map/ppermute | solution.py:271
  20.7 8.0 %collective-permute-start.6 = (bf16[4,128,128]{2,1,0:T(8,128)(2,1)S(1)}, bf16[4,128,128]{2,1,0:T(8,128)(2,1)S(1)}, u32[]{:S(2)}, u32[]{:S(2)}) collective-permute-start(bf16[4,128,128]{2,1,0:T(8,128)(2,1)S(1)} %get-tuple-element.38), channel_id=1, source_target_pairs={{0,4},{4,0},{8,12},{12,8},{1,5},{5,1},{9,13},{13,9},{2,6},{6,2},{1... | collective-permute-start | bytes 393224 | tf_op jit(solution)/shard_map/ppermute | solution.py:271
  24.3 5.0 %collective-permute-start.7 = (bf16[4,128,128]{2,1,0:T(8,128)(2,1)S(1)}, bf16[4,128,128]{2,1,0:T(8,128)(2,1)S(1)}, u32[]{:S(2)}, u32[]{:S(2)}) collective-permute-start(bf16[4,128,128]{2,1,0:T(8,128)(2,1)S(1)} %get-tuple-element.39), channel_id=1, source_target_pairs={{0,2},{1,3},{2,0},{3,1},{4,6},{5,7},{6,4},{7,5},{8,10},{9,11},{10,... | collective-permute-start | bytes 393224 | tf_op jit(solution)/shard_map/ppermute | solution.py:271

commit v17 on v11

--- a/solution.py
+++ b/solution.py
@@ -246,14 +246,21 @@
     sum_ref[...] = total(two_ref[...], three_ref[...])
 
 
-def final_kernel(mask_ref, near_ref, one_ref, cross_ref, sum_ref, out_ref):
-    a_rows, strip = sum_ref.shape[1], out_ref.shape[1]
-    for first, last in ((0, a_rows), (a_rows, strip)):
-        parts = [ref[:, first:last, :] for ref in (near_ref, one_ref, cross_ref)]
-        if not first:
-            parts += [sum_ref[...]]
-        inside = mask_ref[:, first:last, :].astype(jnp.float32) > 0.0
-        out_ref[:, first:last, :] = jnp.where(inside, total(*parts), 0.0).astype(jnp.bfloat16)
+def final_kernel(mask_ref, near_ref, one_ref, cross_ref, sum_ref, out_hbm, out, sems):
+    a_rows, (targets, strip, _) = sum_ref.shape[1], out.shape
+    copies = []
+    for t in range(targets):
+        for first, last in ((0, a_rows), (a_rows, strip)):
+            parts = [ref[t, first:last, :] for ref in (near_ref, one_ref, cross_ref)]
+            if not first:
+                parts += [sum_ref[t]]
+            inside = mask_ref[t, first:last, :].astype(jnp.float32) > 0.0
+            out[t, first:last, :] = jnp.where(inside, total(*parts), 0.0).astype(jnp.bfloat16)
+        copy = pltpu.make_async_copy(out.at[t], out_hbm.at[t], sems.at[t])
+        copy.start()
+        copies.append(copy)
+    for copy in copies:
+        copy.wait()
 
 
 def total(*arrays):
@@ -386,7 +393,18 @@
     here = swap(here, "mpo", 2)
     far_sum = jax.ShapeDtypeStruct((targets, a_rows, strip), jnp.float32)
     far_sum = call(far_sum_kernel, far_sum, *own, span=3)
-    return call(final_kernel, like(targets, strip), mask, near, one_near, here, far_sum)
+    return pl.pallas_call(
+        final_kernel,
+        out_shape=like(targets, strip),
+        in_specs=[vmem] * 5,
+        out_specs=hbm,
+        scratch_shapes=[
+            pltpu.VMEM((targets, strip, strip), jnp.bfloat16),
+            pltpu.SemaphoreType.DMA((targets,)),
+        ],
+        compiler_params=SMALL,
+        name="final_kernel",
+    )(mask, near, one_near, here, far_sum)
 
 
 def by_classes(

time: 28.3 us -> 28.3 us (level)
    pallas_call x5 -> x4, Pallas kernels: 1.05 us -> 0.32 us  [call(): pl.pallas_call(kernel, out_shape=out_shape, in_specs=[vmem] * len(args),...]
    pallas_call x0 -> x1, Pallas kernels: none -> 0.73 us  [by_targets(): pl.pallas_call(final_kernel, out_shape=like(targets, strip), in_specs=[vm...]
where the time goes in v17:
time: 28.3 us; the launch traced here: 28.1 us
  starting transfers between devices  12.7 us (45%)
  waiting for transfers between devices  8.64 us (31%)
  Pallas kernels  6.72 us (24%)
    ppermute x10, starting transfers between devices, swap(): lax.ppermute(array, axis, [(i, i ^ mask) for i in range(lax.axis_size(axi...  12.7 us
    ppermute x10, waiting for transfers between devices, swap(): lax.ppermute(array, axis, [(i, i ^ mask) for i in range(lax.axis_size(axi...  8.64 us
    pallas_call x1, Pallas kernels, by_targets(): pl.pallas_call(send_kernel, out_shape=[lead_shape, rest_shape, half_shape...  4.17 us
    pallas_call x1, Pallas kernels, by_targets(): pl.pallas_call(keep_kernel, out_shape=[lead_shape, rest_shape, like(targe...  1.5 us
    pallas_call x1, Pallas kernels, by_targets(): pl.pallas_call(final_kernel, out_shape=like(targets, strip), in_specs=[vm...  0.73 us
  transfers between devices with their start and end apart: 10, of which 5 were waited for; matrix products, arithmetic and copies ran while one was open for 0% of the time, Pallas kernels for 6%

profile of v17, /device:TPU:0, one launch (start us, length us, event | category | flops | bytes accessed | tf_op | source)
XLA Modules:
  0.0 28.1 jit_solution(13882792207394353008)
XLA Ops:
  0.0 4.2 %send_kernel.1 = (bf16[4,576,128]{2,1,0:T(8,128)(2,1)S(1)}, bf16[4,448,128]{2,1,0:T(8,128)(2,1)S(1)}, bf16[3,512,512]{2,1,0:T(8,128)(2,1)S(1)}, bf16[3,256,512]{2,1,0:T(8,128)(2,1)S(1)}) custom-call(s32[1,3]{1,0:T(1,128)} %cls_hbm.3, s32[1,3]{1,0:T(1,128)} %tid_hbm.3, s32[4,5]{1,0:T(4,128)} %pair_hbm.3, s32[2,4]{1,0:T(2,128)} %bitcast.1, f32[50]{0:T(128)} %coef_hbm.3, ...), custom_call_target="tpu_custom_call" | custom-call | flops 1207959552 | bytes 4194304 | tf_op jit(solution)/shard_map/send_kernel/pallas_call | solution.py:321
  4.2 0.5 %collective-permute-start = (bf16[4,576,128]{2,1,0:T(8,128)(2,1)S(1)}, bf16[4,576,128]{2,1,0:T(8,128)(2,1)S(1)}, u32[]{:S(2)}, u32[]{:S(2)}) collective-permute-start(bf16[4,576,128]{2,1,0:T(8,128)(2,1)S(1)} %get-tuple-element.28), channel_id=1, source_target_pairs={{0,1},{1,0},{2,3},{3,2},{4,5},{5,4},{6,7},{7,6},{8,9},{9,8},{10,11... | collective-permute-start | bytes 1769480 | tf_op jit(solution)/shard_map/ppermute | solution.py:278
  4.7 1.5 %keep_kernel.1 = (bf16[4,576,128]{2,1,0:T(8,128)(2,1)S(1)}, bf16[4,448,128]{2,1,0:T(8,128)(2,1)S(1)}, bf16[4,128,128]{2,1,0:T(8,128)(2,1)S(1)}) custom-call(s32[1,3]{1,0:T(1,128)} %cls_hbm.3, s32[1,3]{1,0:T(1,128)} %tid_hbm.3, s32[4,5]{1,0:T(4,128)} %pair_hbm.3, s32[2,4]{1,0:T(2,128)} %bitcast.2, f32[50]{0:T(128)} %coef_hbm.3, ...), custom_call_target="tpu_custom_call" | custom-call | flops 1207959552 | tf_op jit(solution)/shard_map/keep_kernel/pallas_call | solution.py:343
  6.2 0.1 collective-permute-done.recv_ref
  6.3 0.1 lead_kernel.1
  6.5 0.4 %collective-permute-start.1 = (bf16[4,448,128]{2,1,0:T(8,128)(2,1)S(1)}, bf16[4,448,128]{2,1,0:T(8,128)(2,1)S(1)}, u32[]{:S(2)}, u32[]{:S(2)}) collective-permute-start(bf16[4,448,128]{2,1,0:T(8,128)(2,1)S(1)} %get-tuple-element.30), channel_id=1, source_target_pairs={{0,1},{1,0},{2,3},{3,2},{4,5},{5,4},{6,7},{7,6},{8,9},{9,8},{10,11... | collective-permute-start | bytes 1376264 | tf_op jit(solution)/shard_map/ppermute | solution.py:278
  6.9 2.6 %collective-permute-start.5 = (bf16[4,192,128]{2,1,0:T(8,128)(2,1)S(1)}, bf16[4,192,128]{2,1,0:T(8,128)(2,1)S(1)}, u32[]{:S(2)}, u32[]{:S(2)}) collective-permute-start(bf16[4,192,128]{2,1,0:T(8,128)(2,1)S(1)} %get-tuple-element.34), channel_id=1, source_target_pairs={{0,2},{1,3},{2,0},{3,1},{4,6},{5,7},{6,4},{7,5},{8,10},{9,11},{10,... | collective-permute-start | bytes 589832 | tf_op jit(solution)/shard_map/ppermute | solution.py:278
  9.5 2.6 %collective-permute-start.3 = (bf16[2,4,32,128]{3,2,1,0:T(8,128)(2,1)S(1)}, bf16[2,4,32,128]{3,2,1,0:T(8,128)(2,1)S(1)}, u32[]{:S(2)}, u32[]{:S(2)}) collective-permute-start(bf16[2,4,32,128]{3,2,1,0:T(8,128)(2,1)S(1)} %get-tuple-element.32), channel_id=1, source_target_pairs={{0,8},{4,12},{8,0},{12,4},{1,9},{5,13},{9,1},{13,5},{2,10},{6,14},... | collective-permute-start | bytes 196616 | tf_op jit(solution)/shard_map/ppermute | solution.py:278
  12.1 1.3 %collective-permute-start.4 = (bf16[2,4,32,128]{3,2,1,0:T(8,128)(2,1)S(1)}, bf16[2,4,32,128]{3,2,1,0:T(8,128)(2,1)S(1)}, u32[]{:S(2)}, u32[]{:S(2)}) collective-permute-start(bf16[2,4,32,128]{3,2,1,0:T(8,128)(2,1)S(1)} %get-tuple-element.33), channel_id=1, source_target_pairs={{0,12},{4,8},{8,4},{12,0},{1,13},{5,9},{9,5},{13,1},{2,14},{6,10},... | collective-permute-start | bytes 196616 | tf_op jit(solution)/shard_map/ppermute | solution.py:278
  13.5 0.2 collective-permute-start.2
  13.7 1.3 %collective-permute-done.5.cross_ref = bf16[4,192,128]{2,1,0:T(8,128)(2,1)S(1)} collective-permute-done((bf16[4,192,128]{2,1,0:T(8,128)(2,1)S(1)}, bf16[4,192,128]{2,1,0:T(8,128)(2,1)S(1)}, u32[]{:S(2)}, u32[]{:S(2)}) %collective-permute-start.5) | collective-permute-done | bytes 196640 | tf_op jit(solution)/shard_map/ppermute | solution.py:278
  15.0 0.0 collective-permute-done.1.recv_ref
  15.0 0.1 own_kernel.1
  15.1 3.9 %collective-permute-start.9 = (bf16[4,96,128]{2,1,0:T(8,128)(2,1)S(1)}, bf16[4,96,128]{2,1,0:T(8,128)(2,1)S(1)}, u32[]{:S(2)}, u32[]{:S(2)}) collective-permute-start(bf16[4,96,128]{2,1,0:T(8,128)(2,1)S(1)} %get-tuple-element.40), channel_id=1, source_target_pairs={{0,12},{4,8},{8,4},{12,0},{1,13},{5,9},{9,5},{13,1},{2,14},{6,10},... | collective-permute-start | bytes 294920 | tf_op jit(solution)/shard_map/ppermute | solution.py:278
  19.0 0.0 collective-permute-start.8
  19.0 0.0 collective-permute-done.3.two_ref
  19.0 0.6 %collective-permute-start.6 = (bf16[4,128,128]{2,1,0:T(8,128)(2,1)S(1)}, bf16[4,128,128]{2,1,0:T(8,128)(2,1)S(1)}, u32[]{:S(2)}, u32[]{:S(2)}) collective-permute-start(bf16[4,128,128]{2,1,0:T(8,128)(2,1)S(1)} %get-tuple-element.38), channel_id=1, source_target_pairs={{0,4},{4,0},{8,12},{12,8},{1,5},{5,1},{9,13},{13,9},{2,6},{6,2},{1... | collective-permute-start | bytes 393224 | tf_op jit(solution)/shard_map/ppermute | solution.py:278
  19.6 0.0 collective-permute-done.4.three_ref
  19.6 1.3 %collective-permute-done.2.one_ref = bf16[4,128,128]{2,1,0:T(8,128)(2,1)S(1)} collective-permute-done((bf16[4,128,128]{2,1,0:T(8,128)(2,1)S(1)}, bf16[4,128,128]{2,1,0:T(8,128)(2,1)S(1)}, u32[]{:S(2)}, u32[]{:S(2)}) %collective-permute-start.2) | collective-permute-done | bytes 131104 | tf_op jit(solution)/shard_map/ppermute | solution.py:278
  20.9 0.1 here_kernel.1
  21.0 0.4 %collective-permute-start.7 = (bf16[4,128,128]{2,1,0:T(8,128)(2,1)S(1)}, bf16[4,128,128]{2,1,0:T(8,128)(2,1)S(1)}, u32[]{:S(2)}, u32[]{:S(2)}) collective-permute-start(bf16[4,128,128]{2,1,0:T(8,128)(2,1)S(1)} %get-tuple-element.39), channel_id=1, source_target_pairs={{0,2},{1,3},{2,0},{3,1},{4,6},{5,7},{6,4},{7,5},{8,10},{9,11},{10,... | collective-permute-start | bytes 393224 | tf_op jit(solution)/shard_map/ppermute | solution.py:278
  21.4 2.5 %collective-permute-done.9.three_ref = bf16[4,96,128]{2,1,0:T(8,128)(2,1)S(1)} collective-permute-done((bf16[4,96,128]{2,1,0:T(8,128)(2,1)S(1)}, bf16[4,96,128]{2,1,0:T(8,128)(2,1)S(1)}, u32[]{:S(2)}, u32[]{:S(2)}) %collective-permute-start.9) | collective-permute-done | bytes 98336 | tf_op jit(solution)/shard_map/ppermute | solution.py:278
  23.9 3.4 %collective-permute-done.8.two_ref = bf16[4,96,128]{2,1,0:T(8,128)(2,1)S(1)} collective-permute-done((bf16[4,96,128]{2,1,0:T(8,128)(2,1)S(1)}, bf16[4,96,128]{2,1,0:T(8,128)(2,1)S(1)}, u32[]{:S(2)}, u32[]{:S(2)}) %collective-permute-start.8) | collective-permute-done | bytes 98336 | tf_op jit(solution)/shard_map/ppermute | solution.py:278
  27.4 0.0 collective-permute-done.6.one_ref
  27.4 0.0 collective-permute-done.7.cross_ref
  27.4 0.7 %final_kernel.1 = bf16[4,128,128]{2,1,0:T(8,128)(2,1)} custom-call(bf16[4,128,128]{2,1,0:T(8,128)(2,1)S(1)} %get-tuple-element.25.mask_ref, f32[4,128,128]{2,1,0:T(8,128)S(1)} %get-tuple-element.37.near_ref, bf16[4,128,128]{2,1,0:T(8,128)(2,1)S(1)} %collective-permute-done.6.one_ref, bf16[4,128,128]{2,1,0:T(8,128)(2,1)S(1)} %collective-permute-done.7.cross_ref, ...), custom_call_target="tpu_custom_call" | custom-call | tf_op jit(solution)/shard_map/final_kernel/pallas_call | solution.py:396
  (1 shorter events, 0.0 us)
Async XLA Ops:
  4.2 2.2 %collective-permute-start = (bf16[4,576,128]{2,1,0:T(8,128)(2,1)S(1)}, bf16[4,576,128]{2,1,0:T(8,128)(2,1)S(1)}, u32[]{:S(2)}, u32[]{:S(2)}) collective-permute-start(bf16[4,576,128]{2,1,0:T(8,128)(2,1)S(1)} %get-tuple-element.28), channel_id=1, source_target_pairs={{0,1},{1,0},{2,3},{3,2},{4,5},{5,4},{6,7},{7,6},{8,9},{9,8},{10,11... | collective-permute-start | bytes 1769480 | tf_op jit(solution)/shard_map/ppermute | solution.py:278
  6.5 8.5 %collective-permute-start.1 = (bf16[4,448,128]{2,1,0:T(8,128)(2,1)S(1)}, bf16[4,448,128]{2,1,0:T(8,128)(2,1)S(1)}, u32[]{:S(2)}, u32[]{:S(2)}) collective-permute-start(bf16[4,448,128]{2,1,0:T(8,128)(2,1)S(1)} %get-tuple-element.30), channel_id=1, source_target_pairs={{0,1},{1,0},{2,3},{3,2},{4,5},{5,4},{6,7},{7,6},{8,9},{9,8},{10,11... | collective-permute-start | bytes 1376264 | tf_op jit(solution)/shard_map/ppermute | solution.py:278
  6.9 8.1 %collective-permute-start.5 = (bf16[4,192,128]{2,1,0:T(8,128)(2,1)S(1)}, bf16[4,192,128]{2,1,0:T(8,128)(2,1)S(1)}, u32[]{:S(2)}, u32[]{:S(2)}) collective-permute-start(bf16[4,192,128]{2,1,0:T(8,128)(2,1)S(1)} %get-tuple-element.34), channel_id=1, source_target_pairs={{0,2},{1,3},{2,0},{3,1},{4,6},{5,7},{6,4},{7,5},{8,10},{9,11},{10,... | collective-permute-start | bytes 589832 | tf_op jit(solution)/shard_map/ppermute | solution.py:278
  9.5 9.4 %collective-permute-start.3 = (bf16[2,4,32,128]{3,2,1,0:T(8,128)(2,1)S(1)}, bf16[2,4,32,128]{3,2,1,0:T(8,128)(2,1)S(1)}, u32[]{:S(2)}, u32[]{:S(2)}) collective-permute-start(bf16[2,4,32,128]{3,2,1,0:T(8,128)(2,1)S(1)} %get-tuple-element.32), channel_id=1, source_target_pairs={{0,8},{4,12},{8,0},{12,4},{1,9},{5,13},{9,1},{13,5},{2,10},{6,14},... | collective-permute-start | bytes 196616 | tf_op jit(solution)/shard_map/ppermute | solution.py:278
  12.1 7.5 %collective-permute-start.4 = (bf16[2,4,32,128]{3,2,1,0:T(8,128)(2,1)S(1)}, bf16[2,4,32,128]{3,2,1,0:T(8,128)(2,1)S(1)}, u32[]{:S(2)}, u32[]{:S(2)}) collective-permute-start(bf16[2,4,32,128]{3,2,1,0:T(8,128)(2,1)S(1)} %get-tuple-element.33), channel_id=1, source_target_pairs={{0,12},{4,8},{8,4},{12,0},{1,13},{5,9},{9,5},{13,1},{2,14},{6,10},... | collective-permute-start | bytes 196616 | tf_op jit(solution)/shard_map/ppermute | solution.py:278
  13.5 7.5 %collective-permute-start.2 = (bf16[4,128,128]{2,1,0:T(8,128)(2,1)S(1)}, bf16[4,128,128]{2,1,0:T(8,128)(2,1)S(1)}, u32[]{:S(2)}, u32[]{:S(2)}) collective-permute-start(bf16[4,128,128]{2,1,0:T(8,128)(2,1)S(1)} %get-tuple-element.31), channel_id=1, source_target_pairs={{0,4},{4,0},{8,12},{12,8},{1,5},{5,1},{9,13},{13,9},{2,6},{6,2},{1... | collective-permute-start | bytes 393224 | tf_op jit(solution)/shard_map/ppermute | solution.py:278
  15.1 8.9 %collective-permute-start.9 = (bf16[4,96,128]{2,1,0:T(8,128)(2,1)S(1)}, bf16[4,96,128]{2,1,0:T(8,128)(2,1)S(1)}, u32[]{:S(2)}, u32[]{:S(2)}) collective-permute-start(bf16[4,96,128]{2,1,0:T(8,128)(2,1)S(1)} %get-tuple-element.40), channel_id=1, source_target_pairs={{0,12},{4,8},{8,4},{12,0},{1,13},{5,9},{9,5},{13,1},{2,14},{6,10},... | collective-permute-start | bytes 294920 | tf_op jit(solution)/shard_map/ppermute | solution.py:278
  19.0 8.4 %collective-permute-start.8 = (bf16[4,96,128]{2,1,0:T(8,128)(2,1)S(1)}, bf16[4,96,128]{2,1,0:T(8,128)(2,1)S(1)}, u32[]{:S(2)}, u32[]{:S(2)}) collective-permute-start(bf16[4,96,128]{2,1,0:T(8,128)(2,1)S(1)} %get-tuple-element.36.after_ref), channel_id=1, source_target_pairs={{0,8},{4,12},{8,0},{12,4},{1,9},{5,13},{9,1},{13,5},{2,10},{6,14},... | collective-permute-start | bytes 294920 | tf_op jit(solution)/shard_map/ppermute | solution.py:278
  19.0 8.4 %collective-permute-start.6 = (bf16[4,128,128]{2,1,0:T(8,128)(2,1)S(1)}, bf16[4,128,128]{2,1,0:T(8,128)(2,1)S(1)}, u32[]{:S(2)}, u32[]{:S(2)}) collective-permute-start(bf16[4,128,128]{2,1,0:T(8,128)(2,1)S(1)} %get-tuple-element.38), channel_id=1, source_target_pairs={{0,4},{4,0},{8,12},{12,8},{1,5},{5,1},{9,13},{13,9},{2,6},{6,2},{1... | collective-permute-start | bytes 393224 | tf_op jit(solution)/shard_map/ppermute | solution.py:278
  21.0 6.4 %collective-permute-start.7 = (bf16[4,128,128]{2,1,0:T(8,128)(2,1)S(1)}, bf16[4,128,128]{2,1,0:T(8,128)(2,1)S(1)}, u32[]{:S(2)}, u32[]{:S(2)}) collective-permute-start(bf16[4,128,128]{2,1,0:T(8,128)(2,1)S(1)} %get-tuple-element.39), channel_id=1, source_target_pairs={{0,2},{1,3},{2,0},{3,1},{4,6},{5,7},{6,4},{7,5},{8,10},{9,11},{10,... | collective-permute-start | bytes 393224 | tf_op jit(solution)/shard_map/ppermute | solution.py:278
